TPU v7x, 32 devices: a whole 2x2x4 slice. The times are simulated.
32 devices in a mesh: pool: 4 (over y, x), seq: 8 (over z, core).
Axes of the slice: x: 2, y: 2, z: 4, core: 2. Of those that a mesh axis runs over, the one named last changes fastest.
Arguments:
- pool_kv: bfloat16 [16, 1024, 1024], P('pool', 'seq'), may hold values from -4 to 4
- span_home: int32 [12], replicated, may hold values from 0 to 15, as said below
- span_order: int32 [4, 3], P('pool'), may hold values from 0 to 11, as said below
- chosen: int32 [4, 3], P('pool'), may hold values from 0 to 23, as said below
- fresh_q: bfloat16 [4, 384, 6144], P('pool', 'seq'), may hold values from -300 to 300
- fresh_kv: bfloat16 [4, 384, 1024], P('pool', 'seq'), may hold values from -5 to 5
Outputs:
- attended: bfloat16 [4, 384, 6144], P('pool', 'seq')
- decode_kv: bfloat16 [4, 8, 4, 24, 4096], P('pool', 'seq')
Inputs may be any that keep to these rules, and one draw needn't show every extreme that they name: `span_home`: all entries differ; home // 4 is the replica of a passage, and the 3 passages r * 3 to r * 3 + 2 of request r lie on different replicas; some replica holds a passage of every request. `span_order`: row r orders the passages r * 3 to r * 3 + 2. `chosen`: each row lists 3 different blocks in rising order; block k holds positions k * 128 to k * 128 + 127.
All inputs are finite; a program needn't handle non-finite values.
Results may differ from a plain program's by a relative error of at most 0.0035.
Values may be sent and summed in bfloat16 or wider, within the bound.
No kernel may reach another device: no remote copies, remote signals or barrier semaphores. Data moves between devices by JAX's collectives and lax.ppermute only.
A program may use at most 192 MiB of HBM per device.

v0:
```python
import math

import jax
import jax.numpy as jnp
from jax import lax
from jax.sharding import PartitionSpec as P

KV_HEADS = 4
HEAD_DIM = 128


masked_low = -1e30


def patch_rows(values, positions, picked, fresh_all, block_len):
    block_ids = positions // block_len
    offsets = positions % block_len
    matches = block_ids[..., None] == picked
    is_fresh = jnp.any(matches, axis=-1)
    slot_ids = jnp.sum(jnp.where(matches, jnp.arange(picked.shape[0], dtype=jnp.int32), 0), axis=-1)
    source = (slot_ids * block_len + offsets).reshape(-1)
    rows_new = jnp.take(fresh_all, source, axis=0).reshape(values.shape)
    return jnp.where(is_fresh[..., None], rows_new, values)


def fold_keys(state_in, shard_piece, queries, query_pos, span_len):
    span_count, piece_rows, kv_width = shard_piece.shape
    key_pos = (
        jnp.arange(span_count, dtype=jnp.int32)[:, None] * span_len
        + jnp.arange(piece_rows, dtype=jnp.int32)[None, :]
    )
    kv_heads, query_rows, head_dim = queries.shape
    flattened = shard_piece.reshape(span_count * piece_rows, kv_heads, 2, head_dim)
    keys_all = flattened[:, :, 0]
    values_all = flattened[:, :, 1]
    pos_all = key_pos.reshape(-1)
    key_count = span_count * piece_rows
    step_len = math.gcd(key_count, 512)
    inv_root = head_dim ** (-0.5)

    def one_block(state_now, turn_at):
        running_max, total_weight, weighted = state_now
        first_key = turn_at * step_len
        key_blk = lax.dynamic_slice_in_dim(keys_all, first_key, step_len, 0)
        value_blk = lax.dynamic_slice_in_dim(values_all, first_key, step_len, 0)
        pos_blk = lax.dynamic_slice_in_dim(pos_all, first_key, step_len, 0)
        scores = (
            jnp.einsum("hqd,khd->hqk", queries, key_blk, preferred_element_type=jnp.float32)
            * inv_root
        )
        allowed = pos_blk[None, None, :] <= query_pos[None, :, None]
        scores = jnp.where(allowed, scores, masked_low)
        newest = jnp.maximum(running_max, jnp.max(scores, axis=-1))
        weights = jnp.where(allowed, jnp.exp(scores - newest[..., None]), 0.0)
        factor = jnp.exp(running_max - newest)
        total_weight = total_weight * factor + jnp.sum(weights, axis=-1)
        weighted = weighted * factor[..., None] + jnp.einsum(
            "hqk,khd->hqd",
            weights.astype(jnp.bfloat16),
            value_blk,
            preferred_element_type=jnp.float32,
        )
        return ((newest, total_weight, weighted), None)

    state_out, _ = lax.scan(one_block, state_in, jnp.arange(key_count // step_len))
    return state_out


def shards(pool_kv, span_home, span_order, chosen, fresh_q, fresh_kv):
    pool_count = lax.axis_size("pool")
    seq_count = lax.axis_size("seq")
    replica = lax.axis_index("pool")
    my_seat = lax.axis_index("seq")
    slot_count, block_len, kv_width = pool_kv.shape
    span_count = span_order.shape[1]
    span_len = block_len * seq_count
    head_dim = HEAD_DIM
    kv_heads = KV_HEADS
    picked = chosen[0]
    span_total = span_home.shape[0]
    home_replica = span_home // slot_count
    home_slot = span_home % slot_count
    span_request = jnp.arange(span_total, dtype=jnp.int32) // span_count
    requests = jnp.arange(pool_count, dtype=jnp.int32)
    held = (home_replica == replica)[None, :] & (span_request[None, :] == requests[:, None])
    in_slot = home_slot[None, :, None] == jnp.arange(slot_count, dtype=jnp.int32)[None, None, :]
    selector = jnp.any(held[:, :, None] & in_slot, axis=1).astype(jnp.bfloat16)
    outgoing = jnp.einsum(
        "rk,ktc->rtc", selector, pool_kv, preferred_element_type=jnp.float32
    ).astype(jnp.bfloat16)
    arrived = lax.all_to_all(outgoing, "pool", split_axis=0, concat_axis=0, tiled=True)
    order_row = span_order[0]
    lookup = order_row[:, None] == jnp.arange(span_total, dtype=jnp.int32)[None, :]
    source_replica = jnp.sum(jnp.where(lookup, home_replica[None, :], 0), axis=1)
    chooser = (source_replica[:, None] == requests[None, :]).astype(jnp.bfloat16)
    cached = jnp.einsum("jp,ptc->jtc", chooser, arrived, preferred_element_type=jnp.float32).astype(
        jnp.bfloat16
    )
    fresh_all = lax.all_gather(fresh_kv[0], "seq", axis=0, tiled=True)
    block_ids = jnp.arange(span_count, dtype=jnp.int32)[:, None] * seq_count + my_seat
    local_pos = block_ids * block_len + jnp.arange(block_len, dtype=jnp.int32)[None, :]
    patched = patch_rows(cached, local_pos, picked, fresh_all, block_len)
    row_count = fresh_q.shape[1]
    q_width = fresh_q.shape[2]
    group = q_width // (kv_heads * head_dim)
    list_rows = my_seat * row_count + jnp.arange(row_count, dtype=jnp.int32)
    list_block = list_rows // block_len
    base_block = jnp.sum(
        jnp.where(
            list_block[:, None] == jnp.arange(picked.shape[0], dtype=jnp.int32)[None, :],
            picked[None, :],
            0,
        ),
        axis=1,
    )
    query_pos = base_block * block_len + list_rows % block_len
    queries = fresh_q[0].reshape(row_count, kv_heads, group, head_dim).transpose(1, 2, 0, 3)
    queries = queries.reshape(kv_heads, group * row_count, head_dim)
    pos_tiled = jnp.tile(query_pos, group)
    start_state = (
        jnp.full((kv_heads, group * row_count), masked_low, jnp.float32),
        jnp.zeros((kv_heads, group * row_count), jnp.float32),
        jnp.zeros((kv_heads, group * row_count, head_dim), jnp.float32),
    )
    final_state = fold_keys(
        start_state,
        lax.all_gather(patched, "seq", axis=1, tiled=True),
        queries,
        pos_tiled,
        span_len,
    )
    running_max, total_weight, weighted = final_state
    attended = (weighted / total_weight[..., None]).reshape(kv_heads, group, row_count, head_dim)
    attended = attended.transpose(2, 0, 1, 3).reshape(1, row_count, q_width).astype(jnp.bfloat16)
    per_group = kv_heads // pool_count
    run_len = block_len // seq_count
    laid = patched.reshape(span_count, seq_count, run_len, pool_count, per_group, 2 * head_dim)
    laid = laid.transpose(3, 1, 4, 0, 2, 5).reshape(
        pool_count, seq_count, per_group, span_count, run_len * 2 * head_dim
    )
    landed = lax.all_to_all(
        lax.all_to_all(laid, "pool", split_axis=0, concat_axis=0, tiled=True),
        "seq",
        split_axis=1,
        concat_axis=1,
        tiled=True,
    )
    decoded = landed.transpose(2, 0, 3, 1, 4).reshape(
        per_group, 1, pool_count, span_count * seq_count, run_len * 2 * head_dim
    )
    return (attended, decoded)


def solution(mesh):
    in_specs = (
        P("pool", "seq", None),
        P(),
        P("pool", None),
        P("pool", None),
        P("pool", "seq", None),
        P("pool", "seq", None),
    )
    out_specs = (P("pool", "seq", None), P("pool", "seq", None, None, None))
    return jax.shard_map(shards, mesh=mesh, in_specs=in_specs, out_specs=out_specs, check_vma=False)
```

profile of v0, /device:TPU:0, one launch (start us, length us, event | category | flops | bytes accessed | tf_op | source)
XLA Modules:
  0.0 240.8 jit_solution(4561812580942280185)
XLA Ops:
  7.2 0.8 and_select_fusion.1
  8.0 0.7 broadcast_compare_fusion.1
  8.7 0.2 and_reduce_fusion
  8.8 0.9 convolution_convert_fusion.1
  9.7 1.3 copy.77
  11.0 5.3 %all-to-all-start = ((bf16[4,128,1024]{2,1,0:T(8,128)(2,1)}), bf16[4,128,1024]{2,1,0:T(8,128)(2,1)S(1)}, u32[]{:S(2)}, u32[]{:S(2)}) async-start(bf16[4,128,1024]{2,1,0:T(8,128)(2,1)} %copy.77), calls=%async_computation | async-start | bytes 2097152 | tf_op jit(solution)/shard_map/all_to_all | solution.py:91
  16.6 0.1 copy.74
  16.7 0.1 compare_reduce_fusion
  16.8 0.1 copy.73
  17.0 15.8 %all-gather = bf16[1,384,1024]{2,1,0:T(8,128)(2,1)S(1)} all-gather(bf16[1,48,1024]{2,1,0:T(8,128)(2,1)S(1)} %copy-done.3), channel_id=2, replica_groups=mesh['pool'=4,'seq'=8] {'seq'}, dimensions={1}, use_global_device_ids=true | all-gather | bytes 884736 | tf_op jit(solution)/shard_map/all_gather | solution.py:99
  32.8 2.7 %gather_fusion = bf16[384,1024]{1,0:T(8,128)(2,1)} fusion(bf16[384,1024]{1,0:T(8,128)(2,1)S(1)} %bitcast.76, s32[1024]{0:T(1024)S(1)} %pad_clamp_fusion), kind=kCustom, calls=%fused_computation | custom fusion | bytes 1574400 | tf_op jit(solution)/shard_map/jit(_take)/gather | solution.py:22
  35.5 0.2 select_reduce_fusion
  35.7 3.6 %fusion.20 = bf16[3,128,1024]{2,0,1:T(4,128)(2,1)S(1)} fusion(bf16[4,128,1024]{2,1,0:T(8,128)(2,1)S(1)} %all-to-all-done, bf16[3,128,1024]{2,1,0:T(8,128)(2,1)} %bitcast.84, pred[3,128]{0,1:T(8,128)(4,1)S(1)} %copy.74, pred[3,128]{0,1:T(8,128)(4,1)S(1)} %copy.73, s32[3]{0:T(128)S(1)} %select_reduce_fusion), kind=kOutput, calls=%fused_computation.28 | convolution fusion | flops 4325388 | bytes 2622220 | tf_op jit(solution)/shard_map/jp,ptc->jtc/dot_general | solution.py:96
  39.2 1.2 copy.79
  40.5 0.7 reshape.348
  41.2 0.4 copy.110
  41.6 0.1 copy.85
  41.7 0.4 reshape.335
  42.1 15.8 %all_to_all.15 = bf16[4,8,1,3,4096]{4,1,3,2,0:T(8,128)(2,1)S(1)} all-to-all(bf16[4,8,1,3,4096]{4,1,3,2,0:T(8,128)(2,1)S(1)} %bitcast.79), channel_id=1, replica_groups=mesh['pool'=4,'seq'=8] {'pool'}, dimensions={0} | all-to-all | bytes 1572864 | tf_op jit(solution)/shard_map/all_to_all | solution.py:142
  57.9 1.5 copy.87
  59.4 4.8 %all-to-all-start.2 = ((bf16[4,8,1,3,4096]{4,0,3,2,1:T(4,128)(2,1)}), bf16[4,8,1,3,4096]{4,0,3,2,1:T(4,128)(2,1)S(1)}, u32[]{:S(2)}, u32[]{:S(2)}) async-start(bf16[4,8,1,3,4096]{4,0,3,2,1:T(4,128)(2,1)} %copy.87), calls=%async_computation.2 | async-start | bytes 1572864 | tf_op jit(solution)/shard_map/all_to_all | solution.py:141
  64.2 1.5 reshape_squeeze.3
  65.8 0.4 copy.81
  66.3 0.1 select_reduce_fusion.1
  66.4 39.6 %all-to-all-done.2 = bf16[4,8,1,3,4096]{4,0,3,2,1:T(4,128)(2,1)S(1)} async-done(((bf16[4,8,1,3,4096]{4,0,3,2,1:T(4,128)(2,1)}), bf16[4,8,1,3,4096]{4,0,3,2,1:T(4,128)(2,1)S(1)}, u32[]{:S(2)}, u32[]{:S(2)}) %all-to-all-start.2) | async-done | bytes 786464 | tf_op jit(solution)/shard_map/all_to_all | solution.py:141
  105.9 1.3 copy.111
  107.2 16.4 %all-gather.3.cloned.1.call-done = bf16[3,1024,1024]{2,1,0:T(8,128)(2,1)} async-done(((bf16[3,128,1024]{2,1,0:T(8,128)(2,1)}), bf16[3,1024,1024]{2,1,0:T(8,128)(2,1)}) %all-gather.3.cloned.1.call-update) | async-done | bytes 6291472 | tf_op jit(solution)/shard_map/all_gather | solution.py:127
  123.6 11.0 %reshape.332 = bf16[3072,4,2,128]{3,2,1,0:T(2,128)(2,1)} reshape(bf16[3,1024,1024]{2,1,0:T(8,128)(2,1)} %all-gather.3.cloned.1.call-done) | data formatting | bytes 12582912 | tf_op jit(solution)/shard_map/reshape | solution.py:33
  134.6 13.4 %fusion.38 = (bf16[3072,4,1,128]{3,2,1,0:T(2,128)(2,1)S(1)}, bf16[3072,4,1,128]{3,2,1,0:T(2,128)(2,1)}) fusion(bf16[3072,4,2,128]{3,2,1,0:T(2,128)(2,1)} %reshape.332), kind=kLoop, calls=%fused_computation.94 | loop fusion | bytes 12582912 | tf_op jit(solution)/shard_map/slice | solution.py:35
  148.1 6.7 %copy_bitcast_fusion = (bf16[3072,4,128]{2,0,1:T(8,128)(2,1)}, bf16[3072,4,128]{2,0,1:T(8,128)(2,1)}) fusion(bf16[3072,4,1,128]{3,2,1,0:T(2,128)(2,1)S(1)} %get-tuple-element.129, bf16[3072,4,1,128]{3,2,1,0:T(2,128)(2,1)} %get-tuple-element.130), kind=kLoop, calls=%fused_computation.24 | loop fusion | bytes 12582912 | tf_op jit(solution)/shard_map/squeeze | solution.py:35
  154.8 77.3 %while.15 = (s32[]{:T(128)}, f32[4,576]{1,0:T(4,128)S(1)}, f32[4,576]{1,0:T(4,128)S(1)}, f32[4,576,128]{2,1,0:T(8,128)S(1)}, s32[6]{0:T(128)S(1)}, /*index=5*/s3...) while((s32[]{:T(128)}, f32[4,576]{1,0:T(4,128)S(1)}, ...), condition=%wide.region_8.9_spmd.clone, body=%wide.region_5.8_spmd.clone.sunk | while | flops 620506368 | bytes 38370736 | solution.py:65
  154.8 0.7 dynamic_slice.29
  156.4 0.2 broadcast_compare_fusion.3
  156.6 4.1 %fusion.50 = (f32[4,576]{1,0:T(4,128)S(1)}, f32[4,512,576]{1,2,0:T(8,128)}) fusion(pred[576,512]{1,0:T(8,128)(4,1)S(1)} %broadcast_compare_fusion.3, bf16[4,576,128]{2,1,0:T(8,128)(2,1)S(1)} %get-tuple-element.239, bf16[3072,4,128]{2,0,1:T(8,128)(2,1)} %get-tuple-element.238, s32[]{:T(128)S(6)} %select_n.201), kind=kOutput, calls=%fused_computation.4.clone.1 | convolution fusion | flops 305526528 | bytes 6136836 | tf_op jit(solution)/shard_map/while/body/eval_jaxpr/hqd,khd->hqk/dot_general | solution.py:48
  160.7 3.9 %fusion.51 = f32[4,576]{1,0:T(4,128)S(1)} fusion(f32[4,512,576]{1,2,0:T(8,128)} %get-tuple-element.201, f32[4,576]{1,0:T(4,128)S(1)} %select_maximum_fusion.2, pred[576,512]{1,0:T(8,128)(4,1)S(1)} %broadcast_compare_fusion.3), kind=kLoop, calls=%fused_computation.6.clone.1 | loop fusion | flops 5895936 | bytes 5031936 | tf_op jit(solution)/shard_map/while/body/eval_jaxpr/reduce_sum | solution.py:56
  164.7 3.0 %fusion.53 = f32[4,576,128]{2,1,0:T(8,128)S(1)} fusion(f32[4,512,576]{1,2,0:T(8,128)S(1)} %copy-done.1, f32[4,576]{1,0:T(4,128)S(1)} %select_maximum_fusion.2, pred[576,512]{1,0:T(8,128)(4,1)S(1)} %broadcast_compare_fusion.3, f32[4,576,128]{2,1,0:T(8,128)S(1)} %get-tuple-element.221, f32[4,576]{1,0:T(4,128)S(1)} %get-tuple-element.203, ...), kind=kOutput, calls=%fused_computation.9.clone.1 | convolution fusion | flops 308772864 | bytes 7915525 | tf_op jit(solution)/shard_map/while/body/eval_jaxpr/hqk,khd->hqd/dot_general | solution.py:57
  167.7 0.7 dynamic_slice.29
  169.2 0.2 broadcast_compare_fusion.3
  169.5 4.1 %fusion.50 = (f32[4,576]{1,0:T(4,128)S(1)}, f32[4,512,576]{1,2,0:T(8,128)}) fusion(pred[576,512]{1,0:T(8,128)(4,1)S(1)} %broadcast_compare_fusion.3, bf16[4,576,128]{2,1,0:T(8,128)(2,1)S(1)} %get-tuple-element.239, bf16[3072,4,128]{2,0,1:T(8,128)(2,1)} %get-tuple-element.238, s32[]{:T(128)S(6)} %select_n.201), kind=kOutput, calls=%fused_computation.4.clone.1 | convolution fusion | flops 305526528 | bytes 6136836 | tf_op jit(solution)/shard_map/while/body/eval_jaxpr/hqd,khd->hqk/dot_general | solution.py:48
  173.6 3.9 %fusion.51 = f32[4,576]{1,0:T(4,128)S(1)} fusion(f32[4,512,576]{1,2,0:T(8,128)} %get-tuple-element.201, f32[4,576]{1,0:T(4,128)S(1)} %select_maximum_fusion.2, pred[576,512]{1,0:T(8,128)(4,1)S(1)} %broadcast_compare_fusion.3), kind=kLoop, calls=%fused_computation.6.clone.1 | loop fusion | flops 5895936 | bytes 5031936 | tf_op jit(solution)/shard_map/while/body/eval_jaxpr/reduce_sum | solution.py:56
  177.5 3.0 %fusion.53 = f32[4,576,128]{2,1,0:T(8,128)S(1)} fusion(f32[4,512,576]{1,2,0:T(8,128)S(1)} %copy-done.1, f32[4,576]{1,0:T(4,128)S(1)} %select_maximum_fusion.2, pred[576,512]{1,0:T(8,128)(4,1)S(1)} %broadcast_compare_fusion.3, f32[4,576,128]{2,1,0:T(8,128)S(1)} %get-tuple-element.221, f32[4,576]{1,0:T(4,128)S(1)} %get-tuple-element.203, ...), kind=kOutput, calls=%fused_computation.9.clone.1 | convolution fusion | flops 308772864 | bytes 7915525 | tf_op jit(solution)/shard_map/while/body/eval_jaxpr/hqk,khd->hqd/dot_general | solution.py:57
  180.6 0.7 dynamic_slice.29
  182.1 0.2 broadcast_compare_fusion.3
  182.4 4.1 %fusion.50 = (f32[4,576]{1,0:T(4,128)S(1)}, f32[4,512,576]{1,2,0:T(8,128)}) fusion(pred[576,512]{1,0:T(8,128)(4,1)S(1)} %broadcast_compare_fusion.3, bf16[4,576,128]{2,1,0:T(8,128)(2,1)S(1)} %get-tuple-element.239, bf16[3072,4,128]{2,0,1:T(8,128)(2,1)} %get-tuple-element.238, s32[]{:T(128)S(6)} %select_n.201), kind=kOutput, calls=%fused_computation.4.clone.1 | convolution fusion | flops 305526528 | bytes 6136836 | tf_op jit(solution)/shard_map/while/body/eval_jaxpr/hqd,khd->hqk/dot_general | solution.py:48
  186.5 3.9 %fusion.51 = f32[4,576]{1,0:T(4,128)S(1)} fusion(f32[4,512,576]{1,2,0:T(8,128)} %get-tuple-element.201, f32[4,576]{1,0:T(4,128)S(1)} %select_maximum_fusion.2, pred[576,512]{1,0:T(8,128)(4,1)S(1)} %broadcast_compare_fusion.3), kind=kLoop, calls=%fused_computation.6.clone.1 | loop fusion | flops 5895936 | bytes 5031936 | tf_op jit(solution)/shard_map/while/body/eval_jaxpr/reduce_sum | solution.py:56
  190.4 3.0 %fusion.53 = f32[4,576,128]{2,1,0:T(8,128)S(1)} fusion(f32[4,512,576]{1,2,0:T(8,128)S(1)} %copy-done.1, f32[4,576]{1,0:T(4,128)S(1)} %select_maximum_fusion.2, pred[576,512]{1,0:T(8,128)(4,1)S(1)} %broadcast_compare_fusion.3, f32[4,576,128]{2,1,0:T(8,128)S(1)} %get-tuple-element.221, f32[4,576]{1,0:T(4,128)S(1)} %get-tuple-element.203, ...), kind=kOutput, calls=%fused_computation.9.clone.1 | convolution fusion | flops 308772864 | bytes 7915525 | tf_op jit(solution)/shard_map/while/body/eval_jaxpr/hqk,khd->hqd/dot_general | solution.py:57
  193.5 0.7 dynamic_slice.29
  195.0 0.2 broadcast_compare_fusion.3
  195.2 4.1 %fusion.50 = (f32[4,576]{1,0:T(4,128)S(1)}, f32[4,512,576]{1,2,0:T(8,128)}) fusion(pred[576,512]{1,0:T(8,128)(4,1)S(1)} %broadcast_compare_fusion.3, bf16[4,576,128]{2,1,0:T(8,128)(2,1)S(1)} %get-tuple-element.239, bf16[3072,4,128]{2,0,1:T(8,128)(2,1)} %get-tuple-element.238, s32[]{:T(128)S(6)} %select_n.201), kind=kOutput, calls=%fused_computation.4.clone.1 | convolution fusion | flops 305526528 | bytes 6136836 | tf_op jit(solution)/shard_map/while/body/eval_jaxpr/hqd,khd->hqk/dot_general | solution.py:48
  199.4 3.9 %fusion.51 = f32[4,576]{1,0:T(4,128)S(1)} fusion(f32[4,512,576]{1,2,0:T(8,128)} %get-tuple-element.201, f32[4,576]{1,0:T(4,128)S(1)} %select_maximum_fusion.2, pred[576,512]{1,0:T(8,128)(4,1)S(1)} %broadcast_compare_fusion.3), kind=kLoop, calls=%fused_computation.6.clone.1 | loop fusion | flops 5895936 | bytes 5031936 | tf_op jit(solution)/shard_map/while/body/eval_jaxpr/reduce_sum | solution.py:56
  203.3 3.0 %fusion.53 = f32[4,576,128]{2,1,0:T(8,128)S(1)} fusion(f32[4,512,576]{1,2,0:T(8,128)S(1)} %copy-done.1, f32[4,576]{1,0:T(4,128)S(1)} %select_maximum_fusion.2, pred[576,512]{1,0:T(8,128)(4,1)S(1)} %broadcast_compare_fusion.3, f32[4,576,128]{2,1,0:T(8,128)S(1)} %get-tuple-element.221, f32[4,576]{1,0:T(4,128)S(1)} %get-tuple-element.203, ...), kind=kOutput, calls=%fused_computation.9.clone.1 | convolution fusion | flops 308772864 | bytes 7915525 | tf_op jit(solution)/shard_map/while/body/eval_jaxpr/hqk,khd->hqd/dot_general | solution.py:57
  206.3 0.7 dynamic_slice.29
  207.9 0.2 broadcast_compare_fusion.3
  208.1 4.1 %fusion.50 = (f32[4,576]{1,0:T(4,128)S(1)}, f32[4,512,576]{1,2,0:T(8,128)}) fusion(pred[576,512]{1,0:T(8,128)(4,1)S(1)} %broadcast_compare_fusion.3, bf16[4,576,128]{2,1,0:T(8,128)(2,1)S(1)} %get-tuple-element.239, bf16[3072,4,128]{2,0,1:T(8,128)(2,1)} %get-tuple-element.238, s32[]{:T(128)S(6)} %select_n.201), kind=kOutput, calls=%fused_computation.4.clone.1 | convolution fusion | flops 305526528 | bytes 6136836 | tf_op jit(solution)/shard_map/while/body/eval_jaxpr/hqd,khd->hqk/dot_general | solution.py:48
  212.2 3.9 %fusion.51 = f32[4,576]{1,0:T(4,128)S(1)} fusion(f32[4,512,576]{1,2,0:T(8,128)} %get-tuple-element.201, f32[4,576]{1,0:T(4,128)S(1)} %select_maximum_fusion.2, pred[576,512]{1,0:T(8,128)(4,1)S(1)} %broadcast_compare_fusion.3), kind=kLoop, calls=%fused_computation.6.clone.1 | loop fusion | flops 5895936 | bytes 5031936 | tf_op jit(solution)/shard_map/while/body/eval_jaxpr/reduce_sum | solution.py:56
  216.2 3.0 %fusion.53 = f32[4,576,128]{2,1,0:T(8,128)S(1)} fusion(f32[4,512,576]{1,2,0:T(8,128)S(1)} %copy-done.1, f32[4,576]{1,0:T(4,128)S(1)} %select_maximum_fusion.2, pred[576,512]{1,0:T(8,128)(4,1)S(1)} %broadcast_compare_fusion.3, f32[4,576,128]{2,1,0:T(8,128)S(1)} %get-tuple-element.221, f32[4,576]{1,0:T(4,128)S(1)} %get-tuple-element.203, ...), kind=kOutput, calls=%fused_computation.9.clone.1 | convolution fusion | flops 308772864 | bytes 7915525 | tf_op jit(solution)/shard_map/while/body/eval_jaxpr/hqk,khd->hqd/dot_general | solution.py:57
  219.2 0.7 dynamic_slice.29
  220.8 0.2 broadcast_compare_fusion.3
  221.0 4.1 %fusion.50 = (f32[4,576]{1,0:T(4,128)S(1)}, f32[4,512,576]{1,2,0:T(8,128)}) fusion(pred[576,512]{1,0:T(8,128)(4,1)S(1)} %broadcast_compare_fusion.3, bf16[4,576,128]{2,1,0:T(8,128)(2,1)S(1)} %get-tuple-element.239, bf16[3072,4,128]{2,0,1:T(8,128)(2,1)} %get-tuple-element.238, s32[]{:T(128)S(6)} %select_n.201), kind=kOutput, calls=%fused_computation.4.clone.1 | convolution fusion | flops 305526528 | bytes 6136836 | tf_op jit(solution)/shard_map/while/body/eval_jaxpr/hqd,khd->hqk/dot_general | solution.py:48
  225.1 3.9 %fusion.51 = f32[4,576]{1,0:T(4,128)S(1)} fusion(f32[4,512,576]{1,2,0:T(8,128)} %get-tuple-element.201, f32[4,576]{1,0:T(4,128)S(1)} %select_maximum_fusion.2, pred[576,512]{1,0:T(8,128)(4,1)S(1)} %broadcast_compare_fusion.3), kind=kLoop, calls=%fused_computation.6.clone.1 | loop fusion | flops 5895936 | bytes 5031936 | tf_op jit(solution)/shard_map/while/body/eval_jaxpr/reduce_sum | solution.py:56
  229.1 3.0 %fusion.53 = f32[4,576,128]{2,1,0:T(8,128)S(1)} fusion(f32[4,512,576]{1,2,0:T(8,128)S(1)} %copy-done.1, f32[4,576]{1,0:T(4,128)S(1)} %select_maximum_fusion.2, pred[576,512]{1,0:T(8,128)(4,1)S(1)} %broadcast_compare_fusion.3, f32[4,576,128]{2,1,0:T(8,128)S(1)} %get-tuple-element.221, f32[4,576]{1,0:T(4,128)S(1)} %get-tuple-element.203, ...), kind=kOutput, calls=%fused_computation.9.clone.1 | convolution fusion | flops 308772864 | bytes 7915525 | tf_op jit(solution)/shard_map/while/body/eval_jaxpr/hqk,khd->hqd/dot_general | solution.py:57
  232.1 0.4 divide_convert_fusion
  232.5 0.2 copy.112
  232.7 1.2 convert_element_type.36
  (80 shorter events, 1.6 us)
Async XLA Ops:
  7.2 1.7 copy-start
  7.2 9.2 %copy-start.4 = (s32[1,3]{1,0:T(1,128)S(1)}, s32[1,3]{1,0:T(1,128)}, u32[]{:S(2)}) copy-start(s32[1,3]{1,0:T(1,128)} %param.11) | copy-start | bytes 40
  7.2 9.8 %copy-start.3 = (bf16[1,48,1024]{2,1,0:T(8,128)(2,1)S(1)}, bf16[1,48,1024]{2,1,0:T(8,128)(2,1)}, u32[]{:S(2)}) copy-start(bf16[1,48,1024]{2,1,0:T(8,128)(2,1)} %param.13) | copy-start | bytes 294916
  11.0 24.4 %copy-start.5 = (s32[1,3]{1,0:T(1,128)S(1)}, s32[1,3]{1,0:T(1,128)}, u32[]{:S(2)}) copy-start(s32[1,3]{1,0:T(1,128)} %param.10) | copy-start | bytes 40
  11.0 24.6 %all-to-all-start = ((bf16[4,128,1024]{2,1,0:T(8,128)(2,1)}), bf16[4,128,1024]{2,1,0:T(8,128)(2,1)S(1)}, u32[]{:S(2)}, u32[]{:S(2)}) async-start(bf16[4,128,1024]{2,1,0:T(8,128)(2,1)} %copy.77), calls=%async_computation | async-start | bytes 2097152 | tf_op jit(solution)/shard_map/all_to_all | solution.py:91
  16.3 107.3 %all-gather.3.cloned.1.call-start = ((), (), s32[]{:S(2)}) async-start(), calls=%async_computation.3 | async-start | bytes 7077888 | tf_op jit(solution)/shard_map/all_gather | solution.py:127
  59.4 46.5 %all-to-all-start.2 = ((bf16[4,8,1,3,4096]{4,0,3,2,1:T(4,128)(2,1)}), bf16[4,8,1,3,4096]{4,0,3,2,1:T(4,128)(2,1)S(1)}, u32[]{:S(2)}, u32[]{:S(2)}) async-start(bf16[4,8,1,3,4096]{4,0,3,2,1:T(4,128)(2,1)} %copy.87), calls=%async_computation.2 | async-start | bytes 1572864 | tf_op jit(solution)/shard_map/all_to_all | solution.py:141
  148.1 6.8 %copy-start.2 = (f32[4,576,128]{2,1,0:T(8,128)S(1)}, f32[4,576,128]{2,1,0:T(8,128)}, u32[]{:S(2)}) copy-start(f32[4,576,128]{2,1,0:T(8,128)} %custom-call.2) | copy-start | bytes 3538948
  160.7 3.9 %copy-start.1 = (f32[4,512,576]{1,2,0:T(8,128)S(1)}, f32[4,512,576]{1,2,0:T(8,128)}, u32[]{:S(2)}) copy-start(f32[4,512,576]{1,2,0:T(8,128)} %get-tuple-element.201) | copy-start | bytes 14155780 | tf_op jit(solution)/shard_map/while
  173.6 3.9 %copy-start.1 = (f32[4,512,576]{1,2,0:T(8,128)S(1)}, f32[4,512,576]{1,2,0:T(8,128)}, u32[]{:S(2)}) copy-start(f32[4,512,576]{1,2,0:T(8,128)} %get-tuple-element.201) | copy-start | bytes 14155780 | tf_op jit(solution)/shard_map/while
  186.5 3.9 %copy-start.1 = (f32[4,512,576]{1,2,0:T(8,128)S(1)}, f32[4,512,576]{1,2,0:T(8,128)}, u32[]{:S(2)}) copy-start(f32[4,512,576]{1,2,0:T(8,128)} %get-tuple-element.201) | copy-start | bytes 14155780 | tf_op jit(solution)/shard_map/while
  199.4 3.9 %copy-start.1 = (f32[4,512,576]{1,2,0:T(8,128)S(1)}, f32[4,512,576]{1,2,0:T(8,128)}, u32[]{:S(2)}) copy-start(f32[4,512,576]{1,2,0:T(8,128)} %get-tuple-element.201) | copy-start | bytes 14155780 | tf_op jit(solution)/shard_map/while
  212.2 3.9 %copy-start.1 = (f32[4,512,576]{1,2,0:T(8,128)S(1)}, f32[4,512,576]{1,2,0:T(8,128)}, u32[]{:S(2)}) copy-start(f32[4,512,576]{1,2,0:T(8,128)} %get-tuple-element.201) | copy-start | bytes 14155780 | tf_op jit(solution)/shard_map/while
  225.1 3.9 %copy-start.1 = (f32[4,512,576]{1,2,0:T(8,128)S(1)}, f32[4,512,576]{1,2,0:T(8,128)}, u32[]{:S(2)}) copy-start(f32[4,512,576]{1,2,0:T(8,128)} %get-tuple-element.201) | copy-start | bytes 14155780 | tf_op jit(solution)/shard_map/while
Sparse Core Ops, SparseCore 0:
  40.6 82.9 all-gather.2
where the time goes:
time: 242 us; the launch traced here: 241 us
  waiting for transfers between devices  56 us (23%)
  local copies, waits for them, and re-layouts  49.4 us (20%)
  matrix products  47.3 us (20%)
  blocking collectives  31.6 us (13%)
  other arithmetic  27.7 us (11%)
  between operations  14.2 us (6%)
  starting transfers between devices  10.1 us (4%)
  loops' own time  4.53 us (2%)
    all_to_all x1, waiting for transfers between devices, shards(): lax.all_to_all(lax.all_to_all(laid, 'pool', split_axis=0, concat_axis=0,...  39.6 us
    dot_general x6, matrix products, one_block(): jnp.einsum('hqd,khd->hqk', queries, key_blk, preferred_element_type=jnp.f...  24.7 us
    reduce_sum x6, other arithmetic, one_block(): total_weight = total_weight * factor + jnp.sum(weights, axis=-1)  23.4 us
    dot_general x6, matrix products, one_block(): jnp.einsum('hqk,khd->hqd', weights.astype(jnp.bfloat16), value_blk, prefe...  18.1 us
    all_gather x1, waiting for transfers between devices, shards(): lax.all_gather(patched, 'seq', axis=1, tiled=True)  16.4 us
    all_to_all x1, blocking collectives, shards(): lax.all_to_all(laid, 'pool', split_axis=0, concat_axis=0, tiled=True)  15.8 us
    all_gather x1, blocking collectives, shards(): fresh_all = lax.all_gather(fresh_kv[0], 'seq', axis=0, tiled=True)  15.8 us
    slice x1, local copies, waits for them, and re-layouts, fold_keys(): values_all = flattened[:, :, 1]  13.4 us
  transfers between devices with their start and end apart: 3, of which 2 were waited for; matrix products, arithmetic and copies ran while one was open for 4% of the time, Pallas kernels for 0%

commit v1 on v0

v1 whole, which is shorter than its diff:
```python
import functools
import math

import jax
import jax.numpy as jnp
from jax import lax
from jax.experimental import pallas as pl
from jax.experimental.pallas import tpu as pltpu
from jax.sharding import Mesh, PartitionSpec as P

KV_HEADS = 4
HEAD_DIM = 128
LOW = -1e30

SMEM = pl.BlockSpec(memory_space=pltpu.SMEM)
VMEM = pl.BlockSpec(memory_space=pltpu.VMEM)
ANY = pl.BlockSpec(memory_space=pl.ANY)
PARAMS = pltpu.CompilerParams(vmem_limit_bytes=40 * 1024 * 1024)


def pack_kernel(slots, spans, ids, home, pool_kv, fresh_q, fresh_kv, *rest):
    sems = rest[-1]
    pool_count, heads = sems.shape[1], KV_HEADS
    to_pool, to_head = rest[:pool_count], rest[pool_count : pool_count + heads]
    me, head = ids[0], ids[2]
    q_width = fresh_q.shape[2] // heads
    kv_width = fresh_kv.shape[2] // heads
    copies = []
    for d in range(pool_count):
        request = me ^ d
        slot = jnp.int32(0)
        for t in range(spans):
            at = home[request * spans + t]
            slot = jnp.where(at // slots == me, at % slots, slot)
        copies.append(pltpu.make_async_copy(pool_kv.at[slot], to_pool[d], sems.at[0, d]))
        copies[-1].start()
    for d in range(heads):
        other = head ^ d
        q_at = pl.ds(pl.multiple_of(other * q_width, HEAD_DIM), q_width)
        kv_at = pl.ds(pl.multiple_of(other * kv_width, HEAD_DIM), kv_width)
        copies.append(
            pltpu.make_async_copy(fresh_q.at[0, :, q_at], to_head[d].at[:, pl.ds(0, q_width)], sems.at[1, d])
        )
        copies[-1].start()
        copies.append(
            pltpu.make_async_copy(fresh_kv.at[0, :, kv_at], to_head[d].at[:, pl.ds(q_width, kv_width)], sems.at[2, d])
        )
        copies[-1].start()
    for copy in copies:
        copy.wait()


def choose_kernel(slots, ids, home, order, *rest):
    sems = rest[-1]
    spans, heads = sems.shape
    pool_count = len(rest) - 1 - heads
    arrived, out = rest[:pool_count], rest[pool_count : pool_count + heads]
    me, head = ids[0], ids[2]
    width = out[0].shape[2]
    for start in (True, False):
        for j in range(spans):
            source = (home[order[0, j]] // slots) ^ me
            for d in range(heads):
                at = pl.ds(pl.multiple_of((head ^ d) * width, HEAD_DIM), width)
                if start:
                    for p in range(pool_count):

                        @pl.when(source == p)
                        def _(p=p):
                            pltpu.make_async_copy(arrived[p].at[:, at], out[d].at[j], sems.at[j, d]).start()

                else:
                    pltpu.make_async_copy(arrived[0].at[:, at], out[d].at[j], sems.at[j, d]).wait()


def patch_into(dest, at, source, chosen, fresh, message, seq_count):
    spans, block, _ = message.shape
    for j in range(spans):
        dest[pl.ds((at * spans + j) * block, block), :] = message[j]
    for i in range(chosen.shape[1]):
        picked = chosen[0, i]

        @pl.when(picked % seq_count == source)
        def _():
            row = pl.multiple_of((at * spans + picked // seq_count) * block, block)
            dest[pl.ds(row, block), :] = fresh[pl.ds(i * block, block), :]


def attend_kernel(ks, first, last, seq_count, rows, ids, chosen, q, fresh, *rest):
    n = len(ks)
    messages, rest = rest[:n], rest[n:]
    spans, block, _ = messages[0].shape
    quad_rows = q.shape[0]
    group = (q.shape[1] - 2 * HEAD_DIM) // HEAD_DIM
    if not first:
        (acc_in, ml_in), rest = rest[:2], rest[2:]
    outs, (kv, bias) = rest[:-2], rest[-2:]
    me = ids[1] * KV_HEADS + ids[2]
    for at, k in enumerate(ks):
        patch_into(kv, at, me ^ k, chosen, fresh, messages[at], seq_count)

    local = lax.broadcasted_iota(jnp.int32, (quad_rows, 1), 0)
    part = local // rows
    listed = (ids[1] * KV_HEADS + (ids[2] ^ part)) * rows + local % rows
    which = listed // block
    place = jnp.zeros((quad_rows, 1), jnp.int32)
    for i in range(chosen.shape[1]):
        place = jnp.where(which == i, chosen[0, i] * block, place)
    place = place + listed % block
    for at, k in enumerate(ks):
        for j in range(spans):
            key = (j * seq_count + (me ^ k)) * block + lax.broadcasted_iota(jnp.int32, (quad_rows, block), 1)
            bias[:, pl.ds((at * spans + j) * block, block)] = jnp.where(key <= place, 0.0, LOW)

    scale = math.log2(math.e) / math.sqrt(HEAD_DIM)
    lane = lax.broadcasted_iota(jnp.int32, (quad_rows, HEAD_DIM), 1)

    def one_head(h, carry):
        cols = pl.ds(pl.multiple_of(h * HEAD_DIM, HEAD_DIM), HEAD_DIM)
        keys, values = kv[:, :HEAD_DIM], kv[:, HEAD_DIM:]
        s = lax.dot_general(q[:, cols], keys, (((1,), (1,)), ((), ())), preferred_element_type=jnp.float32)
        s = s * scale + bias[...]
        top = jnp.max(s, axis=1, keepdims=True)
        if not first:
            top_in = ml_in[h][:, :1]
            top = jnp.maximum(top, top_in)
        p = jnp.exp2(s - top)
        total = jnp.sum(p, axis=1, keepdims=True)
        acc = jnp.dot(p.astype(jnp.bfloat16), values, preferred_element_type=jnp.float32)
        if not first:
            factor = jnp.exp2(top_in - top)
            total = total + factor * ml_in[h][:, HEAD_DIM // 2 : HEAD_DIM // 2 + 1]
            acc = acc + factor * acc_in[h]
        if last:
            done = acc / total
            for d, out in enumerate(outs):
                out[:, cols] = done[d * rows : (d + 1) * rows].astype(jnp.bfloat16)
        else:
            outs[0][h] = acc
            outs[1][h] = jnp.where(lane < HEAD_DIM // 2, top, total)
        return carry

    lax.fori_loop(0, group, one_head, 0)


def attend(ks, state, last, seq_count, rows, ids, chosen, q, fresh, messages):
    quad_rows, width = q.shape
    group = (width - 2 * HEAD_DIM) // HEAD_DIM
    spans, block, kv_width = messages[0].shape
    keys = len(ks) * spans * block
    if last:
        out_shape = [jax.ShapeDtypeStruct((rows, group * HEAD_DIM), jnp.bfloat16)] * (quad_rows // rows)
    else:
        out_shape = [jax.ShapeDtypeStruct((group, quad_rows, HEAD_DIM), jnp.float32)] * 2
    inputs = [ids, chosen, q, fresh, *messages, *(state or ())]
    return pl.pallas_call(
        functools.partial(attend_kernel, ks, state is None, last, seq_count, rows),
        out_shape=out_shape,
        in_specs=[SMEM, SMEM] + [VMEM] * (len(inputs) - 2),
        out_specs=[VMEM] * len(out_shape),
        scratch_shapes=[pltpu.VMEM((keys, kv_width), jnp.bfloat16), pltpu.VMEM((quad_rows, keys), jnp.float32)],
        compiler_params=PARAMS,
        cost_estimate=pl.CostEstimate(
            flops=4 * group * quad_rows * keys * HEAD_DIM,
            bytes_accessed=4 * quad_rows * width + 2 * keys * kv_width,
            transcendentals=group * quad_rows * keys,
        ),
        name="attend",
    )(*inputs)


def shards(pool_kv, span_home, span_order, chosen, fresh_q, fresh_kv):
    pool_count, quads, heads = (lax.axis_size(a) for a in ("pool", "quad", "head"))
    seq_count = quads * heads
    me, quad, head = (lax.axis_index(a) for a in ("pool", "quad", "head"))
    slots, block, width = pool_kv.shape
    spans = span_order.shape[1]
    rows, q_width = fresh_q.shape[1:]
    kv_width = width // heads
    q_part = q_width // heads
    run = block // seq_count
    ids = jnp.stack([me, quad, head]).astype(jnp.int32)
    seat = quad * heads + head
    bf16 = jnp.bfloat16

    packed = pl.pallas_call(
        functools.partial(pack_kernel, slots, spans),
        out_shape=[jax.ShapeDtypeStruct((block, width), bf16)] * pool_count
        + [jax.ShapeDtypeStruct((rows, q_part + kv_width), bf16)] * heads,
        in_specs=[SMEM, SMEM, ANY, ANY, ANY],
        out_specs=[ANY] * (pool_count + heads),
        scratch_shapes=[pltpu.SemaphoreType.DMA((3, max(pool_count, heads)))],
        compiler_params=PARAMS,
        name="pack",
    )(ids, span_home, pool_kv, fresh_q, fresh_kv)
    to_pool, to_head = packed[:pool_count], packed[pool_count:]

    def swap(value, axes, count, k):
        return lax.ppermute(value, axes, [(i, i ^ k) for i in range(count)])

    arrived = [to_pool[0]] + [None] * (pool_count - 1)
    for k in reversed(range(1, pool_count)):
        arrived[k] = swap(to_pool[k], "pool", pool_count, k)
    gathered = [to_head[0]] + [swap(to_head[k], "head", heads, k) for k in range(1, heads)]
    q = jnp.concatenate(gathered, axis=0)

    kv_out = pl.pallas_call(
        functools.partial(choose_kernel, slots),
        out_shape=[jax.ShapeDtypeStruct((spans, block, kv_width), bf16)] * heads,
        in_specs=[SMEM, SMEM, SMEM] + [ANY] * pool_count,
        out_specs=[ANY] * heads,
        scratch_shapes=[pltpu.SemaphoreType.DMA((spans, heads))],
        compiler_params=PARAMS,
        name="choose",
    )(ids, span_home, span_order, *arrived)

    seq = ("quad", "head")
    messages = [kv_out[0]] + [None] * (seq_count - 1)
    for k in list(range(heads, seq_count)) + list(range(1, heads)):
        messages[k] = swap(kv_out[k % heads], seq, seq_count, k)

    near = q[:, q_part:]
    parts = [near] + [swap(near, "quad", quads, k) for k in range(1, quads)]
    listed = jnp.stack(parts).reshape(seq_count, rows, kv_width)
    fresh = jnp.take(listed, seat ^ jnp.arange(seq_count), axis=0).reshape(seq_count * rows, kv_width)

    groups = [list(range(heads))] + [[k, k + 1] for k in range(heads, seq_count, 2)]
    state = None
    for ks in groups:
        state = attend(
            ks, state, ks is groups[-1], seq_count, rows, ids, chosen, q, fresh, [messages[k] for k in ks]
        )
    back = [state[0]] + [swap(state[k], "head", heads, k) for k in range(1, heads)]
    attended = jnp.take(jnp.stack(back, axis=1), head ^ jnp.arange(heads), axis=1)
    attended = attended.reshape(1, rows, q_width)

    blocks = jnp.stack(messages, axis=1)
    blocks = jnp.take(blocks, seat ^ jnp.arange(seq_count), axis=1).reshape(spans * seq_count, block, kv_width)
    blocks = blocks.at[chosen[0]].set(fresh.reshape(-1, block, kv_width))
    blocks = blocks.reshape(spans * seq_count, quads, heads, run, kv_width)
    mine = lax.dynamic_index_in_dim(blocks, quad, axis=1, keepdims=False)
    landed = []
    for k in range(pool_count):
        perm = [
            ((r * quads + a) * heads + g, (g * quads + a) * heads + (r ^ k))
            for r in range(pool_count)
            for a in range(quads)
            for g in range(heads)
        ]
        part = lax.dynamic_index_in_dim(mine, me ^ k, axis=1, keepdims=False)
        landed.append(lax.ppermute(part, ("pool", "quad", "head"), perm))
    landed = jnp.take(jnp.stack(landed), head ^ jnp.arange(pool_count), axis=0)
    decoded = landed.reshape(1, 1, pool_count, spans * seq_count, run * kv_width)
    return (attended, decoded)


def solution(mesh):
    pool_count, seq_count = mesh.shape["pool"], mesh.shape["seq"]
    fine = Mesh(mesh.devices.reshape(pool_count, seq_count // KV_HEADS, KV_HEADS), ("pool", "quad", "head"))
    seq = ("quad", "head")
    in_specs = (
        P("pool", seq, None),
        P(),
        P("pool", None),
        P("pool", None),
        P("pool", seq, None),
        P("pool", seq, None),
    )
    out_specs = (P("pool", seq, None), P("pool", seq, None, None, None))
    return jax.shard_map(shards, mesh=fine, in_specs=in_specs, out_specs=out_specs, check_vma=False)
```

time: 242 us -> 119 us (0.49)
  matrix products: 47.3 us -> 0 us
  blocking collectives: 31.6 us -> 0 us
  Pallas kernels: 0 us -> 30.4 us
  local copies, waits for them, and re-layouts: 49.4 us -> 20.2 us
  waiting for transfers between devices: 56 us -> 28 us
  starting transfers between devices: 10.1 us -> 35.3 us
  other arithmetic: 27.7 us -> 3.34 us
  between operations: 14.2 us -> 0.99 us
  loops' own time: 4.53 us -> 0 us
    dot_general x14 -> x0, matrix products: 47.3 us -> none  [the longest x6 24.7 us: one_block(): jnp.einsum('hqd,khd->hqk', queries, key_blk, preferred_element_type=jnp.f...]
    all_to_all x2 -> x0, waiting for transfers between devices: 39.6 us -> none  [the longest x1 39.6 us: shards(): lax.all_to_all(lax.all_to_all(laid, 'pool', split_axis=0, concat_axis=0,...]
    ppermute x0 -> x21, starting transfers between devices: none -> 35.3 us  [the longest x17 27.8 us: swap(): return lax.ppermute(value, axes, [(i, i ^ k) for i in range(count)])]
    pallas_call x0 -> x5, Pallas kernels: none -> 30.4 us  [the longest x3 28.4 us: attend(): pl.pallas_call(functools.partial(attend_kernel, ks, state is None, last,...]
    ppermute x0 -> x21, waiting for transfers between devices: none -> 28 us  [the longest x17 21.4 us: swap(): return lax.ppermute(value, axes, [(i, i ^ k) for i in range(count)])]
    reduce_sum x9 -> x0, other arithmetic: 23.7 us -> none  [the longest x6 23.4 us: one_block(): total_weight = total_weight * factor + jnp.sum(weights, axis=-1)]
    all_gather x1 -> x0, waiting for transfers between devices: 16.4 us -> none  [shards(): lax.all_gather(patched, 'seq', axis=1, tiled=True)]
    all_to_all x1 -> x0, blocking collectives: 15.8 us -> none  [shards(): lax.all_to_all(laid, 'pool', split_axis=0, concat_axis=0, tiled=True)]
  transfers between devices with their start and end apart: 3 -> 21, of which waited for: 2 -> 6; matrix products, arithmetic and copies ran while one was open for 4% -> 10% of each run, Pallas kernels for 0% -> 1%
where the time goes in v1:
time: 119 us; the launch traced here: 118 us
  starting transfers between devices  35.3 us (30%)
  Pallas kernels  30.4 us (26%)
  waiting for transfers between devices  28 us (24%)
  local copies, waits for them, and re-layouts  20.2 us (17%)
  other arithmetic  3.34 us (3%)
    pallas_call x3, Pallas kernels, attend(): pl.pallas_call(functools.partial(attend_kernel, ks, state is None, last,...  28.4 us
    ppermute x17, starting transfers between devices, swap(): return lax.ppermute(value, axes, [(i, i ^ k) for i in range(count)])  27.8 us
    ppermute x17, waiting for transfers between devices, swap(): return lax.ppermute(value, axes, [(i, i ^ k) for i in range(count)])  21.4 us
    unnamed x28, local copies, waits for them, and re-layouts  9.63 us
    ppermute x4, starting transfers between devices, shards(): landed.append(lax.ppermute(part, ('pool', 'quad', 'head'), perm))  7.49 us
    ppermute x4, waiting for transfers between devices, shards(): landed.append(lax.ppermute(part, ('pool', 'quad', 'head'), perm))  6.58 us
    gather x2, local copies, waits for them, and re-layouts, shards(): jnp.take(blocks, seat ^ jnp.arange(seq_count), axis=1)  4.75 us
  transfers between devices with their start and end apart: 21, of which 6 were waited for; matrix products, arithmetic and copies ran while one was open for 10% of the time, Pallas kernels for 1%

profile of v1, /device:TPU:0, one launch (start us, length us, event | category | flops | bytes accessed | tf_op | source)
XLA Modules:
  0.0 118.2 jit_solution(13774544514544406839)
XLA Ops:
  0.6 0.1 pad_add_fusion.ids
  0.7 1.2 %copy-done = bf16[4,128,1024]{2,1,0:T(8,128)(2,1)S(1)} copy-done((bf16[4,128,1024]{2,1,0:T(8,128)(2,1)S(1)}, bf16[4,128,1024]{2,1,0:T(8,128)(2,1)}, u32[]{:S(2)}) %copy-start) | copy-done | bytes 1048600
  2.0 1.1 copy-done.1
  3.0 0.9 copy-done.2
  3.9 0.7 copy-done.3
  4.6 1.0 pack.1
  5.6 3.0 %collective-permute-start.4 = (bf16[128,1024]{1,0:T(8,128)(2,1)S(1)}, bf16[128,1024]{1,0:T(8,128)(2,1)S(1)}, u32[]{:S(2)}, u32[]{:S(2)}) collective-permute-start(bf16[128,1024]{1,0:T(8,128)(2,1)S(1)} %get-tuple-element.27), channel_id=1, source_target_pairs={{0,8},{8,0},{16,24},{24,16},{1,9},{9,1},{17,25},{25,17},{2,10},{10... | collective-permute-start | bytes 786440 | tf_op jit(solution)/shard_map/ppermute | solution.py:199
  8.6 1.5 %collective-permute-start.5 = (bf16[128,1024]{1,0:T(8,128)(2,1)S(1)}, bf16[128,1024]{1,0:T(8,128)(2,1)S(1)}, u32[]{:S(2)}, u32[]{:S(2)}) collective-permute-start(bf16[128,1024]{1,0:T(8,128)(2,1)S(1)} %get-tuple-element.28), channel_id=1, source_target_pairs={{0,16},{8,24},{16,0},{24,8},{1,17},{9,25},{17,1},{25,9},{2,18},{10... | collective-permute-start | bytes 786440 | tf_op jit(solution)/shard_map/ppermute | solution.py:199
  10.1 0.0 collective-permute-start.6
  10.1 2.0 %collective-permute-start.1 = (bf16[48,1792]{1,0:T(8,128)(2,1)S(1)}, bf16[48,1792]{1,0:T(8,128)(2,1)S(1)}, u32[]{:S(2)}, u32[]{:S(2)}) collective-permute-start(bf16[48,1792]{1,0:T(8,128)(2,1)S(1)} %get-tuple-element.24), channel_id=1, source_target_pairs={{0,2},{1,3},{2,0},{3,1},{4,6},{5,7},{6,4},{7,5},{8,10},{9,11},{10,... | collective-permute-start | bytes 516104 | tf_op jit(solution)/shard_map/ppermute | solution.py:199
  12.2 0.1 broadcast_in_dim.62
  12.3 0.1 broadcast_in_dim.72
  12.4 0.1 broadcast_in_dim.63
  12.5 0.1 broadcast_in_dim.69
  12.6 0.6 pad_clamp_fusion
  13.2 0.1 broadcast_in_dim.59
  13.4 0.2 collective-permute-start.2
  13.5 0.9 constant_dynamic-update-slice_fusion.2
  14.5 2.9 %collective-permute-done.1 = bf16[48,1792]{1,0:T(8,128)(2,1)S(1)} collective-permute-done((bf16[48,1792]{1,0:T(8,128)(2,1)S(1)}, bf16[48,1792]{1,0:T(8,128)(2,1)S(1)}, u32[]{:S(2)}, u32[]{:S(2)}) %collective-permute-start.1) | collective-permute-done | bytes 172064 | tf_op jit(solution)/shard_map/ppermute | solution.py:199
  17.4 3.3 %collective-permute-done.2 = bf16[48,1792]{1,0:T(8,128)(2,1)S(1)} collective-permute-done((bf16[48,1792]{1,0:T(8,128)(2,1)S(1)}, bf16[48,1792]{1,0:T(8,128)(2,1)S(1)}, u32[]{:S(2)}, u32[]{:S(2)}) %collective-permute-start.2) | collective-permute-done | bytes 172064 | tf_op jit(solution)/shard_map/ppermute | solution.py:199
  20.7 2.6 %collective-permute-start.3 = (bf16[192,256]{1,0:T(8,128)(2,1)S(1)}, bf16[192,256]{1,0:T(8,128)(2,1)S(1)}, u32[]{:S(2)}, u32[]{:S(2)}) collective-permute-start(bf16[192,256]{1,0:T(8,128)(2,1)S(1)} %get-tuple-element.47), channel_id=1, source_target_pairs={{0,4},{4,0},{1,5},{5,1},{2,6},{6,2},{3,7},{7,3},{8,12},{12,8},{9,1... | collective-permute-start | bytes 294920 | tf_op jit(solution)/shard_map/ppermute | solution.py:199
  23.4 1.0 choose.1
  24.4 0.7 bitcast_dynamic-update-slice_fusion.7
  25.1 1.2 collective-permute-start.9
  26.3 1.9 %collective-permute-start.10 = (bf16[3,128,256]{2,1,0:T(8,128)(2,1)S(1)}, bf16[3,128,256]{2,1,0:T(8,128)(2,1)S(1)}, u32[]{:S(2)}, u32[]{:S(2)}) collective-permute-start(bf16[3,128,256]{2,1,0:T(8,128)(2,1)S(1)} %get-tuple-element.33), channel_id=1, source_target_pairs={{0,5},{1,4},{2,7},{3,6},{4,1},{5,0},{6,3},{7,2},{8,13},{9,12},{10,... | collective-permute-start | bytes 589832 | tf_op jit(solution)/shard_map/ppermute | solution.py:199
  28.1 1.6 %collective-permute-start.12 = (bf16[3,128,256]{2,1,0:T(8,128)(2,1)S(1)}, bf16[3,128,256]{2,1,0:T(8,128)(2,1)S(1)}, u32[]{:S(2)}, u32[]{:S(2)}) collective-permute-start(bf16[3,128,256]{2,1,0:T(8,128)(2,1)S(1)} %get-tuple-element.30), channel_id=1, source_target_pairs={{0,2},{1,3},{2,0},{3,1},{4,6},{5,7},{6,4},{7,5},{8,10},{9,11},{10,... | collective-permute-start | bytes 589832 | tf_op jit(solution)/shard_map/ppermute | solution.py:199
  29.7 11.2 %collective-permute-start.7 = (bf16[3,128,256]{2,1,0:T(8,128)(2,1)S(1)}, bf16[3,128,256]{2,1,0:T(8,128)(2,1)S(1)}, u32[]{:S(2)}, u32[]{:S(2)}) collective-permute-start(bf16[3,128,256]{2,1,0:T(8,128)(2,1)S(1)} %get-tuple-element.30), channel_id=1, source_target_pairs={{0,6},{1,7},{2,4},{3,5},{4,2},{5,3},{6,0},{7,1},{8,14},{9,15},{10,... | collective-permute-start | bytes 589832 | tf_op jit(solution)/shard_map/ppermute | solution.py:199
  41.0 0.6 gather_fusion
  41.5 0.1 bitcast_select_fusion.1.fresh
  41.7 0.1 broadcast_select_fusion.2
  41.8 0.1 collective-permute-start.13
  41.9 0.7 bitcast_dynamic-update-slice_fusion.6
  42.6 0.7 bitcast_dynamic-update-slice_fusion.5
  43.3 15.2 %collective-permute-done.13.rest_3_ = bf16[3,128,256]{2,1,0:T(8,128)(2,1)S(1)} collective-permute-done((bf16[3,128,256]{2,1,0:T(8,128)(2,1)S(1)}, bf16[3,128,256]{2,1,0:T(8,128)(2,1)S(1)}, u32[]{:S(2)}, u32[]{:S(2)}) %collective-permute-start.13) | collective-permute-done | bytes 196640 | tf_op jit(solution)/shard_map/ppermute | solution.py:199
  58.4 0.7 bitcast_dynamic-update-slice_fusion.4
  59.1 0.7 bitcast_dynamic-update-slice_fusion.3
  59.8 0.7 bitcast_dynamic-update-slice_fusion.2
  60.5 0.7 bitcast_dynamic-update-slice_fusion.1
  61.2 0.7 bitcast_dynamic-update-slice_fusion
  61.9 3.2 %gather_fusion.2 = bf16[8,3,128,256]{3,2,1,0:T(8,128)(2,1)} fusion(bf16[3,8,128,256]{3,2,0,1:T(8,128)(2,1)} %bitcast_dynamic-update-slice_fusion, s32[1024]{0:T(1024)S(1)} %pad_clamp_fusion.1), kind=kCustom, calls=%fused_computation.2 | custom fusion | bytes 3145760 | tf_op jit(solution)/shard_map/jit(_take)/gather | solution.py:238
  65.1 1.5 %copy.9 = bf16[3,8,128,256]{3,2,1,0:T(8,128)(2,1)S(1)} copy(bf16[3,8,128,256]{3,2,0,1:T(8,128)(2,1)} %bitcast.58) | data formatting | bytes 3145728 | tf_op jit(solution)/shard_map/jit(_take)/gather | solution.py:238
  66.6 10.0 %attend.3 = (f32[12,192,128]{2,1,0:T(8,128)S(1)}, f32[12,192,128]{2,1,0:T(8,128)S(1)}) custom-call(s32[3]{0:T(128)S(1)} %pad_add_fusion.ids, s32[1,3]{1,0:T(1,128)S(1)} %copy-done.5, bf16[192,1792]{1,0:T(8,128)(2,1)S(1)} %constant_dynamic-update-slice_fusion.q, bf16[384,256]{1,0:T(8,128)(2,1)S(1)} %bitcast_select_fusion.1.fresh, ...), custom_call_target="tpu_custom_call" | custom-call | flops 1811939328 | bytes 2162688 | tf_op jit(solution)/shard_map/attend/pallas_call | solution.py:156
  76.6 9.2 %attend.4 = (f32[12,192,128]{2,1,0:T(8,128)S(1)}, f32[12,192,128]{2,1,0:T(8,128)S(1)}) custom-call(s32[3]{0:T(128)S(1)} %pad_add_fusion.ids, s32[1,3]{1,0:T(1,128)S(1)} %copy-done.5, bf16[192,1792]{1,0:T(8,128)(2,1)S(1)} %constant_dynamic-update-slice_fusion.q, bf16[384,256]{1,0:T(8,128)(2,1)S(1)} %bitcast_select_fusion.1.fresh, ...), custom_call_target="tpu_custom_call" | custom-call | flops 905969664 | bytes 1769472 | tf_op jit(solution)/shard_map/attend/pallas_call | solution.py:156
  85.8 9.2 %attend.5 = (bf16[48,1536]{1,0:T(8,128)(2,1)S(1)}, bf16[48,1536]{1,0:T(8,128)(2,1)S(1)}, bf16[48,1536]{1,0:T(8,128)(2,1)S(1)}, bf16[48,1536]{1,0:T(8,128)(2,1)S(1)}) custom-call(s32[3]{0:T(128)S(1)} %pad_add_fusion.ids, s32[1,3]{1,0:T(1,128)S(1)} %copy-done.5, bf16[192,1792]{1,0:T(8,128)(2,1)S(1)} %constant_dynamic-update-slice_fusion.q, ...), custom_call_target="tpu_custom_call" | custom-call | flops 905969664 | bytes 1769472 | tf_op jit(solution)/shard_map/attend/pallas_call | solution.py:156
  95.0 2.3 %collective-permute-start.15 = (bf16[48,1536]{1,0:T(8,128)(2,1)S(1)}, bf16[48,1536]{1,0:T(8,128)(2,1)S(1)}, u32[]{:S(2)}, u32[]{:S(2)}) collective-permute-start(bf16[48,1536]{1,0:T(8,128)(2,1)S(1)} %get-tuple-element.40), channel_id=1, source_target_pairs={{0,2},{1,3},{2,0},{3,1},{4,6},{5,7},{6,4},{7,5},{8,10},{9,11},{10,... | collective-permute-start | bytes 442376 | tf_op jit(solution)/shard_map/ppermute | solution.py:199
  97.3 0.2 collective-permute-start.14
  97.5 0.3 bitcast_select_fusion
  97.8 0.7 scatter_fusion
  98.5 0.8 dynamic-slice_bitcast_fusion.3
  99.3 1.6 %collective-permute-start.17 = (bf16[24,16,256]{2,1,0:T(8,128)(2,1)}, bf16[24,16,256]{2,1,0:T(8,128)(2,1)S(1)}, u32[]{:S(2)}, u32[]{:S(2)}) collective-permute-start(bf16[24,16,256]{2,1,0:T(8,128)(2,1)} %get-tuple-element.42), channel_id=1, source_target_pairs={{0,0},{1,8},{2,16},{3,24},{4,4},{5,12},{6,20},{7,28},{8,1},{9,9},{... | collective-permute-start | bytes 589832 | tf_op jit(solution)/shard_map/ppermute | solution.py:251
  100.9 2.0 %collective-permute-start.18 = (bf16[24,16,256]{2,1,0:T(8,128)(2,1)}, bf16[24,16,256]{2,1,0:T(8,128)(2,1)S(1)}, u32[]{:S(2)}, u32[]{:S(2)}) collective-permute-start(bf16[24,16,256]{2,1,0:T(8,128)(2,1)} %get-tuple-element.45), channel_id=1, source_target_pairs={{0,1},{1,9},{2,17},{3,25},{4,5},{5,13},{6,21},{7,29},{8,0},{9,8},{... | collective-permute-start | bytes 589832 | tf_op jit(solution)/shard_map/ppermute | solution.py:251
  102.9 3.9 %collective-permute-start.19 = (bf16[24,16,256]{2,1,0:T(8,128)(2,1)S(1)}, bf16[24,16,256]{2,1,0:T(8,128)(2,1)S(1)}, u32[]{:S(2)}, u32[]{:S(2)}) collective-permute-start(bf16[24,16,256]{2,1,0:T(8,128)(2,1)S(1)} %get-tuple-element.44), channel_id=1, source_target_pairs={{0,2},{1,10},{2,18},{3,26},{4,6},{5,14},{6,22},{7,30},{8,3},{9,11}... | collective-permute-start | bytes 589832 | tf_op jit(solution)/shard_map/ppermute | solution.py:251
  106.8 0.1 pad_maximum_fusion.1
  106.9 0.7 gather_fusion.1
  107.6 0.5 copy.8
  108.0 0.4 gather.29
  108.5 0.9 broadcast_select_fusion.1
  109.4 2.1 %collective-permute-done.18 = bf16[24,16,256]{2,1,0:T(8,128)(2,1)S(1)} collective-permute-done((bf16[24,16,256]{2,1,0:T(8,128)(2,1)}, bf16[24,16,256]{2,1,0:T(8,128)(2,1)S(1)}, u32[]{:S(2)}, u32[]{:S(2)}) %collective-permute-start.18) | collective-permute-done | bytes 196640 | tf_op jit(solution)/shard_map/ppermute | solution.py:251
  111.5 1.4 %collective-permute-done.19 = bf16[24,16,256]{2,1,0:T(8,128)(2,1)S(1)} collective-permute-done((bf16[24,16,256]{2,1,0:T(8,128)(2,1)S(1)}, bf16[24,16,256]{2,1,0:T(8,128)(2,1)S(1)}, u32[]{:S(2)}, u32[]{:S(2)}) %collective-permute-start.19) | collective-permute-done | bytes 196640 | tf_op jit(solution)/shard_map/ppermute | solution.py:251
  112.9 3.1 %collective-permute-done.20 = bf16[24,16,256]{2,1,0:T(8,128)(2,1)S(1)} collective-permute-done((bf16[24,16,256]{2,1,0:T(8,128)(2,1)S(1)}, bf16[24,16,256]{2,1,0:T(8,128)(2,1)S(1)}, u32[]{:S(2)}, u32[]{:S(2)}) %collective-permute-start.20) | collective-permute-done | bytes 196640 | tf_op jit(solution)/shard_map/ppermute | solution.py:251
  116.0 0.1 pad_maximum_fusion
  116.1 0.7 gather_fusion.3
  116.8 0.4 gather.34
  117.2 1.0 broadcast_select_fusion
  (47 shorter events, 0.2 us)
Async XLA Ops:
  0.6 12.7 %copy-start.5 = (s32[1,3]{1,0:T(1,128)S(1)}, s32[1,3]{1,0:T(1,128)}, u32[]{:S(2)}) copy-start(s32[1,3]{1,0:T(1,128)} %chosen.5) | copy-start | bytes 40
  0.7 1.2 %copy-start = (bf16[4,128,1024]{2,1,0:T(8,128)(2,1)S(1)}, bf16[4,128,1024]{2,1,0:T(8,128)(2,1)}, u32[]{:S(2)}) copy-start(bf16[4,128,1024]{2,1,0:T(8,128)(2,1)} %pool_kv.1) | copy-start | bytes 3145732
  2.0 1.1 copy-start.1
  3.0 0.9 copy-start.2
  3.9 0.7 copy-start.3
  4.6 18.8 %copy-start.4 = (s32[12]{0:T(128)S(1)}, s32[12]{0:T(128)}, u32[]{:S(2)}) copy-start(s32[12]{0:T(128)} %home.3) | copy-start | bytes 148
  4.6 18.8 %copy-start.6 = (s32[1,3]{1,0:T(1,128)S(1)}, s32[1,3]{1,0:T(1,128)}, u32[]{:S(2)}) copy-start(s32[1,3]{1,0:T(1,128)} %order.1) | copy-start | bytes 40
  5.6 17.8 %collective-permute-start.4 = (bf16[128,1024]{1,0:T(8,128)(2,1)S(1)}, bf16[128,1024]{1,0:T(8,128)(2,1)S(1)}, u32[]{:S(2)}, u32[]{:S(2)}) collective-permute-start(bf16[128,1024]{1,0:T(8,128)(2,1)S(1)} %get-tuple-element.27), channel_id=1, source_target_pairs={{0,8},{8,0},{16,24},{24,16},{1,9},{9,1},{17,25},{25,17},{2,10},{10... | collective-permute-start | bytes 786440 | tf_op jit(solution)/shard_map/ppermute | solution.py:199
  8.6 14.8 %collective-permute-start.5 = (bf16[128,1024]{1,0:T(8,128)(2,1)S(1)}, bf16[128,1024]{1,0:T(8,128)(2,1)S(1)}, u32[]{:S(2)}, u32[]{:S(2)}) collective-permute-start(bf16[128,1024]{1,0:T(8,128)(2,1)S(1)} %get-tuple-element.28), channel_id=1, source_target_pairs={{0,16},{8,24},{16,0},{24,8},{1,17},{9,25},{17,1},{25,9},{2,18},{10... | collective-permute-start | bytes 786440 | tf_op jit(solution)/shard_map/ppermute | solution.py:199
  10.1 13.3 %collective-permute-start.6 = (bf16[128,1024]{1,0:T(8,128)(2,1)S(1)}, bf16[128,1024]{1,0:T(8,128)(2,1)S(1)}, u32[]{:S(2)}, u32[]{:S(2)}) collective-permute-start(bf16[128,1024]{1,0:T(8,128)(2,1)S(1)} %get-tuple-element.29), channel_id=1, source_target_pairs={{0,24},{8,16},{16,8},{24,0},{1,25},{9,17},{17,9},{25,1},{2,26},{10... | collective-permute-start | bytes 786440 | tf_op jit(solution)/shard_map/ppermute | solution.py:199
  10.1 3.2 %collective-permute-start = (bf16[48,1792]{1,0:T(8,128)(2,1)S(1)}, bf16[48,1792]{1,0:T(8,128)(2,1)}, u32[]{:S(2)}, u32[]{:S(2)}) collective-permute-start(bf16[48,1792]{1,0:T(8,128)(2,1)S(1)} %get-tuple-element.23), channel_id=1, source_target_pairs={{0,1},{1,0},{2,3},{3,2},{4,5},{5,4},{6,7},{7,6},{8,9},{9,8},{10,11... | collective-permute-start | bytes 516104 | tf_op jit(solution)/shard_map/ppermute | solution.py:199
  10.1 7.3 %collective-permute-start.1 = (bf16[48,1792]{1,0:T(8,128)(2,1)S(1)}, bf16[48,1792]{1,0:T(8,128)(2,1)S(1)}, u32[]{:S(2)}, u32[]{:S(2)}) collective-permute-start(bf16[48,1792]{1,0:T(8,128)(2,1)S(1)} %get-tuple-element.24), channel_id=1, source_target_pairs={{0,2},{1,3},{2,0},{3,1},{4,6},{5,7},{6,4},{7,5},{8,10},{9,11},{10,... | collective-permute-start | bytes 516104 | tf_op jit(solution)/shard_map/ppermute | solution.py:199
  12.2 12.9 %copy-start.7 = (pred[4]{0:T(512)(128)(4,1)}, pred[4]{0:T(512)(128)(4,1)S(1)}, u32[]{:S(2)}) copy-start(pred[4]{0:T(512)(128)(4,1)S(1)} %compare_and_fusion.1) | copy-start | bytes 16
  13.4 7.3 %collective-permute-start.2 = (bf16[48,1792]{1,0:T(8,128)(2,1)S(1)}, bf16[48,1792]{1,0:T(8,128)(2,1)S(1)}, u32[]{:S(2)}, u32[]{:S(2)}) collective-permute-start(bf16[48,1792]{1,0:T(8,128)(2,1)S(1)} %get-tuple-element.25), channel_id=1, source_target_pairs={{0,3},{1,2},{2,1},{3,0},{4,7},{5,6},{6,5},{7,4},{8,11},{9,10},{10,... | collective-permute-start | bytes 516104 | tf_op jit(solution)/shard_map/ppermute | solution.py:199
  20.7 9.0 %collective-permute-start.3 = (bf16[192,256]{1,0:T(8,128)(2,1)S(1)}, bf16[192,256]{1,0:T(8,128)(2,1)S(1)}, u32[]{:S(2)}, u32[]{:S(2)}) collective-permute-start(bf16[192,256]{1,0:T(8,128)(2,1)S(1)} %get-tuple-element.47), channel_id=1, source_target_pairs={{0,4},{4,0},{1,5},{5,1},{2,6},{6,2},{3,7},{7,3},{8,12},{12,8},{9,1... | collective-permute-start | bytes 294920 | tf_op jit(solution)/shard_map/ppermute | solution.py:199
  25.1 34.0 %collective-permute-start.9 = (bf16[3,128,256]{2,1,0:T(8,128)(2,1)S(1)}, bf16[3,128,256]{2,1,0:T(8,128)(2,1)S(1)}, u32[]{:S(2)}, u32[]{:S(2)}) collective-permute-start(bf16[3,128,256]{2,1,0:T(8,128)(2,1)S(1)} %get-tuple-element.32.rest_0_), channel_id=1, source_target_pairs={{0,4},{1,5},{2,6},{3,7},{4,0},{5,1},{6,2},{7,3},{8,12},{9,13},{10,... | collective-permute-start | bytes 589832 | tf_op jit(solution)/shard_map/ppermute | solution.py:199
  26.3 15.5 %collective-permute-start.11 = (bf16[3,128,256]{2,1,0:T(8,128)(2,1)S(1)}, bf16[3,128,256]{2,1,0:T(8,128)(2,1)S(1)}, u32[]{:S(2)}, u32[]{:S(2)}) collective-permute-start(bf16[3,128,256]{2,1,0:T(8,128)(2,1)S(1)} %get-tuple-element.33), channel_id=1, source_target_pairs={{0,1},{1,0},{2,3},{3,2},{4,5},{5,4},{6,7},{7,6},{8,9},{9,8},{10,11... | collective-permute-start | bytes 589832 | tf_op jit(solution)/shard_map/ppermute | solution.py:199
  26.3 33.5 %collective-permute-start.10 = (bf16[3,128,256]{2,1,0:T(8,128)(2,1)S(1)}, bf16[3,128,256]{2,1,0:T(8,128)(2,1)S(1)}, u32[]{:S(2)}, u32[]{:S(2)}) collective-permute-start(bf16[3,128,256]{2,1,0:T(8,128)(2,1)S(1)} %get-tuple-element.33), channel_id=1, source_target_pairs={{0,5},{1,4},{2,7},{3,6},{4,1},{5,0},{6,3},{7,2},{8,13},{9,12},{10,... | collective-permute-start | bytes 589832 | tf_op jit(solution)/shard_map/ppermute | solution.py:199
  28.1 14.4 %collective-permute-start.12 = (bf16[3,128,256]{2,1,0:T(8,128)(2,1)S(1)}, bf16[3,128,256]{2,1,0:T(8,128)(2,1)S(1)}, u32[]{:S(2)}, u32[]{:S(2)}) collective-permute-start(bf16[3,128,256]{2,1,0:T(8,128)(2,1)S(1)} %get-tuple-element.30), channel_id=1, source_target_pairs={{0,2},{1,3},{2,0},{3,1},{4,6},{5,7},{6,4},{7,5},{8,10},{9,11},{10,... | collective-permute-start | bytes 589832 | tf_op jit(solution)/shard_map/ppermute | solution.py:199
  29.7 30.8 %collective-permute-start.7 = (bf16[3,128,256]{2,1,0:T(8,128)(2,1)S(1)}, bf16[3,128,256]{2,1,0:T(8,128)(2,1)S(1)}, u32[]{:S(2)}, u32[]{:S(2)}) collective-permute-start(bf16[3,128,256]{2,1,0:T(8,128)(2,1)S(1)} %get-tuple-element.30), channel_id=1, source_target_pairs={{0,6},{1,7},{2,4},{3,5},{4,2},{5,3},{6,0},{7,1},{8,14},{9,15},{10,... | collective-permute-start | bytes 589832 | tf_op jit(solution)/shard_map/ppermute | solution.py:199
  41.8 16.6 %collective-permute-start.13 = (bf16[3,128,256]{2,1,0:T(8,128)(2,1)S(1)}, bf16[3,128,256]{2,1,0:T(8,128)(2,1)S(1)}, u32[]{:S(2)}, u32[]{:S(2)}) collective-permute-start(bf16[3,128,256]{2,1,0:T(8,128)(2,1)S(1)} %get-tuple-element.31), channel_id=1, source_target_pairs={{0,3},{1,2},{2,1},{3,0},{4,7},{5,6},{6,5},{7,4},{8,11},{9,10},{10,... | collective-permute-start | bytes 589832 | tf_op jit(solution)/shard_map/ppermute | solution.py:199
  42.6 18.6 %collective-permute-start.8 = (bf16[3,128,256]{2,1,0:T(8,128)(2,1)S(1)}, bf16[3,128,256]{2,1,0:T(8,128)(2,1)S(1)}, u32[]{:S(2)}, u32[]{:S(2)}) collective-permute-start(bf16[3,128,256]{2,1,0:T(8,128)(2,1)S(1)} %get-tuple-element.31), channel_id=1, source_target_pairs={{0,7},{1,6},{2,5},{3,4},{4,3},{5,2},{6,1},{7,0},{8,15},{9,14},{10,... | collective-permute-start | bytes 589832 | tf_op jit(solution)/shard_map/ppermute | solution.py:199
  95.0 7.8 %collective-permute-start.15 = (bf16[48,1536]{1,0:T(8,128)(2,1)S(1)}, bf16[48,1536]{1,0:T(8,128)(2,1)S(1)}, u32[]{:S(2)}, u32[]{:S(2)}) collective-permute-start(bf16[48,1536]{1,0:T(8,128)(2,1)S(1)} %get-tuple-element.40), channel_id=1, source_target_pairs={{0,2},{1,3},{2,0},{3,1},{4,6},{5,7},{6,4},{7,5},{8,10},{9,11},{10,... | collective-permute-start | bytes 442376 | tf_op jit(solution)/shard_map/ppermute | solution.py:199
  97.3 9.5 %collective-permute-start.16 = (bf16[48,1536]{1,0:T(8,128)(2,1)S(1)}, bf16[48,1536]{1,0:T(8,128)(2,1)S(1)}, u32[]{:S(2)}, u32[]{:S(2)}) collective-permute-start(bf16[48,1536]{1,0:T(8,128)(2,1)S(1)} %get-tuple-element.41), channel_id=1, source_target_pairs={{0,3},{1,2},{2,1},{3,0},{4,7},{5,6},{6,5},{7,4},{8,11},{9,10},{10,... | collective-permute-start | bytes 442376 | tf_op jit(solution)/shard_map/ppermute | solution.py:199
  97.3 9.5 %collective-permute-start.14 = (bf16[48,1536]{1,0:T(8,128)(2,1)S(1)}, bf16[48,1536]{1,0:T(8,128)(2,1)S(1)}, u32[]{:S(2)}, u32[]{:S(2)}) collective-permute-start(bf16[48,1536]{1,0:T(8,128)(2,1)S(1)} %get-tuple-element.39), channel_id=1, source_target_pairs={{0,1},{1,0},{2,3},{3,2},{4,5},{5,4},{6,7},{7,6},{8,9},{9,8},{10,11... | collective-permute-start | bytes 442376 | tf_op jit(solution)/shard_map/ppermute | solution.py:199
  99.3 10.1 %collective-permute-start.17 = (bf16[24,16,256]{2,1,0:T(8,128)(2,1)}, bf16[24,16,256]{2,1,0:T(8,128)(2,1)S(1)}, u32[]{:S(2)}, u32[]{:S(2)}) collective-permute-start(bf16[24,16,256]{2,1,0:T(8,128)(2,1)} %get-tuple-element.42), channel_id=1, source_target_pairs={{0,0},{1,8},{2,16},{3,24},{4,4},{5,12},{6,20},{7,28},{8,1},{9,9},{... | collective-permute-start | bytes 589832 | tf_op jit(solution)/shard_map/ppermute | solution.py:251
  100.9 10.6 %collective-permute-start.18 = (bf16[24,16,256]{2,1,0:T(8,128)(2,1)}, bf16[24,16,256]{2,1,0:T(8,128)(2,1)S(1)}, u32[]{:S(2)}, u32[]{:S(2)}) collective-permute-start(bf16[24,16,256]{2,1,0:T(8,128)(2,1)} %get-tuple-element.45), channel_id=1, source_target_pairs={{0,1},{1,9},{2,17},{3,25},{4,5},{5,13},{6,21},{7,29},{8,0},{9,8},{... | collective-permute-start | bytes 589832 | tf_op jit(solution)/shard_map/ppermute | solution.py:251
  102.9 10.0 %collective-permute-start.19 = (bf16[24,16,256]{2,1,0:T(8,128)(2,1)S(1)}, bf16[24,16,256]{2,1,0:T(8,128)(2,1)S(1)}, u32[]{:S(2)}, u32[]{:S(2)}) collective-permute-start(bf16[24,16,256]{2,1,0:T(8,128)(2,1)S(1)} %get-tuple-element.44), channel_id=1, source_target_pairs={{0,2},{1,10},{2,18},{3,26},{4,6},{5,14},{6,22},{7,30},{8,3},{9,11}... | collective-permute-start | bytes 589832 | tf_op jit(solution)/shard_map/ppermute | solution.py:251
  106.8 9.2 %collective-permute-start.20 = (bf16[24,16,256]{2,1,0:T(8,128)(2,1)S(1)}, bf16[24,16,256]{2,1,0:T(8,128)(2,1)S(1)}, u32[]{:S(2)}, u32[]{:S(2)}) collective-permute-start(bf16[24,16,256]{2,1,0:T(8,128)(2,1)S(1)} %get-tuple-element.43), channel_id=1, source_target_pairs={{0,3},{1,11},{2,19},{3,27},{4,7},{5,15},{6,23},{7,31},{8,2},{9,10}... | collective-permute-start | bytes 589832 | tf_op jit(solution)/shard_map/ppermute | solution.py:251
  116.1 1.1 copy-start.8

commit v2 on v1

v2 whole, which is shorter than its diff:
```python
import functools
import math

import jax
import jax.numpy as jnp
from jax import lax
from jax.experimental import pallas as pl
from jax.experimental.pallas import tpu as pltpu
from jax.sharding import Mesh, PartitionSpec as P

KV_HEADS = 4
HEAD_DIM = 128
LOW = -1e30
BF16 = jnp.bfloat16
F32 = jnp.float32

SMEM = pl.BlockSpec(memory_space=pltpu.SMEM)
VMEM = pl.BlockSpec(memory_space=pltpu.VMEM)
ANY = pl.BlockSpec(memory_space=pl.ANY)
HBM = pl.BlockSpec(memory_space=pltpu.HBM)
PARAMS = pltpu.CompilerParams(vmem_limit_bytes=40 * 1024 * 1024)


def pack_kernel(slots, spans, ids, home, pool_kv, fresh_q, fresh_kv, *rest):
    sems = rest[-1]
    pool_count, heads = (len(rest) - 1 - KV_HEADS) // 2, KV_HEADS
    to_pool, to_head = rest[: 2 * pool_count], rest[2 * pool_count : -1]
    me, head = ids[0], ids[2]
    half = pool_kv.shape[2] // 2
    q_width = fresh_q.shape[2] // heads
    kv_width = fresh_kv.shape[2] // heads
    copies = []
    for d in range(pool_count):
        request = me ^ d
        slot = jnp.int32(0)
        for t in range(spans):
            at = home[request * spans + t]
            slot = jnp.where(at // slots == me, at % slots, slot)
        for c in range(2):
            at = pl.ds(pl.multiple_of(((head // (heads // 2)) ^ c) * half, HEAD_DIM), half)
            copies.append(
                pltpu.make_async_copy(
                    pool_kv.at[slot, :, at], to_pool[c * pool_count + d], sems.at[0, c * pool_count + d]
                )
            )
            copies[-1].start()
    for d in range(heads):
        other = head ^ d
        q_at = pl.ds(pl.multiple_of(other * q_width, HEAD_DIM), q_width)
        kv_at = pl.ds(pl.multiple_of(other * kv_width, HEAD_DIM), kv_width)
        copies.append(
            pltpu.make_async_copy(fresh_q.at[0, :, q_at], to_head[d].at[:, pl.ds(0, q_width)], sems.at[1, d])
        )
        copies[-1].start()
        copies.append(
            pltpu.make_async_copy(fresh_kv.at[0, :, kv_at], to_head[d].at[:, pl.ds(q_width, kv_width)], sems.at[2, d])
        )
        copies[-1].start()
    for copy in copies:
        copy.wait()


def choose_kernel(slots, ids, home, order, *rest):
    sems = rest[-1]
    spans, heads = sems.shape
    arrived, out = rest[: -1 - heads], rest[-1 - heads : -1]
    me, head = ids[0], ids[2]
    width = out[0].shape[2]
    for start in (True, False):
        for j in range(spans):
            source = (home[order[0, j]] // slots) ^ me
            for d in range(heads):
                at = pl.ds(pl.multiple_of(((head % heads) ^ d) * width, HEAD_DIM), width)
                if start:
                    for p in range(len(arrived)):

                        @pl.when(source == p)
                        def _(p=p):
                            pltpu.make_async_copy(arrived[p].at[:, at], out[d].at[j], sems.at[j, d]).start()

                else:
                    pltpu.make_async_copy(arrived[0].at[:, at], out[d].at[j], sems.at[j, d]).wait()


def attend_kernel(ks, first, last, seq_count, rows, stacked, ids, chosen, q, fresh, *rest):
    messages, rest = rest[: len(ks)], rest[len(ks) :]
    spans, block, _ = messages[0].shape
    quad_rows = q.shape[0]
    group = (q.shape[1] - 2 * HEAD_DIM) // HEAD_DIM
    if not first:
        (acc_in, top_in, total_in), rest = rest[:3], rest[3:]
    outs, (keys, values, bias) = rest[:-3], rest[-3:]
    count = keys.shape[0]
    me = ids[1] * KV_HEADS + ids[2]

    values[:, HEAD_DIM:] = jnp.ones((count, HEAD_DIM), BF16)
    for at, k in enumerate(ks):
        for j in range(spans):
            row = pl.ds((at * spans + j) * block, block)
            keys[row, :] = messages[at][j, :, :HEAD_DIM]
            values[row, :HEAD_DIM] = messages[at][j, :, HEAD_DIM:]
        for i in range(chosen.shape[1]):
            picked = chosen[0, i]

            @pl.when(picked % seq_count == me ^ k)
            def _():
                row = pl.ds(pl.multiple_of((at * spans + picked // seq_count) * block, block), block)
                keys[row, :] = fresh[pl.ds(i * block, block), :HEAD_DIM]
                values[row, :HEAD_DIM] = fresh[pl.ds(i * block, block), HEAD_DIM:]

    local = lax.broadcasted_iota(jnp.int32, (quad_rows, 1), 0)
    listed = (ids[1] * KV_HEADS + (ids[2] ^ (local // rows))) * rows + local % rows
    which = listed // block
    place = jnp.zeros((quad_rows, 1), jnp.int32)
    for i in range(chosen.shape[1]):
        place = jnp.where(which == i, chosen[0, i] * block, place)
    place = place + listed % block
    for at, k in enumerate(ks):
        for j in range(spans):
            key = (j * seq_count + (me ^ k)) * block + lax.broadcasted_iota(jnp.int32, (quad_rows, block), 1)
            bias[:, pl.ds((at * spans + j) * block, block)] = jnp.where(key <= place, 0.0, LOW)

    scale = math.log2(math.e) / math.sqrt(HEAD_DIM)
    wide = stacked * quad_rows
    for h in range(0, group, stacked):
        cols = [pl.ds((h + i) * HEAD_DIM, HEAD_DIM) for i in range(stacked)]
        query = jnp.concatenate([q[:, c] for c in cols], axis=0)
        s = lax.dot_general(query, keys[...], (((1,), (1,)), ((), ())), preferred_element_type=F32)
        s = (s.reshape(stacked, quad_rows, count) * scale + bias[...][None]).reshape(wide, count)
        top = jnp.broadcast_to(jnp.max(s, axis=1, keepdims=True), (wide, HEAD_DIM))
        if not first:
            before = top_in[h // stacked]
            top = jnp.maximum(top, before)
        p = jnp.exp2(s - jnp.concatenate([top] * (count // HEAD_DIM), axis=1))
        both = jnp.dot(p.astype(BF16), values[...], preferred_element_type=F32)
        acc, total = both[:, :HEAD_DIM], both[:, HEAD_DIM:]
        if not first:
            factor = jnp.exp2(before - top)
            acc = acc + factor * acc_in[h // stacked]
            total = total + factor * total_in[h // stacked]
        if last:
            done = acc / total
            for i in range(stacked):
                for d, out in enumerate(outs):
                    at = i * quad_rows + d * rows
                    out[:, cols[i]] = done[at : at + rows].astype(BF16)
        else:
            outs[0][h // stacked] = acc
            outs[1][h // stacked] = top
            outs[2][h // stacked] = total


def attend(ks, state, last, seq_count, rows, ids, chosen, q, fresh, messages):
    quad_rows, width = q.shape
    group = (width - 2 * HEAD_DIM) // HEAD_DIM
    spans, block, kv_width = messages[0].shape
    keys = len(ks) * spans * block
    stacked = 2 - group % 2
    if last:
        out_shape = [jax.ShapeDtypeStruct((rows, group * HEAD_DIM), BF16)] * (quad_rows // rows)
    else:
        out_shape = [jax.ShapeDtypeStruct((group // stacked, stacked * quad_rows, HEAD_DIM), F32)] * 3
    inputs = [ids, chosen, q, fresh, *messages, *(state or ())]
    return pl.pallas_call(
        functools.partial(attend_kernel, ks, state is None, last, seq_count, rows, stacked),
        out_shape=out_shape,
        in_specs=[SMEM, SMEM] + [VMEM] * (len(inputs) - 2),
        out_specs=[VMEM] * len(out_shape),
        scratch_shapes=[
            pltpu.VMEM((keys, HEAD_DIM), BF16),
            pltpu.VMEM((keys, 2 * HEAD_DIM), BF16),
            pltpu.VMEM((quad_rows, keys), F32),
        ],
        compiler_params=PARAMS,
        cost_estimate=pl.CostEstimate(
            flops=4 * group * quad_rows * keys * HEAD_DIM,
            bytes_accessed=4 * quad_rows * width + 2 * keys * kv_width,
            transcendentals=group * quad_rows * keys,
        ),
        name="attend",
    )(*inputs)


def runs_kernel(ks, seq_count, ids, chosen, fresh, *rest):
    messages, outs = rest[: len(ks)], rest[len(ks) :]
    spans, block, _ = messages[0].shape
    run = outs[0].shape[2]
    me = ids[1] * KV_HEADS + ids[2]
    slab = len(outs) * run
    offset = ids[1] * slab

    def put(at, j, source, first):
        for m, out in enumerate(outs):
            if run % 16:
                rows = source[pl.ds(pl.multiple_of(first + offset, slab), slab), :].astype(F32)
                out[at, j] = rows[m * run : (m + 1) * run].astype(BF16)
            else:
                row = first + offset + (ids[0] ^ m) * run
                out[at, j] = source[pl.ds(pl.multiple_of(row, run), run), :]

    for at, k in enumerate(ks):
        for j in range(spans):
            put(at, j, messages[at].at[j], 0)
        for i in range(chosen.shape[1]):
            picked = chosen[0, i]

            @pl.when(picked % seq_count == me ^ k)
            def _():
                put(at, picked // seq_count, fresh, i * block)


def cut_runs(ks, seq_count, run, heads, ids, chosen, fresh, messages):
    spans, _, kv_width = messages[0].shape
    return pl.pallas_call(
        functools.partial(runs_kernel, ks, seq_count),
        out_shape=[jax.ShapeDtypeStruct((len(ks), spans, run, kv_width), BF16)] * heads,
        in_specs=[SMEM, SMEM, VMEM] + [VMEM] * len(ks),
        out_specs=[VMEM] * heads,
        compiler_params=PARAMS,
        name="runs",
    )(ids, chosen, fresh, *messages)


def lay_kernel(seq_count, pieces, ids, *rest):
    landed, out = rest[:-1], rest[-1]
    spans, run, width = landed[0].shape[1:]
    count = seq_count * spans * run
    blocks = spans * seq_count
    seat = ids[1] * KV_HEADS + ids[0]
    at = lax.broadcasted_iota(jnp.int32, (count, count), 1)
    source = seat ^ (at // (spans * run))
    target = (at % run) * blocks + (at // run) % spans * seq_count + source
    order = (lax.broadcasted_iota(jnp.int32, (count, count), 0) == target).astype(F32).astype(BF16)
    for k in range(len(landed) // pieces):
        parts = [landed[k * pieces + i][...] for i in range(pieces)]
        if run % 16:
            parts = [part.astype(F32) for part in parts]
        rows = jnp.concatenate([part.reshape(-1, width) for part in parts], axis=0).astype(BF16)
        laid = jnp.dot(order, rows, preferred_element_type=F32)
        request = ids[2] ^ k
        for u in range(run):
            out[0, 0, request, :, pl.ds(u * width, width)] = laid[u * blocks : (u + 1) * blocks].astype(BF16)


def join_kernel(ids, *rest):
    parts, out = rest[:-1], rest[-1]
    width = parts[0].shape[1]
    for d, part in enumerate(parts):
        out[0, :, pl.ds(pl.multiple_of((ids[2] ^ d) * width, HEAD_DIM), width)] = part[...]


def shards(pool_kv, span_home, span_order, chosen, fresh_q, fresh_kv):
    pool_count, quads, heads = (lax.axis_size(a) for a in ("pool", "quad", "head"))
    seq_count = quads * heads
    me, quad, head = (lax.axis_index(a) for a in ("pool", "quad", "head"))
    slots, block, width = pool_kv.shape
    spans = span_order.shape[1]
    rows, q_width = fresh_q.shape[1:]
    kv_width = width // heads
    q_part = q_width // heads
    run = block // seq_count
    ids = jnp.stack([me, quad, head]).astype(jnp.int32)
    seat = quad * heads + head

    packed = pl.pallas_call(
        functools.partial(pack_kernel, slots, spans),
        out_shape=[jax.ShapeDtypeStruct((block, width // 2), BF16)] * (2 * pool_count)
        + [jax.ShapeDtypeStruct((rows, q_part + kv_width), BF16)] * heads,
        in_specs=[SMEM, SMEM, HBM, HBM, HBM],
        out_specs=[ANY] * (2 * pool_count + heads),
        scratch_shapes=[pltpu.SemaphoreType.DMA((3, 2 * max(pool_count, heads)))],
        compiler_params=PARAMS,
        name="pack",
    )(ids, span_home, pool_kv, fresh_q, fresh_kv)
    to_pool = packed[:pool_count], packed[pool_count : 2 * pool_count]
    to_head = packed[2 * pool_count :]

    def swap(value, axes, count, k):
        return lax.ppermute(value, axes, [(i, i ^ k) for i in range(count)])

    def from_pool(values):
        arrived = [values[0]] + [None] * (pool_count - 1)
        for k in reversed(range(1, pool_count)):
            arrived[k] = swap(values[k], "pool", pool_count, k)
        return pl.pallas_call(
            functools.partial(choose_kernel, slots),
            out_shape=[jax.ShapeDtypeStruct((spans, block, kv_width), BF16)] * (heads // 2),
            in_specs=[SMEM, SMEM, SMEM] + [ANY] * pool_count,
            out_specs=[ANY] * (heads // 2),
            scratch_shapes=[pltpu.SemaphoreType.DMA((spans, heads // 2))],
            compiler_params=PARAMS,
            name="choose",
        )(ids, span_home, span_order, *arrived)

    seq = ("quad", "head")
    near_kv = from_pool(to_pool[0])
    gathered = [to_head[0]] + [swap(to_head[k], "head", heads, k) for k in range(1, heads)]
    q = jnp.concatenate(gathered, axis=0)
    far_kv = from_pool(to_pool[1])
    kv_out = [*near_kv, *far_kv]

    messages = [kv_out[0]] + [None] * (seq_count - 1)
    for k in range(1, seq_count):
        messages[k] = swap(kv_out[k % heads], seq, seq_count, k)

    own = q[:, q_part:]
    parts = [own] + [swap(own, "quad", quads, k) for k in range(1, quads)]
    listed = jnp.stack(parts).reshape(seq_count, rows, kv_width)
    fresh = jnp.take(listed, seat ^ jnp.arange(seq_count), axis=0).reshape(seq_count * rows, kv_width)

    groups = [[k, k + 1] for k in range(0, seq_count, 2)]
    state = None
    for ks in groups:
        state = attend(
            ks, state, ks is groups[-1], seq_count, rows, ids, chosen, q, fresh, [messages[k] for k in ks]
        )

    landed = []
    for ks in (range(seq_count - 2), range(seq_count - 2, seq_count)):
        cut = cut_runs(list(ks), seq_count, run, heads, ids, chosen, fresh, [messages[k] for k in ks])
        if run % 16:
            cut = [lax.dynamic_index_in_dim(jnp.stack(cut), me ^ k, axis=0, keepdims=False) for k in range(heads)]
        went = []
        for k in range(pool_count):
            perm = [
                ((r * quads + a) * heads + g, (g * quads + a) * heads + (r ^ k))
                for r in range(pool_count)
                for a in range(quads)
                for g in range(heads)
            ]
            went.append(lax.ppermute(cut[k], ("pool", "quad", "head"), perm))
        landed.append(went)
    decoded = pl.pallas_call(
        functools.partial(lay_kernel, seq_count, len(landed)),
        out_shape=jax.ShapeDtypeStruct((1, 1, pool_count, spans * seq_count, run * kv_width), BF16),
        in_specs=[SMEM] + [VMEM] * (len(landed) * pool_count),
        out_specs=VMEM,
        compiler_params=PARAMS,
        name="lay",
    )(ids, *[part for parts in zip(*landed) for part in parts])

    back = [state[0]] + [swap(state[k], "head", heads, k) for k in range(1, heads)]
    attended = pl.pallas_call(
        join_kernel,
        out_shape=jax.ShapeDtypeStruct((1, rows, q_width), BF16),
        in_specs=[SMEM] + [VMEM] * heads,
        out_specs=VMEM,
        compiler_params=PARAMS,
        name="join",
    )(ids, *back)
    return (attended, decoded)


def solution(mesh):
    pool_count, seq_count = mesh.shape["pool"], mesh.shape["seq"]
    fine = Mesh(mesh.devices.reshape(pool_count, seq_count // KV_HEADS, KV_HEADS), ("pool", "quad", "head"))
    seq = ("quad", "head")
    in_specs = (
        P("pool", seq, None),
        P(),
        P("pool", None),
        P("pool", None),
        P("pool", seq, None),
        P("pool", seq, None),
    )
    out_specs = (P("pool", seq, None), P("pool", seq, None, None, None))
    return jax.shard_map(shards, mesh=fine, in_specs=in_specs, out_specs=out_specs, check_vma=False)
```

time: 119 us -> 99.7 us (0.84)
  local copies, waits for them, and re-layouts: 20.2 us -> 4.64 us
  starting transfers between devices: 35.3 us -> 50.7 us
  Pallas kernels: 30.4 us -> 22.1 us
  waiting for transfers between devices: 28 us -> 20.8 us
  other arithmetic: 3.34 us -> 0.24 us
    pallas_call x3 -> x4, Pallas kernels: 28.4 us -> 14.5 us  [attend(): pl.pallas_call(functools.partial(attend_kernel, ks, state is None, last,...]
    ppermute x4 -> x8, starting transfers between devices: 7.49 us -> 15.8 us  [shards(): went.append(lax.ppermute(cut[k], ('pool', 'quad', 'head'), perm))]
    ppermute x17 -> x20, waiting for transfers between devices: 21.4 us -> 14 us  [swap(): return lax.ppermute(value, axes, [(i, i ^ k) for i in range(count)])]
    gather x7 -> x0, local copies, waits for them, and re-layouts: 7.43 us -> none  [the longest x2 4.75 us: shards(): jnp.take(blocks, seat ^ jnp.arange(seq_count), axis=1)]
    ppermute x17 -> x20, starting transfers between devices: 27.8 us -> 34.9 us  [swap(): return lax.ppermute(value, axes, [(i, i ^ k) for i in range(count)])]
    unnamed x28 -> x17, local copies, waits for them, and re-layouts: 9.63 us -> 3.89 us
    pallas_call x1 -> x6, Pallas kernels: 1.01 us -> 6.46 us  [the longest x1 2.01 us: shards(): pl.pallas_call(functools.partial(lay_kernel, seq_count, len(landed)), out...]
    select_n x5 -> x0, other arithmetic: 2.2 us -> none  [the longest x1 1.02 us: shards(): landed = jnp.take(jnp.stack(landed), head ^ jnp.arange(pool_count), axis=0)]
  transfers between devices with their start and end apart: 21 -> 28, of which waited for: 6 -> 8; matrix products, arithmetic and copies ran while one was open for 10% -> 1% of each run, Pallas kernels for 1% -> 15%
where the time goes in v2:
time: 99.7 us; the launch traced here: 99.5 us
  starting transfers between devices  50.7 us (51%)
  Pallas kernels  22.1 us (22%)
  waiting for transfers between devices  20.8 us (21%)
  local copies, waits for them, and re-layouts  4.64 us (5%)
    ppermute x20, starting transfers between devices, swap(): return lax.ppermute(value, axes, [(i, i ^ k) for i in range(count)])  34.9 us
    ppermute x8, starting transfers between devices, shards(): went.append(lax.ppermute(cut[k], ('pool', 'quad', 'head'), perm))  15.8 us
    pallas_call x4, Pallas kernels, attend(): pl.pallas_call(functools.partial(attend_kernel, ks, state is None, last,...  14.5 us
    ppermute x20, waiting for transfers between devices, swap(): return lax.ppermute(value, axes, [(i, i ^ k) for i in range(count)])  14 us
    ppermute x8, waiting for transfers between devices, shards(): went.append(lax.ppermute(cut[k], ('pool', 'quad', 'head'), perm))  6.86 us
    unnamed x17, local copies, waits for them, and re-layouts  3.89 us
    pallas_call x1, Pallas kernels, shards(): pl.pallas_call(functools.partial(lay_kernel, seq_count, len(landed)), out...  2.01 us
  transfers between devices with their start and end apart: 28, of which 8 were waited for; matrix products, arithmetic and copies ran while one was open for 1% of the time, Pallas kernels for 15%

profile of v2, /device:TPU:0, one launch (start us, length us, event | category | flops | bytes accessed | tf_op | source)
XLA Modules:
  0.0 99.5 jit_solution(3010366575411838490)
XLA Ops:
  0.6 0.1 pad_add_fusion.ids
  0.7 1.2 %copy-done = bf16[4,128,1024]{2,1,0:T(8,128)(2,1)S(1)} copy-done((bf16[4,128,1024]{2,1,0:T(8,128)(2,1)S(1)}, bf16[4,128,1024]{2,1,0:T(8,128)(2,1)}, u32[]{:S(2)}) %copy-start) | copy-done | bytes 1048600
  1.9 1.1 %copy-done.1 = bf16[1,48,6144]{2,1,0:T(8,128)(2,1)S(1)} copy-done((bf16[1,48,6144]{2,1,0:T(8,128)(2,1)S(1)}, bf16[1,48,6144]{2,1,0:T(8,128)(2,1)}, u32[]{:S(2)}) %copy-start.1) | copy-done | bytes 589848
  3.0 0.9 copy-done.2
  3.9 0.7 copy-done.4
  4.6 1.2 %pack.1 = (bf16[128,512]{1,0:T(8,128)(2,1)S(1)}, bf16[128,512]{1,0:T(8,128)(2,1)S(1)}, bf16[128,512]{1,0:T(8,128)(2,1)S(1)}, bf16[128,512]{1,0:T(8,128)(2,1)S(1)...) custom-call(s32[3]{0:T(128)S(1)} %pad_add_fusion.ids, ...), custom_call_target="tpu_custom_call" | custom-call | tf_op jit(solution)/shard_map/pack/pallas_call | solution.py:265
  5.8 0.0 copy-start.5
  5.8 0.0 copy-start.6
  5.8 0.5 collective-permute-start
  6.3 2.6 %collective-permute-start.1 = (bf16[48,1792]{1,0:T(8,128)(2,1)S(1)}, bf16[48,1792]{1,0:T(8,128)(2,1)S(1)}, u32[]{:S(2)}, u32[]{:S(2)}) collective-permute-start(bf16[48,1792]{1,0:T(8,128)(2,1)S(1)} %get-tuple-element.41), channel_id=1, source_target_pairs={{0,2},{1,3},{2,0},{3,1},{4,6},{5,7},{6,4},{7,5},{8,10},{9,11},{10,... | collective-permute-start | bytes 516104 | tf_op jit(solution)/shard_map/ppermute | solution.py:279
  9.0 0.1 collective-permute-start.2
  9.1 1.6 %collective-permute-start.4 = (bf16[128,512]{1,0:T(8,128)(2,1)S(1)}, bf16[128,512]{1,0:T(8,128)(2,1)S(1)}, u32[]{:S(2)}, u32[]{:S(2)}) collective-permute-start(bf16[128,512]{1,0:T(8,128)(2,1)S(1)} %get-tuple-element.44), channel_id=1, source_target_pairs={{0,8},{8,0},{16,24},{24,16},{1,9},{9,1},{17,25},{25,17},{2,10},{10... | collective-permute-start | bytes 393224 | tf_op jit(solution)/shard_map/ppermute | solution.py:279
  10.7 1.5 %collective-permute-start.5 = (bf16[128,512]{1,0:T(8,128)(2,1)S(1)}, bf16[128,512]{1,0:T(8,128)(2,1)S(1)}, u32[]{:S(2)}, u32[]{:S(2)}) collective-permute-start(bf16[128,512]{1,0:T(8,128)(2,1)S(1)} %get-tuple-element.45), channel_id=1, source_target_pairs={{0,16},{8,24},{16,0},{24,8},{1,17},{9,25},{17,1},{25,9},{2,18},{10... | collective-permute-start | bytes 393224 | tf_op jit(solution)/shard_map/ppermute | solution.py:279
  12.2 0.1 broadcast_in_dim.14
  12.3 0.1 broadcast_in_dim.15
  12.4 0.4 collective-permute-start.6
  12.8 1.4 %collective-permute-done.1 = bf16[48,1792]{1,0:T(8,128)(2,1)S(1)} collective-permute-done((bf16[48,1792]{1,0:T(8,128)(2,1)S(1)}, bf16[48,1792]{1,0:T(8,128)(2,1)S(1)}, u32[]{:S(2)}, u32[]{:S(2)}) %collective-permute-start.1) | collective-permute-done | bytes 172064 | tf_op jit(solution)/shard_map/ppermute | solution.py:279
  14.2 1.9 %collective-permute-start.9 = (bf16[128,512]{1,0:T(8,128)(2,1)S(1)}, bf16[128,512]{1,0:T(8,128)(2,1)S(1)}, u32[]{:S(2)}, u32[]{:S(2)}) collective-permute-start(bf16[128,512]{1,0:T(8,128)(2,1)S(1)} %get-tuple-element.50), channel_id=1, source_target_pairs={{0,8},{8,0},{16,24},{24,16},{1,9},{9,1},{17,25},{25,17},{2,10},{10... | collective-permute-start | bytes 393224 | tf_op jit(solution)/shard_map/ppermute | solution.py:279
  16.1 1.3 %collective-permute-done.2 = bf16[48,1792]{1,0:T(8,128)(2,1)S(1)} collective-permute-done((bf16[48,1792]{1,0:T(8,128)(2,1)S(1)}, bf16[48,1792]{1,0:T(8,128)(2,1)S(1)}, u32[]{:S(2)}, u32[]{:S(2)}) %collective-permute-start.2) | collective-permute-done | bytes 172064 | tf_op jit(solution)/shard_map/ppermute | solution.py:279
  17.4 1.5 %collective-permute-start.10 = (bf16[128,512]{1,0:T(8,128)(2,1)S(1)}, bf16[128,512]{1,0:T(8,128)(2,1)S(1)}, u32[]{:S(2)}, u32[]{:S(2)}) collective-permute-start(bf16[128,512]{1,0:T(8,128)(2,1)S(1)} %get-tuple-element.51), channel_id=1, source_target_pairs={{0,16},{8,24},{16,0},{24,8},{1,17},{9,25},{17,1},{25,9},{2,18},{10... | collective-permute-start | bytes 393224 | tf_op jit(solution)/shard_map/ppermute | solution.py:279
  18.9 1.6 %collective-permute-done.9.rest_1_ = bf16[128,512]{1,0:T(8,128)(2,1)S(1)} collective-permute-done((bf16[128,512]{1,0:T(8,128)(2,1)S(1)}, bf16[128,512]{1,0:T(8,128)(2,1)S(1)}, u32[]{:S(2)}, u32[]{:S(2)}) %collective-permute-start.9) | collective-permute-done | bytes 131104 | tf_op jit(solution)/shard_map/ppermute | solution.py:279
  20.5 2.5 %collective-permute-start.11 = (bf16[128,512]{1,0:T(8,128)(2,1)S(1)}, bf16[128,512]{1,0:T(8,128)(2,1)S(1)}, u32[]{:S(2)}, u32[]{:S(2)}) collective-permute-start(bf16[128,512]{1,0:T(8,128)(2,1)S(1)} %get-tuple-element.52), channel_id=1, source_target_pairs={{0,24},{8,16},{16,8},{24,0},{1,25},{9,17},{17,9},{25,1},{2,26},{10... | collective-permute-start | bytes 393224 | tf_op jit(solution)/shard_map/ppermute | solution.py:279
  23.0 0.0 copy-start.3
  23.1 0.1 collective-permute-done.10.rest_2_
  23.2 2.8 %collective-permute-start.3 = (bf16[192,256]{1,0:T(8,128)(2,1)S(1)}, bf16[192,256]{1,0:T(8,128)(2,1)S(1)}, u32[]{:S(2)}, u32[]{:S(2)}) collective-permute-start(bf16[192,256]{1,0:T(8,128)(2,1)S(1)} %get-tuple-element.77), channel_id=1, source_target_pairs={{0,4},{4,0},{1,5},{5,1},{2,6},{6,2},{3,7},{7,3},{8,12},{12,8},{9,1... | collective-permute-start | bytes 294920 | tf_op jit(solution)/shard_map/ppermute | solution.py:279
  25.9 0.4 collective-permute-done.11.rest_3_
  26.4 0.8 choose.3
  27.2 0.6 collective-permute-start.13
  27.7 0.0 collective-permute-done.4.rest_1_
  27.7 2.4 %collective-permute-start.16 = (bf16[3,128,256]{2,1,0:T(8,128)(2,1)S(1)}, bf16[3,128,256]{2,1,0:T(8,128)(2,1)S(1)}, u32[]{:S(2)}, u32[]{:S(2)}) collective-permute-start(bf16[3,128,256]{2,1,0:T(8,128)(2,1)S(1)} %get-tuple-element.54), channel_id=1, source_target_pairs={{0,1},{1,0},{2,3},{3,2},{4,5},{5,4},{6,7},{7,6},{8,9},{9,8},{10,11... | collective-permute-start | bytes 589832 | tf_op jit(solution)/shard_map/ppermute | solution.py:279
  30.1 0.2 collective-permute-start.12
  30.3 0.0 collective-permute-done.6.rest_3_
  30.3 0.8 choose.2
  31.1 1.8 %collective-permute-start.14 = (bf16[3,128,256]{2,1,0:T(8,128)(2,1)S(1)}, bf16[3,128,256]{2,1,0:T(8,128)(2,1)S(1)}, u32[]{:S(2)}, u32[]{:S(2)}) collective-permute-start(bf16[3,128,256]{2,1,0:T(8,128)(2,1)S(1)} %get-tuple-element.47), channel_id=1, source_target_pairs={{0,2},{1,3},{2,0},{3,1},{4,6},{5,7},{6,4},{7,5},{8,10},{9,11},{10,... | collective-permute-start | bytes 589832 | tf_op jit(solution)/shard_map/ppermute | solution.py:279
  32.8 0.0 collective-permute-done.3
  32.8 5.6 %collective-permute-start.15 = (bf16[3,128,256]{2,1,0:T(8,128)(2,1)S(1)}, bf16[3,128,256]{2,1,0:T(8,128)(2,1)S(1)}, u32[]{:S(2)}, u32[]{:S(2)}) collective-permute-start(bf16[3,128,256]{2,1,0:T(8,128)(2,1)S(1)} %get-tuple-element.48), channel_id=1, source_target_pairs={{0,3},{1,2},{2,1},{3,0},{4,7},{5,6},{6,5},{7,4},{8,11},{9,10},{10,... | collective-permute-start | bytes 589832 | tf_op jit(solution)/shard_map/ppermute | solution.py:279
  38.5 0.6 gather_fusion
  39.1 0.1 bitcast_select_fusion.fresh
  39.2 0.6 collective-permute-done.14.rest_0_.rest_2_
  39.8 4.9 %collective-permute-start.7 = (bf16[3,128,256]{2,1,0:T(8,128)(2,1)S(1)}, bf16[3,128,256]{2,1,0:T(8,128)(2,1)S(1)}, u32[]{:S(2)}, u32[]{:S(2)}) collective-permute-start(bf16[3,128,256]{2,1,0:T(8,128)(2,1)S(1)} %get-tuple-element.47), channel_id=1, source_target_pairs={{0,6},{1,7},{2,4},{3,5},{4,2},{5,3},{6,0},{7,1},{8,14},{9,15},{10,... | collective-permute-start | bytes 589832 | tf_op jit(solution)/shard_map/ppermute | solution.py:279
  44.7 1.7 %collective-permute-start.8 = (bf16[3,128,256]{2,1,0:T(8,128)(2,1)S(1)}, bf16[3,128,256]{2,1,0:T(8,128)(2,1)S(1)}, u32[]{:S(2)}, u32[]{:S(2)}) collective-permute-start(bf16[3,128,256]{2,1,0:T(8,128)(2,1)S(1)} %get-tuple-element.48), channel_id=1, source_target_pairs={{0,7},{1,6},{2,5},{3,4},{4,3},{5,2},{6,1},{7,0},{8,15},{9,14},{10,... | collective-permute-start | bytes 589832 | tf_op jit(solution)/shard_map/ppermute | solution.py:279
  46.4 3.5 %attend.4 = (f32[6,384,128]{2,1,0:T(8,128)S(1)}, f32[6,384,128]{2,1,0:T(8,128)S(1)}, f32[6,384,128]{2,1,0:T(8,128)S(1)}) custom-call(s32[3]{0:T(128)S(1)} %pad_add_fusion.ids, s32[1,3]{1,0:T(1,128)S(1)} %copy-done.3, bf16[192,1792]{1,0:T(8,128)(2,1)S(1)} %constant_dynamic-update-slice_fusion.q, bf16[384,256]{1,0:T(8,128)(2,1)S(1)} %bitcast_select_fusion.fresh, ...), custom_call_target="tpu_custom_call" | custom-call | flops 905969664 | bytes 1769472 | tf_op jit(solution)/shard_map/attend/pallas_call | solution.py:164
  49.9 8.6 %collective-permute-done.15.rest_1_.rest_3_ = bf16[3,128,256]{2,1,0:T(8,128)(2,1)S(1)} collective-permute-done((bf16[3,128,256]{2,1,0:T(8,128)(2,1)S(1)}, bf16[3,128,256]{2,1,0:T(8,128)(2,1)S(1)}, u32[]{:S(2)}, u32[]{:S(2)}) %collective-permute-start.15) | collective-permute-done | bytes 196640 | tf_op jit(solution)/shard_map/ppermute | solution.py:279
  58.5 3.6 %attend.5 = (f32[6,384,128]{2,1,0:T(8,128)S(1)}, f32[6,384,128]{2,1,0:T(8,128)S(1)}, f32[6,384,128]{2,1,0:T(8,128)S(1)}) custom-call(s32[3]{0:T(128)S(1)} %pad_add_fusion.ids, s32[1,3]{1,0:T(1,128)S(1)} %copy-done.3, bf16[192,1792]{1,0:T(8,128)(2,1)S(1)} %constant_dynamic-update-slice_fusion.q, bf16[384,256]{1,0:T(8,128)(2,1)S(1)} %bitcast_select_fusion.fresh, ...), custom_call_target="tpu_custom_call" | custom-call | flops 905969664 | bytes 1769472 | tf_op jit(solution)/shard_map/attend/pallas_call | solution.py:164
  62.2 0.0 collective-permute-done.13.rest_1_.rest_5_
  62.2 3.6 %attend.6 = (f32[6,384,128]{2,1,0:T(8,128)S(1)}, f32[6,384,128]{2,1,0:T(8,128)S(1)}, f32[6,384,128]{2,1,0:T(8,128)S(1)}) custom-call(s32[3]{0:T(128)S(1)} %pad_add_fusion.ids, s32[1,3]{1,0:T(1,128)S(1)} %copy-done.3, bf16[192,1792]{1,0:T(8,128)(2,1)S(1)} %constant_dynamic-update-slice_fusion.q, bf16[384,256]{1,0:T(8,128)(2,1)S(1)} %bitcast_select_fusion.fresh, ...), custom_call_target="tpu_custom_call" | custom-call | flops 905969664 | bytes 1769472 | tf_op jit(solution)/shard_map/attend/pallas_call | solution.py:164
  65.8 0.0 collective-permute-done.7.rest_0_
  65.8 0.0 collective-permute-done.8.rest_1_
  65.8 3.7 %attend.7 = (bf16[48,1536]{1,0:T(8,128)(2,1)S(1)}, bf16[48,1536]{1,0:T(8,128)(2,1)S(1)}, bf16[48,1536]{1,0:T(8,128)(2,1)S(1)}, bf16[48,1536]{1,0:T(8,128)(2,1)S(1)}) custom-call(s32[3]{0:T(128)S(1)} %pad_add_fusion.ids, s32[1,3]{1,0:T(1,128)S(1)} %copy-done.3, bf16[192,1792]{1,0:T(8,128)(2,1)S(1)} %constant_dynamic-update-slice_fusion.q, ...), custom_call_target="tpu_custom_call" | custom-call | flops 905969664 | bytes 1769472 | tf_op jit(solution)/shard_map/attend/pallas_call | solution.py:164
  69.6 0.9 collective-permute-start.17
  70.5 0.0 collective-permute-start.18
  70.5 0.6 runs.3
  71.1 0.7 collective-permute-start.21
  71.8 3.1 %collective-permute-start.23 = (bf16[2,3,16,256]{3,2,1,0:T(8,128)(2,1)S(1)}, bf16[2,3,16,256]{3,2,1,0:T(8,128)(2,1)S(1)}, u32[]{:S(2)}, u32[]{:S(2)}) collective-permute-start(bf16[2,3,16,256]{3,2,1,0:T(8,128)(2,1)S(1)} %get-tuple-element.71), channel_id=1, source_target_pairs={{0,1},{1,9},{2,17},{3,25},{4,5},{5,13},{6,21},{7,29},{8,0},{9,8},{... | collective-permute-start | bytes 147464 | tf_op jit(solution)/shard_map/ppermute | solution.py:331
  74.9 4.0 %collective-permute-start.25 = (bf16[2,3,16,256]{3,2,1,0:T(8,128)(2,1)S(1)}, bf16[2,3,16,256]{3,2,1,0:T(8,128)(2,1)S(1)}, u32[]{:S(2)}, u32[]{:S(2)}) collective-permute-start(bf16[2,3,16,256]{3,2,1,0:T(8,128)(2,1)S(1)} %get-tuple-element.73), channel_id=1, source_target_pairs={{0,2},{1,10},{2,18},{3,26},{4,6},{5,14},{6,22},{7,30},{8,3},{9,11}... | collective-permute-start | bytes 147464 | tf_op jit(solution)/shard_map/ppermute | solution.py:331
  78.8 1.4 %collective-permute-start.19 = (bf16[48,1536]{1,0:T(8,128)(2,1)S(1)}, bf16[48,1536]{1,0:T(8,128)(2,1)S(1)}, u32[]{:S(2)}, u32[]{:S(2)}) collective-permute-start(bf16[48,1536]{1,0:T(8,128)(2,1)S(1)} %get-tuple-element.67), channel_id=1, source_target_pairs={{0,3},{1,2},{2,1},{3,0},{4,7},{5,6},{6,5},{7,4},{8,11},{9,10},{10,... | collective-permute-start | bytes 442376 | tf_op jit(solution)/shard_map/ppermute | solution.py:279
  80.2 0.8 runs.2
  81.1 0.7 collective-permute-start.20
  81.7 1.5 %collective-permute-start.22 = (bf16[6,3,16,256]{3,2,1,0:T(8,128)(2,1)S(1)}, bf16[6,3,16,256]{3,2,1,0:T(8,128)(2,1)S(1)}, u32[]{:S(2)}, u32[]{:S(2)}) collective-permute-start(bf16[6,3,16,256]{3,2,1,0:T(8,128)(2,1)S(1)} %get-tuple-element.70), channel_id=1, source_target_pairs={{0,1},{1,9},{2,17},{3,25},{4,5},{5,13},{6,21},{7,29},{8,0},{9,8},{... | collective-permute-start | bytes 442376 | tf_op jit(solution)/shard_map/ppermute | solution.py:331
  83.2 3.9 %collective-permute-start.24 = (bf16[6,3,16,256]{3,2,1,0:T(8,128)(2,1)S(1)}, bf16[6,3,16,256]{3,2,1,0:T(8,128)(2,1)S(1)}, u32[]{:S(2)}, u32[]{:S(2)}) collective-permute-start(bf16[6,3,16,256]{3,2,1,0:T(8,128)(2,1)S(1)} %get-tuple-element.72), channel_id=1, source_target_pairs={{0,2},{1,10},{2,18},{3,26},{4,6},{5,14},{6,22},{7,30},{8,3},{9,11}... | collective-permute-start | bytes 442376 | tf_op jit(solution)/shard_map/ppermute | solution.py:331
  87.1 2.1 %collective-permute-start.27 = (bf16[2,3,16,256]{3,2,1,0:T(8,128)(2,1)S(1)}, bf16[2,3,16,256]{3,2,1,0:T(8,128)(2,1)S(1)}, u32[]{:S(2)}, u32[]{:S(2)}) collective-permute-start(bf16[2,3,16,256]{3,2,1,0:T(8,128)(2,1)S(1)} %get-tuple-element.75), channel_id=1, source_target_pairs={{0,3},{1,11},{2,19},{3,27},{4,7},{5,15},{6,23},{7,31},{8,2},{9,10}... | collective-permute-start | bytes 147464 | tf_op jit(solution)/shard_map/ppermute | solution.py:331
  89.2 1.4 %join.1 = bf16[1,48,6144]{2,1,0:T(8,128)(2,1)} custom-call(s32[3]{0:T(128)S(1)} %pad_add_fusion.ids, bf16[48,1536]{1,0:T(8,128)(2,1)S(1)} %get-tuple-element.64.rest_0_, bf16[48,1536]{1,0:T(8,128)(2,1)S(1)} %collective-permute-done.17.rest_1_, bf16[48,1536]{1,0:T(8,128)(2,1)S(1)} %collective-permute-done.18.rest_2_, ...), custom_call_target="tpu_custom_call" | custom-call | tf_op jit(solution)/shard_map/join/pallas_call | solution.py:343
  90.6 6.8 %collective-permute-done.27.rest_7_ = bf16[2,3,16,256]{3,2,1,0:T(8,128)(2,1)S(1)} collective-permute-done((bf16[2,3,16,256]{3,2,1,0:T(8,128)(2,1)S(1)}, bf16[2,3,16,256]{3,2,1,0:T(8,128)(2,1)S(1)}, u32[]{:S(2)}, u32[]{:S(2)}) %collective-permute-start.27) | collective-permute-done | bytes 49184 | tf_op jit(solution)/shard_map/ppermute | solution.py:331
  97.5 2.0 %lay.1 = bf16[1,1,4,24,4096]{4,3,2,1,0:T(8,128)(2,1)} custom-call(s32[3]{0:T(128)S(1)} %pad_add_fusion.ids, bf16[6,3,16,256]{3,2,1,0:T(8,128)(2,1)S(1)} %collective-permute-done.20.rest_0_, bf16[2,3,16,256]{3,2,1,0:T(8,128)(2,1)S(1)} %collective-permute-done.21.rest_1_, bf16[6,3,16,256]{3,2,1,0:T(8,128)(2,1)S(1)} %collective-permute-done.22.rest_2_, ...), custom_call_target="tpu_custom_call" | custom-call | tf_op jit(solution)/shard_map/lay/pallas_call | solution.py:333
  (31 shorter events, 0.2 us)
Async XLA Ops:
  0.7 1.2 %copy-start = (bf16[4,128,1024]{2,1,0:T(8,128)(2,1)S(1)}, bf16[4,128,1024]{2,1,0:T(8,128)(2,1)}, u32[]{:S(2)}) copy-start(bf16[4,128,1024]{2,1,0:T(8,128)(2,1)} %pool_kv.1) | copy-start | bytes 3145732
  1.9 1.1 %copy-start.1 = (bf16[1,48,6144]{2,1,0:T(8,128)(2,1)S(1)}, bf16[1,48,6144]{2,1,0:T(8,128)(2,1)}, u32[]{:S(2)}) copy-start(bf16[1,48,6144]{2,1,0:T(8,128)(2,1)} %fresh_q.1) | copy-start | bytes 1769476
  3.0 0.9 copy-start.2
  3.9 0.7 copy-start.4
  5.8 20.6 %copy-start.5 = (s32[12]{0:T(128)S(1)}, s32[12]{0:T(128)}, u32[]{:S(2)}) copy-start(s32[12]{0:T(128)} %home.5) | copy-start | bytes 148
  5.8 20.5 %copy-start.6 = (s32[1,3]{1,0:T(1,128)S(1)}, s32[1,3]{1,0:T(1,128)}, u32[]{:S(2)}) copy-start(s32[1,3]{1,0:T(1,128)} %order.3) | copy-start | bytes 40
  5.8 6.6 %collective-permute-start = (bf16[48,1792]{1,0:T(8,128)(2,1)S(1)}, bf16[48,1792]{1,0:T(8,128)(2,1)S(1)}, u32[]{:S(2)}, u32[]{:S(2)}) collective-permute-start(bf16[48,1792]{1,0:T(8,128)(2,1)S(1)} %get-tuple-element.40), channel_id=1, source_target_pairs={{0,1},{1,0},{2,3},{3,2},{4,5},{5,4},{6,7},{7,6},{8,9},{9,8},{10,11... | collective-permute-start | bytes 516104 | tf_op jit(solution)/shard_map/ppermute | solution.py:279
  6.3 7.9 %collective-permute-start.1 = (bf16[48,1792]{1,0:T(8,128)(2,1)S(1)}, bf16[48,1792]{1,0:T(8,128)(2,1)S(1)}, u32[]{:S(2)}, u32[]{:S(2)}) collective-permute-start(bf16[48,1792]{1,0:T(8,128)(2,1)S(1)} %get-tuple-element.41), channel_id=1, source_target_pairs={{0,2},{1,3},{2,0},{3,1},{4,6},{5,7},{6,4},{7,5},{8,10},{9,11},{10,... | collective-permute-start | bytes 516104 | tf_op jit(solution)/shard_map/ppermute | solution.py:279
  9.0 8.4 %collective-permute-start.2 = (bf16[48,1792]{1,0:T(8,128)(2,1)S(1)}, bf16[48,1792]{1,0:T(8,128)(2,1)S(1)}, u32[]{:S(2)}, u32[]{:S(2)}) collective-permute-start(bf16[48,1792]{1,0:T(8,128)(2,1)S(1)} %get-tuple-element.42), channel_id=1, source_target_pairs={{0,3},{1,2},{2,1},{3,0},{4,7},{5,6},{6,5},{7,4},{8,11},{9,10},{10,... | collective-permute-start | bytes 516104 | tf_op jit(solution)/shard_map/ppermute | solution.py:279
  9.1 18.6 %collective-permute-start.4 = (bf16[128,512]{1,0:T(8,128)(2,1)S(1)}, bf16[128,512]{1,0:T(8,128)(2,1)S(1)}, u32[]{:S(2)}, u32[]{:S(2)}) collective-permute-start(bf16[128,512]{1,0:T(8,128)(2,1)S(1)} %get-tuple-element.44), channel_id=1, source_target_pairs={{0,8},{8,0},{16,24},{24,16},{1,9},{9,1},{17,25},{25,17},{2,10},{10... | collective-permute-start | bytes 393224 | tf_op jit(solution)/shard_map/ppermute | solution.py:279
  10.7 19.4 %collective-permute-start.5 = (bf16[128,512]{1,0:T(8,128)(2,1)S(1)}, bf16[128,512]{1,0:T(8,128)(2,1)S(1)}, u32[]{:S(2)}, u32[]{:S(2)}) collective-permute-start(bf16[128,512]{1,0:T(8,128)(2,1)S(1)} %get-tuple-element.45), channel_id=1, source_target_pairs={{0,16},{8,24},{16,0},{24,8},{1,17},{9,25},{17,1},{25,9},{2,18},{10... | collective-permute-start | bytes 393224 | tf_op jit(solution)/shard_map/ppermute | solution.py:279
  12.4 17.8 %collective-permute-start.6 = (bf16[128,512]{1,0:T(8,128)(2,1)S(1)}, bf16[128,512]{1,0:T(8,128)(2,1)S(1)}, u32[]{:S(2)}, u32[]{:S(2)}) collective-permute-start(bf16[128,512]{1,0:T(8,128)(2,1)S(1)} %get-tuple-element.46), channel_id=1, source_target_pairs={{0,24},{8,16},{16,8},{24,0},{1,25},{9,17},{17,9},{25,1},{2,26},{10... | collective-permute-start | bytes 393224 | tf_op jit(solution)/shard_map/ppermute | solution.py:279
  14.2 6.3 %collective-permute-start.9 = (bf16[128,512]{1,0:T(8,128)(2,1)S(1)}, bf16[128,512]{1,0:T(8,128)(2,1)S(1)}, u32[]{:S(2)}, u32[]{:S(2)}) collective-permute-start(bf16[128,512]{1,0:T(8,128)(2,1)S(1)} %get-tuple-element.50), channel_id=1, source_target_pairs={{0,8},{8,0},{16,24},{24,16},{1,9},{9,1},{17,25},{25,17},{2,10},{10... | collective-permute-start | bytes 393224 | tf_op jit(solution)/shard_map/ppermute | solution.py:279
  17.4 5.8 %collective-permute-start.10 = (bf16[128,512]{1,0:T(8,128)(2,1)S(1)}, bf16[128,512]{1,0:T(8,128)(2,1)S(1)}, u32[]{:S(2)}, u32[]{:S(2)}) collective-permute-start(bf16[128,512]{1,0:T(8,128)(2,1)S(1)} %get-tuple-element.51), channel_id=1, source_target_pairs={{0,16},{8,24},{16,0},{24,8},{1,17},{9,25},{17,1},{25,9},{2,18},{10... | collective-permute-start | bytes 393224 | tf_op jit(solution)/shard_map/ppermute | solution.py:279
  20.5 5.9 %collective-permute-start.11 = (bf16[128,512]{1,0:T(8,128)(2,1)S(1)}, bf16[128,512]{1,0:T(8,128)(2,1)S(1)}, u32[]{:S(2)}, u32[]{:S(2)}) collective-permute-start(bf16[128,512]{1,0:T(8,128)(2,1)S(1)} %get-tuple-element.52), channel_id=1, source_target_pairs={{0,24},{8,16},{16,8},{24,0},{1,25},{9,17},{17,9},{25,1},{2,26},{10... | collective-permute-start | bytes 393224 | tf_op jit(solution)/shard_map/ppermute | solution.py:279
  23.0 23.4 %copy-start.3 = (s32[1,3]{1,0:T(1,128)S(1)}, s32[1,3]{1,0:T(1,128)}, u32[]{:S(2)}) copy-start(s32[1,3]{1,0:T(1,128)} %chosen.11) | copy-start | bytes 40
  23.2 9.7 %collective-permute-start.3 = (bf16[192,256]{1,0:T(8,128)(2,1)S(1)}, bf16[192,256]{1,0:T(8,128)(2,1)S(1)}, u32[]{:S(2)}, u32[]{:S(2)}) collective-permute-start(bf16[192,256]{1,0:T(8,128)(2,1)S(1)} %get-tuple-element.77), channel_id=1, source_target_pairs={{0,4},{4,0},{1,5},{5,1},{2,6},{6,2},{3,7},{7,3},{8,12},{12,8},{9,1... | collective-permute-start | bytes 294920 | tf_op jit(solution)/shard_map/ppermute | solution.py:279
  27.2 35.0 %collective-permute-start.13 = (bf16[3,128,256]{2,1,0:T(8,128)(2,1)S(1)}, bf16[3,128,256]{2,1,0:T(8,128)(2,1)S(1)}, u32[]{:S(2)}, u32[]{:S(2)}) collective-permute-start(bf16[3,128,256]{2,1,0:T(8,128)(2,1)S(1)} %get-tuple-element.54), channel_id=1, source_target_pairs={{0,5},{1,4},{2,7},{3,6},{4,1},{5,0},{6,3},{7,2},{8,13},{9,12},{10,... | collective-permute-start | bytes 589832 | tf_op jit(solution)/shard_map/ppermute | solution.py:279
  27.7 17.0 %collective-permute-start.16 = (bf16[3,128,256]{2,1,0:T(8,128)(2,1)S(1)}, bf16[3,128,256]{2,1,0:T(8,128)(2,1)S(1)}, u32[]{:S(2)}, u32[]{:S(2)}) collective-permute-start(bf16[3,128,256]{2,1,0:T(8,128)(2,1)S(1)} %get-tuple-element.54), channel_id=1, source_target_pairs={{0,1},{1,0},{2,3},{3,2},{4,5},{5,4},{6,7},{7,6},{8,9},{9,8},{10,11... | collective-permute-start | bytes 589832 | tf_op jit(solution)/shard_map/ppermute | solution.py:279
  30.1 32.1 %collective-permute-start.12 = (bf16[3,128,256]{2,1,0:T(8,128)(2,1)S(1)}, bf16[3,128,256]{2,1,0:T(8,128)(2,1)S(1)}, u32[]{:S(2)}, u32[]{:S(2)}) collective-permute-start(bf16[3,128,256]{2,1,0:T(8,128)(2,1)S(1)} %get-tuple-element.53.rest_0_), channel_id=1, source_target_pairs={{0,4},{1,5},{2,6},{3,7},{4,0},{5,1},{6,2},{7,3},{8,12},{9,13},{10,... | collective-permute-start | bytes 589832 | tf_op jit(solution)/shard_map/ppermute | solution.py:279
  31.1 8.7 %collective-permute-start.14 = (bf16[3,128,256]{2,1,0:T(8,128)(2,1)S(1)}, bf16[3,128,256]{2,1,0:T(8,128)(2,1)S(1)}, u32[]{:S(2)}, u32[]{:S(2)}) collective-permute-start(bf16[3,128,256]{2,1,0:T(8,128)(2,1)S(1)} %get-tuple-element.47), channel_id=1, source_target_pairs={{0,2},{1,3},{2,0},{3,1},{4,6},{5,7},{6,4},{7,5},{8,10},{9,11},{10,... | collective-permute-start | bytes 589832 | tf_op jit(solution)/shard_map/ppermute | solution.py:279
  32.8 25.7 %collective-permute-start.15 = (bf16[3,128,256]{2,1,0:T(8,128)(2,1)S(1)}, bf16[3,128,256]{2,1,0:T(8,128)(2,1)S(1)}, u32[]{:S(2)}, u32[]{:S(2)}) collective-permute-start(bf16[3,128,256]{2,1,0:T(8,128)(2,1)S(1)} %get-tuple-element.48), channel_id=1, source_target_pairs={{0,3},{1,2},{2,1},{3,0},{4,7},{5,6},{6,5},{7,4},{8,11},{9,10},{10,... | collective-permute-start | bytes 589832 | tf_op jit(solution)/shard_map/ppermute | solution.py:279
  39.8 26.0 %collective-permute-start.7 = (bf16[3,128,256]{2,1,0:T(8,128)(2,1)S(1)}, bf16[3,128,256]{2,1,0:T(8,128)(2,1)S(1)}, u32[]{:S(2)}, u32[]{:S(2)}) collective-permute-start(bf16[3,128,256]{2,1,0:T(8,128)(2,1)S(1)} %get-tuple-element.47), channel_id=1, source_target_pairs={{0,6},{1,7},{2,4},{3,5},{4,2},{5,3},{6,0},{7,1},{8,14},{9,15},{10,... | collective-permute-start | bytes 589832 | tf_op jit(solution)/shard_map/ppermute | solution.py:279
  44.7 21.1 %collective-permute-start.8 = (bf16[3,128,256]{2,1,0:T(8,128)(2,1)S(1)}, bf16[3,128,256]{2,1,0:T(8,128)(2,1)S(1)}, u32[]{:S(2)}, u32[]{:S(2)}) collective-permute-start(bf16[3,128,256]{2,1,0:T(8,128)(2,1)S(1)} %get-tuple-element.48), channel_id=1, source_target_pairs={{0,7},{1,6},{2,5},{3,4},{4,3},{5,2},{6,1},{7,0},{8,15},{9,14},{10,... | collective-permute-start | bytes 589832 | tf_op jit(solution)/shard_map/ppermute | solution.py:279
  69.6 13.7 %collective-permute-start.17 = (bf16[48,1536]{1,0:T(8,128)(2,1)S(1)}, bf16[48,1536]{1,0:T(8,128)(2,1)S(1)}, u32[]{:S(2)}, u32[]{:S(2)}) collective-permute-start(bf16[48,1536]{1,0:T(8,128)(2,1)S(1)} %get-tuple-element.65), channel_id=1, source_target_pairs={{0,1},{1,0},{2,3},{3,2},{4,5},{5,4},{6,7},{7,6},{8,9},{9,8},{10,11... | collective-permute-start | bytes 442376 | tf_op jit(solution)/shard_map/ppermute | solution.py:279
  70.5 16.6 %collective-permute-start.18 = (bf16[48,1536]{1,0:T(8,128)(2,1)S(1)}, bf16[48,1536]{1,0:T(8,128)(2,1)S(1)}, u32[]{:S(2)}, u32[]{:S(2)}) collective-permute-start(bf16[48,1536]{1,0:T(8,128)(2,1)S(1)} %get-tuple-element.66), channel_id=1, source_target_pairs={{0,2},{1,3},{2,0},{3,1},{4,6},{5,7},{6,4},{7,5},{8,10},{9,11},{10,... | collective-permute-start | bytes 442376 | tf_op jit(solution)/shard_map/ppermute | solution.py:279
  71.1 7.7 %collective-permute-start.21 = (bf16[2,3,16,256]{3,2,1,0:T(8,128)(2,1)S(1)}, bf16[2,3,16,256]{3,2,1,0:T(8,128)(2,1)S(1)}, u32[]{:S(2)}, u32[]{:S(2)}) collective-permute-start(bf16[2,3,16,256]{3,2,1,0:T(8,128)(2,1)S(1)} %get-tuple-element.69), channel_id=1, source_target_pairs={{0,0},{1,8},{2,16},{3,24},{4,4},{5,12},{6,20},{7,28},{8,1},{9,9},{... | collective-permute-start | bytes 147464 | tf_op jit(solution)/shard_map/ppermute | solution.py:331
  71.8 9.3 %collective-permute-start.23 = (bf16[2,3,16,256]{3,2,1,0:T(8,128)(2,1)S(1)}, bf16[2,3,16,256]{3,2,1,0:T(8,128)(2,1)S(1)}, u32[]{:S(2)}, u32[]{:S(2)}) collective-permute-start(bf16[2,3,16,256]{3,2,1,0:T(8,128)(2,1)S(1)} %get-tuple-element.71), channel_id=1, source_target_pairs={{0,1},{1,9},{2,17},{3,25},{4,5},{5,13},{6,21},{7,29},{8,0},{9,8},{... | collective-permute-start | bytes 147464 | tf_op jit(solution)/shard_map/ppermute | solution.py:331
  74.9 6.9 %collective-permute-start.25 = (bf16[2,3,16,256]{3,2,1,0:T(8,128)(2,1)S(1)}, bf16[2,3,16,256]{3,2,1,0:T(8,128)(2,1)S(1)}, u32[]{:S(2)}, u32[]{:S(2)}) collective-permute-start(bf16[2,3,16,256]{3,2,1,0:T(8,128)(2,1)S(1)} %get-tuple-element.73), channel_id=1, source_target_pairs={{0,2},{1,10},{2,18},{3,26},{4,6},{5,14},{6,22},{7,30},{8,3},{9,11}... | collective-permute-start | bytes 147464 | tf_op jit(solution)/shard_map/ppermute | solution.py:331
  78.8 8.3 %collective-permute-start.19 = (bf16[48,1536]{1,0:T(8,128)(2,1)S(1)}, bf16[48,1536]{1,0:T(8,128)(2,1)S(1)}, u32[]{:S(2)}, u32[]{:S(2)}) collective-permute-start(bf16[48,1536]{1,0:T(8,128)(2,1)S(1)} %get-tuple-element.67), channel_id=1, source_target_pairs={{0,3},{1,2},{2,1},{3,0},{4,7},{5,6},{6,5},{7,4},{8,11},{9,10},{10,... | collective-permute-start | bytes 442376 | tf_op jit(solution)/shard_map/ppermute | solution.py:279
  81.1 16.4 %collective-permute-start.20 = (bf16[6,3,16,256]{3,2,1,0:T(8,128)(2,1)S(1)}, bf16[6,3,16,256]{3,2,1,0:T(8,128)(2,1)S(1)}, u32[]{:S(2)}, u32[]{:S(2)}) collective-permute-start(bf16[6,3,16,256]{3,2,1,0:T(8,128)(2,1)S(1)} %get-tuple-element.68), channel_id=1, source_target_pairs={{0,0},{1,8},{2,16},{3,24},{4,4},{5,12},{6,20},{7,28},{8,1},{9,9},{... | collective-permute-start | bytes 442376 | tf_op jit(solution)/shard_map/ppermute | solution.py:331
  81.7 15.7 %collective-permute-start.22 = (bf16[6,3,16,256]{3,2,1,0:T(8,128)(2,1)S(1)}, bf16[6,3,16,256]{3,2,1,0:T(8,128)(2,1)S(1)}, u32[]{:S(2)}, u32[]{:S(2)}) collective-permute-start(bf16[6,3,16,256]{3,2,1,0:T(8,128)(2,1)S(1)} %get-tuple-element.70), channel_id=1, source_target_pairs={{0,1},{1,9},{2,17},{3,25},{4,5},{5,13},{6,21},{7,29},{8,0},{9,8},{... | collective-permute-start | bytes 442376 | tf_op jit(solution)/shard_map/ppermute | solution.py:331
  83.2 14.2 %collective-permute-start.24 = (bf16[6,3,16,256]{3,2,1,0:T(8,128)(2,1)S(1)}, bf16[6,3,16,256]{3,2,1,0:T(8,128)(2,1)S(1)}, u32[]{:S(2)}, u32[]{:S(2)}) collective-permute-start(bf16[6,3,16,256]{3,2,1,0:T(8,128)(2,1)S(1)} %get-tuple-element.72), channel_id=1, source_target_pairs={{0,2},{1,10},{2,18},{3,26},{4,6},{5,14},{6,22},{7,30},{8,3},{9,11}... | collective-permute-start | bytes 442376 | tf_op jit(solution)/shard_map/ppermute | solution.py:331
  87.1 10.4 %collective-permute-start.26 = (bf16[6,3,16,256]{3,2,1,0:T(8,128)(2,1)S(1)}, bf16[6,3,16,256]{3,2,1,0:T(8,128)(2,1)S(1)}, u32[]{:S(2)}, u32[]{:S(2)}) collective-permute-start(bf16[6,3,16,256]{3,2,1,0:T(8,128)(2,1)S(1)} %get-tuple-element.74), channel_id=1, source_target_pairs={{0,3},{1,11},{2,19},{3,27},{4,7},{5,15},{6,23},{7,31},{8,2},{9,10}... | collective-permute-start | bytes 442376 | tf_op jit(solution)/shard_map/ppermute | solution.py:331
  87.1 10.3 %collective-permute-start.27 = (bf16[2,3,16,256]{3,2,1,0:T(8,128)(2,1)S(1)}, bf16[2,3,16,256]{3,2,1,0:T(8,128)(2,1)S(1)}, u32[]{:S(2)}, u32[]{:S(2)}) collective-permute-start(bf16[2,3,16,256]{3,2,1,0:T(8,128)(2,1)S(1)} %get-tuple-element.75), channel_id=1, source_target_pairs={{0,3},{1,11},{2,19},{3,27},{4,7},{5,15},{6,23},{7,31},{8,2},{9,10}... | collective-permute-start | bytes 147464 | tf_op jit(solution)/shard_map/ppermute | solution.py:331

commit v3 on v2

v3 whole, which is shorter than its diff:
```python
import functools
import math

import jax
import jax.numpy as jnp
from jax import lax
from jax.experimental import pallas as pl
from jax.experimental.pallas import tpu as pltpu
from jax.sharding import Mesh, PartitionSpec as P

KV_HEADS = 4
HEAD_DIM = 128
LOW = -1e30
HOME = 4
BF16 = jnp.bfloat16
F32 = jnp.float32

SMEM = pl.BlockSpec(memory_space=pltpu.SMEM)
VMEM = pl.BlockSpec(memory_space=pltpu.VMEM)
ANY = pl.BlockSpec(memory_space=pl.ANY)
HBM = pl.BlockSpec(memory_space=pltpu.HBM)
PARAMS = pltpu.CompilerParams(vmem_limit_bytes=40 * 1024 * 1024)
CHEAP = pl.CostEstimate(flops=1, bytes_accessed=1, transcendentals=1)
FULL = pltpu.CompilerParams(vmem_limit_bytes=60 * 1024 * 1024)


def turn(d):
    return (d & 1) * 3 ^ d >> 1


def pack_kernel(slots, spans, ids, pool_kv, *rest):
    outs, sems = rest[:-1], rest[-1]
    copies = []
    for d, out in enumerate(outs):
        slot = jnp.int32(0)
        for t in range(spans):
            held = ids[HOME + (ids[0] ^ d) * spans + t]
            slot = jnp.where(held // slots == ids[0], held % slots, slot)
        copies.append(pltpu.make_async_copy(pool_kv.at[slot], out, sems.at[d]))
        copies[-1].start()
    for copy in copies:
        copy.wait()


def split_kernel(ids, fresh_q, near, far, *rest):
    keep, give, send, sems = rest
    outs = (keep, give.at[0], send.at[0], send.at[1])
    q_width = fresh_q.shape[2] // KV_HEADS
    kv_width = near.shape[2] // KV_HEADS
    copies = []

    def copy(source, out, at):
        copies.append(pltpu.make_async_copy(source, out.at[:, at], sems.at[len(copies)]))
        copies[-1].start()

    for d, out in enumerate(outs):
        other = ids[3] ^ turn(d)
        q_at = pl.ds(pl.multiple_of(other * q_width, HEAD_DIM), q_width)
        kv_at = pl.ds(pl.multiple_of(other * kv_width, HEAD_DIM), kv_width)
        copy(fresh_q.at[0, :, q_at], out, pl.ds(0, q_width))
        copy(near.at[0, :, kv_at], out, pl.ds(q_width, kv_width))
        for a in range(far.shape[0]):
            copy(far.at[a, :, kv_at], out, pl.ds(q_width + (a + 1) * kv_width, kv_width))
    for each in copies:
        each.wait()


def arrays_of(views):
    arrays = []
    for array, _ in views:
        if not any(array is a for a in arrays):
            arrays.append(array)
    return arrays, [(next(i for i, a in enumerate(arrays) if a is array), index) for array, index in views]


def look(refs, views):
    return [refs[i] if index is None else refs[i].at[index] for i, index in views]


def sort_kernel(quads, views, ids, *rest):
    parts, out = look(rest[:-1], views), rest[-1]
    rows, width = parts[0].shape[0], out.shape[1]
    for d, part in enumerate(parts):
        for a in range(quads):
            seat = (ids[1] ^ a) * KV_HEADS + (ids[2] ^ d)
            first = part.shape[1] - (quads - a) * width
            out[pl.ds(pl.multiple_of(seat * rows, rows), rows), :] = part[:, first : first + width]


def choose_kernel(slots, pool_count, ids, *rest):
    arrived, (near, give, send), sems = rest[:pool_count], rest[pool_count:-1], rest[-1]
    outs = (near.at[0], give.at[0], send.at[0], give.at[1])
    spans, heads = sems.shape
    width = near.shape[3]
    for start in (True, False):
        for j in range(spans):
            source = (ids[HOME + ids[HOME + pool_count * spans + j]] // slots) ^ ids[0]
            for d in range(heads):
                at = pl.ds(pl.multiple_of((ids[3] ^ turn(d)) * width, HEAD_DIM), width)
                if start:
                    for p in range(pool_count):

                        @pl.when(source == p)
                        def _(p=p):
                            pltpu.make_async_copy(arrived[p].at[:, at], outs[d].at[j], sems.at[j, d]).start()

                else:
                    pltpu.make_async_copy(arrived[0].at[:, at], outs[d].at[j], sems.at[j, d]).wait()


def place_kernel(got, near_in, send_in, near, send):
    del near_in, send_in
    near[1] = got[0]
    send[1] = got[1]


def follow_kernel(got, give_in, give):
    del give_in
    give[1] = got[1]


def attend_kernel(ks, first, last, seq_count, rows, stacked, group, count_in, views, q_views, at_chosen, ids, fresh, *rest):
    messages, q = look(rest[:count_in], views), look(rest[:count_in], q_views)
    rest = rest[count_in:]
    spans, block, _ = messages[0].shape
    quad_rows = KV_HEADS * rows
    if not first:
        (acc_in, top_in, total_in), rest = rest[:3], rest[3:]
    outs, (keys, values, bias) = rest[:-3], rest[-3:]
    count = keys.shape[0]
    me = ids[1] * KV_HEADS + ids[2]

    values[:, HEAD_DIM:] = jnp.ones((count, HEAD_DIM), BF16)
    for at, k in enumerate(ks):
        for j in range(spans):
            row = pl.ds((at * spans + j) * block, block)
            keys[row, :] = messages[at][j, :, :HEAD_DIM]
            values[row, :HEAD_DIM] = messages[at][j, :, HEAD_DIM:]
        for i in range(ids.shape[0] - at_chosen):
            picked = ids[at_chosen + i]

            @pl.when(picked % seq_count == me ^ k)
            def _():
                row = pl.ds(pl.multiple_of((at * spans + picked // seq_count) * block, block), block)
                keys[row, :] = fresh[pl.ds(i * block, block), :HEAD_DIM]
                values[row, :HEAD_DIM] = fresh[pl.ds(i * block, block), HEAD_DIM:]

    local = lax.broadcasted_iota(jnp.int32, (quad_rows, 1), 0)
    listed = (ids[1] * KV_HEADS + (ids[2] ^ (local // rows))) * rows + local % rows
    which = listed // block
    place = jnp.zeros((quad_rows, 1), jnp.int32)
    for i in range(ids.shape[0] - at_chosen):
        place = jnp.where(which == i, ids[at_chosen + i] * block, place)
    place = place + listed % block
    for at, k in enumerate(ks):
        for j in range(spans):
            key = (j * seq_count + (me ^ k)) * block + lax.broadcasted_iota(jnp.int32, (quad_rows, block), 1)
            bias[:, pl.ds((at * spans + j) * block, block)] = jnp.where(key <= place, 0.0, LOW)

    scale = math.log2(math.e) / math.sqrt(HEAD_DIM)
    wide = stacked * quad_rows
    for h in range(0, group, stacked):
        cols = [pl.ds((h + i) * HEAD_DIM, HEAD_DIM) for i in range(stacked)]
        query = jnp.concatenate([part[:, c] for c in cols for part in q], axis=0)
        s = lax.dot_general(query, keys[...], (((1,), (1,)), ((), ())), preferred_element_type=F32)
        s = (s.reshape(stacked, quad_rows, count) * scale + bias[...][None]).reshape(wide, count)
        top = jnp.broadcast_to(jnp.max(s, axis=1, keepdims=True), (wide, HEAD_DIM))
        if not first:
            before = top_in[h // stacked]
            top = jnp.maximum(top, before)
        p = jnp.exp2(s - jnp.concatenate([top] * (count // HEAD_DIM), axis=1))
        both = jnp.dot(p.astype(BF16), values[...], preferred_element_type=F32)
        acc, total = both[:, :HEAD_DIM], both[:, HEAD_DIM:]
        if not first:
            factor = jnp.exp2(before - top)
            acc = acc + factor * acc_in[h // stacked]
            total = total + factor * total_in[h // stacked]
        if last:
            done = acc / total
            for i in range(stacked):
                for d in range(KV_HEADS):
                    at = i * quad_rows + d * rows
                    outs[d // 2][d % 2, :, cols[i]] = done[at : at + rows].astype(BF16)
        else:
            outs[0][h // stacked] = acc
            outs[1][h // stacked] = top
            outs[2][h // stacked] = total


def attend(ks, state, last, seq_count, rows, group, at_chosen, ids, q, fresh, messages):
    quad_rows = KV_HEADS * rows
    arrays, views = arrays_of([*messages, *q])
    spans, block, kv_width = messages[0][0].shape[-3:]
    keys = len(ks) * spans * block
    stacked = 2 - group % 2
    if last:
        out_shape = [jax.ShapeDtypeStruct((2, rows, group * HEAD_DIM), BF16)] * (KV_HEADS // 2)
    else:
        out_shape = [jax.ShapeDtypeStruct((group // stacked, stacked * quad_rows, HEAD_DIM), F32)] * 3
    inputs = [ids, fresh, *arrays, *(state or ())]
    return pl.pallas_call(
        functools.partial(
            attend_kernel,
            ks,
            state is None,
            last,
            seq_count,
            rows,
            stacked,
            group,
            len(arrays),
            views[: len(ks)],
            views[len(ks) :],
            at_chosen,
        ),
        out_shape=out_shape,
        in_specs=[SMEM] + [VMEM] * (len(inputs) - 1),
        out_specs=[VMEM] * len(out_shape),
        scratch_shapes=[
            pltpu.VMEM((keys, HEAD_DIM), BF16),
            pltpu.VMEM((keys, 2 * HEAD_DIM), BF16),
            pltpu.VMEM((quad_rows, keys), F32),
        ],
        compiler_params=PARAMS,
        cost_estimate=CHEAP,
        name="attend",
    )(*inputs)


def runs_kernel(ks, seq_count, count_in, views, at_chosen, ids, fresh, *rest):
    messages, outs = look(rest[:count_in], views), rest[count_in:]
    spans, block, _ = messages[0].shape
    run = outs[0].shape[2]
    me = ids[1] * KV_HEADS + ids[2]
    slab = len(outs) * run
    offset = ids[1] * slab

    def put(k, j, source, first):
        slot = ks.index(k) // KV_HEADS * KV_HEADS + (ids[2] ^ k % KV_HEADS)
        for m, out in enumerate(outs):
            if run % 16:
                rows = source[pl.ds(pl.multiple_of(first + offset, slab), slab), :].astype(F32)
                out[slot, j] = rows[m * run : (m + 1) * run].astype(BF16)
            else:
                row = first + offset + (ids[2] ^ m) * run
                out[slot, j] = source[pl.ds(pl.multiple_of(row, run), run), :]

    for at, k in enumerate(ks):
        for j in range(spans):
            put(k, j, messages[at].at[j], 0)
        for i in range(ids.shape[0] - at_chosen):
            picked = ids[at_chosen + i]

            @pl.when(picked % seq_count == me ^ k)
            def _():
                put(k, picked // seq_count, fresh, i * block)


def cut_runs(ks, seq_count, run, heads, at_chosen, ids, fresh, messages):
    arrays, views = arrays_of(messages)
    spans, _, kv_width = messages[0][0].shape[-3:]
    return pl.pallas_call(
        functools.partial(runs_kernel, ks, seq_count, len(arrays), views, at_chosen),
        out_shape=[jax.ShapeDtypeStruct((len(ks), spans, run, kv_width), BF16)] * heads,
        in_specs=[SMEM, VMEM] + [VMEM] * len(arrays),
        out_specs=[VMEM] * heads,
        compiler_params=PARAMS,
        cost_estimate=CHEAP,
        name="runs",
    )(ids, fresh, *arrays)


def lay_kernel(seq_count, parts, ids, *rest):
    landed, out = rest[:-1], rest[-1]
    spans, run, width = landed[0].shape[1:]
    count = seq_count * spans * run
    blocks = spans * seq_count
    at = lax.broadcasted_iota(jnp.int32, (count, count), 1)
    source = ids[1] * KV_HEADS ^ (at // (spans * run))
    target = (at % run) * blocks + (at // run) % spans * seq_count + source
    order = (lax.broadcasted_iota(jnp.int32, (count, count), 0) == target).astype(F32).astype(BF16)
    for k in range(KV_HEADS):
        rows = [landed[i * KV_HEADS + k][...] for i in range(parts)]
        if run % 16:
            rows = [part.astype(F32) for part in rows]
        rows = jnp.concatenate([part.reshape(-1, width) for part in rows], axis=0).astype(BF16)
        laid = jnp.dot(order, rows, preferred_element_type=F32)
        request = ids[0] ^ turn(ids[2] ^ k)
        for u in range(run):
            out[0, 0, request, :, pl.ds(u * width, width)] = laid[u * blocks : (u + 1) * blocks].astype(BF16)


def join_kernel(views, ids, *rest):
    parts, out = look(rest[:-1], views), rest[-1]
    width = parts[0].shape[1]
    for d, part in enumerate(parts):
        out[0, :, pl.ds(pl.multiple_of((ids[3] ^ turn(d)) * width, HEAD_DIM), width)] = part[...]


def shards(pool_kv, span_home, span_order, chosen, fresh_q, fresh_kv):
    pool_count, quads, heads = (lax.axis_size(a) for a in ("pool", "quad", "head"))
    seq_count = quads * heads
    me, quad, head = (lax.axis_index(a) for a in ("pool", "quad", "head"))
    slots, block, width = pool_kv.shape
    spans = span_order.shape[1]
    rows, q_width = fresh_q.shape[1:]
    kv_width = width // heads
    q_part = q_width // heads
    run = block // seq_count
    group = q_part // HEAD_DIM
    place = jnp.stack([me, quad, head, me ^ turn(head)]).astype(jnp.int32)
    ids = jnp.concatenate([place, span_home, span_order[0], chosen[0]])
    at_chosen = HOME + span_home.shape[0] + spans
    seat = quad * heads + head

    def after(value, *others):
        return lax.optimization_barrier((value, others))[0]

    def swap(value, axes, count, k):
        return lax.ppermute(value, axes, [(i, i ^ k) for i in range(count)])

    seq = ("quad", "head")
    to_pool = pl.pallas_call(
        functools.partial(pack_kernel, slots, spans),
        out_shape=[jax.ShapeDtypeStruct((block, width), BF16)] * pool_count,
        in_specs=[SMEM, ANY],
        out_specs=[ANY] * pool_count,
        scratch_shapes=[pltpu.SemaphoreType.DMA((pool_count,))],
        compiler_params=PARAMS,
        cost_estimate=CHEAP,
        name="pack",
    )(ids, pool_kv)
    far = [swap(after(fresh_kv, to_pool[0]), "quad", quads, k) for k in range(1, quads)]
    arrived = [to_pool[0]] + [None] * (pool_count - 1)
    for k in reversed(range(1, pool_count)):
        arrived[k] = swap(to_pool[k], "pool", pool_count, k)
    one = jax.ShapeDtypeStruct((rows, q_part + quads * kv_width), BF16)
    pair = jax.ShapeDtypeStruct((2, *one.shape), BF16)
    keep, give, send = pl.pallas_call(
        split_kernel,
        out_shape=[one, pair, pair],
        in_specs=[SMEM, ANY, ANY, ANY],
        out_specs=[ANY] * 3,
        scratch_shapes=[pltpu.SemaphoreType.DMA(((1 + quads) * heads,))],
        compiler_params=PARAMS,
        cost_estimate=CHEAP,
        name="split",
    )(ids, fresh_q, fresh_kv, far[0] if quads == 2 else jnp.concatenate(far, axis=0))
    chip = swap(send, "head", heads, 2)
    give = pl.pallas_call(
        follow_kernel,
        out_shape=pair,
        in_specs=[VMEM] * 2,
        out_specs=VMEM,
        input_output_aliases={1: 0},
        compiler_params=PARAMS,
        cost_estimate=CHEAP,
        name="follow",
    )(chip, give)
    core = swap(give, "head", heads, 1)
    q_give, q = give, [(keep, None), (core, 0), (chip, 0), (core, 1)]

    pair = jax.ShapeDtypeStruct((2, spans, block, kv_width), BF16)
    near, give, send = pl.pallas_call(
        functools.partial(choose_kernel, slots, pool_count),
        out_shape=[pair] * 3,
        in_specs=[SMEM] + [ANY] * pool_count,
        out_specs=[ANY] * 3,
        scratch_shapes=[pltpu.SemaphoreType.DMA((spans, heads))],
        compiler_params=PARAMS,
        cost_estimate=CHEAP,
        name="choose",
    )(ids, *after(arrived, send))

    def place(got, near, send):
        like = [jax.ShapeDtypeStruct(x.shape, x.dtype) for x in (near, send)]
        return pl.pallas_call(
            place_kernel,
            out_shape=like,
            in_specs=[VMEM] * 3,
            out_specs=[VMEM] * 2,
            input_output_aliases={1: 0, 2: 1},
            compiler_params=PARAMS,
            cost_estimate=CHEAP,
            name="place",
        )(got, near, send)

    near, send = place(after(swap(give, "head", heads, 1), q_give), near, send)
    rest = swap(send, "head", heads, 2)
    messages = [(near, 0), (near, 1), (rest, 0), (rest, 1)]

    if rows % 16:
        q = [(jnp.concatenate([part if index is None else part[index] for part, index in q], axis=0), None)]
        listed = q[0][0][:, q_part:].reshape(heads, rows, quads, kv_width).transpose(2, 0, 1, 3)
        listed = listed.reshape(seq_count, rows, kv_width)
        fresh = jnp.take(listed, seat ^ jnp.arange(seq_count), axis=0).reshape(seq_count * rows, kv_width)
    else:
        arrays, views = arrays_of(q)
        fresh = pl.pallas_call(
            functools.partial(sort_kernel, quads, views),
            out_shape=jax.ShapeDtypeStruct((seq_count * rows, kv_width), BF16),
            in_specs=[SMEM] + [VMEM] * len(arrays),
            out_specs=VMEM,
            compiler_params=PARAMS,
            cost_estimate=CHEAP,
            name="sort",
        )(ids, *arrays)

    def to_decode(ks, *dep):
        arrays, views = arrays_of([messages[k] for k in ks])
        arrays = after(arrays, dep)
        parts = [(arrays[i], index) for i, index in views]
        cut = cut_runs(ks, seq_count, run, heads, at_chosen, ids, fresh, parts)
        if run % 16:
            cut = [lax.dynamic_index_in_dim(jnp.stack(cut), head ^ k, axis=0, keepdims=False) for k in range(heads)]
        went = [None] * heads
        for k in reversed(range(heads)):
            perm = [
                ((r * quads + a) * heads + i, ((r ^ turn(i)) * quads + a) * heads + (i ^ k))
                for r in range(pool_count)
                for a in range(quads)
                for i in range(heads)
            ]
            went[k] = lax.ppermute(cut[k], ("pool", "quad", "head"), perm)
        return went, cut

    def work(ks, state, last=False):
        return attend(ks, state, last, seq_count, rows, group, at_chosen, ids, q, fresh, [messages[k] for k in ks])

    for a in range(1, quads):
        for half in (near, rest):
            crossed = swap(half, "quad", quads, a)
            messages += [(crossed, 0), (crossed, 1)]
    state = work(list(range(heads)), None)
    groups = [[k, k + 1] for k in range(heads, seq_count, 2)]
    far_ks = list(range(seq_count - heads, seq_count))
    for ks in groups[:-1]:
        if ks[0] == far_ks[0]:
            landed = [to_decode(list(range(far_ks[0])), state)]
            state = after(state, landed[0][1])
        state = work(ks, state)
    kept, sent = work(groups[-1], state, True)
    chip = swap(after(sent, landed[0][0]), "head", heads, 2)
    landed.append(to_decode(far_ks, kept))
    chip = after(chip, landed[1][0])
    core = swap(jnp.stack([kept[1], chip[1]]), "head", heads, 1)
    arrays, views = arrays_of([(kept, 0), (core, 0), (chip, 0), (core, 1)])
    attended = pl.pallas_call(
        functools.partial(join_kernel, views),
        out_shape=jax.ShapeDtypeStruct((1, rows, q_width), BF16),
        in_specs=[SMEM] + [VMEM] * len(arrays),
        out_specs=VMEM,
        compiler_params=PARAMS,
        cost_estimate=CHEAP,
        name="join",
    )(ids, *arrays)
    arrays = [part for went, _ in landed for part in went]
    decoded = pl.pallas_call(
        functools.partial(lay_kernel, seq_count, len(landed)),
        out_shape=jax.ShapeDtypeStruct((1, 1, pool_count, spans * seq_count, run * kv_width), BF16),
        in_specs=[SMEM] + [VMEM] * len(arrays),
        out_specs=VMEM,
        compiler_params=PARAMS,
        cost_estimate=CHEAP,
        name="lay",
    )(ids, *arrays)
    return (attended, decoded)


def solution(mesh):
    pool_count, seq_count = mesh.shape["pool"], mesh.shape["seq"]
    fine = Mesh(mesh.devices.reshape(pool_count, seq_count // KV_HEADS, KV_HEADS), ("pool", "quad", "head"))
    seq = ("quad", "head")
    in_specs = (
        P("pool", seq, None),
        P(),
        P("pool", None),
        P("pool", None),
        P("pool", seq, None),
        P("pool", seq, None),
    )
    out_specs = (P("pool", seq, None), P("pool", seq, None, None, None))
    return jax.shard_map(shards, mesh=fine, in_specs=in_specs, out_specs=out_specs, check_vma=False)
```

time: 99.7 us -> 88.1 us (0.88)
  starting transfers between devices: 50.7 us -> 29.2 us
  waiting for transfers between devices: 20.8 us -> 32.8 us
  local copies, waits for them, and re-layouts: 4.64 us -> 2.91 us
    ppermute x20 -> x12, starting transfers between devices: 34.9 us -> 18.7 us  [swap(): return lax.ppermute(value, axes, [(i, i ^ k) for i in range(count)])]
    ppermute x20 -> x12, waiting for transfers between devices: 14 us -> 25.9 us  [swap(): return lax.ppermute(value, axes, [(i, i ^ k) for i in range(count)])]
    ppermute x8, starting transfers between devices: 15.8 us -> 10.4 us  [to_decode(): went[k] = lax.ppermute(cut[k], ('pool', 'quad', 'head'), perm)]
    unnamed x17 -> x6, local copies, waits for them, and re-layouts: 3.89 us -> 2.12 us
    pallas_call x5 -> x8, Pallas kernels: 4.44 us -> 5.36 us  [the longest x2 1.48 us: cut_runs(): pl.pallas_call(functools.partial(runs_kernel, ks, seq_count, len(arrays),...]
    pallas_call x4 -> x3, Pallas kernels: 14.5 us -> 14 us  [attend(): pl.pallas_call(functools.partial(attend_kernel, ks, state is None, last,...]
  transfers between devices with their start and end apart: 28 -> 20, of which waited for: 8 -> 10; matrix products, arithmetic and copies ran while one was open for 1% -> 0% of each run, Pallas kernels for 15% -> 23%
where the time goes in v3:
time: 88.1 us; the launch traced here: 87.9 us
  waiting for transfers between devices  32.8 us (37%)
  starting transfers between devices  29.2 us (33%)
  Pallas kernels  22.1 us (25%)
  local copies, waits for them, and re-layouts  2.91 us (3%)
    ppermute x12, waiting for transfers between devices, swap(): return lax.ppermute(value, axes, [(i, i ^ k) for i in range(count)])  25.9 us
    ppermute x12, starting transfers between devices, swap(): return lax.ppermute(value, axes, [(i, i ^ k) for i in range(count)])  18.7 us
    pallas_call x3, Pallas kernels, attend(): pl.pallas_call(functools.partial(attend_kernel, ks, state is None, last,...  14 us
    ppermute x8, starting transfers between devices, to_decode(): went[k] = lax.ppermute(cut[k], ('pool', 'quad', 'head'), perm)  10.4 us
    ppermute x8, waiting for transfers between devices, to_decode(): went[k] = lax.ppermute(cut[k], ('pool', 'quad', 'head'), perm)  6.87 us
    unnamed x6, local copies, waits for them, and re-layouts  2.12 us
    pallas_call x1, Pallas kernels, shards(): pl.pallas_call(functools.partial(lay_kernel, seq_count, len(landed)), out...  2.01 us
  transfers between devices with their start and end apart: 20, of which 10 were waited for; matrix products, arithmetic and copies ran while one was open for 0% of the time, Pallas kernels for 23%

profile of v3, /device:TPU:0, one launch (start us, length us, event | category | flops | bytes accessed | tf_op | source)
XLA Modules:
  0.0 87.9 jit_solution(10250718876039379339)
XLA Ops:
  0.6 0.8 concatenate.3.ids
  1.4 0.0 copy-start
  1.4 1.2 %copy-done = bf16[4,128,1024]{2,1,0:T(8,128)(2,1)S(1)} copy-done((bf16[4,128,1024]{2,1,0:T(8,128)(2,1)S(1)}, bf16[4,128,1024]{2,1,0:T(8,128)(2,1)}, u32[]{:S(2)}) %copy-start) | copy-done | bytes 1048600
  2.6 0.0 copy-start.1
  2.6 0.8 pack.1
  3.4 3.0 %collective-permute-start.3 = (bf16[128,1024]{1,0:T(8,128)(2,1)S(1)}, bf16[128,1024]{1,0:T(8,128)(2,1)S(1)}, u32[]{:S(2)}, u32[]{:S(2)}) collective-permute-start(bf16[128,1024]{1,0:T(8,128)(2,1)S(1)} %get-tuple-element.50), channel_id=1, source_target_pairs={{0,8},{8,0},{16,24},{24,16},{1,9},{9,1},{17,25},{25,17},{2,10},{10... | collective-permute-start | bytes 786440 | tf_op jit(solution)/shard_map/ppermute | solution.py:320
  6.4 1.5 %collective-permute-start.4 = (bf16[128,1024]{1,0:T(8,128)(2,1)S(1)}, bf16[128,1024]{1,0:T(8,128)(2,1)S(1)}, u32[]{:S(2)}, u32[]{:S(2)}) collective-permute-start(bf16[128,1024]{1,0:T(8,128)(2,1)S(1)} %get-tuple-element.51), channel_id=1, source_target_pairs={{0,16},{8,24},{16,0},{24,8},{1,17},{9,25},{17,1},{25,9},{2,18},{10... | collective-permute-start | bytes 786440 | tf_op jit(solution)/shard_map/ppermute | solution.py:320
  7.9 0.0 collective-permute-start.5
  8.0 3.0 %collective-permute-start = (bf16[1,48,1024]{2,1,0:T(8,128)(2,1)}, bf16[1,48,1024]{2,1,0:T(8,128)(2,1)S(1)}, u32[]{:S(2)}, u32[]{:S(2)}) collective-permute-start(bf16[1,48,1024]{2,1,0:T(8,128)(2,1)} %near.1), channel_id=1, source_target_pairs={{0,4},{4,0},{1,5},{5,1},{2,6},{6,2},{3,7},{7,3},{8,12},{12,8},{9,1... | collective-permute-start | bytes 294920 | tf_op jit(solution)/shard_map/ppermute | solution.py:320
  11.0 4.3 %collective-permute-done.far = bf16[1,48,1024]{2,1,0:T(8,128)(2,1)S(1)} collective-permute-done((bf16[1,48,1024]{2,1,0:T(8,128)(2,1)}, bf16[1,48,1024]{2,1,0:T(8,128)(2,1)S(1)}, u32[]{:S(2)}, u32[]{:S(2)}) %collective-permute-start) | collective-permute-done | bytes 98336 | tf_op jit(solution)/shard_map/ppermute | solution.py:320
  15.3 0.0 copy-done.1
  15.3 0.0 copy-start.2
  15.3 0.9 %copy-done.2 = bf16[1,48,1024]{2,1,0:T(8,128)(2,1)S(1)} copy-done((bf16[1,48,1024]{2,1,0:T(8,128)(2,1)S(1)}, bf16[1,48,1024]{2,1,0:T(8,128)(2,1)}, u32[]{:S(2)}) %copy-start.2) | copy-done | bytes 98328
  16.2 0.9 split.1
  17.0 0.9 %collective-permute-start.1 = (bf16[2,48,2048]{2,1,0:T(8,128)(2,1)S(1)}, bf16[2,48,2048]{2,1,0:T(8,128)(2,1)S(1)}, u32[]{:S(2)}, u32[]{:S(2)}) collective-permute-start(bf16[2,48,2048]{2,1,0:T(8,128)(2,1)S(1)} %get-tuple-element.48), channel_id=1, source_target_pairs={{0,2},{1,3},{2,0},{3,1},{4,6},{5,7},{6,4},{7,5},{8,10},{9,11},{10,... | collective-permute-start | bytes 1179656 | tf_op jit(solution)/shard_map/ppermute | solution.py:320
  17.9 0.0 collective-permute-done.3.rest_1_
  17.9 1.9 %collective-permute-done.4.rest_2_ = bf16[128,1024]{1,0:T(8,128)(2,1)S(1)} collective-permute-done((bf16[128,1024]{1,0:T(8,128)(2,1)S(1)}, bf16[128,1024]{1,0:T(8,128)(2,1)S(1)}, u32[]{:S(2)}, u32[]{:S(2)}) %collective-permute-start.4) | collective-permute-done | bytes 262176 | tf_op jit(solution)/shard_map/ppermute | solution.py:320
  19.8 0.0 collective-permute-done.5.rest_3_
  19.8 1.0 %choose.1 = (bf16[2,3,128,256]{3,2,1,0:T(8,128)(2,1)S(1)}, bf16[2,3,128,256]{3,2,1,0:T(8,128)(2,1)S(1)}, bf16[2,3,128,256]{3,2,1,0:T(8,128)(2,1)S(1)}) custom-call(s32[22]{0:T(128)S(1)} %concatenate.3.ids, bf16[128,1024]{1,0:T(8,128)(2,1)S(1)} %get-tuple-element.53.rest_0_, bf16[128,1024]{1,0:T(8,128)(2,1)S(1)} %collective-permute-done.3.rest_1_, ...), custom_call_target="tpu_custom_call" | custom-call | flops 1 | bytes 1 | tf_op jit(solution)/shard_map/choose/pallas_call | solution.py:364
  20.8 0.1 collective-permute-start.6
  20.9 4.4 %collective-permute-done.1.got.rest_2_.rest_4_.rest_3_ = bf16[2,48,2048]{2,1,0:T(8,128)(2,1)S(1)} collective-permute-done((bf16[2,48,2048]{2,1,0:T(8,128)(2,1)S(1)}, bf16[2,48,2048]{2,1,0:T(8,128)(2,1)S(1)}, u32[]{:S(2)}, u32[]{:S(2)}) %collective-permute-start.1) | collective-permute-done | bytes 393248 | tf_op jit(solution)/shard_map/ppermute | solution.py:320
  25.3 0.0 collective-permute-done.6.got
  25.4 1.8 %collective-permute-start.7 = (bf16[2,3,128,256]{3,2,1,0:T(8,128)(2,1)S(1)}, bf16[2,3,128,256]{3,2,1,0:T(8,128)(2,1)S(1)}, u32[]{:S(2)}, u32[]{:S(2)}) collective-permute-start(bf16[2,3,128,256]{3,2,1,0:T(8,128)(2,1)S(1)} %get-tuple-element.61), channel_id=1, source_target_pairs={{0,2},{1,3},{2,0},{3,1},{4,6},{5,7},{6,4},{7,5},{8,10},{9,11},{10,... | collective-permute-start | bytes 1179656 | tf_op jit(solution)/shard_map/ppermute | solution.py:320
  27.2 0.0 collective-permute-start.2
  27.2 4.0 %collective-permute-start.9 = (bf16[2,3,128,256]{3,2,1,0:T(8,128)(2,1)S(1)}, bf16[2,3,128,256]{3,2,1,0:T(8,128)(2,1)S(1)}, u32[]{:S(2)}, u32[]{:S(2)}) collective-permute-start(bf16[2,3,128,256]{3,2,1,0:T(8,128)(2,1)S(1)} %get-tuple-element.66.rest_0_), channel_id=1, source_target_pairs={{0,4},{4,0},{1,5},{5,1},{2,6},{6,2},{3,7},{7,3},{8,12},{12,8},{9,1... | collective-permute-start | bytes 1179656 | tf_op jit(solution)/shard_map/ppermute | solution.py:320
  31.1 6.6 %collective-permute-done.7.rest_1_ = bf16[2,3,128,256]{3,2,1,0:T(8,128)(2,1)S(1)} collective-permute-done((bf16[2,3,128,256]{3,2,1,0:T(8,128)(2,1)S(1)}, bf16[2,3,128,256]{3,2,1,0:T(8,128)(2,1)S(1)}, u32[]{:S(2)}, u32[]{:S(2)}) %collective-permute-start.7) | collective-permute-done | bytes 393248 | tf_op jit(solution)/shard_map/ppermute | solution.py:320
  37.7 3.7 %collective-permute-start.8 = (bf16[2,3,128,256]{3,2,1,0:T(8,128)(2,1)S(1)}, bf16[2,3,128,256]{3,2,1,0:T(8,128)(2,1)S(1)}, u32[]{:S(2)}, u32[]{:S(2)}) collective-permute-start(bf16[2,3,128,256]{3,2,1,0:T(8,128)(2,1)S(1)} %collective-permute-done.7.rest_1_), channel_id=1, source_target_pairs={{0,4},{4,0},{1,5},{5,1},{2,6},{6,2},{3,7},{7,3},{8,12},{12,8},{9,1... | collective-permute-start | bytes 1179656 | tf_op jit(solution)/shard_map/ppermute | solution.py:320
  41.4 0.0 collective-permute-done.2.rest_1_.rest_3_.rest_2_
  41.4 0.6 sort.1.fresh
  42.0 6.6 %attend.3 = (f32[6,384,128]{2,1,0:T(8,128)S(1)}, f32[6,384,128]{2,1,0:T(8,128)S(1)}, f32[6,384,128]{2,1,0:T(8,128)S(1)}) custom-call(s32[22]{0:T(128)S(1)} %concatenate.3.ids, bf16[384,256]{1,0:T(8,128)(2,1)S(1)} %sort.1.fresh, bf16[2,3,128,256]{3,2,1,0:T(8,128)(2,1)S(1)} %get-tuple-element.66.rest_0_, ...), custom_call_target="tpu_custom_call" | custom-call | flops 1 | bytes 1 | tf_op jit(solution)/shard_map/attend/pallas_call | solution.py:201
  48.6 0.7 runs.2
  49.3 0.7 collective-permute-start.10
  50.0 0.1 collective-permute-start.11
  50.1 3.8 %collective-permute-start.12 = (bf16[4,3,16,256]{3,2,1,0:T(8,128)(2,1)S(1)}, bf16[4,3,16,256]{3,2,1,0:T(8,128)(2,1)S(1)}, u32[]{:S(2)}, u32[]{:S(2)}) collective-permute-start(bf16[4,3,16,256]{3,2,1,0:T(8,128)(2,1)S(1)} %get-tuple-element.70), channel_id=1, source_target_pairs={{0,2},{1,27},{2,8},{3,17},{4,6},{5,31},{6,12},{7,21},{8,10},{9,19}... | collective-permute-start | bytes 294920 | tf_op jit(solution)/shard_map/ppermute | solution.py:424
  53.9 4.2 %collective-permute-done.9.rest_0_ = bf16[2,3,128,256]{3,2,1,0:T(8,128)(2,1)S(1)} collective-permute-done((bf16[2,3,128,256]{3,2,1,0:T(8,128)(2,1)S(1)}, bf16[2,3,128,256]{3,2,1,0:T(8,128)(2,1)S(1)}, u32[]{:S(2)}, u32[]{:S(2)}) %collective-permute-start.9) | collective-permute-done | bytes 393248 | tf_op jit(solution)/shard_map/ppermute | solution.py:320
  58.1 0.0 collective-permute-start.13
  58.1 3.6 %attend.4 = (f32[6,384,128]{2,1,0:T(8,128)S(1)}, f32[6,384,128]{2,1,0:T(8,128)S(1)}, f32[6,384,128]{2,1,0:T(8,128)S(1)}) custom-call(s32[22]{0:T(128)S(1)} %concatenate.3.ids, bf16[384,256]{1,0:T(8,128)(2,1)S(1)} %sort.1.fresh, bf16[2,3,128,256]{3,2,1,0:T(8,128)(2,1)S(1)} %collective-permute-done.9.rest_0_, ...), custom_call_target="tpu_custom_call" | custom-call | flops 1 | bytes 1 | tf_op jit(solution)/shard_map/attend/pallas_call | solution.py:201
  61.7 4.6 %collective-permute-done.8.rest_0_.rest_1_ = bf16[2,3,128,256]{3,2,1,0:T(8,128)(2,1)S(1)} collective-permute-done((bf16[2,3,128,256]{3,2,1,0:T(8,128)(2,1)S(1)}, bf16[2,3,128,256]{3,2,1,0:T(8,128)(2,1)S(1)}, u32[]{:S(2)}, u32[]{:S(2)}) %collective-permute-start.8) | collective-permute-done | bytes 393248 | tf_op jit(solution)/shard_map/ppermute | solution.py:320
  66.3 3.8 %attend.5 = (bf16[2,48,1536]{2,1,0:T(8,128)(2,1)S(1)}, bf16[2,48,1536]{2,1,0:T(8,128)(2,1)S(1)}) custom-call(s32[22]{0:T(128)S(1)} %concatenate.3.ids, bf16[384,256]{1,0:T(8,128)(2,1)S(1)} %sort.1.fresh, bf16[2,3,128,256]{3,2,1,0:T(8,128)(2,1)S(1)} %collective-permute-done.8.rest_0_.rest_1_, bf16[48,2048]{1,0:T(8,128)(2,1)S(1)} %get-tuple-element.47.rest_0_.rest_2_.rest_1_, ...), custom_call_target="tpu_custom_call" | custom-call | flops 1 | bytes 1 | tf_op jit(solution)/shard_map/attend/pallas_call | solution.py:201
  70.1 0.0 collective-permute-done.10.rest_0_
  70.1 0.0 collective-permute-done.11.rest_1_
  70.1 0.0 collective-permute-done.12.rest_2_
  70.1 1.2 %collective-permute-done.13.rest_3_ = bf16[4,3,16,256]{3,2,1,0:T(8,128)(2,1)S(1)} collective-permute-done((bf16[4,3,16,256]{3,2,1,0:T(8,128)(2,1)S(1)}, bf16[4,3,16,256]{3,2,1,0:T(8,128)(2,1)S(1)}, u32[]{:S(2)}, u32[]{:S(2)}) %collective-permute-start.13) | collective-permute-done | bytes 98336 | tf_op jit(solution)/shard_map/ppermute | solution.py:424
  71.3 0.0 collective-permute-start.14
  71.3 0.7 runs.3
  72.1 0.7 collective-permute-start.15
  72.8 2.5 %collective-permute-start.16 = (bf16[4,3,16,256]{3,2,1,0:T(8,128)(2,1)S(1)}, bf16[4,3,16,256]{3,2,1,0:T(8,128)(2,1)S(1)}, u32[]{:S(2)}, u32[]{:S(2)}) collective-permute-start(bf16[4,3,16,256]{3,2,1,0:T(8,128)(2,1)S(1)} %get-tuple-element.84), channel_id=1, source_target_pairs={{0,1},{1,24},{2,11},{3,18},{4,5},{5,28},{6,15},{7,22},{8,9},{9,16}... | collective-permute-start | bytes 294920 | tf_op jit(solution)/shard_map/ppermute | solution.py:424
  75.3 1.9 %collective-permute-start.17 = (bf16[4,3,16,256]{3,2,1,0:T(8,128)(2,1)S(1)}, bf16[4,3,16,256]{3,2,1,0:T(8,128)(2,1)S(1)}, u32[]{:S(2)}, u32[]{:S(2)}) collective-permute-start(bf16[4,3,16,256]{3,2,1,0:T(8,128)(2,1)S(1)} %get-tuple-element.85), channel_id=1, source_target_pairs={{0,2},{1,27},{2,8},{3,17},{4,6},{5,31},{6,12},{7,21},{8,10},{9,19}... | collective-permute-start | bytes 294920 | tf_op jit(solution)/shard_map/ppermute | solution.py:424
  77.2 0.8 collective-permute-start.18
  78.0 0.0 collective-permute-done.15.rest_4_
  78.0 0.7 collective-permute-done.16.rest_5_
  78.8 4.5 %collective-permute-done.17.rest_6_ = bf16[4,3,16,256]{3,2,1,0:T(8,128)(2,1)S(1)} collective-permute-done((bf16[4,3,16,256]{3,2,1,0:T(8,128)(2,1)S(1)}, bf16[4,3,16,256]{3,2,1,0:T(8,128)(2,1)S(1)}, u32[]{:S(2)}, u32[]{:S(2)}) %collective-permute-start.17) | collective-permute-done | bytes 98336 | tf_op jit(solution)/shard_map/ppermute | solution.py:424
  83.3 0.4 collective-permute-done.18.rest_7_
  83.7 0.0 collective-permute-done.14.rest_2_
  83.7 0.7 collective-permute-start.19
  84.4 2.0 %lay.1 = bf16[1,1,4,24,4096]{4,3,2,1,0:T(8,128)(2,1)} custom-call(s32[22]{0:T(128)S(1)} %concatenate.3.ids, bf16[4,3,16,256]{3,2,1,0:T(8,128)(2,1)S(1)} %collective-permute-done.10.rest_0_, bf16[4,3,16,256]{3,2,1,0:T(8,128)(2,1)S(1)} %collective-permute-done.11.rest_1_, bf16[4,3,16,256]{3,2,1,0:T(8,128)(2,1)S(1)} %collective-permute-done.12.rest_2_, ...), custom_call_target="tpu_custom_call" | custom-call | flops 1 | bytes 1 | tf_op jit(solution)/shard_map/lay/pallas_call | solution.py:458
  86.4 0.0 collective-permute-done.19.rest_1_
  86.5 1.4 %join.1 = bf16[1,48,6144]{2,1,0:T(8,128)(2,1)} custom-call(s32[22]{0:T(128)S(1)} %concatenate.3.ids, bf16[2,48,1536]{2,1,0:T(8,128)(2,1)S(1)} %get-tuple-element.78.rest_0_, bf16[2,48,1536]{2,1,0:T(8,128)(2,1)S(1)} %collective-permute-done.19.rest_1_, bf16[2,48,1536]{2,1,0:T(8,128)(2,1)S(1)} %collective-permute-done.14.rest_2_), custom_call_target="tpu_custom_call" | custom-call | flops 1 | bytes 1 | tf_op jit(solution)/shard_map/join/pallas_call | solution.py:448
  (5 shorter events, 0.1 us)
Async XLA Ops:
  1.4 1.2 %copy-start = (bf16[4,128,1024]{2,1,0:T(8,128)(2,1)S(1)}, bf16[4,128,1024]{2,1,0:T(8,128)(2,1)}, u32[]{:S(2)}) copy-start(bf16[4,128,1024]{2,1,0:T(8,128)(2,1)} %pool_kv.1) | copy-start | bytes 3145732
  2.6 12.6 %copy-start.1 = (bf16[1,48,6144]{2,1,0:T(8,128)(2,1)S(1)}, bf16[1,48,6144]{2,1,0:T(8,128)(2,1)}, u32[]{:S(2)}) copy-start(bf16[1,48,6144]{2,1,0:T(8,128)(2,1)} %fresh_q.1) | copy-start | bytes 1769476
  3.4 14.5 %collective-permute-start.3 = (bf16[128,1024]{1,0:T(8,128)(2,1)S(1)}, bf16[128,1024]{1,0:T(8,128)(2,1)S(1)}, u32[]{:S(2)}, u32[]{:S(2)}) collective-permute-start(bf16[128,1024]{1,0:T(8,128)(2,1)S(1)} %get-tuple-element.50), channel_id=1, source_target_pairs={{0,8},{8,0},{16,24},{24,16},{1,9},{9,1},{17,25},{25,17},{2,10},{10... | collective-permute-start | bytes 786440 | tf_op jit(solution)/shard_map/ppermute | solution.py:320
  6.4 13.4 %collective-permute-start.4 = (bf16[128,1024]{1,0:T(8,128)(2,1)S(1)}, bf16[128,1024]{1,0:T(8,128)(2,1)S(1)}, u32[]{:S(2)}, u32[]{:S(2)}) collective-permute-start(bf16[128,1024]{1,0:T(8,128)(2,1)S(1)} %get-tuple-element.51), channel_id=1, source_target_pairs={{0,16},{8,24},{16,0},{24,8},{1,17},{9,25},{17,1},{25,9},{2,18},{10... | collective-permute-start | bytes 786440 | tf_op jit(solution)/shard_map/ppermute | solution.py:320
  7.9 11.9 %collective-permute-start.5 = (bf16[128,1024]{1,0:T(8,128)(2,1)S(1)}, bf16[128,1024]{1,0:T(8,128)(2,1)S(1)}, u32[]{:S(2)}, u32[]{:S(2)}) collective-permute-start(bf16[128,1024]{1,0:T(8,128)(2,1)S(1)} %get-tuple-element.52), channel_id=1, source_target_pairs={{0,24},{8,16},{16,8},{24,0},{1,25},{9,17},{17,9},{25,1},{2,26},{10... | collective-permute-start | bytes 786440 | tf_op jit(solution)/shard_map/ppermute | solution.py:320
  8.0 7.3 %collective-permute-start = (bf16[1,48,1024]{2,1,0:T(8,128)(2,1)}, bf16[1,48,1024]{2,1,0:T(8,128)(2,1)S(1)}, u32[]{:S(2)}, u32[]{:S(2)}) collective-permute-start(bf16[1,48,1024]{2,1,0:T(8,128)(2,1)} %near.1), channel_id=1, source_target_pairs={{0,4},{4,0},{1,5},{5,1},{2,6},{6,2},{3,7},{7,3},{8,12},{12,8},{9,1... | collective-permute-start | bytes 294920 | tf_op jit(solution)/shard_map/ppermute | solution.py:320
  15.3 0.9 %copy-start.2 = (bf16[1,48,1024]{2,1,0:T(8,128)(2,1)S(1)}, bf16[1,48,1024]{2,1,0:T(8,128)(2,1)}, u32[]{:S(2)}) copy-start(bf16[1,48,1024]{2,1,0:T(8,128)(2,1)} %near.1) | copy-start | bytes 294916
  17.0 8.3 %collective-permute-start.1 = (bf16[2,48,2048]{2,1,0:T(8,128)(2,1)S(1)}, bf16[2,48,2048]{2,1,0:T(8,128)(2,1)S(1)}, u32[]{:S(2)}, u32[]{:S(2)}) collective-permute-start(bf16[2,48,2048]{2,1,0:T(8,128)(2,1)S(1)} %get-tuple-element.48), channel_id=1, source_target_pairs={{0,2},{1,3},{2,0},{3,1},{4,6},{5,7},{6,4},{7,5},{8,10},{9,11},{10,... | collective-permute-start | bytes 1179656 | tf_op jit(solution)/shard_map/ppermute | solution.py:320
  20.8 4.5 %collective-permute-start.6 = (bf16[2,3,128,256]{3,2,1,0:T(8,128)(2,1)S(1)}, bf16[2,3,128,256]{3,2,1,0:T(8,128)(2,1)S(1)}, u32[]{:S(2)}, u32[]{:S(2)}) collective-permute-start(bf16[2,3,128,256]{3,2,1,0:T(8,128)(2,1)S(1)} %get-tuple-element.57), channel_id=1, source_target_pairs={{0,1},{1,0},{2,3},{3,2},{4,5},{5,4},{6,7},{7,6},{8,9},{9,8},{10,11... | collective-permute-start | bytes 1179656 | tf_op jit(solution)/shard_map/ppermute | solution.py:320
  25.4 12.4 %collective-permute-start.7 = (bf16[2,3,128,256]{3,2,1,0:T(8,128)(2,1)S(1)}, bf16[2,3,128,256]{3,2,1,0:T(8,128)(2,1)S(1)}, u32[]{:S(2)}, u32[]{:S(2)}) collective-permute-start(bf16[2,3,128,256]{3,2,1,0:T(8,128)(2,1)S(1)} %get-tuple-element.61), channel_id=1, source_target_pairs={{0,2},{1,3},{2,0},{3,1},{4,6},{5,7},{6,4},{7,5},{8,10},{9,11},{10,... | collective-permute-start | bytes 1179656 | tf_op jit(solution)/shard_map/ppermute | solution.py:320
  27.2 14.3 %collective-permute-start.2 = (bf16[2,48,2048]{2,1,0:T(8,128)(2,1)S(1)}, bf16[2,48,2048]{2,1,0:T(8,128)(2,1)S(1)}, u32[]{:S(2)}, u32[]{:S(2)}) collective-permute-start(bf16[2,48,2048]{2,1,0:T(8,128)(2,1)S(1)} %follow.1), channel_id=1, source_target_pairs={{0,1},{1,0},{2,3},{3,2},{4,5},{5,4},{6,7},{7,6},{8,9},{9,8},{10,11... | collective-permute-start | bytes 1179656 | tf_op jit(solution)/shard_map/ppermute | solution.py:320
  27.2 30.9 %collective-permute-start.9 = (bf16[2,3,128,256]{3,2,1,0:T(8,128)(2,1)S(1)}, bf16[2,3,128,256]{3,2,1,0:T(8,128)(2,1)S(1)}, u32[]{:S(2)}, u32[]{:S(2)}) collective-permute-start(bf16[2,3,128,256]{3,2,1,0:T(8,128)(2,1)S(1)} %get-tuple-element.66.rest_0_), channel_id=1, source_target_pairs={{0,4},{4,0},{1,5},{5,1},{2,6},{6,2},{3,7},{7,3},{8,12},{12,8},{9,1... | collective-permute-start | bytes 1179656 | tf_op jit(solution)/shard_map/ppermute | solution.py:320
  37.7 28.6 %collective-permute-start.8 = (bf16[2,3,128,256]{3,2,1,0:T(8,128)(2,1)S(1)}, bf16[2,3,128,256]{3,2,1,0:T(8,128)(2,1)S(1)}, u32[]{:S(2)}, u32[]{:S(2)}) collective-permute-start(bf16[2,3,128,256]{3,2,1,0:T(8,128)(2,1)S(1)} %collective-permute-done.7.rest_1_), channel_id=1, source_target_pairs={{0,4},{4,0},{1,5},{5,1},{2,6},{6,2},{3,7},{7,3},{8,12},{12,8},{9,1... | collective-permute-start | bytes 1179656 | tf_op jit(solution)/shard_map/ppermute | solution.py:320
  49.3 20.8 %collective-permute-start.10 = (bf16[4,3,16,256]{3,2,1,0:T(8,128)(2,1)S(1)}, bf16[4,3,16,256]{3,2,1,0:T(8,128)(2,1)S(1)}, u32[]{:S(2)}, u32[]{:S(2)}) collective-permute-start(bf16[4,3,16,256]{3,2,1,0:T(8,128)(2,1)S(1)} %get-tuple-element.68), channel_id=1, source_target_pairs={{0,0},{1,25},{2,10},{3,19},{4,4},{5,29},{6,14},{7,23},{8,8},{9,17}... | collective-permute-start | bytes 294920 | tf_op jit(solution)/shard_map/ppermute | solution.py:424
  50.0 20.1 %collective-permute-start.11 = (bf16[4,3,16,256]{3,2,1,0:T(8,128)(2,1)S(1)}, bf16[4,3,16,256]{3,2,1,0:T(8,128)(2,1)S(1)}, u32[]{:S(2)}, u32[]{:S(2)}) collective-permute-start(bf16[4,3,16,256]{3,2,1,0:T(8,128)(2,1)S(1)} %get-tuple-element.69), channel_id=1, source_target_pairs={{0,1},{1,24},{2,11},{3,18},{4,5},{5,28},{6,15},{7,22},{8,9},{9,16}... | collective-permute-start | bytes 294920 | tf_op jit(solution)/shard_map/ppermute | solution.py:424
  50.1 20.0 %collective-permute-start.12 = (bf16[4,3,16,256]{3,2,1,0:T(8,128)(2,1)S(1)}, bf16[4,3,16,256]{3,2,1,0:T(8,128)(2,1)S(1)}, u32[]{:S(2)}, u32[]{:S(2)}) collective-permute-start(bf16[4,3,16,256]{3,2,1,0:T(8,128)(2,1)S(1)} %get-tuple-element.70), channel_id=1, source_target_pairs={{0,2},{1,27},{2,8},{3,17},{4,6},{5,31},{6,12},{7,21},{8,10},{9,19}... | collective-permute-start | bytes 294920 | tf_op jit(solution)/shard_map/ppermute | solution.py:424
  58.1 13.3 %collective-permute-start.13 = (bf16[4,3,16,256]{3,2,1,0:T(8,128)(2,1)S(1)}, bf16[4,3,16,256]{3,2,1,0:T(8,128)(2,1)S(1)}, u32[]{:S(2)}, u32[]{:S(2)}) collective-permute-start(bf16[4,3,16,256]{3,2,1,0:T(8,128)(2,1)S(1)} %get-tuple-element.71), channel_id=1, source_target_pairs={{0,3},{1,26},{2,9},{3,16},{4,7},{5,30},{6,13},{7,20},{8,11},{9,18}... | collective-permute-start | bytes 294920 | tf_op jit(solution)/shard_map/ppermute | solution.py:424
  71.3 12.3 %collective-permute-start.14 = (bf16[2,48,1536]{2,1,0:T(8,128)(2,1)S(1)}, bf16[2,48,1536]{2,1,0:T(8,128)(2,1)S(1)}, u32[]{:S(2)}, u32[]{:S(2)}) collective-permute-start(bf16[2,48,1536]{2,1,0:T(8,128)(2,1)S(1)} %get-tuple-element.80), channel_id=1, source_target_pairs={{0,2},{1,3},{2,0},{3,1},{4,6},{5,7},{6,4},{7,5},{8,10},{9,11},{10,... | collective-permute-start | bytes 884744 | tf_op jit(solution)/shard_map/ppermute | solution.py:320
  72.1 5.9 %collective-permute-start.15 = (bf16[4,3,16,256]{3,2,1,0:T(8,128)(2,1)S(1)}, bf16[4,3,16,256]{3,2,1,0:T(8,128)(2,1)S(1)}, u32[]{:S(2)}, u32[]{:S(2)}) collective-permute-start(bf16[4,3,16,256]{3,2,1,0:T(8,128)(2,1)S(1)} %get-tuple-element.83), channel_id=1, source_target_pairs={{0,0},{1,25},{2,10},{3,19},{4,4},{5,29},{6,14},{7,23},{8,8},{9,17}... | collective-permute-start | bytes 294920 | tf_op jit(solution)/shard_map/ppermute | solution.py:424
  72.8 6.0 %collective-permute-start.16 = (bf16[4,3,16,256]{3,2,1,0:T(8,128)(2,1)S(1)}, bf16[4,3,16,256]{3,2,1,0:T(8,128)(2,1)S(1)}, u32[]{:S(2)}, u32[]{:S(2)}) collective-permute-start(bf16[4,3,16,256]{3,2,1,0:T(8,128)(2,1)S(1)} %get-tuple-element.84), channel_id=1, source_target_pairs={{0,1},{1,24},{2,11},{3,18},{4,5},{5,28},{6,15},{7,22},{8,9},{9,16}... | collective-permute-start | bytes 294920 | tf_op jit(solution)/shard_map/ppermute | solution.py:424
  75.3 8.0 %collective-permute-start.17 = (bf16[4,3,16,256]{3,2,1,0:T(8,128)(2,1)S(1)}, bf16[4,3,16,256]{3,2,1,0:T(8,128)(2,1)S(1)}, u32[]{:S(2)}, u32[]{:S(2)}) collective-permute-start(bf16[4,3,16,256]{3,2,1,0:T(8,128)(2,1)S(1)} %get-tuple-element.85), channel_id=1, source_target_pairs={{0,2},{1,27},{2,8},{3,17},{4,6},{5,31},{6,12},{7,21},{8,10},{9,19}... | collective-permute-start | bytes 294920 | tf_op jit(solution)/shard_map/ppermute | solution.py:424
  77.2 6.5 %collective-permute-start.18 = (bf16[4,3,16,256]{3,2,1,0:T(8,128)(2,1)S(1)}, bf16[4,3,16,256]{3,2,1,0:T(8,128)(2,1)S(1)}, u32[]{:S(2)}, u32[]{:S(2)}) collective-permute-start(bf16[4,3,16,256]{3,2,1,0:T(8,128)(2,1)S(1)} %get-tuple-element.86), channel_id=1, source_target_pairs={{0,3},{1,26},{2,9},{3,16},{4,7},{5,30},{6,13},{7,20},{8,11},{9,18}... | collective-permute-start | bytes 294920 | tf_op jit(solution)/shard_map/ppermute | solution.py:424
  83.7 2.7 %collective-permute-start.19 = (bf16[2,48,1536]{2,1,0:T(8,128)(2,1)S(1)}, bf16[2,48,1536]{2,1,0:T(8,128)(2,1)S(1)}, u32[]{:S(2)}, u32[]{:S(2)}) collective-permute-start(bf16[2,48,1536]{2,1,0:T(8,128)(2,1)S(1)} %pad_maximum_fusion), channel_id=1, source_target_pairs={{0,1},{1,0},{2,3},{3,2},{4,5},{5,4},{6,7},{7,6},{8,9},{9,8},{10,11... | collective-permute-start | bytes 884744 | tf_op jit(solution)/shard_map/ppermute | solution.py:320

commit v4 on v3

--- a/solution.py
+++ b/solution.py
@@ -29,15 +29,20 @@
 
 
 def pack_kernel(slots, spans, ids, pool_kv, *rest):
-    outs, sems = rest[:-1], rest[-1]
+    pool_count = (len(rest) - 1) // 2
+    first, others, sems = rest[:pool_count], rest[pool_count:-1], rest[-1]
+    width = first[0].shape[1]
     copies = []
-    for d, out in enumerate(outs):
+    for d in range(pool_count):
         slot = jnp.int32(0)
         for t in range(spans):
             held = ids[HOME + (ids[0] ^ d) * spans + t]
             slot = jnp.where(held // slots == ids[0], held % slots, slot)
-        copies.append(pltpu.make_async_copy(pool_kv.at[slot], out, sems.at[d]))
-        copies[-1].start()
+        for n in range(KV_HEADS):
+            source = pool_kv.at[slot, :, pl.ds(pl.multiple_of((ids[3] ^ d ^ turn(n)) * width, HEAD_DIM), width)]
+            out = others[d].at[:, pl.ds((n - 1) * width, width)] if n else first[d]
+            copies.append(pltpu.make_async_copy(source, out, sems.at[d, n]))
+            copies[-1].start()
     for copy in copies:
         copy.wait()
 
@@ -88,29 +93,31 @@
 
 
 def choose_kernel(slots, pool_count, ids, *rest):
-    arrived, (near, give, send), sems = rest[:pool_count], rest[pool_count:-1], rest[-1]
-    outs = (near.at[0], give.at[0], send.at[0], give.at[1])
-    spans, heads = sems.shape
-    width = near.shape[3]
+    arrived, outs, sems = rest[:pool_count], rest[pool_count:-1], rest[-1]
+    if len(outs) == 2:
+        give, send = outs
+        outs = (give.at[0], send.at[0], give.at[1])
+    spans = sems.shape[0]
+    width = outs[0].shape[2]
     for start in (True, False):
         for j in range(spans):
             source = (ids[HOME + ids[HOME + pool_count * spans + j]] // slots) ^ ids[0]
-            for d in range(heads):
-                at = pl.ds(pl.multiple_of((ids[3] ^ turn(d)) * width, HEAD_DIM), width)
+            for n, out in enumerate(outs):
+                at = pl.ds(n * width, width)
                 if start:
                     for p in range(pool_count):
 
                         @pl.when(source == p)
                         def _(p=p):
-                            pltpu.make_async_copy(arrived[p].at[:, at], outs[d].at[j], sems.at[j, d]).start()
+                            pltpu.make_async_copy(arrived[p].at[:, at], out.at[j], sems.at[j, n]).start()
 
                 else:
-                    pltpu.make_async_copy(arrived[0].at[:, at], outs[d].at[j], sems.at[j, d]).wait()
-
-
-def place_kernel(got, near_in, send_in, near, send):
-    del near_in, send_in
-    near[1] = got[0]
+                    pltpu.make_async_copy(arrived[0].at[:, at], out.at[j], sems.at[j, n]).wait()
+
+
+def place_kernel(got, send_in, beside, send):
+    del send_in
+    beside[...] = got[0]
     send[1] = got[1]
 
 
@@ -227,6 +234,12 @@
     )(*inputs)
 
 
+def slot_of(ks, k, head):
+    at = ks.index(k)
+    whole = min(KV_HEADS, len(ks) - at // KV_HEADS * KV_HEADS)
+    return at // KV_HEADS * KV_HEADS + ((head ^ k) & (whole - 1))
+
+
 def runs_kernel(ks, seq_count, count_in, views, at_chosen, ids, fresh, *rest):
     messages, outs = look(rest[:count_in], views), rest[count_in:]
     spans, block, _ = messages[0].shape
@@ -236,7 +249,7 @@
     offset = ids[1] * slab
 
     def put(k, j, source, first):
-        slot = ks.index(k) // KV_HEADS * KV_HEADS + (ids[2] ^ k % KV_HEADS)
+        slot = slot_of(ks, k, ids[2])
         for m, out in enumerate(outs):
             if run % 16:
                 rows = source[pl.ds(pl.multiple_of(first + offset, slab), slab), :].astype(F32)
@@ -276,10 +289,17 @@
     count = seq_count * spans * run
     blocks = spans * seq_count
     at = lax.broadcasted_iota(jnp.int32, (count, count), 1)
-    source = ids[1] * KV_HEADS ^ (at // (spans * run))
-    target = (at % run) * blocks + (at // run) % spans * seq_count + source
-    order = (lax.broadcasted_iota(jnp.int32, (count, count), 0) == target).astype(F32).astype(BF16)
+    to = lax.broadcasted_iota(jnp.int32, (count, count), 0)
+
+    def order_of(sender):
+        source = at // (spans * run)
+        half = jnp.where(source < seq_count - KV_HEADS, 0, sender & KV_HEADS // 2)
+        target = (at % run) * blocks + (at // run) % spans * seq_count + (ids[1] * KV_HEADS ^ source ^ half)
+        return (to == target).astype(F32).astype(BF16)
+
     for k in range(KV_HEADS):
+        if k % (KV_HEADS // 2) == 0:
+            order = order_of(ids[2] ^ k)
         rows = [landed[i * KV_HEADS + k][...] for i in range(parts)]
         if run % 16:
             rows = [part.astype(F32) for part in rows]
@@ -322,18 +342,35 @@
     seq = ("quad", "head")
     to_pool = pl.pallas_call(
         functools.partial(pack_kernel, slots, spans),
-        out_shape=[jax.ShapeDtypeStruct((block, width), BF16)] * pool_count,
+        out_shape=[jax.ShapeDtypeStruct((block, kv_width), BF16)] * pool_count
+        + [jax.ShapeDtypeStruct((block, width - kv_width), BF16)] * pool_count,
         in_specs=[SMEM, ANY],
-        out_specs=[ANY] * pool_count,
-        scratch_shapes=[pltpu.SemaphoreType.DMA((pool_count,))],
+        out_specs=[ANY] * (2 * pool_count),
+        scratch_shapes=[pltpu.SemaphoreType.DMA((pool_count, heads))],
         compiler_params=PARAMS,
         cost_estimate=CHEAP,
         name="pack",
     )(ids, pool_kv)
     far = [swap(after(fresh_kv, to_pool[0]), "quad", quads, k) for k in range(1, quads)]
-    arrived = [to_pool[0]] + [None] * (pool_count - 1)
-    for k in reversed(range(1, pool_count)):
-        arrived[k] = swap(to_pool[k], "pool", pool_count, k)
+
+    def from_pool(values, out_shape, *dep):
+        arrived = [values[0]] + [None] * (pool_count - 1)
+        for k in reversed(range(1, pool_count)):
+            arrived[k] = swap(values[k], "pool", pool_count, k)
+        return pl.pallas_call(
+            functools.partial(choose_kernel, slots, pool_count),
+            out_shape=out_shape,
+            in_specs=[SMEM] + [ANY] * pool_count,
+            out_specs=[ANY] * len(out_shape),
+            scratch_shapes=[pltpu.SemaphoreType.DMA((spans, heads - 1))],
+            compiler_params=PARAMS,
+            cost_estimate=CHEAP,
+            name="choose",
+        )(ids, *after(arrived, dep))
+
+    blocks = jax.ShapeDtypeStruct((spans, block, kv_width), BF16)
+    (own,) = from_pool(to_pool[:pool_count], [blocks], far)
+    early = [swap(own, "quad", quads, a) for a in range(1, quads)]
     one = jax.ShapeDtypeStruct((rows, q_part + quads * kv_width), BF16)
     pair = jax.ShapeDtypeStruct((2, *one.shape), BF16)
     keep, give, send = pl.pallas_call(
@@ -360,34 +397,20 @@
     core = swap(give, "head", heads, 1)
     q_give, q = give, [(keep, None), (core, 0), (chip, 0), (core, 1)]
 
-    pair = jax.ShapeDtypeStruct((2, spans, block, kv_width), BF16)
-    near, give, send = pl.pallas_call(
-        functools.partial(choose_kernel, slots, pool_count),
-        out_shape=[pair] * 3,
-        in_specs=[SMEM] + [ANY] * pool_count,
-        out_specs=[ANY] * 3,
-        scratch_shapes=[pltpu.SemaphoreType.DMA((spans, heads))],
-        compiler_params=PARAMS,
-        cost_estimate=CHEAP,
-        name="choose",
-    )(ids, *after(arrived, send))
-
-    def place(got, near, send):
-        like = [jax.ShapeDtypeStruct(x.shape, x.dtype) for x in (near, send)]
-        return pl.pallas_call(
-            place_kernel,
-            out_shape=like,
-            in_specs=[VMEM] * 3,
-            out_specs=[VMEM] * 2,
-            input_output_aliases={1: 0, 2: 1},
-            compiler_params=PARAMS,
-            cost_estimate=CHEAP,
-            name="place",
-        )(got, near, send)
-
-    near, send = place(after(swap(give, "head", heads, 1), q_give), near, send)
-    rest = swap(send, "head", heads, 2)
-    messages = [(near, 0), (near, 1), (rest, 0), (rest, 1)]
+    pair = jax.ShapeDtypeStruct((2, *blocks.shape), BF16)
+    give, kv_send = from_pool(to_pool[pool_count:], [pair] * 2, send, early)
+    beside, kv_send = pl.pallas_call(
+        place_kernel,
+        out_shape=[blocks, pair],
+        in_specs=[VMEM] * 2,
+        out_specs=[VMEM] * 2,
+        input_output_aliases={1: 1},
+        compiler_params=PARAMS,
+        cost_estimate=CHEAP,
+        name="place",
+    )(after(swap(give, "head", heads, 1), q_give), kv_send)
+    rest = swap(kv_send, "head", heads, 2)
+    messages = [(own, None), (beside, None), (rest, 0), (rest, 1)]
 
     if rows % 16:
         q = [(jnp.concatenate([part if index is None else part[index] for part, index in q], axis=0), None)]
@@ -428,20 +451,18 @@
         return attend(ks, state, last, seq_count, rows, group, at_chosen, ids, q, fresh, [messages[k] for k in ks])
 
     for a in range(1, quads):
-        for half in (near, rest):
-            crossed = swap(half, "quad", quads, a)
-            messages += [(crossed, 0), (crossed, 1)]
-    state = work(list(range(heads)), None)
-    groups = [[k, k + 1] for k in range(heads, seq_count, 2)]
-    far_ks = list(range(seq_count - heads, seq_count))
-    for ks in groups[:-1]:
-        if ks[0] == far_ks[0]:
-            landed = [to_decode(list(range(far_ks[0])), state)]
-            state = after(state, landed[0][1])
-        state = work(ks, state)
+        second = swap(beside, "quad", quads, a)
+        crossed = swap(after(rest, second), "quad", quads, a)
+        messages += [(early[a - 1], None), (second, None), (crossed, 0), (crossed, 1)]
+    groups = [list(range(seq_count - 2)), [seq_count - 2, seq_count - 1]]
+    landed = [to_decode(groups[0])]
+    fresh = after(fresh, landed[0][1])
+    state = None
+    for first in range(0, seq_count - 2, 6):
+        state = work(groups[0][first : first + 6], state)
     kept, sent = work(groups[-1], state, True)
     chip = swap(after(sent, landed[0][0]), "head", heads, 2)
-    landed.append(to_decode(far_ks, kept))
+    landed.append(to_decode(groups[1], kept))
     chip = after(chip, landed[1][0])
     core = swap(jnp.stack([kept[1], chip[1]]), "head", heads, 1)
     arrays, views = arrays_of([(kept, 0), (core, 0), (chip, 0), (core, 1)])

time: 88.1 us -> 85.1 us (0.966)
  waiting for transfers between devices: 32.8 us -> 26.9 us
  starting transfers between devices: 29.2 us -> 32.6 us
  local copies, waits for them, and re-layouts: 2.91 us -> 2.02 us
    ppermute x12 -> x16, waiting for transfers between devices: 25.9 us -> 20.4 us  [swap(): return lax.ppermute(value, axes, [(i, i ^ k) for i in range(count)])]
    ppermute x12 -> x16, starting transfers between devices: 18.7 us -> 23.4 us  [swap(): return lax.ppermute(value, axes, [(i, i ^ k) for i in range(count)])]
    ppermute x8, starting transfers between devices: 10.4 us -> 9.19 us  [to_decode(): went[k] = lax.ppermute(cut[k], ('pool', 'quad', 'head'), perm)]
    unnamed x6, local copies, waits for them, and re-layouts: 2.12 us -> 1.23 us
    pallas_call x2 -> x3, Pallas kernels: 1.04 us -> 1.86 us  [the longest x2 1.84 us: from_pool(): pl.pallas_call(functools.partial(choose_kernel, slots, pool_count), out_s...]
    pallas_call x3 -> x2, Pallas kernels: 14 us -> 13.3 us  [attend(): pl.pallas_call(functools.partial(attend_kernel, ks, state is None, last,...]
  transfers between devices with their start and end apart: 20 -> 24, of which waited for: 10 -> 12; matrix products, arithmetic and copies ran while one was open for 0% -> 0% of each run, Pallas kernels for 23% -> 24%
where the time goes in v4:
time: 85.1 us; the launch traced here: 84.9 us
  starting transfers between devices  32.6 us (38%)
  waiting for transfers between devices  26.9 us (32%)
  Pallas kernels  22.5 us (26%)
  local copies, waits for them, and re-layouts  2.02 us (2%)
    ppermute x16, starting transfers between devices, swap(): return lax.ppermute(value, axes, [(i, i ^ k) for i in range(count)])  23.4 us
    ppermute x16, waiting for transfers between devices, swap(): return lax.ppermute(value, axes, [(i, i ^ k) for i in range(count)])  20.4 us
    pallas_call x2, Pallas kernels, attend(): pl.pallas_call(functools.partial(attend_kernel, ks, state is None, last,...  13.3 us
    ppermute x8, starting transfers between devices, to_decode(): went[k] = lax.ppermute(cut[k], ('pool', 'quad', 'head'), perm)  9.19 us
    ppermute x8, waiting for transfers between devices, to_decode(): went[k] = lax.ppermute(cut[k], ('pool', 'quad', 'head'), perm)  6.52 us
    pallas_call x1, Pallas kernels, shards(): pl.pallas_call(functools.partial(lay_kernel, seq_count, len(landed)), out...  2.02 us
    pallas_call x2, Pallas kernels, from_pool(): pl.pallas_call(functools.partial(choose_kernel, slots, pool_count), out_s...  1.84 us
  transfers between devices with their start and end apart: 24, of which 12 were waited for; matrix products, arithmetic and copies ran while one was open for 0% of the time, Pallas kernels for 24%

profile of v4, /device:TPU:0, one launch (start us, length us, event | category | flops | bytes accessed | tf_op | source)
XLA Modules:
  0.0 84.9 jit_solution(7624505217084325767)
XLA Ops:
  0.6 0.8 concatenate.3.ids
  1.4 0.0 copy-start
  1.4 1.2 %copy-done = bf16[4,128,1024]{2,1,0:T(8,128)(2,1)S(1)} copy-done((bf16[4,128,1024]{2,1,0:T(8,128)(2,1)S(1)}, bf16[4,128,1024]{2,1,0:T(8,128)(2,1)}, u32[]{:S(2)}) %copy-start) | copy-done | bytes 1048600
  2.6 1.1 %pack.1 = (bf16[128,256]{1,0:T(8,128)(2,1)S(1)}, bf16[128,256]{1,0:T(8,128)(2,1)S(1)}, bf16[128,256]{1,0:T(8,128)(2,1)S(1)}, bf16[128,256]{1,0:T(8,128)(2,1)S(1)...) custom-call(s32[22]{0:T(128)S(1)} %concatenate.3.ids, ...), custom_call_target="tpu_custom_call" | custom-call | flops 1 | bytes 1 | tf_op jit(solution)/shard_map/pack/pallas_call | solution.py:343
  3.7 4.1 %collective-permute-start = (bf16[1,48,1024]{2,1,0:T(8,128)(2,1)}, bf16[1,48,1024]{2,1,0:T(8,128)(2,1)S(1)}, u32[]{:S(2)}, u32[]{:S(2)}) collective-permute-start(bf16[1,48,1024]{2,1,0:T(8,128)(2,1)} %near.1), channel_id=1, source_target_pairs={{0,4},{4,0},{1,5},{5,1},{2,6},{6,2},{3,7},{7,3},{8,12},{12,8},{9,1... | collective-permute-start | bytes 294920 | tf_op jit(solution)/shard_map/ppermute | solution.py:340
  7.8 1.5 %collective-permute-start.3 = (bf16[128,256]{1,0:T(8,128)(2,1)S(1)}, bf16[128,256]{1,0:T(8,128)(2,1)S(1)}, u32[]{:S(2)}, u32[]{:S(2)}) collective-permute-start(bf16[128,256]{1,0:T(8,128)(2,1)S(1)} %get-tuple-element.55), channel_id=1, source_target_pairs={{0,8},{8,0},{16,24},{24,16},{1,9},{9,1},{17,25},{25,17},{2,10},{10... | collective-permute-start | bytes 196616 | tf_op jit(solution)/shard_map/ppermute | solution.py:340
  9.3 1.5 %collective-permute-start.4 = (bf16[128,256]{1,0:T(8,128)(2,1)S(1)}, bf16[128,256]{1,0:T(8,128)(2,1)S(1)}, u32[]{:S(2)}, u32[]{:S(2)}) collective-permute-start(bf16[128,256]{1,0:T(8,128)(2,1)S(1)} %get-tuple-element.56), channel_id=1, source_target_pairs={{0,16},{8,24},{16,0},{24,8},{1,17},{9,25},{17,1},{25,9},{2,18},{10... | collective-permute-start | bytes 196616 | tf_op jit(solution)/shard_map/ppermute | solution.py:340
  10.8 0.5 collective-permute-start.5
  11.3 1.5 %collective-permute-start.6 = (bf16[128,768]{1,0:T(8,128)(2,1)S(1)}, bf16[128,768]{1,0:T(8,128)(2,1)S(1)}, u32[]{:S(2)}, u32[]{:S(2)}) collective-permute-start(bf16[128,768]{1,0:T(8,128)(2,1)S(1)} %get-tuple-element.63), channel_id=1, source_target_pairs={{0,8},{8,0},{16,24},{24,16},{1,9},{9,1},{17,25},{25,17},{2,10},{10... | collective-permute-start | bytes 589832 | tf_op jit(solution)/shard_map/ppermute | solution.py:340
  12.8 0.0 collective-permute-done.3.rest_1_
  12.8 1.5 %collective-permute-start.7 = (bf16[128,768]{1,0:T(8,128)(2,1)S(1)}, bf16[128,768]{1,0:T(8,128)(2,1)S(1)}, u32[]{:S(2)}, u32[]{:S(2)}) collective-permute-start(bf16[128,768]{1,0:T(8,128)(2,1)S(1)} %get-tuple-element.64), channel_id=1, source_target_pairs={{0,16},{8,24},{16,0},{24,8},{1,17},{9,25},{17,1},{25,9},{2,18},{10... | collective-permute-start | bytes 589832 | tf_op jit(solution)/shard_map/ppermute | solution.py:340
  14.3 0.1 collective-permute-done.4.rest_2_
  14.4 1.3 %collective-permute-start.8 = (bf16[128,768]{1,0:T(8,128)(2,1)S(1)}, bf16[128,768]{1,0:T(8,128)(2,1)S(1)}, u32[]{:S(2)}, u32[]{:S(2)}) collective-permute-start(bf16[128,768]{1,0:T(8,128)(2,1)S(1)} %get-tuple-element.65), channel_id=1, source_target_pairs={{0,24},{8,16},{16,8},{24,0},{1,25},{9,17},{17,9},{25,1},{2,26},{10... | collective-permute-start | bytes 589832 | tf_op jit(solution)/shard_map/ppermute | solution.py:340
  15.7 1.0 %collective-permute-done.5.rest_3_ = bf16[128,256]{1,0:T(8,128)(2,1)S(1)} collective-permute-done((bf16[128,256]{1,0:T(8,128)(2,1)S(1)}, bf16[128,256]{1,0:T(8,128)(2,1)S(1)}, u32[]{:S(2)}, u32[]{:S(2)}) %collective-permute-start.5) | collective-permute-done | bytes 65568 | tf_op jit(solution)/shard_map/ppermute | solution.py:340
  16.7 0.0 collective-permute-done.far
  16.7 1.0 %choose.2.rest_0_ = bf16[3,128,256]{2,1,0:T(8,128)(2,1)S(1)} custom-call(s32[22]{0:T(128)S(1)} %concatenate.3.ids, bf16[128,256]{1,0:T(8,128)(2,1)S(1)} %get-tuple-element.58.rest_0_, bf16[128,256]{1,0:T(8,128)(2,1)S(1)} %collective-permute-done.3.rest_1_, bf16[128,256]{1,0:T(8,128)(2,1)S(1)} %collective-permute-done.4.rest_2_, ...), custom_call_target="tpu_custom_call" | custom-call | flops 1 | bytes 1 | tf_op jit(solution)/shard_map/choose/pallas_call | solution.py:360
  17.7 0.4 collective-permute-start.9
  18.1 0.0 copy-done.1
  18.1 0.0 copy-done.2
  18.1 0.9 %split.1 = (bf16[48,2048]{1,0:T(8,128)(2,1)S(1)}, bf16[2,48,2048]{2,1,0:T(8,128)(2,1)S(1)}, bf16[2,48,2048]{2,1,0:T(8,128)(2,1)S(1)}) custom-call(s32[22]{0:T(128)S(1)} %concatenate.3.ids, bf16[1,48,6144]{2,1,0:T(8,128)(2,1)S(1)} %copy-done.1, bf16[1,48,1024]{2,1,0:T(8,128)(2,1)S(1)} %copy-done.2, bf16[1,48,1024]{2,1,0:T(8,128)(2,1)S(1)} %collective-permute-done.far), custom_call_target="tpu_custom_call" | custom-call | flops 1 | bytes 1 | tf_op jit(solution)/shard_map/split/pallas_call | solution.py:376
  19.0 1.6 %collective-permute-start.1 = (bf16[2,48,2048]{2,1,0:T(8,128)(2,1)S(1)}, bf16[2,48,2048]{2,1,0:T(8,128)(2,1)S(1)}, u32[]{:S(2)}, u32[]{:S(2)}) collective-permute-start(bf16[2,48,2048]{2,1,0:T(8,128)(2,1)S(1)} %get-tuple-element.53), channel_id=1, source_target_pairs={{0,2},{1,3},{2,0},{3,1},{4,6},{5,7},{6,4},{7,5},{8,10},{9,11},{10,... | collective-permute-start | bytes 1179656 | tf_op jit(solution)/shard_map/ppermute | solution.py:340
  20.6 0.0 collective-permute-done.6.rest_1_
  20.7 2.7 %collective-permute-done.7.rest_2_ = bf16[128,768]{1,0:T(8,128)(2,1)S(1)} collective-permute-done((bf16[128,768]{1,0:T(8,128)(2,1)S(1)}, bf16[128,768]{1,0:T(8,128)(2,1)S(1)}, u32[]{:S(2)}, u32[]{:S(2)}) %collective-permute-start.7) | collective-permute-done | bytes 196640 | tf_op jit(solution)/shard_map/ppermute | solution.py:340
  23.4 0.0 collective-permute-done.8.rest_3_
  23.4 2.9 %collective-permute-done.9.rest_3_ = bf16[3,128,256]{2,1,0:T(8,128)(2,1)S(1)} collective-permute-done((bf16[3,128,256]{2,1,0:T(8,128)(2,1)S(1)}, bf16[3,128,256]{2,1,0:T(8,128)(2,1)S(1)}, u32[]{:S(2)}, u32[]{:S(2)}) %collective-permute-start.9) | collective-permute-done | bytes 196640 | tf_op jit(solution)/shard_map/ppermute | solution.py:340
  26.3 0.9 %choose.3 = (bf16[2,3,128,256]{3,2,1,0:T(8,128)(2,1)S(1)}, bf16[2,3,128,256]{3,2,1,0:T(8,128)(2,1)S(1)}) custom-call(s32[22]{0:T(128)S(1)} %concatenate.3.ids, bf16[128,768]{1,0:T(8,128)(2,1)S(1)} %get-tuple-element.66.rest_0_, bf16[128,768]{1,0:T(8,128)(2,1)S(1)} %collective-permute-done.6.rest_1_, bf16[128,768]{1,0:T(8,128)(2,1)S(1)} %collective-permute-done.7.rest_2_, ...), custom_call_target="tpu_custom_call" | custom-call | flops 1 | bytes 1 | tf_op jit(solution)/shard_map/choose/pallas_call | solution.py:360
  27.2 0.1 collective-permute-start.10
  27.3 3.8 %collective-permute-done.1.got.rest_2_.rest_7_.rest_3_ = bf16[2,48,2048]{2,1,0:T(8,128)(2,1)S(1)} collective-permute-done((bf16[2,48,2048]{2,1,0:T(8,128)(2,1)S(1)}, bf16[2,48,2048]{2,1,0:T(8,128)(2,1)S(1)}, u32[]{:S(2)}, u32[]{:S(2)}) %collective-permute-start.1) | collective-permute-done | bytes 393248 | tf_op jit(solution)/shard_map/ppermute | solution.py:340
  31.1 0.0 collective-permute-done.10.got
  31.2 0.8 collective-permute-start.11
  32.0 3.2 %collective-permute-start.12 = (bf16[3,128,256]{2,1,0:T(8,128)(2,1)S(1)}, bf16[3,128,256]{2,1,0:T(8,128)(2,1)S(1)}, u32[]{:S(2)}, u32[]{:S(2)}) collective-permute-start(bf16[3,128,256]{2,1,0:T(8,128)(2,1)S(1)} %get-tuple-element.76.rest_1_), channel_id=1, source_target_pairs={{0,4},{4,0},{1,5},{5,1},{2,6},{6,2},{3,7},{7,3},{8,12},{12,8},{9,1... | collective-permute-start | bytes 589832 | tf_op jit(solution)/shard_map/ppermute | solution.py:340
  35.2 0.0 collective-permute-start.2
  35.2 8.6 %collective-permute-done.12.rest_4_ = bf16[3,128,256]{2,1,0:T(8,128)(2,1)S(1)} collective-permute-done((bf16[3,128,256]{2,1,0:T(8,128)(2,1)S(1)}, bf16[3,128,256]{2,1,0:T(8,128)(2,1)S(1)}, u32[]{:S(2)}, u32[]{:S(2)}) %collective-permute-start.12) | collective-permute-done | bytes 196640 | tf_op jit(solution)/shard_map/ppermute | solution.py:340
  43.8 0.7 collective-permute-done.11.rest_2_
  44.5 2.6 %collective-permute-start.13 = (bf16[2,3,128,256]{3,2,1,0:T(8,128)(2,1)S(1)}, bf16[2,3,128,256]{3,2,1,0:T(8,128)(2,1)S(1)}, u32[]{:S(2)}, u32[]{:S(2)}) collective-permute-start(bf16[2,3,128,256]{3,2,1,0:T(8,128)(2,1)S(1)} %collective-permute-done.11.rest_2_), channel_id=1, source_target_pairs={{0,4},{4,0},{1,5},{5,1},{2,6},{6,2},{3,7},{7,3},{8,12},{12,8},{9,1... | collective-permute-start | bytes 1179656 | tf_op jit(solution)/shard_map/ppermute | solution.py:340
  47.1 0.0 collective-permute-done.2.rest_1_.rest_6_.rest_2_
  47.1 0.6 sort.1.fresh
  47.7 0.8 runs.2
  48.5 0.7 collective-permute-start.14
  49.2 1.1 %collective-permute-start.15 = (bf16[6,3,16,256]{3,2,1,0:T(8,128)(2,1)S(1)}, bf16[6,3,16,256]{3,2,1,0:T(8,128)(2,1)S(1)}, u32[]{:S(2)}, u32[]{:S(2)}) collective-permute-start(bf16[6,3,16,256]{3,2,1,0:T(8,128)(2,1)S(1)} %get-tuple-element.81), channel_id=1, source_target_pairs={{0,1},{1,24},{2,11},{3,18},{4,5},{5,28},{6,15},{7,22},{8,9},{9,16}... | collective-permute-start | bytes 442376 | tf_op jit(solution)/shard_map/ppermute | solution.py:447
  50.3 3.1 %collective-permute-start.16 = (bf16[6,3,16,256]{3,2,1,0:T(8,128)(2,1)S(1)}, bf16[6,3,16,256]{3,2,1,0:T(8,128)(2,1)S(1)}, u32[]{:S(2)}, u32[]{:S(2)}) collective-permute-start(bf16[6,3,16,256]{3,2,1,0:T(8,128)(2,1)S(1)} %get-tuple-element.82), channel_id=1, source_target_pairs={{0,2},{1,27},{2,8},{3,17},{4,6},{5,31},{6,12},{7,21},{8,10},{9,19}... | collective-permute-start | bytes 442376 | tf_op jit(solution)/shard_map/ppermute | solution.py:447
  53.5 0.2 collective-permute-start.17
  53.6 9.7 %attend.2 = (f32[6,384,128]{2,1,0:T(8,128)S(1)}, f32[6,384,128]{2,1,0:T(8,128)S(1)}, f32[6,384,128]{2,1,0:T(8,128)S(1)}) custom-call(s32[22]{0:T(128)S(1)} %concatenate.3.ids, bf16[384,256]{1,0:T(8,128)(2,1)S(1)} %sort.1.fresh, bf16[3,128,256]{2,1,0:T(8,128)(2,1)S(1)} %choose.2.rest_0_, bf16[3,128,256]{2,1,0:T(8,128)(2,1)S(1)} %get-tuple-element.76.rest_1_, ...), custom_call_target="tpu_custom_call" | custom-call | flops 1 | bytes 1 | tf_op jit(solution)/shard_map/attend/pallas_call | solution.py:208
  63.3 0.4 collective-permute-done.13.rest_0_
  63.7 3.6 %attend.3 = (bf16[2,48,1536]{2,1,0:T(8,128)(2,1)S(1)}, bf16[2,48,1536]{2,1,0:T(8,128)(2,1)S(1)}) custom-call(s32[22]{0:T(128)S(1)} %concatenate.3.ids, bf16[384,256]{1,0:T(8,128)(2,1)S(1)} %sort.1.fresh, bf16[2,3,128,256]{3,2,1,0:T(8,128)(2,1)S(1)} %collective-permute-done.13.rest_0_, bf16[48,2048]{1,0:T(8,128)(2,1)S(1)} %get-tuple-element.52.rest_0_.rest_5_.rest_1_, ...), custom_call_target="tpu_custom_call" | custom-call | flops 1 | bytes 1 | tf_op jit(solution)/shard_map/attend/pallas_call | solution.py:208
  67.3 0.0 collective-permute-done.14.rest_0_
  67.3 0.0 collective-permute-done.15.rest_1_
  67.3 0.0 collective-permute-done.16.rest_2_
  67.3 2.3 %collective-permute-done.17.rest_3_ = bf16[6,3,16,256]{3,2,1,0:T(8,128)(2,1)S(1)} collective-permute-done((bf16[6,3,16,256]{3,2,1,0:T(8,128)(2,1)S(1)}, bf16[6,3,16,256]{3,2,1,0:T(8,128)(2,1)S(1)}, u32[]{:S(2)}, u32[]{:S(2)}) %collective-permute-start.17) | collective-permute-done | bytes 147488 | tf_op jit(solution)/shard_map/ppermute | solution.py:447
  69.6 1.1 %collective-permute-start.18 = (bf16[2,48,1536]{2,1,0:T(8,128)(2,1)S(1)}, bf16[2,48,1536]{2,1,0:T(8,128)(2,1)S(1)}, u32[]{:S(2)}, u32[]{:S(2)}) collective-permute-start(bf16[2,48,1536]{2,1,0:T(8,128)(2,1)S(1)} %get-tuple-element.91), channel_id=1, source_target_pairs={{0,2},{1,3},{2,0},{3,1},{4,6},{5,7},{6,4},{7,5},{8,10},{9,11},{10,... | collective-permute-start | bytes 884744 | tf_op jit(solution)/shard_map/ppermute | solution.py:340
  70.6 0.7 runs.3
  71.3 0.7 collective-permute-start.19
  72.0 1.1 %collective-permute-start.20 = (bf16[2,3,16,256]{3,2,1,0:T(8,128)(2,1)S(1)}, bf16[2,3,16,256]{3,2,1,0:T(8,128)(2,1)S(1)}, u32[]{:S(2)}, u32[]{:S(2)}) collective-permute-start(bf16[2,3,16,256]{3,2,1,0:T(8,128)(2,1)S(1)} %get-tuple-element.94), channel_id=1, source_target_pairs={{0,1},{1,24},{2,11},{3,18},{4,5},{5,28},{6,15},{7,22},{8,9},{9,16}... | collective-permute-start | bytes 147464 | tf_op jit(solution)/shard_map/ppermute | solution.py:447
  73.1 2.2 %collective-permute-start.21 = (bf16[2,3,16,256]{3,2,1,0:T(8,128)(2,1)S(1)}, bf16[2,3,16,256]{3,2,1,0:T(8,128)(2,1)S(1)}, u32[]{:S(2)}, u32[]{:S(2)}) collective-permute-start(bf16[2,3,16,256]{3,2,1,0:T(8,128)(2,1)S(1)} %get-tuple-element.95), channel_id=1, source_target_pairs={{0,2},{1,27},{2,8},{3,17},{4,6},{5,31},{6,12},{7,21},{8,10},{9,19}... | collective-permute-start | bytes 147464 | tf_op jit(solution)/shard_map/ppermute | solution.py:447
  75.3 0.2 collective-permute-start.22
  75.5 0.0 collective-permute-done.19.rest_4_
  75.5 1.0 %collective-permute-done.20.rest_5_ = bf16[2,3,16,256]{3,2,1,0:T(8,128)(2,1)S(1)} collective-permute-done((bf16[2,3,16,256]{3,2,1,0:T(8,128)(2,1)S(1)}, bf16[2,3,16,256]{3,2,1,0:T(8,128)(2,1)S(1)}, u32[]{:S(2)}, u32[]{:S(2)}) %collective-permute-start.20) | collective-permute-done | bytes 49184 | tf_op jit(solution)/shard_map/ppermute | solution.py:447
  76.4 3.1 %collective-permute-done.21.rest_6_ = bf16[2,3,16,256]{3,2,1,0:T(8,128)(2,1)S(1)} collective-permute-done((bf16[2,3,16,256]{3,2,1,0:T(8,128)(2,1)S(1)}, bf16[2,3,16,256]{3,2,1,0:T(8,128)(2,1)S(1)}, u32[]{:S(2)}, u32[]{:S(2)}) %collective-permute-start.21) | collective-permute-done | bytes 49184 | tf_op jit(solution)/shard_map/ppermute | solution.py:447
  79.5 0.2 collective-permute-done.22.rest_7_
  79.7 0.0 collective-permute-done.18.rest_2_
  79.7 1.8 %collective-permute-start.23 = (bf16[2,48,1536]{2,1,0:T(8,128)(2,1)S(1)}, bf16[2,48,1536]{2,1,0:T(8,128)(2,1)S(1)}, u32[]{:S(2)}, u32[]{:S(2)}) collective-permute-start(bf16[2,48,1536]{2,1,0:T(8,128)(2,1)S(1)} %pad_maximum_fusion), channel_id=1, source_target_pairs={{0,1},{1,0},{2,3},{3,2},{4,5},{5,4},{6,7},{7,6},{8,9},{9,8},{10,11... | collective-permute-start | bytes 884744 | tf_op jit(solution)/shard_map/ppermute | solution.py:340
  81.5 2.0 %lay.1 = bf16[1,1,4,24,4096]{4,3,2,1,0:T(8,128)(2,1)} custom-call(s32[22]{0:T(128)S(1)} %concatenate.3.ids, bf16[6,3,16,256]{3,2,1,0:T(8,128)(2,1)S(1)} %collective-permute-done.14.rest_0_, bf16[6,3,16,256]{3,2,1,0:T(8,128)(2,1)S(1)} %collective-permute-done.15.rest_1_, bf16[6,3,16,256]{3,2,1,0:T(8,128)(2,1)S(1)} %collective-permute-done.16.rest_2_, ...), custom_call_target="tpu_custom_call" | custom-call | flops 1 | bytes 1 | tf_op jit(solution)/shard_map/lay/pallas_call | solution.py:479
  83.5 0.0 collective-permute-done.23.rest_1_
  83.5 1.4 %join.1 = bf16[1,48,6144]{2,1,0:T(8,128)(2,1)} custom-call(s32[22]{0:T(128)S(1)} %concatenate.3.ids, bf16[2,48,1536]{2,1,0:T(8,128)(2,1)S(1)} %get-tuple-element.89.rest_0_, bf16[2,48,1536]{2,1,0:T(8,128)(2,1)S(1)} %collective-permute-done.23.rest_1_, bf16[2,48,1536]{2,1,0:T(8,128)(2,1)S(1)} %collective-permute-done.18.rest_2_), custom_call_target="tpu_custom_call" | custom-call | flops 1 | bytes 1 | tf_op jit(solution)/shard_map/join/pallas_call | solution.py:469
  (7 shorter events, 0.1 us)
Async XLA Ops:
  1.4 1.2 %copy-start = (bf16[4,128,1024]{2,1,0:T(8,128)(2,1)S(1)}, bf16[4,128,1024]{2,1,0:T(8,128)(2,1)}, u32[]{:S(2)}) copy-start(bf16[4,128,1024]{2,1,0:T(8,128)(2,1)} %pool_kv.1) | copy-start | bytes 3145732
  2.6 15.5 %copy-start.1 = (bf16[1,48,6144]{2,1,0:T(8,128)(2,1)S(1)}, bf16[1,48,6144]{2,1,0:T(8,128)(2,1)}, u32[]{:S(2)}) copy-start(bf16[1,48,6144]{2,1,0:T(8,128)(2,1)} %fresh_q.1) | copy-start | bytes 1769476
  2.6 15.5 %copy-start.2 = (bf16[1,48,1024]{2,1,0:T(8,128)(2,1)S(1)}, bf16[1,48,1024]{2,1,0:T(8,128)(2,1)}, u32[]{:S(2)}) copy-start(bf16[1,48,1024]{2,1,0:T(8,128)(2,1)} %near.1) | copy-start | bytes 294916
  3.7 13.1 %collective-permute-start = (bf16[1,48,1024]{2,1,0:T(8,128)(2,1)}, bf16[1,48,1024]{2,1,0:T(8,128)(2,1)S(1)}, u32[]{:S(2)}, u32[]{:S(2)}) collective-permute-start(bf16[1,48,1024]{2,1,0:T(8,128)(2,1)} %near.1), channel_id=1, source_target_pairs={{0,4},{4,0},{1,5},{5,1},{2,6},{6,2},{3,7},{7,3},{8,12},{12,8},{9,1... | collective-permute-start | bytes 294920 | tf_op jit(solution)/shard_map/ppermute | solution.py:340
  7.8 5.0 %collective-permute-start.3 = (bf16[128,256]{1,0:T(8,128)(2,1)S(1)}, bf16[128,256]{1,0:T(8,128)(2,1)S(1)}, u32[]{:S(2)}, u32[]{:S(2)}) collective-permute-start(bf16[128,256]{1,0:T(8,128)(2,1)S(1)} %get-tuple-element.55), channel_id=1, source_target_pairs={{0,8},{8,0},{16,24},{24,16},{1,9},{9,1},{17,25},{25,17},{2,10},{10... | collective-permute-start | bytes 196616 | tf_op jit(solution)/shard_map/ppermute | solution.py:340
  9.3 5.1 %collective-permute-start.4 = (bf16[128,256]{1,0:T(8,128)(2,1)S(1)}, bf16[128,256]{1,0:T(8,128)(2,1)S(1)}, u32[]{:S(2)}, u32[]{:S(2)}) collective-permute-start(bf16[128,256]{1,0:T(8,128)(2,1)S(1)} %get-tuple-element.56), channel_id=1, source_target_pairs={{0,16},{8,24},{16,0},{24,8},{1,17},{9,25},{17,1},{25,9},{2,18},{10... | collective-permute-start | bytes 196616 | tf_op jit(solution)/shard_map/ppermute | solution.py:340
  10.8 5.9 %collective-permute-start.5 = (bf16[128,256]{1,0:T(8,128)(2,1)S(1)}, bf16[128,256]{1,0:T(8,128)(2,1)S(1)}, u32[]{:S(2)}, u32[]{:S(2)}) collective-permute-start(bf16[128,256]{1,0:T(8,128)(2,1)S(1)} %get-tuple-element.57), channel_id=1, source_target_pairs={{0,24},{8,16},{16,8},{24,0},{1,25},{9,17},{17,9},{25,1},{2,26},{10... | collective-permute-start | bytes 196616 | tf_op jit(solution)/shard_map/ppermute | solution.py:340
  11.3 9.4 %collective-permute-start.6 = (bf16[128,768]{1,0:T(8,128)(2,1)S(1)}, bf16[128,768]{1,0:T(8,128)(2,1)S(1)}, u32[]{:S(2)}, u32[]{:S(2)}) collective-permute-start(bf16[128,768]{1,0:T(8,128)(2,1)S(1)} %get-tuple-element.63), channel_id=1, source_target_pairs={{0,8},{8,0},{16,24},{24,16},{1,9},{9,1},{17,25},{25,17},{2,10},{10... | collective-permute-start | bytes 589832 | tf_op jit(solution)/shard_map/ppermute | solution.py:340
  12.8 10.6 %collective-permute-start.7 = (bf16[128,768]{1,0:T(8,128)(2,1)S(1)}, bf16[128,768]{1,0:T(8,128)(2,1)S(1)}, u32[]{:S(2)}, u32[]{:S(2)}) collective-permute-start(bf16[128,768]{1,0:T(8,128)(2,1)S(1)} %get-tuple-element.64), channel_id=1, source_target_pairs={{0,16},{8,24},{16,0},{24,8},{1,17},{9,25},{17,1},{25,9},{2,18},{10... | collective-permute-start | bytes 589832 | tf_op jit(solution)/shard_map/ppermute | solution.py:340
  14.4 9.0 %collective-permute-start.8 = (bf16[128,768]{1,0:T(8,128)(2,1)S(1)}, bf16[128,768]{1,0:T(8,128)(2,1)S(1)}, u32[]{:S(2)}, u32[]{:S(2)}) collective-permute-start(bf16[128,768]{1,0:T(8,128)(2,1)S(1)} %get-tuple-element.65), channel_id=1, source_target_pairs={{0,24},{8,16},{16,8},{24,0},{1,25},{9,17},{17,9},{25,1},{2,26},{10... | collective-permute-start | bytes 589832 | tf_op jit(solution)/shard_map/ppermute | solution.py:340
  17.7 8.6 %collective-permute-start.9 = (bf16[3,128,256]{2,1,0:T(8,128)(2,1)S(1)}, bf16[3,128,256]{2,1,0:T(8,128)(2,1)S(1)}, u32[]{:S(2)}, u32[]{:S(2)}) collective-permute-start(bf16[3,128,256]{2,1,0:T(8,128)(2,1)S(1)} %choose.2.rest_0_), channel_id=1, source_target_pairs={{0,4},{4,0},{1,5},{5,1},{2,6},{6,2},{3,7},{7,3},{8,12},{12,8},{9,1... | collective-permute-start | bytes 589832 | tf_op jit(solution)/shard_map/ppermute | solution.py:340
  19.0 12.1 %collective-permute-start.1 = (bf16[2,48,2048]{2,1,0:T(8,128)(2,1)S(1)}, bf16[2,48,2048]{2,1,0:T(8,128)(2,1)S(1)}, u32[]{:S(2)}, u32[]{:S(2)}) collective-permute-start(bf16[2,48,2048]{2,1,0:T(8,128)(2,1)S(1)} %get-tuple-element.53), channel_id=1, source_target_pairs={{0,2},{1,3},{2,0},{3,1},{4,6},{5,7},{6,4},{7,5},{8,10},{9,11},{10,... | collective-permute-start | bytes 1179656 | tf_op jit(solution)/shard_map/ppermute | solution.py:340
  27.2 3.9 %collective-permute-start.10 = (bf16[2,3,128,256]{3,2,1,0:T(8,128)(2,1)S(1)}, bf16[2,3,128,256]{3,2,1,0:T(8,128)(2,1)S(1)}, u32[]{:S(2)}, u32[]{:S(2)}) collective-permute-start(bf16[2,3,128,256]{3,2,1,0:T(8,128)(2,1)S(1)} %get-tuple-element.70), channel_id=1, source_target_pairs={{0,1},{1,0},{2,3},{3,2},{4,5},{5,4},{6,7},{7,6},{8,9},{9,8},{10,11... | collective-permute-start | bytes 1179656 | tf_op jit(solution)/shard_map/ppermute | solution.py:340
  31.2 13.3 %collective-permute-start.11 = (bf16[2,3,128,256]{3,2,1,0:T(8,128)(2,1)S(1)}, bf16[2,3,128,256]{3,2,1,0:T(8,128)(2,1)S(1)}, u32[]{:S(2)}, u32[]{:S(2)}) collective-permute-start(bf16[2,3,128,256]{3,2,1,0:T(8,128)(2,1)S(1)} %get-tuple-element.74), channel_id=1, source_target_pairs={{0,2},{1,3},{2,0},{3,1},{4,6},{5,7},{6,4},{7,5},{8,10},{9,11},{10,... | collective-permute-start | bytes 1179656 | tf_op jit(solution)/shard_map/ppermute | solution.py:340
  32.0 11.8 %collective-permute-start.12 = (bf16[3,128,256]{2,1,0:T(8,128)(2,1)S(1)}, bf16[3,128,256]{2,1,0:T(8,128)(2,1)S(1)}, u32[]{:S(2)}, u32[]{:S(2)}) collective-permute-start(bf16[3,128,256]{2,1,0:T(8,128)(2,1)S(1)} %get-tuple-element.76.rest_1_), channel_id=1, source_target_pairs={{0,4},{4,0},{1,5},{5,1},{2,6},{6,2},{3,7},{7,3},{8,12},{12,8},{9,1... | collective-permute-start | bytes 589832 | tf_op jit(solution)/shard_map/ppermute | solution.py:340
  35.2 12.0 %collective-permute-start.2 = (bf16[2,48,2048]{2,1,0:T(8,128)(2,1)S(1)}, bf16[2,48,2048]{2,1,0:T(8,128)(2,1)S(1)}, u32[]{:S(2)}, u32[]{:S(2)}) collective-permute-start(bf16[2,48,2048]{2,1,0:T(8,128)(2,1)S(1)} %follow.1), channel_id=1, source_target_pairs={{0,1},{1,0},{2,3},{3,2},{4,5},{5,4},{6,7},{7,6},{8,9},{9,8},{10,11... | collective-permute-start | bytes 1179656 | tf_op jit(solution)/shard_map/ppermute | solution.py:340
  44.5 19.2 %collective-permute-start.13 = (bf16[2,3,128,256]{3,2,1,0:T(8,128)(2,1)S(1)}, bf16[2,3,128,256]{3,2,1,0:T(8,128)(2,1)S(1)}, u32[]{:S(2)}, u32[]{:S(2)}) collective-permute-start(bf16[2,3,128,256]{3,2,1,0:T(8,128)(2,1)S(1)} %collective-permute-done.11.rest_2_), channel_id=1, source_target_pairs={{0,4},{4,0},{1,5},{5,1},{2,6},{6,2},{3,7},{7,3},{8,12},{12,8},{9,1... | collective-permute-start | bytes 1179656 | tf_op jit(solution)/shard_map/ppermute | solution.py:340
  48.5 18.7 %collective-permute-start.14 = (bf16[6,3,16,256]{3,2,1,0:T(8,128)(2,1)S(1)}, bf16[6,3,16,256]{3,2,1,0:T(8,128)(2,1)S(1)}, u32[]{:S(2)}, u32[]{:S(2)}) collective-permute-start(bf16[6,3,16,256]{3,2,1,0:T(8,128)(2,1)S(1)} %get-tuple-element.80), channel_id=1, source_target_pairs={{0,0},{1,25},{2,10},{3,19},{4,4},{5,29},{6,14},{7,23},{8,8},{9,17}... | collective-permute-start | bytes 442376 | tf_op jit(solution)/shard_map/ppermute | solution.py:447
  49.2 18.1 %collective-permute-start.15 = (bf16[6,3,16,256]{3,2,1,0:T(8,128)(2,1)S(1)}, bf16[6,3,16,256]{3,2,1,0:T(8,128)(2,1)S(1)}, u32[]{:S(2)}, u32[]{:S(2)}) collective-permute-start(bf16[6,3,16,256]{3,2,1,0:T(8,128)(2,1)S(1)} %get-tuple-element.81), channel_id=1, source_target_pairs={{0,1},{1,24},{2,11},{3,18},{4,5},{5,28},{6,15},{7,22},{8,9},{9,16}... | collective-permute-start | bytes 442376 | tf_op jit(solution)/shard_map/ppermute | solution.py:447
  50.3 17.0 %collective-permute-start.16 = (bf16[6,3,16,256]{3,2,1,0:T(8,128)(2,1)S(1)}, bf16[6,3,16,256]{3,2,1,0:T(8,128)(2,1)S(1)}, u32[]{:S(2)}, u32[]{:S(2)}) collective-permute-start(bf16[6,3,16,256]{3,2,1,0:T(8,128)(2,1)S(1)} %get-tuple-element.82), channel_id=1, source_target_pairs={{0,2},{1,27},{2,8},{3,17},{4,6},{5,31},{6,12},{7,21},{8,10},{9,19}... | collective-permute-start | bytes 442376 | tf_op jit(solution)/shard_map/ppermute | solution.py:447
  53.5 16.1 %collective-permute-start.17 = (bf16[6,3,16,256]{3,2,1,0:T(8,128)(2,1)S(1)}, bf16[6,3,16,256]{3,2,1,0:T(8,128)(2,1)S(1)}, u32[]{:S(2)}, u32[]{:S(2)}) collective-permute-start(bf16[6,3,16,256]{3,2,1,0:T(8,128)(2,1)S(1)} %get-tuple-element.83), channel_id=1, source_target_pairs={{0,3},{1,26},{2,9},{3,16},{4,7},{5,30},{6,13},{7,20},{8,11},{9,18}... | collective-permute-start | bytes 442376 | tf_op jit(solution)/shard_map/ppermute | solution.py:447
  69.6 10.1 %collective-permute-start.18 = (bf16[2,48,1536]{2,1,0:T(8,128)(2,1)S(1)}, bf16[2,48,1536]{2,1,0:T(8,128)(2,1)S(1)}, u32[]{:S(2)}, u32[]{:S(2)}) collective-permute-start(bf16[2,48,1536]{2,1,0:T(8,128)(2,1)S(1)} %get-tuple-element.91), channel_id=1, source_target_pairs={{0,2},{1,3},{2,0},{3,1},{4,6},{5,7},{6,4},{7,5},{8,10},{9,11},{10,... | collective-permute-start | bytes 884744 | tf_op jit(solution)/shard_map/ppermute | solution.py:340
  71.3 4.2 %collective-permute-start.19 = (bf16[2,3,16,256]{3,2,1,0:T(8,128)(2,1)S(1)}, bf16[2,3,16,256]{3,2,1,0:T(8,128)(2,1)S(1)}, u32[]{:S(2)}, u32[]{:S(2)}) collective-permute-start(bf16[2,3,16,256]{3,2,1,0:T(8,128)(2,1)S(1)} %get-tuple-element.93), channel_id=1, source_target_pairs={{0,0},{1,25},{2,10},{3,19},{4,4},{5,29},{6,14},{7,23},{8,8},{9,17}... | collective-permute-start | bytes 147464 | tf_op jit(solution)/shard_map/ppermute | solution.py:447
  72.0 4.5 %collective-permute-start.20 = (bf16[2,3,16,256]{3,2,1,0:T(8,128)(2,1)S(1)}, bf16[2,3,16,256]{3,2,1,0:T(8,128)(2,1)S(1)}, u32[]{:S(2)}, u32[]{:S(2)}) collective-permute-start(bf16[2,3,16,256]{3,2,1,0:T(8,128)(2,1)S(1)} %get-tuple-element.94), channel_id=1, source_target_pairs={{0,1},{1,24},{2,11},{3,18},{4,5},{5,28},{6,15},{7,22},{8,9},{9,16}... | collective-permute-start | bytes 147464 | tf_op jit(solution)/shard_map/ppermute | solution.py:447
  73.1 6.5 %collective-permute-start.21 = (bf16[2,3,16,256]{3,2,1,0:T(8,128)(2,1)S(1)}, bf16[2,3,16,256]{3,2,1,0:T(8,128)(2,1)S(1)}, u32[]{:S(2)}, u32[]{:S(2)}) collective-permute-start(bf16[2,3,16,256]{3,2,1,0:T(8,128)(2,1)S(1)} %get-tuple-element.95), channel_id=1, source_target_pairs={{0,2},{1,27},{2,8},{3,17},{4,6},{5,31},{6,12},{7,21},{8,10},{9,19}... | collective-permute-start | bytes 147464 | tf_op jit(solution)/shard_map/ppermute | solution.py:447
  75.3 4.4 %collective-permute-start.22 = (bf16[2,3,16,256]{3,2,1,0:T(8,128)(2,1)S(1)}, bf16[2,3,16,256]{3,2,1,0:T(8,128)(2,1)S(1)}, u32[]{:S(2)}, u32[]{:S(2)}) collective-permute-start(bf16[2,3,16,256]{3,2,1,0:T(8,128)(2,1)S(1)} %get-tuple-element.96), channel_id=1, source_target_pairs={{0,3},{1,26},{2,9},{3,16},{4,7},{5,30},{6,13},{7,20},{8,11},{9,18}... | collective-permute-start | bytes 147464 | tf_op jit(solution)/shard_map/ppermute | solution.py:447
  79.7 3.8 %collective-permute-start.23 = (bf16[2,48,1536]{2,1,0:T(8,128)(2,1)S(1)}, bf16[2,48,1536]{2,1,0:T(8,128)(2,1)S(1)}, u32[]{:S(2)}, u32[]{:S(2)}) collective-permute-start(bf16[2,48,1536]{2,1,0:T(8,128)(2,1)S(1)} %pad_maximum_fusion), channel_id=1, source_target_pairs={{0,1},{1,0},{2,3},{3,2},{4,5},{5,4},{6,7},{7,6},{8,9},{9,8},{10,11... | collective-permute-start | bytes 884744 | tf_op jit(solution)/shard_map/ppermute | solution.py:340

commit v5 on v4

--- a/solution.py
+++ b/solution.py
@@ -82,6 +82,21 @@
     return [refs[i] if index is None else refs[i].at[index] for i, index in views]
 
 
+def ahead(seat):
+    return (seat // (KV_HEADS // 2) ^ seat // KV_HEADS) & 1
+
+
+def arrived_of(refs, seat):
+    if len(refs) == 1:
+        return lambda at: refs[0][at]
+    return lambda at: jnp.where(ahead(seat) == 1, refs[0][at], refs[1][at])
+
+
+def group_views(views, messages):
+    views = iter(views)
+    return [[next(views) for _ in message] for message in messages]
+
+
 def sort_kernel(quads, views, ids, *rest):
     parts, out = look(rest[:-1], views), rest[-1]
     rows, width = parts[0].shape[0], out.shape[1]
@@ -127,9 +142,9 @@
 
 
 def attend_kernel(ks, first, last, seq_count, rows, stacked, group, count_in, views, q_views, at_chosen, ids, fresh, *rest):
-    messages, q = look(rest[:count_in], views), look(rest[:count_in], q_views)
+    messages, q = [look(rest[:count_in], v) for v in views], look(rest[:count_in], q_views)
     rest = rest[count_in:]
-    spans, block, _ = messages[0].shape
+    spans, block, _ = messages[0][0].shape
     quad_rows = KV_HEADS * rows
     if not first:
         (acc_in, top_in, total_in), rest = rest[:3], rest[3:]
@@ -141,8 +156,9 @@
     for at, k in enumerate(ks):
         for j in range(spans):
             row = pl.ds((at * spans + j) * block, block)
-            keys[row, :] = messages[at][j, :, :HEAD_DIM]
-            values[row, :HEAD_DIM] = messages[at][j, :, HEAD_DIM:]
+            both = arrived_of(messages[at], me ^ k)(j)
+            keys[row, :] = both[:, :HEAD_DIM]
+            values[row, :HEAD_DIM] = both[:, HEAD_DIM:]
         for i in range(ids.shape[0] - at_chosen):
             picked = ids[at_chosen + i]
 
@@ -187,7 +203,8 @@
             for i in range(stacked):
                 for d in range(KV_HEADS):
                     at = i * quad_rows + d * rows
-                    outs[d // 2][d % 2, :, cols[i]] = done[at : at + rows].astype(BF16)
+                    out = (outs[0], outs[1].at[0], outs[2].at[0], outs[1].at[1])[d]
+                    out[:, cols[i]] = done[at : at + rows].astype(BF16)
         else:
             outs[0][h // stacked] = acc
             outs[1][h // stacked] = top
@@ -196,12 +213,14 @@
 
 def attend(ks, state, last, seq_count, rows, group, at_chosen, ids, q, fresh, messages):
     quad_rows = KV_HEADS * rows
-    arrays, views = arrays_of([*messages, *q])
-    spans, block, kv_width = messages[0][0].shape[-3:]
+    arrays, views = arrays_of([view for message in messages for view in message] + q)
+    q_views, views = views[-len(q) :], group_views(views, messages)
+    spans, block, kv_width = messages[0][0][0].shape[-3:]
     keys = len(ks) * spans * block
     stacked = 2 - group % 2
     if last:
-        out_shape = [jax.ShapeDtypeStruct((2, rows, group * HEAD_DIM), BF16)] * (KV_HEADS // 2)
+        one = jax.ShapeDtypeStruct((rows, group * HEAD_DIM), BF16)
+        out_shape = [one] + [jax.ShapeDtypeStruct((2, *one.shape), BF16)] * 2
     else:
         out_shape = [jax.ShapeDtypeStruct((group // stacked, stacked * quad_rows, HEAD_DIM), F32)] * 3
     inputs = [ids, fresh, *arrays, *(state or ())]
@@ -216,8 +235,8 @@
             stacked,
             group,
             len(arrays),
-            views[: len(ks)],
-            views[len(ks) :],
+            views,
+            q_views,
             at_chosen,
         ),
         out_shape=out_shape,
@@ -241,8 +260,8 @@
 
 
 def runs_kernel(ks, seq_count, count_in, views, at_chosen, ids, fresh, *rest):
-    messages, outs = look(rest[:count_in], views), rest[count_in:]
-    spans, block, _ = messages[0].shape
+    messages, outs = [look(rest[:count_in], v) for v in views], rest[count_in:]
+    spans, block, _ = messages[0][0].shape
     run = outs[0].shape[2]
     me = ids[1] * KV_HEADS + ids[2]
     slab = len(outs) * run
@@ -252,26 +271,27 @@
         slot = slot_of(ks, k, ids[2])
         for m, out in enumerate(outs):
             if run % 16:
-                rows = source[pl.ds(pl.multiple_of(first + offset, slab), slab), :].astype(F32)
+                rows = source(pl.ds(pl.multiple_of(first + offset, slab), slab)).astype(F32)
                 out[slot, j] = rows[m * run : (m + 1) * run].astype(BF16)
             else:
                 row = first + offset + (ids[2] ^ m) * run
-                out[slot, j] = source[pl.ds(pl.multiple_of(row, run), run), :]
+                out[slot, j] = source(pl.ds(pl.multiple_of(row, run), run))
 
     for at, k in enumerate(ks):
         for j in range(spans):
-            put(k, j, messages[at].at[j], 0)
+            put(k, j, arrived_of([m.at[j] for m in messages[at]], me ^ k), 0)
         for i in range(ids.shape[0] - at_chosen):
             picked = ids[at_chosen + i]
 
             @pl.when(picked % seq_count == me ^ k)
             def _():
-                put(k, picked // seq_count, fresh, i * block)
+                put(k, picked // seq_count, lambda rows: fresh[rows], i * block)
 
 
 def cut_runs(ks, seq_count, run, heads, at_chosen, ids, fresh, messages):
-    arrays, views = arrays_of(messages)
-    spans, _, kv_width = messages[0][0].shape[-3:]
+    arrays, views = arrays_of([view for message in messages for view in message])
+    views = group_views(views, messages)
+    spans, _, kv_width = messages[0][0][0].shape[-3:]
     return pl.pallas_call(
         functools.partial(runs_kernel, ks, seq_count, len(arrays), views, at_chosen),
         out_shape=[jax.ShapeDtypeStruct((len(ks), spans, run, kv_width), BF16)] * heads,
@@ -283,9 +303,15 @@
     )(ids, fresh, *arrays)
 
 
-def lay_kernel(seq_count, parts, ids, *rest):
-    landed, out = rest[:-1], rest[-1]
+def finish_kernel(seq_count, views, count_in, ids, *rest):
+    parts, landed, (joined, out, laid_out, sems) = look(rest[:count_in], views), rest[count_in:-4], rest[-4:]
     spans, run, width = landed[0].shape[1:]
+    part_width = parts[0].shape[1]
+    copies = []
+    for d, part in enumerate(parts):
+        cols = pl.ds(pl.multiple_of((ids[3] ^ turn(d)) * part_width, HEAD_DIM), part_width)
+        copies.append(pltpu.make_async_copy(part, joined.at[0, :, cols], sems.at[0, d]))
+        copies[-1].start()
     count = seq_count * spans * run
     blocks = spans * seq_count
     at = lax.broadcasted_iota(jnp.int32, (count, count), 1)
@@ -300,21 +326,18 @@
     for k in range(KV_HEADS):
         if k % (KV_HEADS // 2) == 0:
             order = order_of(ids[2] ^ k)
-        rows = [landed[i * KV_HEADS + k][...] for i in range(parts)]
+        rows = [landed[i + k][...] for i in range(0, len(landed), KV_HEADS)]
         if run % 16:
             rows = [part.astype(F32) for part in rows]
         rows = jnp.concatenate([part.reshape(-1, width) for part in rows], axis=0).astype(BF16)
         laid = jnp.dot(order, rows, preferred_element_type=F32)
         request = ids[0] ^ turn(ids[2] ^ k)
         for u in range(run):
-            out[0, 0, request, :, pl.ds(u * width, width)] = laid[u * blocks : (u + 1) * blocks].astype(BF16)
-
-
-def join_kernel(views, ids, *rest):
-    parts, out = look(rest[:-1], views), rest[-1]
-    width = parts[0].shape[1]
-    for d, part in enumerate(parts):
-        out[0, :, pl.ds(pl.multiple_of((ids[3] ^ turn(d)) * width, HEAD_DIM), width)] = part[...]
+            laid_out[k, :, pl.ds(u * width, width)] = laid[u * blocks : (u + 1) * blocks].astype(BF16)
+        copies.append(pltpu.make_async_copy(laid_out.at[k], out.at[0, 0, request], sems.at[1, k]))
+        copies[-1].start()
+    for copy in copies:
+        copy.wait()
 
 
 def shards(pool_kv, span_home, span_order, chosen, fresh_q, fresh_kv):
@@ -371,6 +394,19 @@
     blocks = jax.ShapeDtypeStruct((spans, block, kv_width), BF16)
     (own,) = from_pool(to_pool[:pool_count], [blocks], far)
     early = [swap(own, "quad", quads, a) for a in range(1, quads)]
+    def place(got, send):
+        like = jax.ShapeDtypeStruct(send.shape, BF16)
+        return pl.pallas_call(
+            place_kernel,
+            out_shape=[jax.ShapeDtypeStruct(send.shape[1:], BF16), like],
+            in_specs=[VMEM] * 2,
+            out_specs=[VMEM] * 2,
+            input_output_aliases={1: 1},
+            compiler_params=PARAMS,
+            cost_estimate=CHEAP,
+            name="place",
+        )(got, send)
+
     one = jax.ShapeDtypeStruct((rows, q_part + quads * kv_width), BF16)
     pair = jax.ShapeDtypeStruct((2, *one.shape), BF16)
     keep, give, send = pl.pallas_call(
@@ -399,18 +435,9 @@
 
     pair = jax.ShapeDtypeStruct((2, *blocks.shape), BF16)
     give, kv_send = from_pool(to_pool[pool_count:], [pair] * 2, send, early)
-    beside, kv_send = pl.pallas_call(
-        place_kernel,
-        out_shape=[blocks, pair],
-        in_specs=[VMEM] * 2,
-        out_specs=[VMEM] * 2,
-        input_output_aliases={1: 1},
-        compiler_params=PARAMS,
-        cost_estimate=CHEAP,
-        name="place",
-    )(after(swap(give, "head", heads, 1), q_give), kv_send)
+    beside, kv_send = place(after(swap(give, "head", heads, 1), q_give), kv_send)
     rest = swap(kv_send, "head", heads, 2)
-    messages = [(own, None), (beside, None), (rest, 0), (rest, 1)]
+    messages = [[(own, None)], [(beside, None)], [(rest, 0)], [(rest, 1)]]
 
     if rows % 16:
         q = [(jnp.concatenate([part if index is None else part[index] for part, index in q], axis=0), None)]
@@ -430,9 +457,10 @@
         )(ids, *arrays)
 
     def to_decode(ks, *dep):
-        arrays, views = arrays_of([messages[k] for k in ks])
+        parts = [messages[k] for k in ks]
+        arrays, views = arrays_of([view for message in parts for view in message])
         arrays = after(arrays, dep)
-        parts = [(arrays[i], index) for i, index in views]
+        parts = group_views([(arrays[i], index) for i, index in views], parts)
         cut = cut_runs(ks, seq_count, run, heads, at_chosen, ids, fresh, parts)
         if run % 16:
             cut = [lax.dynamic_index_in_dim(jnp.stack(cut), head ^ k, axis=0, keepdims=False) for k in range(heads)]
@@ -450,42 +478,49 @@
     def work(ks, state, last=False):
         return attend(ks, state, last, seq_count, rows, group, at_chosen, ids, q, fresh, [messages[k] for k in ks])
 
+    soons = []
     for a in range(1, quads):
         second = swap(beside, "quad", quads, a)
-        crossed = swap(after(rest, second), "quad", quads, a)
-        messages += [(early[a - 1], None), (second, None), (crossed, 0), (crossed, 1)]
+        messages += [[(early[a - 1], None)], [(second, None)], None, None]
+    first = [0, 1, *range(heads, seq_count, heads)]
+    state = None
+    for at in range(0, len(first), 6):
+        state = work(first[at : at + 6], state)
+    firsts = [i for i in range(seq_count) if ahead(i)]
+    for a in range(1, quads):
+        at = a * heads
+        soon = lax.ppermute(kv_send, ("quad", "head"), [(i, i ^ at ^ 2) for i in firsts])
+        late = lax.ppermute(after(rest, messages[at + 1], state), ("quad", "head"), [(i, i ^ at) for i in firsts])
+        messages[at + 2 : at + 4] = [[(soon, 0), (late, 0)], [(soon, 1), (late, 1)]]
+        soons.append(soon)
     groups = [list(range(seq_count - 2)), [seq_count - 2, seq_count - 1]]
-    landed = [to_decode(groups[0])]
-    fresh = after(fresh, landed[0][1])
-    state = None
-    for first in range(0, seq_count - 2, 6):
-        state = work(groups[0][first : first + 6], state)
-    kept, sent = work(groups[-1], state, True)
-    chip = swap(after(sent, landed[0][0]), "head", heads, 2)
-    landed.append(to_decode(groups[1], kept))
-    chip = after(chip, landed[1][0])
-    core = swap(jnp.stack([kept[1], chip[1]]), "head", heads, 1)
-    arrays, views = arrays_of([(kept, 0), (core, 0), (chip, 0), (core, 1)])
-    attended = pl.pallas_call(
-        functools.partial(join_kernel, views),
-        out_shape=jax.ShapeDtypeStruct((1, rows, q_width), BF16),
-        in_specs=[SMEM] + [VMEM] * len(arrays),
-        out_specs=VMEM,
+    second = [k for k in groups[0] if k not in first]
+    landed = [to_decode(groups[0], state)]
+    state = after(state, soons, landed[0][1])
+    for at in range(0, len(second), 6):
+        state = work(second[at : at + 6], state)
+    keep, give, send = work(groups[-1], state, True)
+    beside, send = place(swap(after(give, landed[0][0]), "head", heads, 1), send)
+    landed.append(to_decode(groups[1], keep))
+    chip = swap(send, "head", heads, 2)
+    arrays, views = arrays_of([(keep, None), (beside, None), (chip, 0), (chip, 1)])
+    runs = [part for went, _ in landed for part in went]
+    return pl.pallas_call(
+        functools.partial(finish_kernel, seq_count, views, len(arrays)),
+        out_shape=[
+            jax.ShapeDtypeStruct((1, rows, q_width), BF16),
+            jax.ShapeDtypeStruct((1, 1, pool_count, spans * seq_count, run * kv_width), BF16),
+        ],
+        in_specs=[SMEM] + [VMEM] * (len(arrays) + len(runs)),
+        out_specs=[ANY] * 2,
+        scratch_shapes=[
+            pltpu.VMEM((pool_count, spans * seq_count, run * kv_width), BF16),
+            pltpu.SemaphoreType.DMA((2, max(pool_count, heads))),
+        ],
         compiler_params=PARAMS,
         cost_estimate=CHEAP,
-        name="join",
-    )(ids, *arrays)
-    arrays = [part for went, _ in landed for part in went]
-    decoded = pl.pallas_call(
-        functools.partial(lay_kernel, seq_count, len(landed)),
-        out_shape=jax.ShapeDtypeStruct((1, 1, pool_count, spans * seq_count, run * kv_width), BF16),
-        in_specs=[SMEM] + [VMEM] * len(arrays),
-        out_specs=VMEM,
-        compiler_params=PARAMS,
-        cost_estimate=CHEAP,
-        name="lay",
-    )(ids, *arrays)
-    return (attended, decoded)
+        name="finish",
+    )(ids, *arrays, *runs)
 
 
 def solution(mesh):

time: 85.1 us -> 83.6 us (0.982)
  waiting for transfers between devices: 26.9 us -> 23.3 us
  starting transfers between devices: 32.6 us -> 35.2 us
    ppermute x8, starting transfers between devices: 9.19 us -> 13.1 us  [to_decode(): went[k] = lax.ppermute(cut[k], ('pool', 'quad', 'head'), perm)]
    ppermute x16 -> x15, starting transfers between devices: 23.4 us -> 20.1 us  [swap(): return lax.ppermute(value, axes, [(i, i ^ k) for i in range(count)])]
    ppermute x16 -> x15, waiting for transfers between devices: 20.4 us -> 17.3 us  [swap(): return lax.ppermute(value, axes, [(i, i ^ k) for i in range(count)])]
    ppermute x0 -> x2, starting transfers between devices: none -> 1.95 us  [the longest x1 1.28 us: shards(): lax.ppermute(after(rest, messages[at + 1], state), ('quad', 'head'), [(i,...]
    pallas_call x3, Pallas kernels: 3.45 us -> 2.01 us  [the longest x1 1.96 us: shards(): pl.pallas_call(functools.partial(finish_kernel, seq_count, views, len(arr...]
    pallas_call x2 -> x3, Pallas kernels: 13.3 us -> 14.1 us  [attend(): pl.pallas_call(functools.partial(attend_kernel, ks, state is None, last,...]
  transfers between devices with their start and end apart: 24 -> 25, of which waited for: 12 -> 11; matrix products, arithmetic and copies ran while one was open for 0% -> 0% of each run, Pallas kernels for 24% -> 23%
where the time goes in v5:
time: 83.6 us; the launch traced here: 83.4 us
  starting transfers between devices  35.2 us (42%)
  waiting for transfers between devices  23.3 us (28%)
  Pallas kernels  21.9 us (26%)
  local copies, waits for them, and re-layouts  2 us (2%)
  between operations  1.01 us (1%)
    ppermute x15, starting transfers between devices, swap(): return lax.ppermute(value, axes, [(i, i ^ k) for i in range(count)])  20.1 us
    ppermute x15, waiting for transfers between devices, swap(): return lax.ppermute(value, axes, [(i, i ^ k) for i in range(count)])  17.3 us
    pallas_call x3, Pallas kernels, attend(): pl.pallas_call(functools.partial(attend_kernel, ks, state is None, last,...  14.1 us
    ppermute x8, starting transfers between devices, to_decode(): went[k] = lax.ppermute(cut[k], ('pool', 'quad', 'head'), perm)  13.1 us
    ppermute x8, waiting for transfers between devices, to_decode(): went[k] = lax.ppermute(cut[k], ('pool', 'quad', 'head'), perm)  5.93 us
    pallas_call x1, Pallas kernels, shards(): pl.pallas_call(functools.partial(finish_kernel, seq_count, views, len(arr...  1.96 us
    pallas_call x2, Pallas kernels, from_pool(): pl.pallas_call(functools.partial(choose_kernel, slots, pool_count), out_s...  1.84 us
  transfers between devices with their start and end apart: 25, of which 11 were waited for; matrix products, arithmetic and copies ran while one was open for 0% of the time, Pallas kernels for 23%

profile of v5, /device:TPU:0, one launch (start us, length us, event | category | flops | bytes accessed | tf_op | source)
XLA Modules:
  0.0 83.4 jit_solution(12988694691373347004)
XLA Ops:
  0.6 0.8 concatenate.3.ids
  1.4 1.2 %copy-done = bf16[4,128,1024]{2,1,0:T(8,128)(2,1)S(1)} copy-done((bf16[4,128,1024]{2,1,0:T(8,128)(2,1)S(1)}, bf16[4,128,1024]{2,1,0:T(8,128)(2,1)}, u32[]{:S(2)}) %copy-start) | copy-done | bytes 1048600
  2.6 1.1 %pack.1 = (bf16[128,256]{1,0:T(8,128)(2,1)S(1)}, bf16[128,256]{1,0:T(8,128)(2,1)S(1)}, bf16[128,256]{1,0:T(8,128)(2,1)S(1)}, bf16[128,256]{1,0:T(8,128)(2,1)S(1)...) custom-call(s32[22]{0:T(128)S(1)} %concatenate.3.ids, ...), custom_call_target="tpu_custom_call" | custom-call | flops 1 | bytes 1 | tf_op jit(solution)/shard_map/pack/pallas_call | solution.py:366
  3.7 4.1 %collective-permute-start = (bf16[1,48,1024]{2,1,0:T(8,128)(2,1)}, bf16[1,48,1024]{2,1,0:T(8,128)(2,1)S(1)}, u32[]{:S(2)}, u32[]{:S(2)}) collective-permute-start(bf16[1,48,1024]{2,1,0:T(8,128)(2,1)} %near.1), channel_id=1, source_target_pairs={{0,4},{4,0},{1,5},{5,1},{2,6},{6,2},{3,7},{7,3},{8,12},{12,8},{9,1... | collective-permute-start | bytes 294920 | tf_op jit(solution)/shard_map/ppermute | solution.py:363
  7.8 1.5 %collective-permute-start.6 = (bf16[128,256]{1,0:T(8,128)(2,1)S(1)}, bf16[128,256]{1,0:T(8,128)(2,1)S(1)}, u32[]{:S(2)}, u32[]{:S(2)}) collective-permute-start(bf16[128,256]{1,0:T(8,128)(2,1)S(1)} %get-tuple-element.67), channel_id=1, source_target_pairs={{0,8},{8,0},{16,24},{24,16},{1,9},{9,1},{17,25},{25,17},{2,10},{10... | collective-permute-start | bytes 196616 | tf_op jit(solution)/shard_map/ppermute | solution.py:363
  9.3 1.5 %collective-permute-start.7 = (bf16[128,256]{1,0:T(8,128)(2,1)S(1)}, bf16[128,256]{1,0:T(8,128)(2,1)S(1)}, u32[]{:S(2)}, u32[]{:S(2)}) collective-permute-start(bf16[128,256]{1,0:T(8,128)(2,1)S(1)} %get-tuple-element.68), channel_id=1, source_target_pairs={{0,16},{8,24},{16,0},{24,8},{1,17},{9,25},{17,1},{25,9},{2,18},{10... | collective-permute-start | bytes 196616 | tf_op jit(solution)/shard_map/ppermute | solution.py:363
  10.8 0.5 collective-permute-start.8
  11.3 1.5 %collective-permute-start.3 = (bf16[128,768]{1,0:T(8,128)(2,1)S(1)}, bf16[128,768]{1,0:T(8,128)(2,1)S(1)}, u32[]{:S(2)}, u32[]{:S(2)}) collective-permute-start(bf16[128,768]{1,0:T(8,128)(2,1)S(1)} %get-tuple-element.64), channel_id=1, source_target_pairs={{0,8},{8,0},{16,24},{24,16},{1,9},{9,1},{17,25},{25,17},{2,10},{10... | collective-permute-start | bytes 589832 | tf_op jit(solution)/shard_map/ppermute | solution.py:363
  12.8 0.0 collective-permute-done.6.rest_1_
  12.8 1.5 %collective-permute-start.4 = (bf16[128,768]{1,0:T(8,128)(2,1)S(1)}, bf16[128,768]{1,0:T(8,128)(2,1)S(1)}, u32[]{:S(2)}, u32[]{:S(2)}) collective-permute-start(bf16[128,768]{1,0:T(8,128)(2,1)S(1)} %get-tuple-element.65), channel_id=1, source_target_pairs={{0,16},{8,24},{16,0},{24,8},{1,17},{9,25},{17,1},{25,9},{2,18},{10... | collective-permute-start | bytes 589832 | tf_op jit(solution)/shard_map/ppermute | solution.py:363
  14.3 0.1 collective-permute-done.7.rest_2_
  14.4 1.3 %collective-permute-start.5 = (bf16[128,768]{1,0:T(8,128)(2,1)S(1)}, bf16[128,768]{1,0:T(8,128)(2,1)S(1)}, u32[]{:S(2)}, u32[]{:S(2)}) collective-permute-start(bf16[128,768]{1,0:T(8,128)(2,1)S(1)} %get-tuple-element.66), channel_id=1, source_target_pairs={{0,24},{8,16},{16,8},{24,0},{1,25},{9,17},{17,9},{25,1},{2,26},{10... | collective-permute-start | bytes 589832 | tf_op jit(solution)/shard_map/ppermute | solution.py:363
  15.7 1.0 %collective-permute-done.8.rest_3_ = bf16[128,256]{1,0:T(8,128)(2,1)S(1)} collective-permute-done((bf16[128,256]{1,0:T(8,128)(2,1)S(1)}, bf16[128,256]{1,0:T(8,128)(2,1)S(1)}, u32[]{:S(2)}, u32[]{:S(2)}) %collective-permute-start.8) | collective-permute-done | bytes 65568 | tf_op jit(solution)/shard_map/ppermute | solution.py:363
  16.7 0.0 collective-permute-done.far
  16.7 1.0 %choose.2.rest_0_ = bf16[3,128,256]{2,1,0:T(8,128)(2,1)S(1)} custom-call(s32[22]{0:T(128)S(1)} %concatenate.3.ids, bf16[128,256]{1,0:T(8,128)(2,1)S(1)} %get-tuple-element.70.rest_0_, bf16[128,256]{1,0:T(8,128)(2,1)S(1)} %collective-permute-done.6.rest_1_, bf16[128,256]{1,0:T(8,128)(2,1)S(1)} %collective-permute-done.7.rest_2_, ...), custom_call_target="tpu_custom_call" | custom-call | flops 1 | bytes 1 | tf_op jit(solution)/shard_map/choose/pallas_call | solution.py:383
  17.7 0.4 collective-permute-start.9
  18.1 0.0 copy-done.1
  18.1 0.9 %split.1 = (bf16[48,2048]{1,0:T(8,128)(2,1)S(1)}, bf16[2,48,2048]{2,1,0:T(8,128)(2,1)S(1)}, bf16[2,48,2048]{2,1,0:T(8,128)(2,1)S(1)}) custom-call(s32[22]{0:T(128)S(1)} %concatenate.3.ids, bf16[1,48,6144]{2,1,0:T(8,128)(2,1)S(1)} %copy-done.1, bf16[1,48,1024]{2,1,0:T(8,128)(2,1)S(1)} %copy-done.2, bf16[1,48,1024]{2,1,0:T(8,128)(2,1)S(1)} %collective-permute-done.far), custom_call_target="tpu_custom_call" | custom-call | flops 1 | bytes 1 | tf_op jit(solution)/shard_map/split/pallas_call | solution.py:412
  19.0 1.6 %collective-permute-start.1 = (bf16[2,48,2048]{2,1,0:T(8,128)(2,1)S(1)}, bf16[2,48,2048]{2,1,0:T(8,128)(2,1)S(1)}, u32[]{:S(2)}, u32[]{:S(2)}) collective-permute-start(bf16[2,48,2048]{2,1,0:T(8,128)(2,1)S(1)} %get-tuple-element.61), channel_id=1, source_target_pairs={{0,2},{1,3},{2,0},{3,1},{4,6},{5,7},{6,4},{7,5},{8,10},{9,11},{10,... | collective-permute-start | bytes 1179656 | tf_op jit(solution)/shard_map/ppermute | solution.py:363
  20.6 0.0 collective-permute-done.3.rest_1_
  20.7 2.7 %collective-permute-done.4.rest_2_ = bf16[128,768]{1,0:T(8,128)(2,1)S(1)} collective-permute-done((bf16[128,768]{1,0:T(8,128)(2,1)S(1)}, bf16[128,768]{1,0:T(8,128)(2,1)S(1)}, u32[]{:S(2)}, u32[]{:S(2)}) %collective-permute-start.4) | collective-permute-done | bytes 196640 | tf_op jit(solution)/shard_map/ppermute | solution.py:363
  23.4 0.0 collective-permute-done.5.rest_3_
  23.4 2.9 %collective-permute-done.9.rest_2_.rest_3_ = bf16[3,128,256]{2,1,0:T(8,128)(2,1)S(1)} collective-permute-done((bf16[3,128,256]{2,1,0:T(8,128)(2,1)S(1)}, bf16[3,128,256]{2,1,0:T(8,128)(2,1)S(1)}, u32[]{:S(2)}, u32[]{:S(2)}) %collective-permute-start.9) | collective-permute-done | bytes 196640 | tf_op jit(solution)/shard_map/ppermute | solution.py:363
  26.3 0.9 %choose.3 = (bf16[2,3,128,256]{3,2,1,0:T(8,128)(2,1)S(1)}, bf16[2,3,128,256]{3,2,1,0:T(8,128)(2,1)S(1)}) custom-call(s32[22]{0:T(128)S(1)} %concatenate.3.ids, bf16[128,768]{1,0:T(8,128)(2,1)S(1)} %get-tuple-element.74.rest_0_, bf16[128,768]{1,0:T(8,128)(2,1)S(1)} %collective-permute-done.3.rest_1_, bf16[128,768]{1,0:T(8,128)(2,1)S(1)} %collective-permute-done.4.rest_2_, ...), custom_call_target="tpu_custom_call" | custom-call | flops 1 | bytes 1 | tf_op jit(solution)/shard_map/choose/pallas_call | solution.py:383
  27.2 0.1 collective-permute-start.10
  27.3 3.8 %collective-permute-done.1.got.rest_2_.rest_5_.rest_4_ = bf16[2,48,2048]{2,1,0:T(8,128)(2,1)S(1)} collective-permute-done((bf16[2,48,2048]{2,1,0:T(8,128)(2,1)S(1)}, bf16[2,48,2048]{2,1,0:T(8,128)(2,1)S(1)}, u32[]{:S(2)}, u32[]{:S(2)}) %collective-permute-start.1) | collective-permute-done | bytes 393248 | tf_op jit(solution)/shard_map/ppermute | solution.py:363
  31.1 0.1 collective-permute-start.2
  31.2 0.0 collective-permute-done.10.got
  31.3 0.8 collective-permute-start.12
  32.1 3.2 %collective-permute-start.13 = (bf16[3,128,256]{2,1,0:T(8,128)(2,1)S(1)}, bf16[3,128,256]{2,1,0:T(8,128)(2,1)S(1)}, u32[]{:S(2)}, u32[]{:S(2)}) collective-permute-start(bf16[3,128,256]{2,1,0:T(8,128)(2,1)S(1)} %get-tuple-element.88.rest_1_), channel_id=1, source_target_pairs={{0,4},{4,0},{1,5},{5,1},{2,6},{6,2},{3,7},{7,3},{8,12},{12,8},{9,1... | collective-permute-start | bytes 589832 | tf_op jit(solution)/shard_map/ppermute | solution.py:363
  35.2 0.7 collective-permute-start.11
  35.9 0.0 collective-permute-done.2.rest_1_.rest_4_.rest_3_
  35.9 0.6 sort.1.fresh
  36.5 5.2 %attend.3 = (f32[6,384,128]{2,1,0:T(8,128)S(1)}, f32[6,384,128]{2,1,0:T(8,128)S(1)}, f32[6,384,128]{2,1,0:T(8,128)S(1)}) custom-call(s32[22]{0:T(128)S(1)} %concatenate.3.ids, bf16[384,256]{1,0:T(8,128)(2,1)S(1)} %sort.1.fresh, bf16[3,128,256]{2,1,0:T(8,128)(2,1)S(1)} %choose.2.rest_0_, bf16[3,128,256]{2,1,0:T(8,128)(2,1)S(1)} %get-tuple-element.88.rest_1_, ...), custom_call_target="tpu_custom_call" | custom-call | flops 1 | bytes 1 | tf_op jit(solution)/shard_map/attend/pallas_call | solution.py:227
  41.7 3.7 %collective-permute-done.13.rest_4_.rest_1_ = bf16[3,128,256]{2,1,0:T(8,128)(2,1)S(1)} collective-permute-done((bf16[3,128,256]{2,1,0:T(8,128)(2,1)S(1)}, bf16[3,128,256]{2,1,0:T(8,128)(2,1)S(1)}, u32[]{:S(2)}, u32[]{:S(2)}) %collective-permute-start.13) | collective-permute-done | bytes 196640 | tf_op jit(solution)/shard_map/ppermute | solution.py:363
  45.4 1.7 %collective-permute-done.12.rest_2_.rest_0_ = bf16[2,3,128,256]{3,2,1,0:T(8,128)(2,1)S(1)} collective-permute-done((bf16[2,3,128,256]{3,2,1,0:T(8,128)(2,1)S(1)}, bf16[2,3,128,256]{3,2,1,0:T(8,128)(2,1)S(1)}, u32[]{:S(2)}, u32[]{:S(2)}) %collective-permute-start.12) | collective-permute-done | bytes 393248 | tf_op jit(solution)/shard_map/ppermute | solution.py:363
  47.0 1.3 %collective-permute-start.14 = (bf16[2,3,128,256]{3,2,1,0:T(8,128)(2,1)S(1)}, bf16[2,3,128,256]{3,2,1,0:T(8,128)(2,1)S(1)}, u32[]{:S(2)}, u32[]{:S(2)}) collective-permute-start(bf16[2,3,128,256]{3,2,1,0:T(8,128)(2,1)S(1)} %collective-permute-done.12.rest_2_.rest_0_), channel_id=1, source_target_pairs={{2,6},{3,7},{4,0},{5,1},{10,14},{11,15},{12,8},{13,9},{18,22},{19,... | collective-permute-start | bytes 1179656 | tf_op jit(solution)/shard_map/ppermute | solution.py:493
  48.3 0.8 runs.2
  49.2 0.7 collective-permute-start.15
  49.8 3.2 %collective-permute-start.16 = (bf16[6,3,16,256]{3,2,1,0:T(8,128)(2,1)S(1)}, bf16[6,3,16,256]{3,2,1,0:T(8,128)(2,1)S(1)}, u32[]{:S(2)}, u32[]{:S(2)}) collective-permute-start(bf16[6,3,16,256]{3,2,1,0:T(8,128)(2,1)S(1)} %get-tuple-element.93), channel_id=1, source_target_pairs={{0,1},{1,24},{2,11},{3,18},{4,5},{5,28},{6,15},{7,22},{8,9},{9,16}... | collective-permute-start | bytes 442376 | tf_op jit(solution)/shard_map/ppermute | solution.py:475
  53.0 3.9 %collective-permute-start.17 = (bf16[6,3,16,256]{3,2,1,0:T(8,128)(2,1)S(1)}, bf16[6,3,16,256]{3,2,1,0:T(8,128)(2,1)S(1)}, u32[]{:S(2)}, u32[]{:S(2)}) collective-permute-start(bf16[6,3,16,256]{3,2,1,0:T(8,128)(2,1)S(1)} %get-tuple-element.94), channel_id=1, source_target_pairs={{0,2},{1,27},{2,8},{3,17},{4,6},{5,31},{6,12},{7,21},{8,10},{9,19}... | collective-permute-start | bytes 442376 | tf_op jit(solution)/shard_map/ppermute | solution.py:475
  57.0 0.0 collective-permute-done.11.rest_0_
  57.0 0.7 collective-permute-start.18
  57.6 5.4 %attend.4 = (f32[6,384,128]{2,1,0:T(8,128)S(1)}, f32[6,384,128]{2,1,0:T(8,128)S(1)}, f32[6,384,128]{2,1,0:T(8,128)S(1)}) custom-call(s32[22]{0:T(128)S(1)} %concatenate.3.ids, bf16[384,256]{1,0:T(8,128)(2,1)S(1)} %sort.1.fresh, bf16[2,3,128,256]{3,2,1,0:T(8,128)(2,1)S(1)} %collective-permute-done.12.rest_2_.rest_0_, ...), custom_call_target="tpu_custom_call" | custom-call | flops 1 | bytes 1 | tf_op jit(solution)/shard_map/attend/pallas_call | solution.py:227
  63.0 0.0 collective-permute-done.14.rest_1_
  63.0 3.6 %attend.5 = (bf16[48,1536]{1,0:T(8,128)(2,1)S(1)}, bf16[2,48,1536]{2,1,0:T(8,128)(2,1)S(1)}, bf16[2,48,1536]{2,1,0:T(8,128)(2,1)S(1)}) custom-call(s32[22]{0:T(128)S(1)} %concatenate.3.ids, bf16[384,256]{1,0:T(8,128)(2,1)S(1)} %sort.1.fresh, bf16[2,3,128,256]{3,2,1,0:T(8,128)(2,1)S(1)} %collective-permute-done.11.rest_0_, ...), custom_call_target="tpu_custom_call" | custom-call | flops 1 | bytes 1 | tf_op jit(solution)/shard_map/attend/pallas_call | solution.py:227
  66.6 0.0 collective-permute-done.15.rest_3_
  66.6 0.0 collective-permute-done.16.rest_4_
  66.6 0.0 collective-permute-done.17.rest_5_
  66.6 1.5 %collective-permute-done.18.rest_6_ = bf16[6,3,16,256]{3,2,1,0:T(8,128)(2,1)S(1)} collective-permute-done((bf16[6,3,16,256]{3,2,1,0:T(8,128)(2,1)S(1)}, bf16[6,3,16,256]{3,2,1,0:T(8,128)(2,1)S(1)}, u32[]{:S(2)}, u32[]{:S(2)}) %collective-permute-start.18) | collective-permute-done | bytes 147488 | tf_op jit(solution)/shard_map/ppermute | solution.py:475
  68.1 0.3 collective-permute-start.19
  68.4 1.3 %collective-permute-done.19.got = bf16[2,48,1536]{2,1,0:T(8,128)(2,1)S(1)} collective-permute-done((bf16[2,48,1536]{2,1,0:T(8,128)(2,1)S(1)}, bf16[2,48,1536]{2,1,0:T(8,128)(2,1)S(1)}, u32[]{:S(2)}, u32[]{:S(2)}) %collective-permute-start.19) | collective-permute-done | bytes 294944 | tf_op jit(solution)/shard_map/ppermute | solution.py:363
  69.7 1.8 %collective-permute-start.20 = (bf16[2,48,1536]{2,1,0:T(8,128)(2,1)S(1)}, bf16[2,48,1536]{2,1,0:T(8,128)(2,1)S(1)}, u32[]{:S(2)}, u32[]{:S(2)}) collective-permute-start(bf16[2,48,1536]{2,1,0:T(8,128)(2,1)S(1)} %get-tuple-element.107), channel_id=1, source_target_pairs={{0,2},{1,3},{2,0},{3,1},{4,6},{5,7},{6,4},{7,5},{8,10},{9,11},{10,... | collective-permute-start | bytes 884744 | tf_op jit(solution)/shard_map/ppermute | solution.py:363
  71.4 0.7 runs.3
  72.1 0.7 collective-permute-start.21
  72.8 1.9 %collective-permute-start.22 = (bf16[2,3,16,256]{3,2,1,0:T(8,128)(2,1)S(1)}, bf16[2,3,16,256]{3,2,1,0:T(8,128)(2,1)S(1)}, u32[]{:S(2)}, u32[]{:S(2)}) collective-permute-start(bf16[2,3,16,256]{3,2,1,0:T(8,128)(2,1)S(1)} %get-tuple-element.111), channel_id=1, source_target_pairs={{0,1},{1,24},{2,11},{3,18},{4,5},{5,28},{6,15},{7,22},{8,9},{9,16}... | collective-permute-start | bytes 147464 | tf_op jit(solution)/shard_map/ppermute | solution.py:475
  74.7 1.4 %collective-permute-start.23 = (bf16[2,3,16,256]{3,2,1,0:T(8,128)(2,1)S(1)}, bf16[2,3,16,256]{3,2,1,0:T(8,128)(2,1)S(1)}, u32[]{:S(2)}, u32[]{:S(2)}) collective-permute-start(bf16[2,3,16,256]{3,2,1,0:T(8,128)(2,1)S(1)} %get-tuple-element.112), channel_id=1, source_target_pairs={{0,2},{1,27},{2,8},{3,17},{4,6},{5,31},{6,12},{7,21},{8,10},{9,19}... | collective-permute-start | bytes 147464 | tf_op jit(solution)/shard_map/ppermute | solution.py:475
  76.1 0.7 collective-permute-start.24
  76.8 0.0 collective-permute-done.21.rest_7_
  76.8 1.6 %collective-permute-done.22.rest_8_ = bf16[2,3,16,256]{3,2,1,0:T(8,128)(2,1)S(1)} collective-permute-done((bf16[2,3,16,256]{3,2,1,0:T(8,128)(2,1)S(1)}, bf16[2,3,16,256]{3,2,1,0:T(8,128)(2,1)S(1)}, u32[]{:S(2)}, u32[]{:S(2)}) %collective-permute-start.22) | collective-permute-done | bytes 49184 | tf_op jit(solution)/shard_map/ppermute | solution.py:475
  78.4 2.9 %collective-permute-done.23.rest_9_ = bf16[2,3,16,256]{3,2,1,0:T(8,128)(2,1)S(1)} collective-permute-done((bf16[2,3,16,256]{3,2,1,0:T(8,128)(2,1)S(1)}, bf16[2,3,16,256]{3,2,1,0:T(8,128)(2,1)S(1)}, u32[]{:S(2)}, u32[]{:S(2)}) %collective-permute-start.23) | collective-permute-done | bytes 49184 | tf_op jit(solution)/shard_map/ppermute | solution.py:475
  81.3 0.0 collective-permute-done.24.rest_10_
  81.3 0.0 collective-permute-done.20.rest_2_
  81.3 2.0 %finish.1 = (bf16[1,48,6144]{2,1,0:T(8,128)(2,1)}, bf16[1,1,4,24,4096]{4,3,2,1,0:T(8,128)(2,1)}) custom-call(s32[22]{0:T(128)S(1)} %concatenate.3.ids, bf16[48,1536]{1,0:T(8,128)(2,1)S(1)} %get-tuple-element.102.rest_0_, bf16[48,1536]{1,0:T(8,128)(2,1)S(1)} %get-tuple-element.106.rest_1_, bf16[2,48,1536]{2,1,0:T(8,128)(2,1)S(1)} %collective-permute-done.20.rest_2_, ...), custom_call_target="tpu_custom_call" | custom-call | flops 1 | bytes 1 | tf_op jit(solution)/shard_map/finish/pallas_call | solution.py:508
  (7 shorter events, 0.1 us)
Async XLA Ops:
  1.4 1.2 %copy-start = (bf16[4,128,1024]{2,1,0:T(8,128)(2,1)S(1)}, bf16[4,128,1024]{2,1,0:T(8,128)(2,1)}, u32[]{:S(2)}) copy-start(bf16[4,128,1024]{2,1,0:T(8,128)(2,1)} %pool_kv.1) | copy-start | bytes 3145732
  2.6 15.5 %copy-start.1 = (bf16[1,48,6144]{2,1,0:T(8,128)(2,1)S(1)}, bf16[1,48,6144]{2,1,0:T(8,128)(2,1)}, u32[]{:S(2)}) copy-start(bf16[1,48,6144]{2,1,0:T(8,128)(2,1)} %fresh_q.1) | copy-start | bytes 1769476
  2.6 15.5 %copy-start.2 = (bf16[1,48,1024]{2,1,0:T(8,128)(2,1)S(1)}, bf16[1,48,1024]{2,1,0:T(8,128)(2,1)}, u32[]{:S(2)}) copy-start(bf16[1,48,1024]{2,1,0:T(8,128)(2,1)} %near.1) | copy-start | bytes 294916
  3.7 13.1 %collective-permute-start = (bf16[1,48,1024]{2,1,0:T(8,128)(2,1)}, bf16[1,48,1024]{2,1,0:T(8,128)(2,1)S(1)}, u32[]{:S(2)}, u32[]{:S(2)}) collective-permute-start(bf16[1,48,1024]{2,1,0:T(8,128)(2,1)} %near.1), channel_id=1, source_target_pairs={{0,4},{4,0},{1,5},{5,1},{2,6},{6,2},{3,7},{7,3},{8,12},{12,8},{9,1... | collective-permute-start | bytes 294920 | tf_op jit(solution)/shard_map/ppermute | solution.py:363
  7.8 5.0 %collective-permute-start.6 = (bf16[128,256]{1,0:T(8,128)(2,1)S(1)}, bf16[128,256]{1,0:T(8,128)(2,1)S(1)}, u32[]{:S(2)}, u32[]{:S(2)}) collective-permute-start(bf16[128,256]{1,0:T(8,128)(2,1)S(1)} %get-tuple-element.67), channel_id=1, source_target_pairs={{0,8},{8,0},{16,24},{24,16},{1,9},{9,1},{17,25},{25,17},{2,10},{10... | collective-permute-start | bytes 196616 | tf_op jit(solution)/shard_map/ppermute | solution.py:363
  9.3 5.1 %collective-permute-start.7 = (bf16[128,256]{1,0:T(8,128)(2,1)S(1)}, bf16[128,256]{1,0:T(8,128)(2,1)S(1)}, u32[]{:S(2)}, u32[]{:S(2)}) collective-permute-start(bf16[128,256]{1,0:T(8,128)(2,1)S(1)} %get-tuple-element.68), channel_id=1, source_target_pairs={{0,16},{8,24},{16,0},{24,8},{1,17},{9,25},{17,1},{25,9},{2,18},{10... | collective-permute-start | bytes 196616 | tf_op jit(solution)/shard_map/ppermute | solution.py:363
  10.8 5.9 %collective-permute-start.8 = (bf16[128,256]{1,0:T(8,128)(2,1)S(1)}, bf16[128,256]{1,0:T(8,128)(2,1)S(1)}, u32[]{:S(2)}, u32[]{:S(2)}) collective-permute-start(bf16[128,256]{1,0:T(8,128)(2,1)S(1)} %get-tuple-element.69), channel_id=1, source_target_pairs={{0,24},{8,16},{16,8},{24,0},{1,25},{9,17},{17,9},{25,1},{2,26},{10... | collective-permute-start | bytes 196616 | tf_op jit(solution)/shard_map/ppermute | solution.py:363
  11.3 9.4 %collective-permute-start.3 = (bf16[128,768]{1,0:T(8,128)(2,1)S(1)}, bf16[128,768]{1,0:T(8,128)(2,1)S(1)}, u32[]{:S(2)}, u32[]{:S(2)}) collective-permute-start(bf16[128,768]{1,0:T(8,128)(2,1)S(1)} %get-tuple-element.64), channel_id=1, source_target_pairs={{0,8},{8,0},{16,24},{24,16},{1,9},{9,1},{17,25},{25,17},{2,10},{10... | collective-permute-start | bytes 589832 | tf_op jit(solution)/shard_map/ppermute | solution.py:363
  12.8 10.6 %collective-permute-start.4 = (bf16[128,768]{1,0:T(8,128)(2,1)S(1)}, bf16[128,768]{1,0:T(8,128)(2,1)S(1)}, u32[]{:S(2)}, u32[]{:S(2)}) collective-permute-start(bf16[128,768]{1,0:T(8,128)(2,1)S(1)} %get-tuple-element.65), channel_id=1, source_target_pairs={{0,16},{8,24},{16,0},{24,8},{1,17},{9,25},{17,1},{25,9},{2,18},{10... | collective-permute-start | bytes 589832 | tf_op jit(solution)/shard_map/ppermute | solution.py:363
  14.4 9.0 %collective-permute-start.5 = (bf16[128,768]{1,0:T(8,128)(2,1)S(1)}, bf16[128,768]{1,0:T(8,128)(2,1)S(1)}, u32[]{:S(2)}, u32[]{:S(2)}) collective-permute-start(bf16[128,768]{1,0:T(8,128)(2,1)S(1)} %get-tuple-element.66), channel_id=1, source_target_pairs={{0,24},{8,16},{16,8},{24,0},{1,25},{9,17},{17,9},{25,1},{2,26},{10... | collective-permute-start | bytes 589832 | tf_op jit(solution)/shard_map/ppermute | solution.py:363
  17.7 8.6 %collective-permute-start.9 = (bf16[3,128,256]{2,1,0:T(8,128)(2,1)S(1)}, bf16[3,128,256]{2,1,0:T(8,128)(2,1)S(1)}, u32[]{:S(2)}, u32[]{:S(2)}) collective-permute-start(bf16[3,128,256]{2,1,0:T(8,128)(2,1)S(1)} %choose.2.rest_0_), channel_id=1, source_target_pairs={{0,4},{4,0},{1,5},{5,1},{2,6},{6,2},{3,7},{7,3},{8,12},{12,8},{9,1... | collective-permute-start | bytes 589832 | tf_op jit(solution)/shard_map/ppermute | solution.py:363
  19.0 12.1 %collective-permute-start.1 = (bf16[2,48,2048]{2,1,0:T(8,128)(2,1)S(1)}, bf16[2,48,2048]{2,1,0:T(8,128)(2,1)S(1)}, u32[]{:S(2)}, u32[]{:S(2)}) collective-permute-start(bf16[2,48,2048]{2,1,0:T(8,128)(2,1)S(1)} %get-tuple-element.61), channel_id=1, source_target_pairs={{0,2},{1,3},{2,0},{3,1},{4,6},{5,7},{6,4},{7,5},{8,10},{9,11},{10,... | collective-permute-start | bytes 1179656 | tf_op jit(solution)/shard_map/ppermute | solution.py:363
  27.2 4.0 %collective-permute-start.10 = (bf16[2,3,128,256]{3,2,1,0:T(8,128)(2,1)S(1)}, bf16[2,3,128,256]{3,2,1,0:T(8,128)(2,1)S(1)}, u32[]{:S(2)}, u32[]{:S(2)}) collective-permute-start(bf16[2,3,128,256]{3,2,1,0:T(8,128)(2,1)S(1)} %get-tuple-element.78), channel_id=1, source_target_pairs={{0,1},{1,0},{2,3},{3,2},{4,5},{5,4},{6,7},{7,6},{8,9},{9,8},{10,11... | collective-permute-start | bytes 1179656 | tf_op jit(solution)/shard_map/ppermute | solution.py:363
  31.1 4.8 %collective-permute-start.2 = (bf16[2,48,2048]{2,1,0:T(8,128)(2,1)S(1)}, bf16[2,48,2048]{2,1,0:T(8,128)(2,1)S(1)}, u32[]{:S(2)}, u32[]{:S(2)}) collective-permute-start(bf16[2,48,2048]{2,1,0:T(8,128)(2,1)S(1)} %follow.1), channel_id=1, source_target_pairs={{0,1},{1,0},{2,3},{3,2},{4,5},{5,4},{6,7},{7,6},{8,9},{9,8},{10,11... | collective-permute-start | bytes 1179656 | tf_op jit(solution)/shard_map/ppermute | solution.py:363
  31.3 15.8 %collective-permute-start.12 = (bf16[2,3,128,256]{3,2,1,0:T(8,128)(2,1)S(1)}, bf16[2,3,128,256]{3,2,1,0:T(8,128)(2,1)S(1)}, u32[]{:S(2)}, u32[]{:S(2)}) collective-permute-start(bf16[2,3,128,256]{3,2,1,0:T(8,128)(2,1)S(1)} %get-tuple-element.81), channel_id=1, source_target_pairs={{0,2},{1,3},{2,0},{3,1},{4,6},{5,7},{6,4},{7,5},{8,10},{9,11},{10,... | collective-permute-start | bytes 1179656 | tf_op jit(solution)/shard_map/ppermute | solution.py:363
  32.1 13.3 %collective-permute-start.13 = (bf16[3,128,256]{2,1,0:T(8,128)(2,1)S(1)}, bf16[3,128,256]{2,1,0:T(8,128)(2,1)S(1)}, u32[]{:S(2)}, u32[]{:S(2)}) collective-permute-start(bf16[3,128,256]{2,1,0:T(8,128)(2,1)S(1)} %get-tuple-element.88.rest_1_), channel_id=1, source_target_pairs={{0,4},{4,0},{1,5},{5,1},{2,6},{6,2},{3,7},{7,3},{8,12},{12,8},{9,1... | collective-permute-start | bytes 589832 | tf_op jit(solution)/shard_map/ppermute | solution.py:363
  35.2 21.7 %collective-permute-start.11 = (bf16[2,3,128,256]{3,2,1,0:T(8,128)(2,1)S(1)}, bf16[2,3,128,256]{3,2,1,0:T(8,128)(2,1)S(1)}, u32[]{:S(2)}, u32[]{:S(2)}) collective-permute-start(bf16[2,3,128,256]{3,2,1,0:T(8,128)(2,1)S(1)} %get-tuple-element.81), channel_id=1, source_target_pairs={{2,4},{3,5},{4,2},{5,3},{10,12},{11,13},{12,10},{13,11},{18,20},{1... | collective-permute-start | bytes 1179656 | tf_op jit(solution)/shard_map/ppermute | solution.py:492
  47.0 15.9 %collective-permute-start.14 = (bf16[2,3,128,256]{3,2,1,0:T(8,128)(2,1)S(1)}, bf16[2,3,128,256]{3,2,1,0:T(8,128)(2,1)S(1)}, u32[]{:S(2)}, u32[]{:S(2)}) collective-permute-start(bf16[2,3,128,256]{3,2,1,0:T(8,128)(2,1)S(1)} %collective-permute-done.12.rest_2_.rest_0_), channel_id=1, source_target_pairs={{2,6},{3,7},{4,0},{5,1},{10,14},{11,15},{12,8},{13,9},{18,22},{19,... | collective-permute-start | bytes 1179656 | tf_op jit(solution)/shard_map/ppermute | solution.py:493
  49.2 17.4 %collective-permute-start.15 = (bf16[6,3,16,256]{3,2,1,0:T(8,128)(2,1)S(1)}, bf16[6,3,16,256]{3,2,1,0:T(8,128)(2,1)S(1)}, u32[]{:S(2)}, u32[]{:S(2)}) collective-permute-start(bf16[6,3,16,256]{3,2,1,0:T(8,128)(2,1)S(1)} %get-tuple-element.92), channel_id=1, source_target_pairs={{0,0},{1,25},{2,10},{3,19},{4,4},{5,29},{6,14},{7,23},{8,8},{9,17}... | collective-permute-start | bytes 442376 | tf_op jit(solution)/shard_map/ppermute | solution.py:475
  49.8 16.8 %collective-permute-start.16 = (bf16[6,3,16,256]{3,2,1,0:T(8,128)(2,1)S(1)}, bf16[6,3,16,256]{3,2,1,0:T(8,128)(2,1)S(1)}, u32[]{:S(2)}, u32[]{:S(2)}) collective-permute-start(bf16[6,3,16,256]{3,2,1,0:T(8,128)(2,1)S(1)} %get-tuple-element.93), channel_id=1, source_target_pairs={{0,1},{1,24},{2,11},{3,18},{4,5},{5,28},{6,15},{7,22},{8,9},{9,16}... | collective-permute-start | bytes 442376 | tf_op jit(solution)/shard_map/ppermute | solution.py:475
  53.0 13.6 %collective-permute-start.17 = (bf16[6,3,16,256]{3,2,1,0:T(8,128)(2,1)S(1)}, bf16[6,3,16,256]{3,2,1,0:T(8,128)(2,1)S(1)}, u32[]{:S(2)}, u32[]{:S(2)}) collective-permute-start(bf16[6,3,16,256]{3,2,1,0:T(8,128)(2,1)S(1)} %get-tuple-element.94), channel_id=1, source_target_pairs={{0,2},{1,27},{2,8},{3,17},{4,6},{5,31},{6,12},{7,21},{8,10},{9,19}... | collective-permute-start | bytes 442376 | tf_op jit(solution)/shard_map/ppermute | solution.py:475
  57.0 11.1 %collective-permute-start.18 = (bf16[6,3,16,256]{3,2,1,0:T(8,128)(2,1)S(1)}, bf16[6,3,16,256]{3,2,1,0:T(8,128)(2,1)S(1)}, u32[]{:S(2)}, u32[]{:S(2)}) collective-permute-start(bf16[6,3,16,256]{3,2,1,0:T(8,128)(2,1)S(1)} %get-tuple-element.95), channel_id=1, source_target_pairs={{0,3},{1,26},{2,9},{3,16},{4,7},{5,30},{6,13},{7,20},{8,11},{9,18}... | collective-permute-start | bytes 442376 | tf_op jit(solution)/shard_map/ppermute | solution.py:475
  68.1 1.6 %collective-permute-start.19 = (bf16[2,48,1536]{2,1,0:T(8,128)(2,1)S(1)}, bf16[2,48,1536]{2,1,0:T(8,128)(2,1)S(1)}, u32[]{:S(2)}, u32[]{:S(2)}) collective-permute-start(bf16[2,48,1536]{2,1,0:T(8,128)(2,1)S(1)} %get-tuple-element.104), channel_id=1, source_target_pairs={{0,1},{1,0},{2,3},{3,2},{4,5},{5,4},{6,7},{7,6},{8,9},{9,8},{10,11... | collective-permute-start | bytes 884744 | tf_op jit(solution)/shard_map/ppermute | solution.py:363
  69.7 11.6 %collective-permute-start.20 = (bf16[2,48,1536]{2,1,0:T(8,128)(2,1)S(1)}, bf16[2,48,1536]{2,1,0:T(8,128)(2,1)S(1)}, u32[]{:S(2)}, u32[]{:S(2)}) collective-permute-start(bf16[2,48,1536]{2,1,0:T(8,128)(2,1)S(1)} %get-tuple-element.107), channel_id=1, source_target_pairs={{0,2},{1,3},{2,0},{3,1},{4,6},{5,7},{6,4},{7,5},{8,10},{9,11},{10,... | collective-permute-start | bytes 884744 | tf_op jit(solution)/shard_map/ppermute | solution.py:363
  72.1 4.7 %collective-permute-start.21 = (bf16[2,3,16,256]{3,2,1,0:T(8,128)(2,1)S(1)}, bf16[2,3,16,256]{3,2,1,0:T(8,128)(2,1)S(1)}, u32[]{:S(2)}, u32[]{:S(2)}) collective-permute-start(bf16[2,3,16,256]{3,2,1,0:T(8,128)(2,1)S(1)} %get-tuple-element.110), channel_id=1, source_target_pairs={{0,0},{1,25},{2,10},{3,19},{4,4},{5,29},{6,14},{7,23},{8,8},{9,17}... | collective-permute-start | bytes 147464 | tf_op jit(solution)/shard_map/ppermute | solution.py:475
  72.8 5.7 %collective-permute-start.22 = (bf16[2,3,16,256]{3,2,1,0:T(8,128)(2,1)S(1)}, bf16[2,3,16,256]{3,2,1,0:T(8,128)(2,1)S(1)}, u32[]{:S(2)}, u32[]{:S(2)}) collective-permute-start(bf16[2,3,16,256]{3,2,1,0:T(8,128)(2,1)S(1)} %get-tuple-element.111), channel_id=1, source_target_pairs={{0,1},{1,24},{2,11},{3,18},{4,5},{5,28},{6,15},{7,22},{8,9},{9,16}... | collective-permute-start | bytes 147464 | tf_op jit(solution)/shard_map/ppermute | solution.py:475
  74.7 6.6 %collective-permute-start.23 = (bf16[2,3,16,256]{3,2,1,0:T(8,128)(2,1)S(1)}, bf16[2,3,16,256]{3,2,1,0:T(8,128)(2,1)S(1)}, u32[]{:S(2)}, u32[]{:S(2)}) collective-permute-start(bf16[2,3,16,256]{3,2,1,0:T(8,128)(2,1)S(1)} %get-tuple-element.112), channel_id=1, source_target_pairs={{0,2},{1,27},{2,8},{3,17},{4,6},{5,31},{6,12},{7,21},{8,10},{9,19}... | collective-permute-start | bytes 147464 | tf_op jit(solution)/shard_map/ppermute | solution.py:475
  76.1 5.2 %collective-permute-start.24 = (bf16[2,3,16,256]{3,2,1,0:T(8,128)(2,1)S(1)}, bf16[2,3,16,256]{3,2,1,0:T(8,128)(2,1)S(1)}, u32[]{:S(2)}, u32[]{:S(2)}) collective-permute-start(bf16[2,3,16,256]{3,2,1,0:T(8,128)(2,1)S(1)} %get-tuple-element.113), channel_id=1, source_target_pairs={{0,3},{1,26},{2,9},{3,16},{4,7},{5,30},{6,13},{7,20},{8,11},{9,18}... | collective-permute-start | bytes 147464 | tf_op jit(solution)/shard_map/ppermute | solution.py:475

commit v6 on v5

--- a/solution.py
+++ b/solution.py
@@ -259,7 +259,7 @@
     return at // KV_HEADS * KV_HEADS + ((head ^ k) & (whole - 1))
 
 
-def runs_kernel(ks, seq_count, count_in, views, at_chosen, ids, fresh, *rest):
+def runs_kernel(ks, turned, seq_count, count_in, views, at_chosen, ids, fresh, *rest):
     messages, outs = [look(rest[:count_in], v) for v in views], rest[count_in:]
     spans, block, _ = messages[0][0].shape
     run = outs[0].shape[2]
@@ -274,7 +274,7 @@
                 rows = source(pl.ds(pl.multiple_of(first + offset, slab), slab)).astype(F32)
                 out[slot, j] = rows[m * run : (m + 1) * run].astype(BF16)
             else:
-                row = first + offset + (ids[2] ^ m) * run
+                row = first + offset + (ids[2] ^ m ^ turned) * run
                 out[slot, j] = source(pl.ds(pl.multiple_of(row, run), run))
 
     for at, k in enumerate(ks):
@@ -288,12 +288,12 @@
                 put(k, picked // seq_count, lambda rows: fresh[rows], i * block)
 
 
-def cut_runs(ks, seq_count, run, heads, at_chosen, ids, fresh, messages):
+def cut_runs(ks, turned, seq_count, run, heads, at_chosen, ids, fresh, messages):
     arrays, views = arrays_of([view for message in messages for view in message])
     views = group_views(views, messages)
     spans, _, kv_width = messages[0][0][0].shape[-3:]
     return pl.pallas_call(
-        functools.partial(runs_kernel, ks, seq_count, len(arrays), views, at_chosen),
+        functools.partial(runs_kernel, ks, turned, seq_count, len(arrays), views, at_chosen),
         out_shape=[jax.ShapeDtypeStruct((len(ks), spans, run, kv_width), BF16)] * heads,
         in_specs=[SMEM, VMEM] + [VMEM] * len(arrays),
         out_specs=[VMEM] * heads,
@@ -456,24 +456,24 @@
             name="sort",
         )(ids, *arrays)
 
-    def to_decode(ks, *dep):
+    def to_decode(ks, turned, *dep):
         parts = [messages[k] for k in ks]
         arrays, views = arrays_of([view for message in parts for view in message])
         arrays = after(arrays, dep)
         parts = group_views([(arrays[i], index) for i, index in views], parts)
-        cut = cut_runs(ks, seq_count, run, heads, at_chosen, ids, fresh, parts)
+        cut = cut_runs(ks, turned, seq_count, run, heads, at_chosen, ids, fresh, parts)
         if run % 16:
-            cut = [lax.dynamic_index_in_dim(jnp.stack(cut), head ^ k, axis=0, keepdims=False) for k in range(heads)]
+            cut = [lax.dynamic_index_in_dim(jnp.stack(cut), head ^ k ^ turned, axis=0, keepdims=False) for k in range(heads)]
         went = [None] * heads
         for k in reversed(range(heads)):
             perm = [
-                ((r * quads + a) * heads + i, ((r ^ turn(i)) * quads + a) * heads + (i ^ k))
+                ((r * quads + a) * heads + i, ((r ^ turn(i)) * quads + a) * heads + (i ^ k ^ turned))
                 for r in range(pool_count)
                 for a in range(quads)
                 for i in range(heads)
             ]
             went[k] = lax.ppermute(cut[k], ("pool", "quad", "head"), perm)
-        return went, cut
+        return [went[k ^ turned] for k in range(heads)], cut
 
     def work(ks, state, last=False):
         return attend(ks, state, last, seq_count, rows, group, at_chosen, ids, q, fresh, [messages[k] for k in ks])
@@ -495,13 +495,13 @@
         soons.append(soon)
     groups = [list(range(seq_count - 2)), [seq_count - 2, seq_count - 1]]
     second = [k for k in groups[0] if k not in first]
-    landed = [to_decode(groups[0], state)]
+    landed = [to_decode(groups[0], 0, state)]
     state = after(state, soons, landed[0][1])
     for at in range(0, len(second), 6):
         state = work(second[at : at + 6], state)
     keep, give, send = work(groups[-1], state, True)
     beside, send = place(swap(after(give, landed[0][0]), "head", heads, 1), send)
-    landed.append(to_decode(groups[1], keep))
+    landed.append(to_decode(groups[1], heads - 1, keep))
     chip = swap(send, "head", heads, 2)
     arrays, views = arrays_of([(keep, None), (beside, None), (chip, 0), (chip, 1)])
     runs = [part for went, _ in landed for part in went]

time: 83.6 us -> 83.6 us (level)
  no operation moved by 1% of the time
where the time goes in v6:
time: 83.6 us; the launch traced here: 83.4 us
  starting transfers between devices  35.2 us (42%)
  waiting for transfers between devices  23.3 us (28%)
  Pallas kernels  21.9 us (26%)
  local copies, waits for them, and re-layouts  2 us (2%)
  between operations  1.01 us (1%)
    ppermute x15, starting transfers between devices, swap(): return lax.ppermute(value, axes, [(i, i ^ k) for i in range(count)])  20.1 us
    ppermute x15, waiting for transfers between devices, swap(): return lax.ppermute(value, axes, [(i, i ^ k) for i in range(count)])  17.3 us
    pallas_call x3, Pallas kernels, attend(): pl.pallas_call(functools.partial(attend_kernel, ks, state is None, last,...  14.1 us
    ppermute x8, starting transfers between devices, to_decode(): went[k] = lax.ppermute(cut[k], ('pool', 'quad', 'head'), perm)  13.1 us
    ppermute x8, waiting for transfers between devices, to_decode(): went[k] = lax.ppermute(cut[k], ('pool', 'quad', 'head'), perm)  5.97 us
    pallas_call x1, Pallas kernels, shards(): pl.pallas_call(functools.partial(finish_kernel, seq_count, views, len(arr...  1.96 us
    pallas_call x2, Pallas kernels, from_pool(): pl.pallas_call(functools.partial(choose_kernel, slots, pool_count), out_s...  1.84 us
  transfers between devices with their start and end apart: 25, of which 11 were waited for; matrix products, arithmetic and copies ran while one was open for 0% of the time, Pallas kernels for 23%

profile of v6, /device:TPU:0, one launch (start us, length us, event | category | flops | bytes accessed | tf_op | source)
XLA Modules:
  0.0 83.4 jit_solution(547708498757256080)
XLA Ops:
  0.6 0.8 concatenate.3.ids
  1.4 1.2 %copy-done = bf16[4,128,1024]{2,1,0:T(8,128)(2,1)S(1)} copy-done((bf16[4,128,1024]{2,1,0:T(8,128)(2,1)S(1)}, bf16[4,128,1024]{2,1,0:T(8,128)(2,1)}, u32[]{:S(2)}) %copy-start) | copy-done | bytes 1048600
  2.6 1.1 %pack.1 = (bf16[128,256]{1,0:T(8,128)(2,1)S(1)}, bf16[128,256]{1,0:T(8,128)(2,1)S(1)}, bf16[128,256]{1,0:T(8,128)(2,1)S(1)}, bf16[128,256]{1,0:T(8,128)(2,1)S(1)...) custom-call(s32[22]{0:T(128)S(1)} %concatenate.3.ids, ...), custom_call_target="tpu_custom_call" | custom-call | flops 1 | bytes 1 | tf_op jit(solution)/shard_map/pack/pallas_call | solution.py:366
  3.7 4.1 %collective-permute-start = (bf16[1,48,1024]{2,1,0:T(8,128)(2,1)}, bf16[1,48,1024]{2,1,0:T(8,128)(2,1)S(1)}, u32[]{:S(2)}, u32[]{:S(2)}) collective-permute-start(bf16[1,48,1024]{2,1,0:T(8,128)(2,1)} %near.1), channel_id=1, source_target_pairs={{0,4},{4,0},{1,5},{5,1},{2,6},{6,2},{3,7},{7,3},{8,12},{12,8},{9,1... | collective-permute-start | bytes 294920 | tf_op jit(solution)/shard_map/ppermute | solution.py:363
  7.8 1.5 %collective-permute-start.6 = (bf16[128,256]{1,0:T(8,128)(2,1)S(1)}, bf16[128,256]{1,0:T(8,128)(2,1)S(1)}, u32[]{:S(2)}, u32[]{:S(2)}) collective-permute-start(bf16[128,256]{1,0:T(8,128)(2,1)S(1)} %get-tuple-element.67), channel_id=1, source_target_pairs={{0,8},{8,0},{16,24},{24,16},{1,9},{9,1},{17,25},{25,17},{2,10},{10... | collective-permute-start | bytes 196616 | tf_op jit(solution)/shard_map/ppermute | solution.py:363
  9.3 1.5 %collective-permute-start.7 = (bf16[128,256]{1,0:T(8,128)(2,1)S(1)}, bf16[128,256]{1,0:T(8,128)(2,1)S(1)}, u32[]{:S(2)}, u32[]{:S(2)}) collective-permute-start(bf16[128,256]{1,0:T(8,128)(2,1)S(1)} %get-tuple-element.68), channel_id=1, source_target_pairs={{0,16},{8,24},{16,0},{24,8},{1,17},{9,25},{17,1},{25,9},{2,18},{10... | collective-permute-start | bytes 196616 | tf_op jit(solution)/shard_map/ppermute | solution.py:363
  10.8 0.5 collective-permute-start.8
  11.3 1.5 %collective-permute-start.3 = (bf16[128,768]{1,0:T(8,128)(2,1)S(1)}, bf16[128,768]{1,0:T(8,128)(2,1)S(1)}, u32[]{:S(2)}, u32[]{:S(2)}) collective-permute-start(bf16[128,768]{1,0:T(8,128)(2,1)S(1)} %get-tuple-element.64), channel_id=1, source_target_pairs={{0,8},{8,0},{16,24},{24,16},{1,9},{9,1},{17,25},{25,17},{2,10},{10... | collective-permute-start | bytes 589832 | tf_op jit(solution)/shard_map/ppermute | solution.py:363
  12.8 0.0 collective-permute-done.6.rest_1_
  12.8 1.5 %collective-permute-start.4 = (bf16[128,768]{1,0:T(8,128)(2,1)S(1)}, bf16[128,768]{1,0:T(8,128)(2,1)S(1)}, u32[]{:S(2)}, u32[]{:S(2)}) collective-permute-start(bf16[128,768]{1,0:T(8,128)(2,1)S(1)} %get-tuple-element.65), channel_id=1, source_target_pairs={{0,16},{8,24},{16,0},{24,8},{1,17},{9,25},{17,1},{25,9},{2,18},{10... | collective-permute-start | bytes 589832 | tf_op jit(solution)/shard_map/ppermute | solution.py:363
  14.3 0.1 collective-permute-done.7.rest_2_
  14.4 1.3 %collective-permute-start.5 = (bf16[128,768]{1,0:T(8,128)(2,1)S(1)}, bf16[128,768]{1,0:T(8,128)(2,1)S(1)}, u32[]{:S(2)}, u32[]{:S(2)}) collective-permute-start(bf16[128,768]{1,0:T(8,128)(2,1)S(1)} %get-tuple-element.66), channel_id=1, source_target_pairs={{0,24},{8,16},{16,8},{24,0},{1,25},{9,17},{17,9},{25,1},{2,26},{10... | collective-permute-start | bytes 589832 | tf_op jit(solution)/shard_map/ppermute | solution.py:363
  15.7 1.0 %collective-permute-done.8.rest_3_ = bf16[128,256]{1,0:T(8,128)(2,1)S(1)} collective-permute-done((bf16[128,256]{1,0:T(8,128)(2,1)S(1)}, bf16[128,256]{1,0:T(8,128)(2,1)S(1)}, u32[]{:S(2)}, u32[]{:S(2)}) %collective-permute-start.8) | collective-permute-done | bytes 65568 | tf_op jit(solution)/shard_map/ppermute | solution.py:363
  16.7 0.0 collective-permute-done.far
  16.7 1.0 %choose.2.rest_0_ = bf16[3,128,256]{2,1,0:T(8,128)(2,1)S(1)} custom-call(s32[22]{0:T(128)S(1)} %concatenate.3.ids, bf16[128,256]{1,0:T(8,128)(2,1)S(1)} %get-tuple-element.70.rest_0_, bf16[128,256]{1,0:T(8,128)(2,1)S(1)} %collective-permute-done.6.rest_1_, bf16[128,256]{1,0:T(8,128)(2,1)S(1)} %collective-permute-done.7.rest_2_, ...), custom_call_target="tpu_custom_call" | custom-call | flops 1 | bytes 1 | tf_op jit(solution)/shard_map/choose/pallas_call | solution.py:383
  17.7 0.4 collective-permute-start.9
  18.1 0.0 copy-done.1
  18.1 0.9 %split.1 = (bf16[48,2048]{1,0:T(8,128)(2,1)S(1)}, bf16[2,48,2048]{2,1,0:T(8,128)(2,1)S(1)}, bf16[2,48,2048]{2,1,0:T(8,128)(2,1)S(1)}) custom-call(s32[22]{0:T(128)S(1)} %concatenate.3.ids, bf16[1,48,6144]{2,1,0:T(8,128)(2,1)S(1)} %copy-done.1, bf16[1,48,1024]{2,1,0:T(8,128)(2,1)S(1)} %copy-done.2, bf16[1,48,1024]{2,1,0:T(8,128)(2,1)S(1)} %collective-permute-done.far), custom_call_target="tpu_custom_call" | custom-call | flops 1 | bytes 1 | tf_op jit(solution)/shard_map/split/pallas_call | solution.py:412
  19.0 1.6 %collective-permute-start.1 = (bf16[2,48,2048]{2,1,0:T(8,128)(2,1)S(1)}, bf16[2,48,2048]{2,1,0:T(8,128)(2,1)S(1)}, u32[]{:S(2)}, u32[]{:S(2)}) collective-permute-start(bf16[2,48,2048]{2,1,0:T(8,128)(2,1)S(1)} %get-tuple-element.61), channel_id=1, source_target_pairs={{0,2},{1,3},{2,0},{3,1},{4,6},{5,7},{6,4},{7,5},{8,10},{9,11},{10,... | collective-permute-start | bytes 1179656 | tf_op jit(solution)/shard_map/ppermute | solution.py:363
  20.6 0.0 collective-permute-done.3.rest_1_
  20.7 2.7 %collective-permute-done.4.rest_2_ = bf16[128,768]{1,0:T(8,128)(2,1)S(1)} collective-permute-done((bf16[128,768]{1,0:T(8,128)(2,1)S(1)}, bf16[128,768]{1,0:T(8,128)(2,1)S(1)}, u32[]{:S(2)}, u32[]{:S(2)}) %collective-permute-start.4) | collective-permute-done | bytes 196640 | tf_op jit(solution)/shard_map/ppermute | solution.py:363
  23.4 0.0 collective-permute-done.5.rest_3_
  23.4 2.9 %collective-permute-done.9.rest_2_.rest_3_ = bf16[3,128,256]{2,1,0:T(8,128)(2,1)S(1)} collective-permute-done((bf16[3,128,256]{2,1,0:T(8,128)(2,1)S(1)}, bf16[3,128,256]{2,1,0:T(8,128)(2,1)S(1)}, u32[]{:S(2)}, u32[]{:S(2)}) %collective-permute-start.9) | collective-permute-done | bytes 196640 | tf_op jit(solution)/shard_map/ppermute | solution.py:363
  26.3 0.9 %choose.3 = (bf16[2,3,128,256]{3,2,1,0:T(8,128)(2,1)S(1)}, bf16[2,3,128,256]{3,2,1,0:T(8,128)(2,1)S(1)}) custom-call(s32[22]{0:T(128)S(1)} %concatenate.3.ids, bf16[128,768]{1,0:T(8,128)(2,1)S(1)} %get-tuple-element.74.rest_0_, bf16[128,768]{1,0:T(8,128)(2,1)S(1)} %collective-permute-done.3.rest_1_, bf16[128,768]{1,0:T(8,128)(2,1)S(1)} %collective-permute-done.4.rest_2_, ...), custom_call_target="tpu_custom_call" | custom-call | flops 1 | bytes 1 | tf_op jit(solution)/shard_map/choose/pallas_call | solution.py:383
  27.2 0.1 collective-permute-start.10
  27.3 3.8 %collective-permute-done.1.got.rest_2_.rest_5_.rest_4_ = bf16[2,48,2048]{2,1,0:T(8,128)(2,1)S(1)} collective-permute-done((bf16[2,48,2048]{2,1,0:T(8,128)(2,1)S(1)}, bf16[2,48,2048]{2,1,0:T(8,128)(2,1)S(1)}, u32[]{:S(2)}, u32[]{:S(2)}) %collective-permute-start.1) | collective-permute-done | bytes 393248 | tf_op jit(solution)/shard_map/ppermute | solution.py:363
  31.1 0.1 collective-permute-start.2
  31.2 0.0 collective-permute-done.10.got
  31.3 0.8 collective-permute-start.12
  32.1 3.2 %collective-permute-start.13 = (bf16[3,128,256]{2,1,0:T(8,128)(2,1)S(1)}, bf16[3,128,256]{2,1,0:T(8,128)(2,1)S(1)}, u32[]{:S(2)}, u32[]{:S(2)}) collective-permute-start(bf16[3,128,256]{2,1,0:T(8,128)(2,1)S(1)} %get-tuple-element.88.rest_1_), channel_id=1, source_target_pairs={{0,4},{4,0},{1,5},{5,1},{2,6},{6,2},{3,7},{7,3},{8,12},{12,8},{9,1... | collective-permute-start | bytes 589832 | tf_op jit(solution)/shard_map/ppermute | solution.py:363
  35.2 0.7 collective-permute-start.11
  35.9 0.0 collective-permute-done.2.rest_1_.rest_4_.rest_3_
  35.9 0.6 sort.1.fresh
  36.5 5.2 %attend.3 = (f32[6,384,128]{2,1,0:T(8,128)S(1)}, f32[6,384,128]{2,1,0:T(8,128)S(1)}, f32[6,384,128]{2,1,0:T(8,128)S(1)}) custom-call(s32[22]{0:T(128)S(1)} %concatenate.3.ids, bf16[384,256]{1,0:T(8,128)(2,1)S(1)} %sort.1.fresh, bf16[3,128,256]{2,1,0:T(8,128)(2,1)S(1)} %choose.2.rest_0_, bf16[3,128,256]{2,1,0:T(8,128)(2,1)S(1)} %get-tuple-element.88.rest_1_, ...), custom_call_target="tpu_custom_call" | custom-call | flops 1 | bytes 1 | tf_op jit(solution)/shard_map/attend/pallas_call | solution.py:227
  41.7 3.7 %collective-permute-done.13.rest_4_.rest_1_ = bf16[3,128,256]{2,1,0:T(8,128)(2,1)S(1)} collective-permute-done((bf16[3,128,256]{2,1,0:T(8,128)(2,1)S(1)}, bf16[3,128,256]{2,1,0:T(8,128)(2,1)S(1)}, u32[]{:S(2)}, u32[]{:S(2)}) %collective-permute-start.13) | collective-permute-done | bytes 196640 | tf_op jit(solution)/shard_map/ppermute | solution.py:363
  45.4 1.7 %collective-permute-done.12.rest_2_.rest_0_ = bf16[2,3,128,256]{3,2,1,0:T(8,128)(2,1)S(1)} collective-permute-done((bf16[2,3,128,256]{3,2,1,0:T(8,128)(2,1)S(1)}, bf16[2,3,128,256]{3,2,1,0:T(8,128)(2,1)S(1)}, u32[]{:S(2)}, u32[]{:S(2)}) %collective-permute-start.12) | collective-permute-done | bytes 393248 | tf_op jit(solution)/shard_map/ppermute | solution.py:363
  47.0 1.3 %collective-permute-start.14 = (bf16[2,3,128,256]{3,2,1,0:T(8,128)(2,1)S(1)}, bf16[2,3,128,256]{3,2,1,0:T(8,128)(2,1)S(1)}, u32[]{:S(2)}, u32[]{:S(2)}) collective-permute-start(bf16[2,3,128,256]{3,2,1,0:T(8,128)(2,1)S(1)} %collective-permute-done.12.rest_2_.rest_0_), channel_id=1, source_target_pairs={{2,6},{3,7},{4,0},{5,1},{10,14},{11,15},{12,8},{13,9},{18,22},{19,... | collective-permute-start | bytes 1179656 | tf_op jit(solution)/shard_map/ppermute | solution.py:493
  48.3 0.8 %runs.2 = (bf16[6,3,16,256]{3,2,1,0:T(8,128)(2,1)S(1)}, bf16[6,3,16,256]{3,2,1,0:T(8,128)(2,1)S(1)}, bf16[6,3,16,256]{3,2,1,0:T(8,128)(2,1)S(1)}, bf16[6,3,16,256]{3,2,1,0:T(8,128)(2,1)S(1)}) custom-call(s32[22]{0:T(128)S(1)} %concatenate.3.ids, bf16[384,256]{1,0:T(8,128)(2,1)S(1)} %sort.1.fresh, bf16[3,128,256]{2,1,0:T(8,128)(2,1)S(1)} %choose.2.rest_0_, ...), custom_call_target="tpu_custom_call" | custom-call | flops 1 | bytes 1 | tf_op jit(solution)/shard_map/runs/pallas_call | solution.py:295
  49.2 0.7 collective-permute-start.15
  49.9 3.2 %collective-permute-start.16 = (bf16[6,3,16,256]{3,2,1,0:T(8,128)(2,1)S(1)}, bf16[6,3,16,256]{3,2,1,0:T(8,128)(2,1)S(1)}, u32[]{:S(2)}, u32[]{:S(2)}) collective-permute-start(bf16[6,3,16,256]{3,2,1,0:T(8,128)(2,1)S(1)} %get-tuple-element.93), channel_id=1, source_target_pairs={{0,1},{1,24},{2,11},{3,18},{4,5},{5,28},{6,15},{7,22},{8,9},{9,16}... | collective-permute-start | bytes 442376 | tf_op jit(solution)/shard_map/ppermute | solution.py:475
  53.0 3.9 %collective-permute-start.17 = (bf16[6,3,16,256]{3,2,1,0:T(8,128)(2,1)S(1)}, bf16[6,3,16,256]{3,2,1,0:T(8,128)(2,1)S(1)}, u32[]{:S(2)}, u32[]{:S(2)}) collective-permute-start(bf16[6,3,16,256]{3,2,1,0:T(8,128)(2,1)S(1)} %get-tuple-element.94), channel_id=1, source_target_pairs={{0,2},{1,27},{2,8},{3,17},{4,6},{5,31},{6,12},{7,21},{8,10},{9,19}... | collective-permute-start | bytes 442376 | tf_op jit(solution)/shard_map/ppermute | solution.py:475
  57.0 0.0 collective-permute-done.11.rest_0_
  57.0 0.7 collective-permute-start.18
  57.6 5.4 %attend.4 = (f32[6,384,128]{2,1,0:T(8,128)S(1)}, f32[6,384,128]{2,1,0:T(8,128)S(1)}, f32[6,384,128]{2,1,0:T(8,128)S(1)}) custom-call(s32[22]{0:T(128)S(1)} %concatenate.3.ids, bf16[384,256]{1,0:T(8,128)(2,1)S(1)} %sort.1.fresh, bf16[2,3,128,256]{3,2,1,0:T(8,128)(2,1)S(1)} %collective-permute-done.12.rest_2_.rest_0_, ...), custom_call_target="tpu_custom_call" | custom-call | flops 1 | bytes 1 | tf_op jit(solution)/shard_map/attend/pallas_call | solution.py:227
  63.0 0.0 collective-permute-done.14.rest_1_
  63.0 3.6 %attend.5 = (bf16[48,1536]{1,0:T(8,128)(2,1)S(1)}, bf16[2,48,1536]{2,1,0:T(8,128)(2,1)S(1)}, bf16[2,48,1536]{2,1,0:T(8,128)(2,1)S(1)}) custom-call(s32[22]{0:T(128)S(1)} %concatenate.3.ids, bf16[384,256]{1,0:T(8,128)(2,1)S(1)} %sort.1.fresh, bf16[2,3,128,256]{3,2,1,0:T(8,128)(2,1)S(1)} %collective-permute-done.11.rest_0_, ...), custom_call_target="tpu_custom_call" | custom-call | flops 1 | bytes 1 | tf_op jit(solution)/shard_map/attend/pallas_call | solution.py:227
  66.6 0.0 collective-permute-done.15.rest_3_
  66.6 0.0 collective-permute-done.16.rest_4_
  66.6 0.0 collective-permute-done.17.rest_5_
  66.6 1.5 %collective-permute-done.18.rest_6_ = bf16[6,3,16,256]{3,2,1,0:T(8,128)(2,1)S(1)} collective-permute-done((bf16[6,3,16,256]{3,2,1,0:T(8,128)(2,1)S(1)}, bf16[6,3,16,256]{3,2,1,0:T(8,128)(2,1)S(1)}, u32[]{:S(2)}, u32[]{:S(2)}) %collective-permute-start.18) | collective-permute-done | bytes 147488 | tf_op jit(solution)/shard_map/ppermute | solution.py:475
  68.1 0.3 collective-permute-start.19
  68.4 1.3 %collective-permute-done.19.got = bf16[2,48,1536]{2,1,0:T(8,128)(2,1)S(1)} collective-permute-done((bf16[2,48,1536]{2,1,0:T(8,128)(2,1)S(1)}, bf16[2,48,1536]{2,1,0:T(8,128)(2,1)S(1)}, u32[]{:S(2)}, u32[]{:S(2)}) %collective-permute-start.19) | collective-permute-done | bytes 294944 | tf_op jit(solution)/shard_map/ppermute | solution.py:363
  69.7 1.8 %collective-permute-start.20 = (bf16[2,48,1536]{2,1,0:T(8,128)(2,1)S(1)}, bf16[2,48,1536]{2,1,0:T(8,128)(2,1)S(1)}, u32[]{:S(2)}, u32[]{:S(2)}) collective-permute-start(bf16[2,48,1536]{2,1,0:T(8,128)(2,1)S(1)} %get-tuple-element.107), channel_id=1, source_target_pairs={{0,2},{1,3},{2,0},{3,1},{4,6},{5,7},{6,4},{7,5},{8,10},{9,11},{10,... | collective-permute-start | bytes 884744 | tf_op jit(solution)/shard_map/ppermute | solution.py:363
  71.4 0.7 runs.3
  72.1 0.7 collective-permute-start.21
  72.8 1.9 %collective-permute-start.22 = (bf16[2,3,16,256]{3,2,1,0:T(8,128)(2,1)S(1)}, bf16[2,3,16,256]{3,2,1,0:T(8,128)(2,1)S(1)}, u32[]{:S(2)}, u32[]{:S(2)}) collective-permute-start(bf16[2,3,16,256]{3,2,1,0:T(8,128)(2,1)S(1)} %get-tuple-element.111), channel_id=1, source_target_pairs={{0,1},{1,24},{2,11},{3,18},{4,5},{5,28},{6,15},{7,22},{8,9},{9,16}... | collective-permute-start | bytes 147464 | tf_op jit(solution)/shard_map/ppermute | solution.py:475
  74.6 1.5 %collective-permute-start.23 = (bf16[2,3,16,256]{3,2,1,0:T(8,128)(2,1)S(1)}, bf16[2,3,16,256]{3,2,1,0:T(8,128)(2,1)S(1)}, u32[]{:S(2)}, u32[]{:S(2)}) collective-permute-start(bf16[2,3,16,256]{3,2,1,0:T(8,128)(2,1)S(1)} %get-tuple-element.112), channel_id=1, source_target_pairs={{0,2},{1,27},{2,8},{3,17},{4,6},{5,31},{6,12},{7,21},{8,10},{9,19}... | collective-permute-start | bytes 147464 | tf_op jit(solution)/shard_map/ppermute | solution.py:475
  76.1 0.7 collective-permute-start.24
  76.8 0.0 collective-permute-done.21.rest_7_
  76.8 1.6 %collective-permute-done.22.rest_8_ = bf16[2,3,16,256]{3,2,1,0:T(8,128)(2,1)S(1)} collective-permute-done((bf16[2,3,16,256]{3,2,1,0:T(8,128)(2,1)S(1)}, bf16[2,3,16,256]{3,2,1,0:T(8,128)(2,1)S(1)}, u32[]{:S(2)}, u32[]{:S(2)}) %collective-permute-start.22) | collective-permute-done | bytes 49184 | tf_op jit(solution)/shard_map/ppermute | solution.py:475
  78.4 2.9 %collective-permute-done.23.rest_9_ = bf16[2,3,16,256]{3,2,1,0:T(8,128)(2,1)S(1)} collective-permute-done((bf16[2,3,16,256]{3,2,1,0:T(8,128)(2,1)S(1)}, bf16[2,3,16,256]{3,2,1,0:T(8,128)(2,1)S(1)}, u32[]{:S(2)}, u32[]{:S(2)}) %collective-permute-start.23) | collective-permute-done | bytes 49184 | tf_op jit(solution)/shard_map/ppermute | solution.py:475
  81.3 0.0 collective-permute-done.24.rest_10_
  81.3 0.0 collective-permute-done.20.rest_2_
  81.3 2.0 %finish.1 = (bf16[1,48,6144]{2,1,0:T(8,128)(2,1)}, bf16[1,1,4,24,4096]{4,3,2,1,0:T(8,128)(2,1)}) custom-call(s32[22]{0:T(128)S(1)} %concatenate.3.ids, bf16[48,1536]{1,0:T(8,128)(2,1)S(1)} %get-tuple-element.102.rest_0_, bf16[48,1536]{1,0:T(8,128)(2,1)S(1)} %get-tuple-element.106.rest_1_, bf16[2,48,1536]{2,1,0:T(8,128)(2,1)S(1)} %collective-permute-done.20.rest_2_, ...), custom_call_target="tpu_custom_call" | custom-call | flops 1 | bytes 1 | tf_op jit(solution)/shard_map/finish/pallas_call | solution.py:508
  (7 shorter events, 0.1 us)
Async XLA Ops:
  1.4 1.2 %copy-start = (bf16[4,128,1024]{2,1,0:T(8,128)(2,1)S(1)}, bf16[4,128,1024]{2,1,0:T(8,128)(2,1)}, u32[]{:S(2)}) copy-start(bf16[4,128,1024]{2,1,0:T(8,128)(2,1)} %pool_kv.1) | copy-start | bytes 3145732
  2.6 15.5 %copy-start.1 = (bf16[1,48,6144]{2,1,0:T(8,128)(2,1)S(1)}, bf16[1,48,6144]{2,1,0:T(8,128)(2,1)}, u32[]{:S(2)}) copy-start(bf16[1,48,6144]{2,1,0:T(8,128)(2,1)} %fresh_q.1) | copy-start | bytes 1769476
  2.6 15.5 %copy-start.2 = (bf16[1,48,1024]{2,1,0:T(8,128)(2,1)S(1)}, bf16[1,48,1024]{2,1,0:T(8,128)(2,1)}, u32[]{:S(2)}) copy-start(bf16[1,48,1024]{2,1,0:T(8,128)(2,1)} %near.1) | copy-start | bytes 294916
  3.7 13.1 %collective-permute-start = (bf16[1,48,1024]{2,1,0:T(8,128)(2,1)}, bf16[1,48,1024]{2,1,0:T(8,128)(2,1)S(1)}, u32[]{:S(2)}, u32[]{:S(2)}) collective-permute-start(bf16[1,48,1024]{2,1,0:T(8,128)(2,1)} %near.1), channel_id=1, source_target_pairs={{0,4},{4,0},{1,5},{5,1},{2,6},{6,2},{3,7},{7,3},{8,12},{12,8},{9,1... | collective-permute-start | bytes 294920 | tf_op jit(solution)/shard_map/ppermute | solution.py:363
  7.8 5.0 %collective-permute-start.6 = (bf16[128,256]{1,0:T(8,128)(2,1)S(1)}, bf16[128,256]{1,0:T(8,128)(2,1)S(1)}, u32[]{:S(2)}, u32[]{:S(2)}) collective-permute-start(bf16[128,256]{1,0:T(8,128)(2,1)S(1)} %get-tuple-element.67), channel_id=1, source_target_pairs={{0,8},{8,0},{16,24},{24,16},{1,9},{9,1},{17,25},{25,17},{2,10},{10... | collective-permute-start | bytes 196616 | tf_op jit(solution)/shard_map/ppermute | solution.py:363
  9.3 5.1 %collective-permute-start.7 = (bf16[128,256]{1,0:T(8,128)(2,1)S(1)}, bf16[128,256]{1,0:T(8,128)(2,1)S(1)}, u32[]{:S(2)}, u32[]{:S(2)}) collective-permute-start(bf16[128,256]{1,0:T(8,128)(2,1)S(1)} %get-tuple-element.68), channel_id=1, source_target_pairs={{0,16},{8,24},{16,0},{24,8},{1,17},{9,25},{17,1},{25,9},{2,18},{10... | collective-permute-start | bytes 196616 | tf_op jit(solution)/shard_map/ppermute | solution.py:363
  10.8 5.9 %collective-permute-start.8 = (bf16[128,256]{1,0:T(8,128)(2,1)S(1)}, bf16[128,256]{1,0:T(8,128)(2,1)S(1)}, u32[]{:S(2)}, u32[]{:S(2)}) collective-permute-start(bf16[128,256]{1,0:T(8,128)(2,1)S(1)} %get-tuple-element.69), channel_id=1, source_target_pairs={{0,24},{8,16},{16,8},{24,0},{1,25},{9,17},{17,9},{25,1},{2,26},{10... | collective-permute-start | bytes 196616 | tf_op jit(solution)/shard_map/ppermute | solution.py:363
  11.3 9.4 %collective-permute-start.3 = (bf16[128,768]{1,0:T(8,128)(2,1)S(1)}, bf16[128,768]{1,0:T(8,128)(2,1)S(1)}, u32[]{:S(2)}, u32[]{:S(2)}) collective-permute-start(bf16[128,768]{1,0:T(8,128)(2,1)S(1)} %get-tuple-element.64), channel_id=1, source_target_pairs={{0,8},{8,0},{16,24},{24,16},{1,9},{9,1},{17,25},{25,17},{2,10},{10... | collective-permute-start | bytes 589832 | tf_op jit(solution)/shard_map/ppermute | solution.py:363
  12.8 10.6 %collective-permute-start.4 = (bf16[128,768]{1,0:T(8,128)(2,1)S(1)}, bf16[128,768]{1,0:T(8,128)(2,1)S(1)}, u32[]{:S(2)}, u32[]{:S(2)}) collective-permute-start(bf16[128,768]{1,0:T(8,128)(2,1)S(1)} %get-tuple-element.65), channel_id=1, source_target_pairs={{0,16},{8,24},{16,0},{24,8},{1,17},{9,25},{17,1},{25,9},{2,18},{10... | collective-permute-start | bytes 589832 | tf_op jit(solution)/shard_map/ppermute | solution.py:363
  14.4 9.0 %collective-permute-start.5 = (bf16[128,768]{1,0:T(8,128)(2,1)S(1)}, bf16[128,768]{1,0:T(8,128)(2,1)S(1)}, u32[]{:S(2)}, u32[]{:S(2)}) collective-permute-start(bf16[128,768]{1,0:T(8,128)(2,1)S(1)} %get-tuple-element.66), channel_id=1, source_target_pairs={{0,24},{8,16},{16,8},{24,0},{1,25},{9,17},{17,9},{25,1},{2,26},{10... | collective-permute-start | bytes 589832 | tf_op jit(solution)/shard_map/ppermute | solution.py:363
  17.7 8.6 %collective-permute-start.9 = (bf16[3,128,256]{2,1,0:T(8,128)(2,1)S(1)}, bf16[3,128,256]{2,1,0:T(8,128)(2,1)S(1)}, u32[]{:S(2)}, u32[]{:S(2)}) collective-permute-start(bf16[3,128,256]{2,1,0:T(8,128)(2,1)S(1)} %choose.2.rest_0_), channel_id=1, source_target_pairs={{0,4},{4,0},{1,5},{5,1},{2,6},{6,2},{3,7},{7,3},{8,12},{12,8},{9,1... | collective-permute-start | bytes 589832 | tf_op jit(solution)/shard_map/ppermute | solution.py:363
  19.0 12.1 %collective-permute-start.1 = (bf16[2,48,2048]{2,1,0:T(8,128)(2,1)S(1)}, bf16[2,48,2048]{2,1,0:T(8,128)(2,1)S(1)}, u32[]{:S(2)}, u32[]{:S(2)}) collective-permute-start(bf16[2,48,2048]{2,1,0:T(8,128)(2,1)S(1)} %get-tuple-element.61), channel_id=1, source_target_pairs={{0,2},{1,3},{2,0},{3,1},{4,6},{5,7},{6,4},{7,5},{8,10},{9,11},{10,... | collective-permute-start | bytes 1179656 | tf_op jit(solution)/shard_map/ppermute | solution.py:363
  27.2 4.0 %collective-permute-start.10 = (bf16[2,3,128,256]{3,2,1,0:T(8,128)(2,1)S(1)}, bf16[2,3,128,256]{3,2,1,0:T(8,128)(2,1)S(1)}, u32[]{:S(2)}, u32[]{:S(2)}) collective-permute-start(bf16[2,3,128,256]{3,2,1,0:T(8,128)(2,1)S(1)} %get-tuple-element.78), channel_id=1, source_target_pairs={{0,1},{1,0},{2,3},{3,2},{4,5},{5,4},{6,7},{7,6},{8,9},{9,8},{10,11... | collective-permute-start | bytes 1179656 | tf_op jit(solution)/shard_map/ppermute | solution.py:363
  31.1 4.8 %collective-permute-start.2 = (bf16[2,48,2048]{2,1,0:T(8,128)(2,1)S(1)}, bf16[2,48,2048]{2,1,0:T(8,128)(2,1)S(1)}, u32[]{:S(2)}, u32[]{:S(2)}) collective-permute-start(bf16[2,48,2048]{2,1,0:T(8,128)(2,1)S(1)} %follow.1), channel_id=1, source_target_pairs={{0,1},{1,0},{2,3},{3,2},{4,5},{5,4},{6,7},{7,6},{8,9},{9,8},{10,11... | collective-permute-start | bytes 1179656 | tf_op jit(solution)/shard_map/ppermute | solution.py:363
  31.3 15.8 %collective-permute-start.12 = (bf16[2,3,128,256]{3,2,1,0:T(8,128)(2,1)S(1)}, bf16[2,3,128,256]{3,2,1,0:T(8,128)(2,1)S(1)}, u32[]{:S(2)}, u32[]{:S(2)}) collective-permute-start(bf16[2,3,128,256]{3,2,1,0:T(8,128)(2,1)S(1)} %get-tuple-element.81), channel_id=1, source_target_pairs={{0,2},{1,3},{2,0},{3,1},{4,6},{5,7},{6,4},{7,5},{8,10},{9,11},{10,... | collective-permute-start | bytes 1179656 | tf_op jit(solution)/shard_map/ppermute | solution.py:363
  32.1 13.3 %collective-permute-start.13 = (bf16[3,128,256]{2,1,0:T(8,128)(2,1)S(1)}, bf16[3,128,256]{2,1,0:T(8,128)(2,1)S(1)}, u32[]{:S(2)}, u32[]{:S(2)}) collective-permute-start(bf16[3,128,256]{2,1,0:T(8,128)(2,1)S(1)} %get-tuple-element.88.rest_1_), channel_id=1, source_target_pairs={{0,4},{4,0},{1,5},{5,1},{2,6},{6,2},{3,7},{7,3},{8,12},{12,8},{9,1... | collective-permute-start | bytes 589832 | tf_op jit(solution)/shard_map/ppermute | solution.py:363
  35.2 21.7 %collective-permute-start.11 = (bf16[2,3,128,256]{3,2,1,0:T(8,128)(2,1)S(1)}, bf16[2,3,128,256]{3,2,1,0:T(8,128)(2,1)S(1)}, u32[]{:S(2)}, u32[]{:S(2)}) collective-permute-start(bf16[2,3,128,256]{3,2,1,0:T(8,128)(2,1)S(1)} %get-tuple-element.81), channel_id=1, source_target_pairs={{2,4},{3,5},{4,2},{5,3},{10,12},{11,13},{12,10},{13,11},{18,20},{1... | collective-permute-start | bytes 1179656 | tf_op jit(solution)/shard_map/ppermute | solution.py:492
  47.0 15.9 %collective-permute-start.14 = (bf16[2,3,128,256]{3,2,1,0:T(8,128)(2,1)S(1)}, bf16[2,3,128,256]{3,2,1,0:T(8,128)(2,1)S(1)}, u32[]{:S(2)}, u32[]{:S(2)}) collective-permute-start(bf16[2,3,128,256]{3,2,1,0:T(8,128)(2,1)S(1)} %collective-permute-done.12.rest_2_.rest_0_), channel_id=1, source_target_pairs={{2,6},{3,7},{4,0},{5,1},{10,14},{11,15},{12,8},{13,9},{18,22},{19,... | collective-permute-start | bytes 1179656 | tf_op jit(solution)/shard_map/ppermute | solution.py:493
  49.2 17.4 %collective-permute-start.15 = (bf16[6,3,16,256]{3,2,1,0:T(8,128)(2,1)S(1)}, bf16[6,3,16,256]{3,2,1,0:T(8,128)(2,1)S(1)}, u32[]{:S(2)}, u32[]{:S(2)}) collective-permute-start(bf16[6,3,16,256]{3,2,1,0:T(8,128)(2,1)S(1)} %get-tuple-element.92), channel_id=1, source_target_pairs={{0,0},{1,25},{2,10},{3,19},{4,4},{5,29},{6,14},{7,23},{8,8},{9,17}... | collective-permute-start | bytes 442376 | tf_op jit(solution)/shard_map/ppermute | solution.py:475
  49.9 16.7 %collective-permute-start.16 = (bf16[6,3,16,256]{3,2,1,0:T(8,128)(2,1)S(1)}, bf16[6,3,16,256]{3,2,1,0:T(8,128)(2,1)S(1)}, u32[]{:S(2)}, u32[]{:S(2)}) collective-permute-start(bf16[6,3,16,256]{3,2,1,0:T(8,128)(2,1)S(1)} %get-tuple-element.93), channel_id=1, source_target_pairs={{0,1},{1,24},{2,11},{3,18},{4,5},{5,28},{6,15},{7,22},{8,9},{9,16}... | collective-permute-start | bytes 442376 | tf_op jit(solution)/shard_map/ppermute | solution.py:475
  53.0 13.5 %collective-permute-start.17 = (bf16[6,3,16,256]{3,2,1,0:T(8,128)(2,1)S(1)}, bf16[6,3,16,256]{3,2,1,0:T(8,128)(2,1)S(1)}, u32[]{:S(2)}, u32[]{:S(2)}) collective-permute-start(bf16[6,3,16,256]{3,2,1,0:T(8,128)(2,1)S(1)} %get-tuple-element.94), channel_id=1, source_target_pairs={{0,2},{1,27},{2,8},{3,17},{4,6},{5,31},{6,12},{7,21},{8,10},{9,19}... | collective-permute-start | bytes 442376 | tf_op jit(solution)/shard_map/ppermute | solution.py:475
  57.0 11.1 %collective-permute-start.18 = (bf16[6,3,16,256]{3,2,1,0:T(8,128)(2,1)S(1)}, bf16[6,3,16,256]{3,2,1,0:T(8,128)(2,1)S(1)}, u32[]{:S(2)}, u32[]{:S(2)}) collective-permute-start(bf16[6,3,16,256]{3,2,1,0:T(8,128)(2,1)S(1)} %get-tuple-element.95), channel_id=1, source_target_pairs={{0,3},{1,26},{2,9},{3,16},{4,7},{5,30},{6,13},{7,20},{8,11},{9,18}... | collective-permute-start | bytes 442376 | tf_op jit(solution)/shard_map/ppermute | solution.py:475
  68.1 1.6 %collective-permute-start.19 = (bf16[2,48,1536]{2,1,0:T(8,128)(2,1)S(1)}, bf16[2,48,1536]{2,1,0:T(8,128)(2,1)S(1)}, u32[]{:S(2)}, u32[]{:S(2)}) collective-permute-start(bf16[2,48,1536]{2,1,0:T(8,128)(2,1)S(1)} %get-tuple-element.104), channel_id=1, source_target_pairs={{0,1},{1,0},{2,3},{3,2},{4,5},{5,4},{6,7},{7,6},{8,9},{9,8},{10,11... | collective-permute-start | bytes 884744 | tf_op jit(solution)/shard_map/ppermute | solution.py:363
  69.7 11.6 %collective-permute-start.20 = (bf16[2,48,1536]{2,1,0:T(8,128)(2,1)S(1)}, bf16[2,48,1536]{2,1,0:T(8,128)(2,1)S(1)}, u32[]{:S(2)}, u32[]{:S(2)}) collective-permute-start(bf16[2,48,1536]{2,1,0:T(8,128)(2,1)S(1)} %get-tuple-element.107), channel_id=1, source_target_pairs={{0,2},{1,3},{2,0},{3,1},{4,6},{5,7},{6,4},{7,5},{8,10},{9,11},{10,... | collective-permute-start | bytes 884744 | tf_op jit(solution)/shard_map/ppermute | solution.py:363
  72.1 4.7 %collective-permute-start.21 = (bf16[2,3,16,256]{3,2,1,0:T(8,128)(2,1)S(1)}, bf16[2,3,16,256]{3,2,1,0:T(8,128)(2,1)S(1)}, u32[]{:S(2)}, u32[]{:S(2)}) collective-permute-start(bf16[2,3,16,256]{3,2,1,0:T(8,128)(2,1)S(1)} %get-tuple-element.110), channel_id=1, source_target_pairs={{0,0},{1,25},{2,10},{3,19},{4,4},{5,29},{6,14},{7,23},{8,8},{9,17}... | collective-permute-start | bytes 147464 | tf_op jit(solution)/shard_map/ppermute | solution.py:475
  72.8 5.7 %collective-permute-start.22 = (bf16[2,3,16,256]{3,2,1,0:T(8,128)(2,1)S(1)}, bf16[2,3,16,256]{3,2,1,0:T(8,128)(2,1)S(1)}, u32[]{:S(2)}, u32[]{:S(2)}) collective-permute-start(bf16[2,3,16,256]{3,2,1,0:T(8,128)(2,1)S(1)} %get-tuple-element.111), channel_id=1, source_target_pairs={{0,1},{1,24},{2,11},{3,18},{4,5},{5,28},{6,15},{7,22},{8,9},{9,16}... | collective-permute-start | bytes 147464 | tf_op jit(solution)/shard_map/ppermute | solution.py:475
  74.6 6.7 %collective-permute-start.23 = (bf16[2,3,16,256]{3,2,1,0:T(8,128)(2,1)S(1)}, bf16[2,3,16,256]{3,2,1,0:T(8,128)(2,1)S(1)}, u32[]{:S(2)}, u32[]{:S(2)}) collective-permute-start(bf16[2,3,16,256]{3,2,1,0:T(8,128)(2,1)S(1)} %get-tuple-element.112), channel_id=1, source_target_pairs={{0,2},{1,27},{2,8},{3,17},{4,6},{5,31},{6,12},{7,21},{8,10},{9,19}... | collective-permute-start | bytes 147464 | tf_op jit(solution)/shard_map/ppermute | solution.py:475
  76.1 5.2 %collective-permute-start.24 = (bf16[2,3,16,256]{3,2,1,0:T(8,128)(2,1)S(1)}, bf16[2,3,16,256]{3,2,1,0:T(8,128)(2,1)S(1)}, u32[]{:S(2)}, u32[]{:S(2)}) collective-permute-start(bf16[2,3,16,256]{3,2,1,0:T(8,128)(2,1)S(1)} %get-tuple-element.113), channel_id=1, source_target_pairs={{0,3},{1,26},{2,9},{3,16},{4,7},{5,30},{6,13},{7,20},{8,11},{9,18}... | collective-permute-start | bytes 147464 | tf_op jit(solution)/shard_map/ppermute | solution.py:475

commit v7 on v5

--- a/solution.py
+++ b/solution.py
@@ -489,7 +489,7 @@
     firsts = [i for i in range(seq_count) if ahead(i)]
     for a in range(1, quads):
         at = a * heads
-        soon = lax.ppermute(kv_send, ("quad", "head"), [(i, i ^ at ^ 2) for i in firsts])
+        soon = lax.ppermute(after(kv_send, fresh), ("quad", "head"), [(i, i ^ at ^ 2) for i in firsts])
         late = lax.ppermute(after(rest, messages[at + 1], state), ("quad", "head"), [(i, i ^ at) for i in firsts])
         messages[at + 2 : at + 4] = [[(soon, 0), (late, 0)], [(soon, 1), (late, 1)]]
         soons.append(soon)

time: 83.6 us -> 83.6 us (level)
  no operation moved by 1% of the time
where the time goes in v7:
time: 83.6 us; the launch traced here: 83.4 us
  starting transfers between devices  35.2 us (42%)
  waiting for transfers between devices  23.3 us (28%)
  Pallas kernels  21.9 us (26%)
  local copies, waits for them, and re-layouts  2 us (2%)
  between operations  1 us (1%)
    ppermute x15, starting transfers between devices, swap(): return lax.ppermute(value, axes, [(i, i ^ k) for i in range(count)])  20.1 us
    ppermute x15, waiting for transfers between devices, swap(): return lax.ppermute(value, axes, [(i, i ^ k) for i in range(count)])  17.3 us
    pallas_call x3, Pallas kernels, attend(): pl.pallas_call(functools.partial(attend_kernel, ks, state is None, last,...  14.1 us
    ppermute x8, starting transfers between devices, to_decode(): went[k] = lax.ppermute(cut[k], ('pool', 'quad', 'head'), perm)  13.1 us
    ppermute x8, waiting for transfers between devices, to_decode(): went[k] = lax.ppermute(cut[k], ('pool', 'quad', 'head'), perm)  5.96 us
    pallas_call x1, Pallas kernels, shards(): pl.pallas_call(functools.partial(finish_kernel, seq_count, views, len(arr...  1.96 us
    pallas_call x2, Pallas kernels, from_pool(): pl.pallas_call(functools.partial(choose_kernel, slots, pool_count), out_s...  1.84 us
  transfers between devices with their start and end apart: 25, of which 11 were waited for; matrix products, arithmetic and copies ran while one was open for 0% of the time, Pallas kernels for 23%

profile of v7, /device:TPU:0, one launch (start us, length us, event | category | flops | bytes accessed | tf_op | source)
XLA Modules:
  0.0 83.4 jit_solution(9432863781733124049)
XLA Ops:
  0.6 0.8 concatenate.3.ids
  1.4 1.2 %copy-done = bf16[4,128,1024]{2,1,0:T(8,128)(2,1)S(1)} copy-done((bf16[4,128,1024]{2,1,0:T(8,128)(2,1)S(1)}, bf16[4,128,1024]{2,1,0:T(8,128)(2,1)}, u32[]{:S(2)}) %copy-start) | copy-done | bytes 1048600
  2.6 1.1 %pack.1 = (bf16[128,256]{1,0:T(8,128)(2,1)S(1)}, bf16[128,256]{1,0:T(8,128)(2,1)S(1)}, bf16[128,256]{1,0:T(8,128)(2,1)S(1)}, bf16[128,256]{1,0:T(8,128)(2,1)S(1)...) custom-call(s32[22]{0:T(128)S(1)} %concatenate.3.ids, ...), custom_call_target="tpu_custom_call" | custom-call | flops 1 | bytes 1 | tf_op jit(solution)/shard_map/pack/pallas_call | solution.py:366
  3.7 4.1 %collective-permute-start = (bf16[1,48,1024]{2,1,0:T(8,128)(2,1)}, bf16[1,48,1024]{2,1,0:T(8,128)(2,1)S(1)}, u32[]{:S(2)}, u32[]{:S(2)}) collective-permute-start(bf16[1,48,1024]{2,1,0:T(8,128)(2,1)} %near.1), channel_id=1, source_target_pairs={{0,4},{4,0},{1,5},{5,1},{2,6},{6,2},{3,7},{7,3},{8,12},{12,8},{9,1... | collective-permute-start | bytes 294920 | tf_op jit(solution)/shard_map/ppermute | solution.py:363
  7.8 1.5 %collective-permute-start.6 = (bf16[128,256]{1,0:T(8,128)(2,1)S(1)}, bf16[128,256]{1,0:T(8,128)(2,1)S(1)}, u32[]{:S(2)}, u32[]{:S(2)}) collective-permute-start(bf16[128,256]{1,0:T(8,128)(2,1)S(1)} %get-tuple-element.68), channel_id=1, source_target_pairs={{0,8},{8,0},{16,24},{24,16},{1,9},{9,1},{17,25},{25,17},{2,10},{10... | collective-permute-start | bytes 196616 | tf_op jit(solution)/shard_map/ppermute | solution.py:363
  9.3 1.5 %collective-permute-start.7 = (bf16[128,256]{1,0:T(8,128)(2,1)S(1)}, bf16[128,256]{1,0:T(8,128)(2,1)S(1)}, u32[]{:S(2)}, u32[]{:S(2)}) collective-permute-start(bf16[128,256]{1,0:T(8,128)(2,1)S(1)} %get-tuple-element.69), channel_id=1, source_target_pairs={{0,16},{8,24},{16,0},{24,8},{1,17},{9,25},{17,1},{25,9},{2,18},{10... | collective-permute-start | bytes 196616 | tf_op jit(solution)/shard_map/ppermute | solution.py:363
  10.8 0.5 collective-permute-start.8
  11.3 1.5 %collective-permute-start.3 = (bf16[128,768]{1,0:T(8,128)(2,1)S(1)}, bf16[128,768]{1,0:T(8,128)(2,1)S(1)}, u32[]{:S(2)}, u32[]{:S(2)}) collective-permute-start(bf16[128,768]{1,0:T(8,128)(2,1)S(1)} %get-tuple-element.65), channel_id=1, source_target_pairs={{0,8},{8,0},{16,24},{24,16},{1,9},{9,1},{17,25},{25,17},{2,10},{10... | collective-permute-start | bytes 589832 | tf_op jit(solution)/shard_map/ppermute | solution.py:363
  12.8 0.0 collective-permute-done.6.rest_1_
  12.8 1.5 %collective-permute-start.4 = (bf16[128,768]{1,0:T(8,128)(2,1)S(1)}, bf16[128,768]{1,0:T(8,128)(2,1)S(1)}, u32[]{:S(2)}, u32[]{:S(2)}) collective-permute-start(bf16[128,768]{1,0:T(8,128)(2,1)S(1)} %get-tuple-element.66), channel_id=1, source_target_pairs={{0,16},{8,24},{16,0},{24,8},{1,17},{9,25},{17,1},{25,9},{2,18},{10... | collective-permute-start | bytes 589832 | tf_op jit(solution)/shard_map/ppermute | solution.py:363
  14.3 0.1 collective-permute-done.7.rest_2_
  14.4 1.3 %collective-permute-start.5 = (bf16[128,768]{1,0:T(8,128)(2,1)S(1)}, bf16[128,768]{1,0:T(8,128)(2,1)S(1)}, u32[]{:S(2)}, u32[]{:S(2)}) collective-permute-start(bf16[128,768]{1,0:T(8,128)(2,1)S(1)} %get-tuple-element.67), channel_id=1, source_target_pairs={{0,24},{8,16},{16,8},{24,0},{1,25},{9,17},{17,9},{25,1},{2,26},{10... | collective-permute-start | bytes 589832 | tf_op jit(solution)/shard_map/ppermute | solution.py:363
  15.7 1.0 %collective-permute-done.8.rest_3_ = bf16[128,256]{1,0:T(8,128)(2,1)S(1)} collective-permute-done((bf16[128,256]{1,0:T(8,128)(2,1)S(1)}, bf16[128,256]{1,0:T(8,128)(2,1)S(1)}, u32[]{:S(2)}, u32[]{:S(2)}) %collective-permute-start.8) | collective-permute-done | bytes 65568 | tf_op jit(solution)/shard_map/ppermute | solution.py:363
  16.7 0.0 collective-permute-done.far
  16.7 1.0 %choose.2.rest_0_ = bf16[3,128,256]{2,1,0:T(8,128)(2,1)S(1)} custom-call(s32[22]{0:T(128)S(1)} %concatenate.3.ids, bf16[128,256]{1,0:T(8,128)(2,1)S(1)} %get-tuple-element.71.rest_0_, bf16[128,256]{1,0:T(8,128)(2,1)S(1)} %collective-permute-done.6.rest_1_, bf16[128,256]{1,0:T(8,128)(2,1)S(1)} %collective-permute-done.7.rest_2_, ...), custom_call_target="tpu_custom_call" | custom-call | flops 1 | bytes 1 | tf_op jit(solution)/shard_map/choose/pallas_call | solution.py:383
  17.7 0.4 collective-permute-start.9
  18.1 0.0 copy-done.1
  18.1 0.9 %split.1 = (bf16[48,2048]{1,0:T(8,128)(2,1)S(1)}, bf16[2,48,2048]{2,1,0:T(8,128)(2,1)S(1)}, bf16[2,48,2048]{2,1,0:T(8,128)(2,1)S(1)}) custom-call(s32[22]{0:T(128)S(1)} %concatenate.3.ids, bf16[1,48,6144]{2,1,0:T(8,128)(2,1)S(1)} %copy-done.1, bf16[1,48,1024]{2,1,0:T(8,128)(2,1)S(1)} %copy-done.2, bf16[1,48,1024]{2,1,0:T(8,128)(2,1)S(1)} %collective-permute-done.far), custom_call_target="tpu_custom_call" | custom-call | flops 1 | bytes 1 | tf_op jit(solution)/shard_map/split/pallas_call | solution.py:412
  19.0 1.6 %collective-permute-start.1 = (bf16[2,48,2048]{2,1,0:T(8,128)(2,1)S(1)}, bf16[2,48,2048]{2,1,0:T(8,128)(2,1)S(1)}, u32[]{:S(2)}, u32[]{:S(2)}) collective-permute-start(bf16[2,48,2048]{2,1,0:T(8,128)(2,1)S(1)} %get-tuple-element.62), channel_id=1, source_target_pairs={{0,2},{1,3},{2,0},{3,1},{4,6},{5,7},{6,4},{7,5},{8,10},{9,11},{10,... | collective-permute-start | bytes 1179656 | tf_op jit(solution)/shard_map/ppermute | solution.py:363
  20.6 0.0 collective-permute-done.3.rest_1_
  20.7 2.7 %collective-permute-done.4.rest_2_ = bf16[128,768]{1,0:T(8,128)(2,1)S(1)} collective-permute-done((bf16[128,768]{1,0:T(8,128)(2,1)S(1)}, bf16[128,768]{1,0:T(8,128)(2,1)S(1)}, u32[]{:S(2)}, u32[]{:S(2)}) %collective-permute-start.4) | collective-permute-done | bytes 196640 | tf_op jit(solution)/shard_map/ppermute | solution.py:363
  23.4 0.0 collective-permute-done.5.rest_3_
  23.4 2.9 %collective-permute-done.9.rest_2_.rest_3_ = bf16[3,128,256]{2,1,0:T(8,128)(2,1)S(1)} collective-permute-done((bf16[3,128,256]{2,1,0:T(8,128)(2,1)S(1)}, bf16[3,128,256]{2,1,0:T(8,128)(2,1)S(1)}, u32[]{:S(2)}, u32[]{:S(2)}) %collective-permute-start.9) | collective-permute-done | bytes 196640 | tf_op jit(solution)/shard_map/ppermute | solution.py:363
  26.3 0.9 %choose.3 = (bf16[2,3,128,256]{3,2,1,0:T(8,128)(2,1)S(1)}, bf16[2,3,128,256]{3,2,1,0:T(8,128)(2,1)S(1)}) custom-call(s32[22]{0:T(128)S(1)} %concatenate.3.ids, bf16[128,768]{1,0:T(8,128)(2,1)S(1)} %get-tuple-element.75.rest_0_, bf16[128,768]{1,0:T(8,128)(2,1)S(1)} %collective-permute-done.3.rest_1_, bf16[128,768]{1,0:T(8,128)(2,1)S(1)} %collective-permute-done.4.rest_2_, ...), custom_call_target="tpu_custom_call" | custom-call | flops 1 | bytes 1 | tf_op jit(solution)/shard_map/choose/pallas_call | solution.py:383
  27.2 0.1 collective-permute-start.10
  27.3 3.8 %collective-permute-done.1.got.rest_2_.rest_5_.rest_4_ = bf16[2,48,2048]{2,1,0:T(8,128)(2,1)S(1)} collective-permute-done((bf16[2,48,2048]{2,1,0:T(8,128)(2,1)S(1)}, bf16[2,48,2048]{2,1,0:T(8,128)(2,1)S(1)}, u32[]{:S(2)}, u32[]{:S(2)}) %collective-permute-start.1) | collective-permute-done | bytes 393248 | tf_op jit(solution)/shard_map/ppermute | solution.py:363
  31.1 0.1 collective-permute-start.2
  31.2 0.0 collective-permute-done.10.got
  31.3 0.8 collective-permute-start.12
  32.1 3.2 %collective-permute-start.13 = (bf16[3,128,256]{2,1,0:T(8,128)(2,1)S(1)}, bf16[3,128,256]{2,1,0:T(8,128)(2,1)S(1)}, u32[]{:S(2)}, u32[]{:S(2)}) collective-permute-start(bf16[3,128,256]{2,1,0:T(8,128)(2,1)S(1)} %get-tuple-element.90.rest_1_), channel_id=1, source_target_pairs={{0,4},{4,0},{1,5},{5,1},{2,6},{6,2},{3,7},{7,3},{8,12},{12,8},{9,1... | collective-permute-start | bytes 589832 | tf_op jit(solution)/shard_map/ppermute | solution.py:363
  35.2 0.0 collective-permute-done.2.rest_1_.rest_4_.rest_3_
  35.3 0.6 sort.1.fresh
  35.8 0.7 collective-permute-start.11
  36.5 5.2 %attend.3 = (f32[6,384,128]{2,1,0:T(8,128)S(1)}, f32[6,384,128]{2,1,0:T(8,128)S(1)}, f32[6,384,128]{2,1,0:T(8,128)S(1)}) custom-call(s32[22]{0:T(128)S(1)} %concatenate.3.ids, bf16[384,256]{1,0:T(8,128)(2,1)S(1)} %sort.1.fresh, bf16[3,128,256]{2,1,0:T(8,128)(2,1)S(1)} %choose.2.rest_0_, bf16[3,128,256]{2,1,0:T(8,128)(2,1)S(1)} %get-tuple-element.90.rest_1_, ...), custom_call_target="tpu_custom_call" | custom-call | flops 1 | bytes 1 | tf_op jit(solution)/shard_map/attend/pallas_call | solution.py:227
  41.7 3.7 %collective-permute-done.13.rest_4_.rest_1_ = bf16[3,128,256]{2,1,0:T(8,128)(2,1)S(1)} collective-permute-done((bf16[3,128,256]{2,1,0:T(8,128)(2,1)S(1)}, bf16[3,128,256]{2,1,0:T(8,128)(2,1)S(1)}, u32[]{:S(2)}, u32[]{:S(2)}) %collective-permute-start.13) | collective-permute-done | bytes 196640 | tf_op jit(solution)/shard_map/ppermute | solution.py:363
  45.4 1.7 %collective-permute-done.12.rest_2_.rest_0_ = bf16[2,3,128,256]{3,2,1,0:T(8,128)(2,1)S(1)} collective-permute-done((bf16[2,3,128,256]{3,2,1,0:T(8,128)(2,1)S(1)}, bf16[2,3,128,256]{3,2,1,0:T(8,128)(2,1)S(1)}, u32[]{:S(2)}, u32[]{:S(2)}) %collective-permute-start.12) | collective-permute-done | bytes 393248 | tf_op jit(solution)/shard_map/ppermute | solution.py:363
  47.0 1.3 %collective-permute-start.14 = (bf16[2,3,128,256]{3,2,1,0:T(8,128)(2,1)S(1)}, bf16[2,3,128,256]{3,2,1,0:T(8,128)(2,1)S(1)}, u32[]{:S(2)}, u32[]{:S(2)}) collective-permute-start(bf16[2,3,128,256]{3,2,1,0:T(8,128)(2,1)S(1)} %collective-permute-done.12.rest_2_.rest_0_), channel_id=1, source_target_pairs={{2,6},{3,7},{4,0},{5,1},{10,14},{11,15},{12,8},{13,9},{18,22},{19,... | collective-permute-start | bytes 1179656 | tf_op jit(solution)/shard_map/ppermute | solution.py:493
  48.3 0.8 %runs.2 = (bf16[6,3,16,256]{3,2,1,0:T(8,128)(2,1)S(1)}, bf16[6,3,16,256]{3,2,1,0:T(8,128)(2,1)S(1)}, bf16[6,3,16,256]{3,2,1,0:T(8,128)(2,1)S(1)}, bf16[6,3,16,256]{3,2,1,0:T(8,128)(2,1)S(1)}) custom-call(s32[22]{0:T(128)S(1)} %concatenate.3.ids, bf16[384,256]{1,0:T(8,128)(2,1)S(1)} %sort.1.fresh, bf16[3,128,256]{2,1,0:T(8,128)(2,1)S(1)} %choose.2.rest_0_, ...), custom_call_target="tpu_custom_call" | custom-call | flops 1 | bytes 1 | tf_op jit(solution)/shard_map/runs/pallas_call | solution.py:295
  49.2 0.7 collective-permute-start.15
  49.9 3.2 %collective-permute-start.16 = (bf16[6,3,16,256]{3,2,1,0:T(8,128)(2,1)S(1)}, bf16[6,3,16,256]{3,2,1,0:T(8,128)(2,1)S(1)}, u32[]{:S(2)}, u32[]{:S(2)}) collective-permute-start(bf16[6,3,16,256]{3,2,1,0:T(8,128)(2,1)S(1)} %get-tuple-element.95), channel_id=1, source_target_pairs={{0,1},{1,24},{2,11},{3,18},{4,5},{5,28},{6,15},{7,22},{8,9},{9,16}... | collective-permute-start | bytes 442376 | tf_op jit(solution)/shard_map/ppermute | solution.py:475
  53.0 3.9 %collective-permute-start.17 = (bf16[6,3,16,256]{3,2,1,0:T(8,128)(2,1)S(1)}, bf16[6,3,16,256]{3,2,1,0:T(8,128)(2,1)S(1)}, u32[]{:S(2)}, u32[]{:S(2)}) collective-permute-start(bf16[6,3,16,256]{3,2,1,0:T(8,128)(2,1)S(1)} %get-tuple-element.96), channel_id=1, source_target_pairs={{0,2},{1,27},{2,8},{3,17},{4,6},{5,31},{6,12},{7,21},{8,10},{9,19}... | collective-permute-start | bytes 442376 | tf_op jit(solution)/shard_map/ppermute | solution.py:475
  57.0 0.0 collective-permute-done.11.rest_0_
  57.0 0.6 collective-permute-start.18
  57.6 5.4 %attend.4 = (f32[6,384,128]{2,1,0:T(8,128)S(1)}, f32[6,384,128]{2,1,0:T(8,128)S(1)}, f32[6,384,128]{2,1,0:T(8,128)S(1)}) custom-call(s32[22]{0:T(128)S(1)} %concatenate.3.ids, bf16[384,256]{1,0:T(8,128)(2,1)S(1)} %sort.1.fresh, bf16[2,3,128,256]{3,2,1,0:T(8,128)(2,1)S(1)} %collective-permute-done.12.rest_2_.rest_0_, ...), custom_call_target="tpu_custom_call" | custom-call | flops 1 | bytes 1 | tf_op jit(solution)/shard_map/attend/pallas_call | solution.py:227
  63.0 0.0 collective-permute-done.14.rest_1_
  63.0 3.6 %attend.5 = (bf16[48,1536]{1,0:T(8,128)(2,1)S(1)}, bf16[2,48,1536]{2,1,0:T(8,128)(2,1)S(1)}, bf16[2,48,1536]{2,1,0:T(8,128)(2,1)S(1)}) custom-call(s32[22]{0:T(128)S(1)} %concatenate.3.ids, bf16[384,256]{1,0:T(8,128)(2,1)S(1)} %sort.1.fresh, bf16[2,3,128,256]{3,2,1,0:T(8,128)(2,1)S(1)} %collective-permute-done.11.rest_0_, ...), custom_call_target="tpu_custom_call" | custom-call | flops 1 | bytes 1 | tf_op jit(solution)/shard_map/attend/pallas_call | solution.py:227
  66.6 0.0 collective-permute-done.15.rest_3_
  66.6 0.0 collective-permute-done.16.rest_4_
  66.6 0.0 collective-permute-done.17.rest_5_
  66.6 1.5 %collective-permute-done.18.rest_6_ = bf16[6,3,16,256]{3,2,1,0:T(8,128)(2,1)S(1)} collective-permute-done((bf16[6,3,16,256]{3,2,1,0:T(8,128)(2,1)S(1)}, bf16[6,3,16,256]{3,2,1,0:T(8,128)(2,1)S(1)}, u32[]{:S(2)}, u32[]{:S(2)}) %collective-permute-start.18) | collective-permute-done | bytes 147488 | tf_op jit(solution)/shard_map/ppermute | solution.py:475
  68.1 0.3 collective-permute-start.19
  68.4 1.3 %collective-permute-done.19.got = bf16[2,48,1536]{2,1,0:T(8,128)(2,1)S(1)} collective-permute-done((bf16[2,48,1536]{2,1,0:T(8,128)(2,1)S(1)}, bf16[2,48,1536]{2,1,0:T(8,128)(2,1)S(1)}, u32[]{:S(2)}, u32[]{:S(2)}) %collective-permute-start.19) | collective-permute-done | bytes 294944 | tf_op jit(solution)/shard_map/ppermute | solution.py:363
  69.7 1.8 %collective-permute-start.20 = (bf16[2,48,1536]{2,1,0:T(8,128)(2,1)S(1)}, bf16[2,48,1536]{2,1,0:T(8,128)(2,1)S(1)}, u32[]{:S(2)}, u32[]{:S(2)}) collective-permute-start(bf16[2,48,1536]{2,1,0:T(8,128)(2,1)S(1)} %get-tuple-element.109), channel_id=1, source_target_pairs={{0,2},{1,3},{2,0},{3,1},{4,6},{5,7},{6,4},{7,5},{8,10},{9,11},{10,... | collective-permute-start | bytes 884744 | tf_op jit(solution)/shard_map/ppermute | solution.py:363
  71.5 0.7 runs.3
  72.1 0.7 collective-permute-start.21
  72.8 1.9 %collective-permute-start.22 = (bf16[2,3,16,256]{3,2,1,0:T(8,128)(2,1)S(1)}, bf16[2,3,16,256]{3,2,1,0:T(8,128)(2,1)S(1)}, u32[]{:S(2)}, u32[]{:S(2)}) collective-permute-start(bf16[2,3,16,256]{3,2,1,0:T(8,128)(2,1)S(1)} %get-tuple-element.113), channel_id=1, source_target_pairs={{0,1},{1,24},{2,11},{3,18},{4,5},{5,28},{6,15},{7,22},{8,9},{9,16}... | collective-permute-start | bytes 147464 | tf_op jit(solution)/shard_map/ppermute | solution.py:475
  74.7 1.4 %collective-permute-start.23 = (bf16[2,3,16,256]{3,2,1,0:T(8,128)(2,1)S(1)}, bf16[2,3,16,256]{3,2,1,0:T(8,128)(2,1)S(1)}, u32[]{:S(2)}, u32[]{:S(2)}) collective-permute-start(bf16[2,3,16,256]{3,2,1,0:T(8,128)(2,1)S(1)} %get-tuple-element.114), channel_id=1, source_target_pairs={{0,2},{1,27},{2,8},{3,17},{4,6},{5,31},{6,12},{7,21},{8,10},{9,19}... | collective-permute-start | bytes 147464 | tf_op jit(solution)/shard_map/ppermute | solution.py:475
  76.1 0.7 collective-permute-start.24
  76.8 0.0 collective-permute-done.21.rest_7_
  76.8 1.6 %collective-permute-done.22.rest_8_ = bf16[2,3,16,256]{3,2,1,0:T(8,128)(2,1)S(1)} collective-permute-done((bf16[2,3,16,256]{3,2,1,0:T(8,128)(2,1)S(1)}, bf16[2,3,16,256]{3,2,1,0:T(8,128)(2,1)S(1)}, u32[]{:S(2)}, u32[]{:S(2)}) %collective-permute-start.22) | collective-permute-done | bytes 49184 | tf_op jit(solution)/shard_map/ppermute | solution.py:475
  78.5 2.8 %collective-permute-done.23.rest_9_ = bf16[2,3,16,256]{3,2,1,0:T(8,128)(2,1)S(1)} collective-permute-done((bf16[2,3,16,256]{3,2,1,0:T(8,128)(2,1)S(1)}, bf16[2,3,16,256]{3,2,1,0:T(8,128)(2,1)S(1)}, u32[]{:S(2)}, u32[]{:S(2)}) %collective-permute-start.23) | collective-permute-done | bytes 49184 | tf_op jit(solution)/shard_map/ppermute | solution.py:475
  81.3 0.0 collective-permute-done.24.rest_10_
  81.3 0.0 collective-permute-done.20.rest_2_
  81.3 2.0 %finish.1 = (bf16[1,48,6144]{2,1,0:T(8,128)(2,1)}, bf16[1,1,4,24,4096]{4,3,2,1,0:T(8,128)(2,1)}) custom-call(s32[22]{0:T(128)S(1)} %concatenate.3.ids, bf16[48,1536]{1,0:T(8,128)(2,1)S(1)} %get-tuple-element.104.rest_0_, bf16[48,1536]{1,0:T(8,128)(2,1)S(1)} %get-tuple-element.108.rest_1_, bf16[2,48,1536]{2,1,0:T(8,128)(2,1)S(1)} %collective-permute-done.20.rest_2_, ...), custom_call_target="tpu_custom_call" | custom-call | flops 1 | bytes 1 | tf_op jit(solution)/shard_map/finish/pallas_call | solution.py:508
  (7 shorter events, 0.1 us)
Async XLA Ops:
  1.4 1.2 %copy-start = (bf16[4,128,1024]{2,1,0:T(8,128)(2,1)S(1)}, bf16[4,128,1024]{2,1,0:T(8,128)(2,1)}, u32[]{:S(2)}) copy-start(bf16[4,128,1024]{2,1,0:T(8,128)(2,1)} %pool_kv.1) | copy-start | bytes 3145732
  2.6 15.5 %copy-start.1 = (bf16[1,48,6144]{2,1,0:T(8,128)(2,1)S(1)}, bf16[1,48,6144]{2,1,0:T(8,128)(2,1)}, u32[]{:S(2)}) copy-start(bf16[1,48,6144]{2,1,0:T(8,128)(2,1)} %fresh_q.1) | copy-start | bytes 1769476
  2.6 15.5 %copy-start.2 = (bf16[1,48,1024]{2,1,0:T(8,128)(2,1)S(1)}, bf16[1,48,1024]{2,1,0:T(8,128)(2,1)}, u32[]{:S(2)}) copy-start(bf16[1,48,1024]{2,1,0:T(8,128)(2,1)} %near.1) | copy-start | bytes 294916
  3.7 13.1 %collective-permute-start = (bf16[1,48,1024]{2,1,0:T(8,128)(2,1)}, bf16[1,48,1024]{2,1,0:T(8,128)(2,1)S(1)}, u32[]{:S(2)}, u32[]{:S(2)}) collective-permute-start(bf16[1,48,1024]{2,1,0:T(8,128)(2,1)} %near.1), channel_id=1, source_target_pairs={{0,4},{4,0},{1,5},{5,1},{2,6},{6,2},{3,7},{7,3},{8,12},{12,8},{9,1... | collective-permute-start | bytes 294920 | tf_op jit(solution)/shard_map/ppermute | solution.py:363
  7.8 5.0 %collective-permute-start.6 = (bf16[128,256]{1,0:T(8,128)(2,1)S(1)}, bf16[128,256]{1,0:T(8,128)(2,1)S(1)}, u32[]{:S(2)}, u32[]{:S(2)}) collective-permute-start(bf16[128,256]{1,0:T(8,128)(2,1)S(1)} %get-tuple-element.68), channel_id=1, source_target_pairs={{0,8},{8,0},{16,24},{24,16},{1,9},{9,1},{17,25},{25,17},{2,10},{10... | collective-permute-start | bytes 196616 | tf_op jit(solution)/shard_map/ppermute | solution.py:363
  9.3 5.1 %collective-permute-start.7 = (bf16[128,256]{1,0:T(8,128)(2,1)S(1)}, bf16[128,256]{1,0:T(8,128)(2,1)S(1)}, u32[]{:S(2)}, u32[]{:S(2)}) collective-permute-start(bf16[128,256]{1,0:T(8,128)(2,1)S(1)} %get-tuple-element.69), channel_id=1, source_target_pairs={{0,16},{8,24},{16,0},{24,8},{1,17},{9,25},{17,1},{25,9},{2,18},{10... | collective-permute-start | bytes 196616 | tf_op jit(solution)/shard_map/ppermute | solution.py:363
  10.8 5.9 %collective-permute-start.8 = (bf16[128,256]{1,0:T(8,128)(2,1)S(1)}, bf16[128,256]{1,0:T(8,128)(2,1)S(1)}, u32[]{:S(2)}, u32[]{:S(2)}) collective-permute-start(bf16[128,256]{1,0:T(8,128)(2,1)S(1)} %get-tuple-element.70), channel_id=1, source_target_pairs={{0,24},{8,16},{16,8},{24,0},{1,25},{9,17},{17,9},{25,1},{2,26},{10... | collective-permute-start | bytes 196616 | tf_op jit(solution)/shard_map/ppermute | solution.py:363
  11.3 9.4 %collective-permute-start.3 = (bf16[128,768]{1,0:T(8,128)(2,1)S(1)}, bf16[128,768]{1,0:T(8,128)(2,1)S(1)}, u32[]{:S(2)}, u32[]{:S(2)}) collective-permute-start(bf16[128,768]{1,0:T(8,128)(2,1)S(1)} %get-tuple-element.65), channel_id=1, source_target_pairs={{0,8},{8,0},{16,24},{24,16},{1,9},{9,1},{17,25},{25,17},{2,10},{10... | collective-permute-start | bytes 589832 | tf_op jit(solution)/shard_map/ppermute | solution.py:363
  12.8 10.6 %collective-permute-start.4 = (bf16[128,768]{1,0:T(8,128)(2,1)S(1)}, bf16[128,768]{1,0:T(8,128)(2,1)S(1)}, u32[]{:S(2)}, u32[]{:S(2)}) collective-permute-start(bf16[128,768]{1,0:T(8,128)(2,1)S(1)} %get-tuple-element.66), channel_id=1, source_target_pairs={{0,16},{8,24},{16,0},{24,8},{1,17},{9,25},{17,1},{25,9},{2,18},{10... | collective-permute-start | bytes 589832 | tf_op jit(solution)/shard_map/ppermute | solution.py:363
  14.4 9.0 %collective-permute-start.5 = (bf16[128,768]{1,0:T(8,128)(2,1)S(1)}, bf16[128,768]{1,0:T(8,128)(2,1)S(1)}, u32[]{:S(2)}, u32[]{:S(2)}) collective-permute-start(bf16[128,768]{1,0:T(8,128)(2,1)S(1)} %get-tuple-element.67), channel_id=1, source_target_pairs={{0,24},{8,16},{16,8},{24,0},{1,25},{9,17},{17,9},{25,1},{2,26},{10... | collective-permute-start | bytes 589832 | tf_op jit(solution)/shard_map/ppermute | solution.py:363
  17.7 8.6 %collective-permute-start.9 = (bf16[3,128,256]{2,1,0:T(8,128)(2,1)S(1)}, bf16[3,128,256]{2,1,0:T(8,128)(2,1)S(1)}, u32[]{:S(2)}, u32[]{:S(2)}) collective-permute-start(bf16[3,128,256]{2,1,0:T(8,128)(2,1)S(1)} %choose.2.rest_0_), channel_id=1, source_target_pairs={{0,4},{4,0},{1,5},{5,1},{2,6},{6,2},{3,7},{7,3},{8,12},{12,8},{9,1... | collective-permute-start | bytes 589832 | tf_op jit(solution)/shard_map/ppermute | solution.py:363
  19.0 12.1 %collective-permute-start.1 = (bf16[2,48,2048]{2,1,0:T(8,128)(2,1)S(1)}, bf16[2,48,2048]{2,1,0:T(8,128)(2,1)S(1)}, u32[]{:S(2)}, u32[]{:S(2)}) collective-permute-start(bf16[2,48,2048]{2,1,0:T(8,128)(2,1)S(1)} %get-tuple-element.62), channel_id=1, source_target_pairs={{0,2},{1,3},{2,0},{3,1},{4,6},{5,7},{6,4},{7,5},{8,10},{9,11},{10,... | collective-permute-start | bytes 1179656 | tf_op jit(solution)/shard_map/ppermute | solution.py:363
  27.2 4.0 %collective-permute-start.10 = (bf16[2,3,128,256]{3,2,1,0:T(8,128)(2,1)S(1)}, bf16[2,3,128,256]{3,2,1,0:T(8,128)(2,1)S(1)}, u32[]{:S(2)}, u32[]{:S(2)}) collective-permute-start(bf16[2,3,128,256]{3,2,1,0:T(8,128)(2,1)S(1)} %get-tuple-element.79), channel_id=1, source_target_pairs={{0,1},{1,0},{2,3},{3,2},{4,5},{5,4},{6,7},{7,6},{8,9},{9,8},{10,11... | collective-permute-start | bytes 1179656 | tf_op jit(solution)/shard_map/ppermute | solution.py:363
  31.1 4.1 %collective-permute-start.2 = (bf16[2,48,2048]{2,1,0:T(8,128)(2,1)S(1)}, bf16[2,48,2048]{2,1,0:T(8,128)(2,1)S(1)}, u32[]{:S(2)}, u32[]{:S(2)}) collective-permute-start(bf16[2,48,2048]{2,1,0:T(8,128)(2,1)S(1)} %follow.1), channel_id=1, source_target_pairs={{0,1},{1,0},{2,3},{3,2},{4,5},{5,4},{6,7},{7,6},{8,9},{9,8},{10,11... | collective-permute-start | bytes 1179656 | tf_op jit(solution)/shard_map/ppermute | solution.py:363
  31.3 15.8 %collective-permute-start.12 = (bf16[2,3,128,256]{3,2,1,0:T(8,128)(2,1)S(1)}, bf16[2,3,128,256]{3,2,1,0:T(8,128)(2,1)S(1)}, u32[]{:S(2)}, u32[]{:S(2)}) collective-permute-start(bf16[2,3,128,256]{3,2,1,0:T(8,128)(2,1)S(1)} %get-tuple-element.83), channel_id=1, source_target_pairs={{0,2},{1,3},{2,0},{3,1},{4,6},{5,7},{6,4},{7,5},{8,10},{9,11},{10,... | collective-permute-start | bytes 1179656 | tf_op jit(solution)/shard_map/ppermute | solution.py:363
  32.1 13.3 %collective-permute-start.13 = (bf16[3,128,256]{2,1,0:T(8,128)(2,1)S(1)}, bf16[3,128,256]{2,1,0:T(8,128)(2,1)S(1)}, u32[]{:S(2)}, u32[]{:S(2)}) collective-permute-start(bf16[3,128,256]{2,1,0:T(8,128)(2,1)S(1)} %get-tuple-element.90.rest_1_), channel_id=1, source_target_pairs={{0,4},{4,0},{1,5},{5,1},{2,6},{6,2},{3,7},{7,3},{8,12},{12,8},{9,1... | collective-permute-start | bytes 589832 | tf_op jit(solution)/shard_map/ppermute | solution.py:363
  35.8 21.1 %collective-permute-start.11 = (bf16[2,3,128,256]{3,2,1,0:T(8,128)(2,1)S(1)}, bf16[2,3,128,256]{3,2,1,0:T(8,128)(2,1)S(1)}, u32[]{:S(2)}, u32[]{:S(2)}) collective-permute-start(bf16[2,3,128,256]{3,2,1,0:T(8,128)(2,1)S(1)} %get-tuple-element.83), channel_id=1, source_target_pairs={{2,4},{3,5},{4,2},{5,3},{10,12},{11,13},{12,10},{13,11},{18,20},{1... | collective-permute-start | bytes 1179656 | tf_op jit(solution)/shard_map/ppermute | solution.py:492
  47.0 15.9 %collective-permute-start.14 = (bf16[2,3,128,256]{3,2,1,0:T(8,128)(2,1)S(1)}, bf16[2,3,128,256]{3,2,1,0:T(8,128)(2,1)S(1)}, u32[]{:S(2)}, u32[]{:S(2)}) collective-permute-start(bf16[2,3,128,256]{3,2,1,0:T(8,128)(2,1)S(1)} %collective-permute-done.12.rest_2_.rest_0_), channel_id=1, source_target_pairs={{2,6},{3,7},{4,0},{5,1},{10,14},{11,15},{12,8},{13,9},{18,22},{19,... | collective-permute-start | bytes 1179656 | tf_op jit(solution)/shard_map/ppermute | solution.py:493
  49.2 17.4 %collective-permute-start.15 = (bf16[6,3,16,256]{3,2,1,0:T(8,128)(2,1)S(1)}, bf16[6,3,16,256]{3,2,1,0:T(8,128)(2,1)S(1)}, u32[]{:S(2)}, u32[]{:S(2)}) collective-permute-start(bf16[6,3,16,256]{3,2,1,0:T(8,128)(2,1)S(1)} %get-tuple-element.94), channel_id=1, source_target_pairs={{0,0},{1,25},{2,10},{3,19},{4,4},{5,29},{6,14},{7,23},{8,8},{9,17}... | collective-permute-start | bytes 442376 | tf_op jit(solution)/shard_map/ppermute | solution.py:475
  49.9 16.7 %collective-permute-start.16 = (bf16[6,3,16,256]{3,2,1,0:T(8,128)(2,1)S(1)}, bf16[6,3,16,256]{3,2,1,0:T(8,128)(2,1)S(1)}, u32[]{:S(2)}, u32[]{:S(2)}) collective-permute-start(bf16[6,3,16,256]{3,2,1,0:T(8,128)(2,1)S(1)} %get-tuple-element.95), channel_id=1, source_target_pairs={{0,1},{1,24},{2,11},{3,18},{4,5},{5,28},{6,15},{7,22},{8,9},{9,16}... | collective-permute-start | bytes 442376 | tf_op jit(solution)/shard_map/ppermute | solution.py:475
  53.0 13.6 %collective-permute-start.17 = (bf16[6,3,16,256]{3,2,1,0:T(8,128)(2,1)S(1)}, bf16[6,3,16,256]{3,2,1,0:T(8,128)(2,1)S(1)}, u32[]{:S(2)}, u32[]{:S(2)}) collective-permute-start(bf16[6,3,16,256]{3,2,1,0:T(8,128)(2,1)S(1)} %get-tuple-element.96), channel_id=1, source_target_pairs={{0,2},{1,27},{2,8},{3,17},{4,6},{5,31},{6,12},{7,21},{8,10},{9,19}... | collective-permute-start | bytes 442376 | tf_op jit(solution)/shard_map/ppermute | solution.py:475
  57.0 11.1 %collective-permute-start.18 = (bf16[6,3,16,256]{3,2,1,0:T(8,128)(2,1)S(1)}, bf16[6,3,16,256]{3,2,1,0:T(8,128)(2,1)S(1)}, u32[]{:S(2)}, u32[]{:S(2)}) collective-permute-start(bf16[6,3,16,256]{3,2,1,0:T(8,128)(2,1)S(1)} %get-tuple-element.97), channel_id=1, source_target_pairs={{0,3},{1,26},{2,9},{3,16},{4,7},{5,30},{6,13},{7,20},{8,11},{9,18}... | collective-permute-start | bytes 442376 | tf_op jit(solution)/shard_map/ppermute | solution.py:475
  68.1 1.6 %collective-permute-start.19 = (bf16[2,48,1536]{2,1,0:T(8,128)(2,1)S(1)}, bf16[2,48,1536]{2,1,0:T(8,128)(2,1)S(1)}, u32[]{:S(2)}, u32[]{:S(2)}) collective-permute-start(bf16[2,48,1536]{2,1,0:T(8,128)(2,1)S(1)} %get-tuple-element.106), channel_id=1, source_target_pairs={{0,1},{1,0},{2,3},{3,2},{4,5},{5,4},{6,7},{7,6},{8,9},{9,8},{10,11... | collective-permute-start | bytes 884744 | tf_op jit(solution)/shard_map/ppermute | solution.py:363
  69.7 11.6 %collective-permute-start.20 = (bf16[2,48,1536]{2,1,0:T(8,128)(2,1)S(1)}, bf16[2,48,1536]{2,1,0:T(8,128)(2,1)S(1)}, u32[]{:S(2)}, u32[]{:S(2)}) collective-permute-start(bf16[2,48,1536]{2,1,0:T(8,128)(2,1)S(1)} %get-tuple-element.109), channel_id=1, source_target_pairs={{0,2},{1,3},{2,0},{3,1},{4,6},{5,7},{6,4},{7,5},{8,10},{9,11},{10,... | collective-permute-start | bytes 884744 | tf_op jit(solution)/shard_map/ppermute | solution.py:363
  72.1 4.7 %collective-permute-start.21 = (bf16[2,3,16,256]{3,2,1,0:T(8,128)(2,1)S(1)}, bf16[2,3,16,256]{3,2,1,0:T(8,128)(2,1)S(1)}, u32[]{:S(2)}, u32[]{:S(2)}) collective-permute-start(bf16[2,3,16,256]{3,2,1,0:T(8,128)(2,1)S(1)} %get-tuple-element.112), channel_id=1, source_target_pairs={{0,0},{1,25},{2,10},{3,19},{4,4},{5,29},{6,14},{7,23},{8,8},{9,17}... | collective-permute-start | bytes 147464 | tf_op jit(solution)/shard_map/ppermute | solution.py:475
  72.8 5.7 %collective-permute-start.22 = (bf16[2,3,16,256]{3,2,1,0:T(8,128)(2,1)S(1)}, bf16[2,3,16,256]{3,2,1,0:T(8,128)(2,1)S(1)}, u32[]{:S(2)}, u32[]{:S(2)}) collective-permute-start(bf16[2,3,16,256]{3,2,1,0:T(8,128)(2,1)S(1)} %get-tuple-element.113), channel_id=1, source_target_pairs={{0,1},{1,24},{2,11},{3,18},{4,5},{5,28},{6,15},{7,22},{8,9},{9,16}... | collective-permute-start | bytes 147464 | tf_op jit(solution)/shard_map/ppermute | solution.py:475
  74.7 6.6 %collective-permute-start.23 = (bf16[2,3,16,256]{3,2,1,0:T(8,128)(2,1)S(1)}, bf16[2,3,16,256]{3,2,1,0:T(8,128)(2,1)S(1)}, u32[]{:S(2)}, u32[]{:S(2)}) collective-permute-start(bf16[2,3,16,256]{3,2,1,0:T(8,128)(2,1)S(1)} %get-tuple-element.114), channel_id=1, source_target_pairs={{0,2},{1,27},{2,8},{3,17},{4,6},{5,31},{6,12},{7,21},{8,10},{9,19}... | collective-permute-start | bytes 147464 | tf_op jit(solution)/shard_map/ppermute | solution.py:475
  76.1 5.2 %collective-permute-start.24 = (bf16[2,3,16,256]{3,2,1,0:T(8,128)(2,1)S(1)}, bf16[2,3,16,256]{3,2,1,0:T(8,128)(2,1)S(1)}, u32[]{:S(2)}, u32[]{:S(2)}) collective-permute-start(bf16[2,3,16,256]{3,2,1,0:T(8,128)(2,1)S(1)} %get-tuple-element.115), channel_id=1, source_target_pairs={{0,3},{1,26},{2,9},{3,16},{4,7},{5,30},{6,13},{7,20},{8,11},{9,18}... | collective-permute-start | bytes 147464 | tf_op jit(solution)/shard_map/ppermute | solution.py:475
